TPU v7x, 256 devices: a whole 4x4x8 slice. The times are simulated.
256 devices in a mesh: member: 8 (over y, core), lon: 16 (over z, x_lo), lat: 2 (over x_hi).
Axes of the slice: x: 4 (x_hi: 2, x_lo: 2; x = x_hi * 2 + x_lo), y: 4, z: 8, core: 2. Of those that a mesh axis runs over, the one named last changes fastest.
Arguments:
- member_state: float32 [8, 16, 256, 6144], P('member', None, 'lat', 'lon'), may hold values from -12 to 12
- column_depth: float32 [256, 6144], P('lat', 'lon'), may hold values from 0.5 to 2
- rotation: float32 [256, 6144], P('lat', 'lon'), may hold values from -0.2 to 0.2
- diffusivity: float32 [5, 256, 6144], P(None, 'lat', 'lon'), may hold values from 0.02 to 0.2
- ocean_mask: int32 [256, 6144], P('lat', 'lon'), may hold values from 0 to 1, as said below
- region_id: int32 [256, 6144], P('lat', 'lon'), may hold values from 0 to 15, as said below
- target_rms: float32 [16], replicated, may hold values from 0.2 to 1
Outputs:
- bred_state: float32 [8, 16, 256, 6144], P('member', None, 'lat', 'lon')
- growth_rms: float32 [8, 16], P('member')
Inputs may be any that keep to these rules, and one draw needn't show every extreme that they name: `ocean_mask`: 1 marks an ocean cell. `region_id`: every region id holds ocean cells.
All inputs are finite; a program needn't handle non-finite values.
Results may differ from a plain program's by a relative error of at most 0.0003.
Values sent between devices are 32-bit elements; how exact they have to be, the bound alone decides.
No kernel may reach another device: no remote copies, remote signals or barrier semaphores. Data moves between devices by JAX's collectives and lax.ppermute only.
A program may use at most 64 MiB of HBM per device.

v0:
```python
import functools
import jax
import jax.numpy as jnp
from jax import lax
from jax.experimental import pallas as pl
from jax.experimental.pallas import tpu as pltpu
from jax.sharding import PartitionSpec as P

LEV = 5
CH = 16
FIELDS = 24
REGIONS = 16
ROWS, COLS = 128, 384
ROWS_X, COLS_X = 136, 512
HALO = 4
EPSILON = 1e-06
VMEM = pl.BlockSpec(memory_space=pltpu.VMEM)
ANY = pl.BlockSpec(memory_space=pl.ANY)
SMEM = pl.BlockSpec(memory_space=pltpu.SMEM)
F32 = jnp.float32


def call(kernel, out, in_specs, out_specs, scratch=(), flops=1 << 22, nbytes=1 << 23):
    return pl.pallas_call(
        kernel,
        out_shape=out,
        in_specs=in_specs,
        out_specs=out_specs,
        scratch_shapes=list(scratch),
        compiler_params=pltpu.CompilerParams(vmem_limit_bytes=48 << 20),
        cost_estimate=pl.CostEstimate(flops=flops, bytes_accessed=nbytes, transcendentals=0),
    )


def iota(shape, dim):
    return lax.broadcasted_iota(jnp.int32, shape, dim)


def pack_kernel(lat, state, depth, rotation, diff, mask, west, east, rows, c_west, c_east):
    def field(k, r, c):
        if k < CH:
            return state[k, r, c]
        if k == CH:
            return depth[r, c]
        if k == CH + 1:
            return rotation[r, c]
        if k < CH + 2 + LEV:
            return diff[k - CH - 2, r, c]
        return mask[r, c].astype(F32)

    lane = iota((ROWS, 128), 1)
    full = slice(0, ROWS)
    w = jnp.zeros((ROWS, 128), F32)
    e = jnp.zeros((ROWS, 128), F32)
    for k in range(FIELDS):
        own = (lane >= HALO * k) & (lane < HALO * k + HALO)
        a = field(k, full, slice(0, 128))
        b = field(k, full, slice(COLS - 128, COLS))
        w = jnp.where(own, pltpu.roll(a, HALO * k, 1) if k else a, w)
        e = jnp.where(own, pltpu.roll(b, HALO * k + HALO, 1), e)
    west[...] = w
    east[...] = e
    upper = lat[0] == 0
    r0 = pl.multiple_of(jnp.where(upper, ROWS - 8, 0), 8)
    tile = pl.ds(r0, 8)
    c_west[...] = west[tile, :]
    c_east[...] = east[tile, :]
    sub = iota((8, COLS), 0)
    mine = (sub >= 4) == upper
    half = FIELDS // 2
    for k in range(half):
        x = field(k, tile, slice(0, COLS))
        y = field(k + half, tile, slice(0, COLS))
        rows[8 * k : 8 * k + 8, :] = jnp.where(mine, x, pltpu.roll(y, 4, 0))


def pack(lat, state, statics):
    shapes = [(ROWS, 128), (ROWS, 128), (FIELDS * 4, COLS), (8, 128), (8, 128)]
    return call(
        pack_kernel,
        [jax.ShapeDtypeStruct(s, F32) for s in shapes],
        [SMEM] + [VMEM] * 5,
        [VMEM] * 5,
    )(lat, state, *statics)


def exchange(west, east, rows, c_west, c_east):
    n = lax.axis_size("lon")
    up = [(i, (i + 1) % n) for i in range(n)]
    down = [((i + 1) % n, i) for i in range(n)]
    other = [(0, 1), (1, 0)]
    both = ("lon", "lat")
    up2 = [(2 * i + j, 2 * k + 1 - j) for i, k in up for j in range(2)]
    down2 = [(2 * i + j, 2 * k + 1 - j) for i, k in down for j in range(2)]
    return (
        lax.ppermute(east, "lon", up),
        lax.ppermute(west, "lon", down),
        lax.ppermute(rows, "lat", other),
        lax.ppermute(c_east, both, up2),
        lax.ppermute(c_west, both, down2),
    )


def fill_halo(x, count, half, lat, from_west, from_east, rows, c_west, c_east):
    def margin(k, w, e):
        lane = iota(w.shape, 1)
        s = (128 - HALO * k) % 128
        e = pltpu.roll(e, s, 1) if s else e
        return jnp.where(lane < 64, e, pltpu.roll(w, (124 - HALO * k) % 128, 1))

    sub = iota((8, COLS), 0)
    got = (sub < 4) == (lat[0] == 0)
    got_c = got[:, :128]
    w, e = from_west[...], from_east[...]
    cw, ce = c_west[...], c_east[...]
    for k in range(count):
        x[k, 0:ROWS, COLS:COLS_X] = margin(k, w, e)
        j = k % half
        tile = rows[8 * j : 8 * j + 8, :]
        if k >= half:
            tile = pltpu.roll(tile, 4, 0)
        x[k, ROWS:ROWS_X, 0:COLS] = jnp.where(got, tile, 0.0)
        x[k, ROWS:ROWS_X, COLS:COLS_X] = jnp.where(got_c, margin(k, cw, ce), 0.0)


TILES = ROWS_X // 8


def tile_at(t):
    return pl.ds(pl.multiple_of(t * 8, 8), 8)


def step(x, static, ub, vb, h2, store, tiles):
    sub = iota((8, COLS_X), 0)

    def around(t):
        return tile_at(jnp.where(t == 0, TILES - 1, t - 1)), tile_at(t), tile_at(jnp.where(t == TILES - 1, 0, t + 1))

    def north(cur, nxt):
        return pltpu.roll(jnp.where(sub == 0, nxt, cur), 7, 0)

    def south(cur, prv):
        return pltpu.roll(jnp.where(sub == 7, prv, cur), 1, 0)

    def east(cur):
        return pltpu.roll(cur, COLS_X - 1, 1)

    def west(cur):
        return pltpu.roll(cur, 1, 1)

    def sums(t, _):
        c = tile_at(t)
        u = x[1, c, :]
        v = x[1 + LEV, c, :]
        for l in range(1, LEV):
            u = u + x[1 + l, c, :]
            v = v + x[1 + LEV + l, c, :]
        ub[c, :] = east(u) - west(u)
        vb[c, :] = v
        return 0

    lax.fori_loop(0, TILES, sums, 0)

    def surface(t, _):
        p, c, n = around(t)
        v = vb[c, :]
        div = ub[c, :] + (north(v, vb[n, :]) - south(v, vb[p, :]))
        h2[c, :] = static[7, c, :] * (x[0, c, :] - (0.25 / LEV) * static[0, c, :] * div)
        return 0

    lax.fori_loop(0, TILES, surface, 0)

    def rest(t, _):
        p, c, n = around(t)
        oc = static[7, c, :]
        rot = static[1, c, :]
        h = h2[c, :]
        store(0, c, h)
        px = 0.25 * (east(h) - west(h))
        py = 0.25 * (north(h, h2[n, :]) - south(h, h2[p, :]))
        for l in range(LEV):
            k = static[2 + l, c, :]

            def near(ch):
                q = x[ch, c, :]
                return q, east(q), west(q), north(q, x[ch, n, :]), south(q, x[ch, p, :])

            q, e, w, a, b = near(1 + 2 * LEV + l)
            cx = e - w
            cy = a - b
            c0 = q + k * ((e + w) + (a + b) - 4.0 * q)
            u, e, w, a, b = near(1 + l)
            lap_u = (e + w) + (a + b) - 4.0 * u
            v, e, w, a, b = near(1 + LEV + l)
            lap_v = (e + w) + (a + b) - 4.0 * v
            u2 = oc * (u + rot * v - px - 0.1 * cx + k * lap_u)
            v2 = oc * (v - rot * u - py - 0.1 * cy + k * lap_v)
            store(1 + l, c, u2)
            store(1 + LEV + l, c, v2)
            store(1 + 2 * LEV + l, c, oc * (c0 - 0.05 * (u2 * cx + v2 * cy)))
        return 0

    lax.fori_loop(0, tiles, rest, 0)


def two_steps(x, static, y, ub, vb, h2, out):
    def keep(ch, c, value):
        y[ch, c, :] = value

    def give(ch, c, value):
        out[ch, c, :] = value[:, :COLS]

    step(x, static, ub, vb, h2, keep, TILES)
    step(y, static, ub, vb, h2, give, ROWS // 8)


STEP_SCRATCH = [
    pltpu.VMEM((CH, ROWS_X, COLS_X), F32),
    pltpu.VMEM((ROWS_X, COLS_X), F32),
    pltpu.VMEM((ROWS_X, COLS_X), F32),
    pltpu.VMEM((ROWS_X, COLS_X), F32),
]


def own_kernel(lat, state, depth, rotation, diff, mask, fw, fe, rows, cw, ce, out, x, y, ub, vb, h2, sem):
    main = (slice(0, ROWS), slice(0, COLS))
    copies = [
        pltpu.make_async_copy(state, x.at[(slice(0, CH),) + main], sem.at[0]),
        pltpu.make_async_copy(depth, x.at[(CH,) + main], sem.at[1]),
        pltpu.make_async_copy(rotation, x.at[(CH + 1,) + main], sem.at[2]),
        pltpu.make_async_copy(diff, x.at[(slice(CH + 2, CH + 2 + LEV),) + main], sem.at[3]),
    ]
    for copy in copies:
        copy.start()
    x[(FIELDS - 1,) + main] = mask[...].astype(F32)
    fill_halo(x, FIELDS, FIELDS // 2, lat, fw, fe, rows, cw, ce)
    for copy in copies:
        copy.wait()
    two_steps(x, x.at[CH:FIELDS], y, ub, vb, h2, out)


def own_steps(lat, state, statics, halos):
    return call(
        own_kernel,
        jax.ShapeDtypeStruct((CH, ROWS, COLS), F32),
        [SMEM] + [ANY] * 4 + [VMEM] * 6,
        VMEM,
        [pltpu.VMEM((FIELDS, ROWS_X, COLS_X), F32)] + STEP_SCRATCH + [pltpu.SemaphoreType.DMA((4,))],
        flops=1 << 28,
    )(lat, state, *statics, *halos)


def broadcast(state):
    m = lax.axis_index("member")
    a, b = state[: CH // 2], state[CH // 2 :]

    def send(value, pairs):
        return lax.ppermute(value, "member", pairs)

    first = m == 0
    p1 = send(a, [(0, 2)])
    m1 = send(b, [(0, 7)])
    u = jnp.where(first, b, p1)
    v = jnp.where(first, a, jnp.where(m == 2, p1, m1))
    p2 = send(u, [(0, 2), (2, 4)])
    m2 = send(v, [(0, 7), (7, 5)])
    e1 = send(v, [(0, 1), (2, 3), (7, 6)])
    e2 = send(jnp.where(first, b, jnp.where(m < 5, p2, m2)), [(0, 1), (2, 3), (4, 5), (5, 4), (7, 6)])

    def pick(options):
        value = options[-1]
        for i in range(len(options) - 1):
            value = jnp.where(m == i, options[i], value)
        return value

    top = pick([a, e1, p1, e1, p2, e2, e2, m2])
    low = pick([b, e2, p2, e2, e2, m2, e1, m1])
    return top, low


def sums_kernel(own, top, low, mask, region, out):
    half = CH // 2

    def body(t, carry):
        c = tile_at(t)
        acc = None
        for k in range(CH):
            ref = top[k, c, :] if k < half else low[k - half, c, :]
            d = own[k, c, :] - ref
            acc = d * d if acc is None else acc + d * d
        oc = mask[c, :].astype(F32)
        cell = oc * acc
        reg = region[c, :]
        new = []
        for r in range(REGIONS):
            hit = reg == r
            s = jnp.where(hit, cell, 0.0)
            n = jnp.where(hit, oc, 0.0)
            new.append(carry[2 * r] + (s[:, :128] + s[:, 128:256] + s[:, 256:]))
            new.append(carry[2 * r + 1] + (n[:, :128] + n[:, 128:256] + n[:, 256:]))
        return tuple(new)

    zero = jnp.zeros((8, 128), F32)
    total = lax.fori_loop(0, ROWS // 8, body, (zero,) * (2 * REGIONS))
    lane = iota((8, 128), 1)
    row = zero
    for r in range(REGIONS):
        for j in range(2):
            s = jnp.sum(jnp.sum(total[2 * r + j], axis=0, keepdims=True), axis=1, keepdims=True)
            row = jnp.where(lane == REGIONS * j + r, s, row)
    for i in range(32):
        out[i] = row


def local_sums(own, top, low, mask, region):
    return call(sums_kernel, jax.ShapeDtypeStruct((32, 8, 128), F32), [VMEM] * 5, VMEM)(
        own, top, low, mask, region
    )


def final_kernel(own, top, low, region, parts, target, out, growth):
    total = parts[0]
    for i in range(1, 32):
        total = total + parts[i]
    lane = iota((8, 128), 1)
    counts = jnp.where(lane < REGIONS, pltpu.roll(total, 128 - REGIONS, 1), 1.0)
    squares = jnp.where(lane < REGIONS, total, 1.0)
    g = jnp.sqrt(squares / (counts * CH) + EPSILON)
    growth[...] = g
    factor = target[...] / g

    half = CH // 2

    def body(t, _):
        c = tile_at(t)
        reg = region[c, :]
        f = [
            jnp.take_along_axis(factor, reg[:, 128 * j : 128 * j + 128], axis=1, mode="promise_in_bounds")
            for j in range(3)
        ]
        f = jnp.concatenate(f, axis=1)
        for k in range(CH):
            ref = top[k, c, :] if k < half else low[k - half, c, :]
            out[k, c, :] = ref + f * (own[k, c, :] - ref)
        return 0

    lax.fori_loop(0, ROWS // 8, body, 0)


def rescale(own, top, low, region, parts, target):
    target = jnp.broadcast_to(jnp.pad(target, (0, 128 - REGIONS), constant_values=1.0), (8, 128))
    return call(
        final_kernel,
        [jax.ShapeDtypeStruct((CH, ROWS, COLS), F32), jax.ShapeDtypeStruct((8, 128), F32)],
        [VMEM] * 6,
        [VMEM] * 2,
    )(own, top, low, region, parts, target)


def per_device(member_state, depth, rotation, diff, mask, region, target):
    state = member_state[0]
    statics = (depth, rotation, diff, mask)
    lat = lax.axis_index("lat").astype(jnp.int32).reshape(1)
    halos = exchange(*pack(lat, state, statics))
    own = own_steps(lat, state, statics, halos)
    top, low = broadcast(own)
    parts = local_sums(own, top, low, mask, region)
    parts = lax.all_to_all(parts, ("lon", "lat"), 0, 0)
    bred, growth = rescale(own, top, low, region, parts, target)
    return bred[None], growth[:1, :REGIONS]


def solution(mesh):
    return jax.shard_map(
        per_device,
        mesh=mesh,
        in_specs=(
            P("member", None, "lat", "lon"),
            P("lat", "lon"),
            P("lat", "lon"),
            P(None, "lat", "lon"),
            P("lat", "lon"),
            P("lat", "lon"),
            P(),
        ),
        out_specs=(P("member", None, "lat", "lon"), P("member", None)),
        check_vma=False,
    )
```

profile of v0, /device:TPU:24, one launch (start us, length us, event | category | flops | bytes accessed | tf_op | source)
XLA Modules:
  0.0 138.7 jit_solution(10585297776811524136)
XLA Ops:
  0.6 0.0 copy-start.5
  0.6 1.9 %copy-done.5 = f32[1,16,128,384]{3,2,1,0:T(8,128)S(1)} copy-done((f32[1,16,128,384]{3,2,1,0:T(8,128)S(1)}, f32[1,16,128,384]{3,2,1,0:T(8,128)}, u32[]{:S(2)}) %copy-start.5) | copy-done | bytes 3145752
  2.5 1.2 copy-done.6
  3.7 0.9 copy-done.7
  4.7 0.9 copy-done.9
  5.6 0.9 copy-done.10
  6.5 0.9 shard_map.86
  7.4 3.1 %collective-permute-start.2 = (f32[96,384]{1,0:T(8,128)S(1)}, f32[96,384]{1,0:T(8,128)S(1)}, u32[]{:S(2)}, u32[]{:S(2)}) collective-permute-start(f32[96,384]{1,0:T(8,128)S(1)} %get-tuple-element.11), channel_id=1, source_target_pairs={{0,1},{1,0},{2,3},{3,2},{4,5},{5,4},{6,7},{7,6},{8,9},{9,8},{10,11... | collective-permute-start | bytes 442376 | tf_op jit(solution)/shard_map/ppermute | solution.py:98
  10.5 0.6 collective-permute-start
  11.1 5.3 %collective-permute-start.1 = (f32[128,128]{1,0:T(8,128)S(1)}, f32[128,128]{1,0:T(8,128)S(1)}, u32[]{:S(2)}, u32[]{:S(2)}) collective-permute-start(f32[128,128]{1,0:T(8,128)S(1)} %get-tuple-element.10), channel_id=1, source_target_pairs={{2,0},{4,2},{6,4},{8,6},{10,8},{12,10},{14,12},{16,14},{18,16},{20... | collective-permute-start | bytes 196616 | tf_op jit(solution)/shard_map/ppermute | solution.py:97
  16.4 0.0 collective-permute-start.3
  16.4 5.3 %collective-permute-start.4 = (f32[8,128]{1,0:T(8,128)S(1)}, f32[8,128]{1,0:T(8,128)S(1)}, u32[]{:S(2)}, u32[]{:S(2)}) collective-permute-start(f32[8,128]{1,0:T(8,128)S(1)} %get-tuple-element.13), channel_id=1, source_target_pairs={{2,1},{3,0},{4,3},{5,2},{6,5},{7,4},{8,7},{9,6},{10,9},{11,8},{12,... | collective-permute-start | bytes 12296 | tf_op jit(solution)/shard_map/ppermute | solution.py:100
  21.8 1.6 %collective-permute-done.3.cw = f32[8,128]{1,0:T(8,128)S(1)} collective-permute-done((f32[8,128]{1,0:T(8,128)S(1)}, f32[8,128]{1,0:T(8,128)S(1)}, u32[]{:S(2)}, u32[]{:S(2)}) %collective-permute-start.3) | collective-permute-done | bytes 4128 | tf_op jit(solution)/shard_map/ppermute | solution.py:99
  23.3 0.0 collective-permute-done.4.ce
  23.3 0.0 collective-permute-done.fw
  23.3 0.0 collective-permute-done.1.fe
  23.4 0.0 collective-permute-done.2.rows
  23.4 12.7 %shard_map.87.own = f32[16,128,384]{2,1,0:T(8,128)S(1)} custom-call(s32[1]{0:T(128)} %bitcast.lat, f32[16,128,384]{2,1,0:T(8,128)} %bitcast.3, f32[128,384]{1,0:T(8,128)S(1)} %copy-done.9, f32[128,384]{1,0:T(8,128)S(1)} %copy-done.10, f32[5,128,384]{2,1,0:T(8,128)S(1)} %copy-done.6, s32[128,384]{1,0:T(8,128)S(1)} %copy-done.7, ...), custom_call_target="tpu_custom_call" | custom-call | flops 268435456 | bytes 8388608 | tf_op jit(solution)/shard_map/pallas_call | solution.py:243
  36.0 0.0 copy-start
  36.0 2.1 %fusion.2 = (f32[8,128,384]{2,1,0:T(8,128)}, f32[8,128,384]{2,1,0:T(8,128)}) fusion(f32[16,128,384]{2,1,0:T(8,128)S(1)} %shard_map.87.own), kind=kLoop, calls=%fused_computation.7 | loop fusion | bytes 6291456 | tf_op jit(solution)/shard_map/slice | solution.py:255
  38.2 1.8 %collective-permute-start.5 = (f32[8,128,384]{2,1,0:T(8,128)}, f32[8,128,384]{2,1,0:T(8,128)}, u32[]{:S(2)}, u32[]{:S(2)}) collective-permute-start(f32[8,128,384]{2,1,0:T(8,128)} %get-tuple-element.21), channel_id=1, source_target_pairs={{0,64},{1,65},{2,66},{3,67},{4,68},{5,69},{6,70},{7,71},{8,72},{9,... | collective-permute-start | bytes 4718600 | tf_op jit(solution)/shard_map/ppermute | solution.py:258
  40.0 1.9 %collective-permute-start.7 = (f32[8,128,384]{2,1,0:T(8,128)}, f32[8,128,384]{2,1,0:T(8,128)}, u32[]{:S(2)}, u32[]{:S(2)}) collective-permute-start(f32[8,128,384]{2,1,0:T(8,128)} %get-tuple-element.20), channel_id=1, source_target_pairs={{0,224},{1,225},{2,226},{3,227},{4,228},{5,229},{6,230},{7,231},{8... | collective-permute-start | bytes 4718600 | tf_op jit(solution)/shard_map/ppermute | solution.py:258
  41.8 0.0 collective-permute-done.5
  41.8 0.0 collective-permute-done.7
  41.9 3.9 %select_select_fusion.3 = (f32[8,128,384]{2,1,0:T(8,128)}, f32[8,128,384]{2,1,0:T(8,128)}) fusion(f32[8,128,384]{2,1,0:T(8,128)} %collective-permute-done.5, f32[8,128,384]{2,1,0:T(8,128)} %collective-permute-done.7, pred[]{:T(512)S(6)} %eq.32, pred[]{:T(512)S(6)} %eq.15, f32[16,128,384]{2,1,0:T(8,128)S(1)} %shard_map.87.own), kind=kLoop, calls=%fused_computation.5 | loop fusion | flops 1179648 | bytes 9437186 | tf_op jit(solution)/shard_map/jit(_where)/select_n | solution.py:264
  45.7 1.8 %collective-permute-start.6 = (f32[8,128,384]{2,1,0:T(8,128)}, f32[8,128,384]{2,1,0:T(8,128)}, u32[]{:S(2)}, u32[]{:S(2)}) collective-permute-start(f32[8,128,384]{2,1,0:T(8,128)} %get-tuple-element.19), channel_id=1, source_target_pairs={{0,64},{64,128},{1,65},{65,129},{2,66},{66,130},{3,67},{67,131},{4... | collective-permute-start | bytes 4718600 | tf_op jit(solution)/shard_map/ppermute | solution.py:258
  47.6 1.9 %collective-permute-start.8 = (f32[8,128,384]{2,1,0:T(8,128)}, f32[8,128,384]{2,1,0:T(8,128)}, u32[]{:S(2)}, u32[]{:S(2)}) collective-permute-start(f32[8,128,384]{2,1,0:T(8,128)} %get-tuple-element.18), channel_id=1, source_target_pairs={{0,224},{224,160},{1,225},{225,161},{2,226},{226,162},{3,227},{227... | collective-permute-start | bytes 4718600 | tf_op jit(solution)/shard_map/ppermute | solution.py:258
  49.5 1.3 collective-permute-start.10
  50.7 0.0 collective-permute-done.6
  50.7 0.0 collective-permute-done.8
  50.8 2.8 %select_select_fusion.2 = f32[8,128,384]{2,1,0:T(8,128)} fusion(f32[8,128,384]{2,1,0:T(8,128)} %collective-permute-done.6, f32[8,128,384]{2,1,0:T(8,128)} %collective-permute-done.8, pred[]{:T(512)S(6)} %lt.3, pred[]{:T(512)S(6)} %eq.15, f32[16,128,384]{2,1,0:T(8,128)S(1)} %shard_map.87.own), kind=kLoop, calls=%fused_computation.4 | loop fusion | flops 786432 | bytes 6291458 | tf_op jit(solution)/shard_map/jit(_where)/select_n | solution.py:268
  53.6 1.3 collective-permute-start.9
  54.9 0.0 copy-start.8
  54.9 0.0 copy-start.11
  54.9 20.1 %collective-permute-done.10 = f32[8,128,384]{2,1,0:T(8,128)} collective-permute-done((f32[8,128,384]{2,1,0:T(8,128)}, f32[8,128,384]{2,1,0:T(8,128)}, u32[]{:S(2)}, u32[]{:S(2)}) %collective-permute-start.10) | collective-permute-done | bytes 1572896 | tf_op jit(solution)/shard_map/ppermute | solution.py:258
  75.0 24.1 %collective-permute-done.9 = f32[8,128,384]{2,1,0:T(8,128)} collective-permute-done((f32[8,128,384]{2,1,0:T(8,128)}, f32[8,128,384]{2,1,0:T(8,128)}, u32[]{:S(2)}, u32[]{:S(2)}) %collective-permute-start.9) | collective-permute-done | bytes 1572896 | tf_op jit(solution)/shard_map/ppermute | solution.py:258
  99.1 0.0 copy-done
  99.1 4.4 %fusion.1 = (f32[8,128,384]{2,1,0:T(8,128)S(1)}, f32[8,128,384]{2,1,0:T(8,128)S(1)}) fusion(f32[8,128,384]{2,1,0:T(8,128)} %collective-permute-done.10, f32[8,128,384]{2,1,0:T(8,128)} %collective-permute-done.8, f32[8,128,384]{2,1,0:T(8,128)} %collective-permute-done.9, f32[8,128,384]{2,1,0:T(8,128)} %collective-permute-done.6, ...), kind=kLoop, calls=%fused_computation.3 | loop fusion | flops 5505024 | bytes 15728647 | tf_op jit(solution)/shard_map/jit(_where)/select_n | solution.py:273
  103.5 0.0 copy-start.12
  103.5 3.7 %shard_map.88 = f32[32,8,128]{2,1,0:T(8,128)} custom-call(f32[16,128,384]{2,1,0:T(8,128)} %copy-done, f32[8,128,384]{2,1,0:T(8,128)S(1)} %get-tuple-element.17.top, f32[8,128,384]{2,1,0:T(8,128)S(1)} %get-tuple-element.16.low, s32[128,384]{1,0:T(8,128)S(1)} %copy-done.8, s32[128,384]{1,0:T(8,128)S(1)} %copy-done.11), custom_call_target="tpu_custom_call" | custom-call | flops 4194304 | bytes 8388608 | tf_op jit(solution)/shard_map/pallas_call | solution.py:316
  107.2 1.2 copy-done.1
  108.4 1.1 copy-done.3
  109.5 9.8 %all-to-all-start = ((f32[32,8,128]{2,1,0:T(8,128)}), f32[32,8,128]{2,1,0:T(8,128)S(1)}, u32[]{:S(2)}, u32[]{:S(2)}) async-start(f32[32,8,128]{2,1,0:T(8,128)} %shard_map.88), calls=%async_computation | async-start | bytes 262144 | tf_op jit(solution)/shard_map/all_to_all | solution.py:368
  119.3 10.8 %all-to-all-done.parts = f32[32,8,128]{2,1,0:T(8,128)S(1)} async-done(((f32[32,8,128]{2,1,0:T(8,128)}), f32[32,8,128]{2,1,0:T(8,128)S(1)}, u32[]{:S(2)}, u32[]{:S(2)}) %all-to-all-start) | async-done | bytes 131104 | tf_op jit(solution)/shard_map/all_to_all | solution.py:368
  130.1 1.4 %copy-done.2 = f32[8,128,384]{2,1,0:T(8,128)S(1)} copy-done((f32[8,128,384]{2,1,0:T(8,128)S(1)}, f32[8,128,384]{2,1,0:T(8,128)}, u32[]{:S(2)}) %copy-start.2) | copy-done | bytes 1572888
  131.5 1.4 %copy-done.4 = f32[8,128,384]{2,1,0:T(8,128)S(1)} copy-done((f32[8,128,384]{2,1,0:T(8,128)S(1)}, f32[8,128,384]{2,1,0:T(8,128)}, u32[]{:S(2)}) %copy-start.4) | copy-done | bytes 1572888
  132.9 5.3 %shard_map.89 = (f32[16,128,384]{2,1,0:T(8,128)}, f32[8,128]{1,0:T(8,128)S(1)}) custom-call(f32[16,128,384]{2,1,0:T(8,128)} %copy-done, f32[8,128,384]{2,1,0:T(8,128)S(1)} %copy-done.4, f32[8,128,384]{2,1,0:T(8,128)S(1)} %copy-done.2, s32[128,384]{1,0:T(8,128)S(1)} %copy-done.11, f32[32,8,128]{2,1,0:T(8,128)S(1)} %all-to-all-done.parts, ...), custom_call_target="tpu_custom_call" | custom-call | flops 4194304 | bytes 8388608 | tf_op jit(solution)/shard_map/pallas_call | solution.py:352
  138.1 0.5 slice.11
  (13 shorter events, 0.0 us)
Async XLA Ops:
  0.6 1.9 %copy-start.5 = (f32[1,16,128,384]{3,2,1,0:T(8,128)S(1)}, f32[1,16,128,384]{3,2,1,0:T(8,128)}, u32[]{:S(2)}) copy-start(f32[1,16,128,384]{3,2,1,0:T(8,128)} %param.7) | copy-start | bytes 9437188
  2.5 1.2 copy-start.6
  3.7 0.9 copy-start.7
  4.7 0.9 copy-start.9
  5.6 0.9 copy-start.10
  7.4 15.9 %collective-permute-start.2 = (f32[96,384]{1,0:T(8,128)S(1)}, f32[96,384]{1,0:T(8,128)S(1)}, u32[]{:S(2)}, u32[]{:S(2)}) collective-permute-start(f32[96,384]{1,0:T(8,128)S(1)} %get-tuple-element.11), channel_id=1, source_target_pairs={{0,1},{1,0},{2,3},{3,2},{4,5},{5,4},{6,7},{7,6},{8,9},{9,8},{10,11... | collective-permute-start | bytes 442376 | tf_op jit(solution)/shard_map/ppermute | solution.py:98
  10.5 12.8 %collective-permute-start = (f32[128,128]{1,0:T(8,128)S(1)}, f32[128,128]{1,0:T(8,128)S(1)}, u32[]{:S(2)}, u32[]{:S(2)}) collective-permute-start(f32[128,128]{1,0:T(8,128)S(1)} %get-tuple-element.9), channel_id=1, source_target_pairs={{0,2},{2,4},{4,6},{6,8},{8,10},{10,12},{12,14},{14,16},{16,18},{18... | collective-permute-start | bytes 196616 | tf_op jit(solution)/shard_map/ppermute | solution.py:96
  11.1 12.2 %collective-permute-start.1 = (f32[128,128]{1,0:T(8,128)S(1)}, f32[128,128]{1,0:T(8,128)S(1)}, u32[]{:S(2)}, u32[]{:S(2)}) collective-permute-start(f32[128,128]{1,0:T(8,128)S(1)} %get-tuple-element.10), channel_id=1, source_target_pairs={{2,0},{4,2},{6,4},{8,6},{10,8},{12,10},{14,12},{16,14},{18,16},{20... | collective-permute-start | bytes 196616 | tf_op jit(solution)/shard_map/ppermute | solution.py:97
  16.4 6.9 %collective-permute-start.3 = (f32[8,128]{1,0:T(8,128)S(1)}, f32[8,128]{1,0:T(8,128)S(1)}, u32[]{:S(2)}, u32[]{:S(2)}) collective-permute-start(f32[8,128]{1,0:T(8,128)S(1)} %get-tuple-element.12), channel_id=1, source_target_pairs={{0,3},{1,2},{2,5},{3,4},{4,7},{5,6},{6,9},{7,8},{8,11},{9,10},{10,... | collective-permute-start | bytes 12296 | tf_op jit(solution)/shard_map/ppermute | solution.py:99
  16.4 6.9 %collective-permute-start.4 = (f32[8,128]{1,0:T(8,128)S(1)}, f32[8,128]{1,0:T(8,128)S(1)}, u32[]{:S(2)}, u32[]{:S(2)}) collective-permute-start(f32[8,128]{1,0:T(8,128)S(1)} %get-tuple-element.13), channel_id=1, source_target_pairs={{2,1},{3,0},{4,3},{5,2},{6,5},{7,4},{8,7},{9,6},{10,9},{11,8},{12,... | collective-permute-start | bytes 12296 | tf_op jit(solution)/shard_map/ppermute | solution.py:100
  36.0 63.0 %copy-start = (f32[16,128,384]{2,1,0:T(8,128)}, f32[16,128,384]{2,1,0:T(8,128)S(1)}, u32[]{:S(2)}) copy-start(f32[16,128,384]{2,1,0:T(8,128)S(1)} %shard_map.87.own) | copy-start | bytes 9437188
  38.2 3.7 %collective-permute-start.5 = (f32[8,128,384]{2,1,0:T(8,128)}, f32[8,128,384]{2,1,0:T(8,128)}, u32[]{:S(2)}, u32[]{:S(2)}) collective-permute-start(f32[8,128,384]{2,1,0:T(8,128)} %get-tuple-element.21), channel_id=1, source_target_pairs={{0,64},{1,65},{2,66},{3,67},{4,68},{5,69},{6,70},{7,71},{8,72},{9,... | collective-permute-start | bytes 4718600 | tf_op jit(solution)/shard_map/ppermute | solution.py:258
  40.0 1.9 %collective-permute-start.7 = (f32[8,128,384]{2,1,0:T(8,128)}, f32[8,128,384]{2,1,0:T(8,128)}, u32[]{:S(2)}, u32[]{:S(2)}) collective-permute-start(f32[8,128,384]{2,1,0:T(8,128)} %get-tuple-element.20), channel_id=1, source_target_pairs={{0,224},{1,225},{2,226},{3,227},{4,228},{5,229},{6,230},{7,231},{8... | collective-permute-start | bytes 4718600 | tf_op jit(solution)/shard_map/ppermute | solution.py:258
  45.7 5.0 %collective-permute-start.6 = (f32[8,128,384]{2,1,0:T(8,128)}, f32[8,128,384]{2,1,0:T(8,128)}, u32[]{:S(2)}, u32[]{:S(2)}) collective-permute-start(f32[8,128,384]{2,1,0:T(8,128)} %get-tuple-element.19), channel_id=1, source_target_pairs={{0,64},{64,128},{1,65},{65,129},{2,66},{66,130},{3,67},{67,131},{4... | collective-permute-start | bytes 4718600 | tf_op jit(solution)/shard_map/ppermute | solution.py:258
  47.6 3.2 %collective-permute-start.8 = (f32[8,128,384]{2,1,0:T(8,128)}, f32[8,128,384]{2,1,0:T(8,128)}, u32[]{:S(2)}, u32[]{:S(2)}) collective-permute-start(f32[8,128,384]{2,1,0:T(8,128)} %get-tuple-element.18), channel_id=1, source_target_pairs={{0,224},{224,160},{1,225},{225,161},{2,226},{226,162},{3,227},{227... | collective-permute-start | bytes 4718600 | tf_op jit(solution)/shard_map/ppermute | solution.py:258
  49.5 25.5 %collective-permute-start.10 = (f32[8,128,384]{2,1,0:T(8,128)}, f32[8,128,384]{2,1,0:T(8,128)}, u32[]{:S(2)}, u32[]{:S(2)}) collective-permute-start(f32[8,128,384]{2,1,0:T(8,128)} %get-tuple-element.18), channel_id=1, source_target_pairs={{0,32},{64,96},{224,192},{1,33},{65,97},{225,193},{2,34},{66,98},{... | collective-permute-start | bytes 4718600 | tf_op jit(solution)/shard_map/ppermute | solution.py:258
  53.6 45.5 %collective-permute-start.9 = (f32[8,128,384]{2,1,0:T(8,128)}, f32[8,128,384]{2,1,0:T(8,128)}, u32[]{:S(2)}, u32[]{:S(2)}) collective-permute-start(f32[8,128,384]{2,1,0:T(8,128)} %select_select_fusion.2), channel_id=1, source_target_pairs={{0,32},{64,96},{128,160},{160,128},{224,192},{1,33},{65,97},{129,1... | collective-permute-start | bytes 4718600 | tf_op jit(solution)/shard_map/ppermute | solution.py:258
  54.9 48.6 %copy-start.8 = (s32[128,384]{1,0:T(8,128)S(1)}, s32[128,384]{1,0:T(8,128)}, u32[]{:S(2)}) copy-start(s32[128,384]{1,0:T(8,128)} %mask.5) | copy-start | bytes 589828
  54.9 48.6 %copy-start.11 = (s32[128,384]{1,0:T(8,128)S(1)}, s32[128,384]{1,0:T(8,128)}, u32[]{:S(2)}) copy-start(s32[128,384]{1,0:T(8,128)} %region.3) | copy-start | bytes 589828
  103.5 15.8 %copy-start.12 = (f32[16]{0:T(128)S(1)}, f32[16]{0:T(128)}, u32[]{:S(2)}) copy-start(f32[16]{0:T(128)} %param.13) | copy-start | bytes 196
  107.2 1.2 copy-start.1
  108.3 1.1 copy-start.3
  109.5 20.6 %all-to-all-start = ((f32[32,8,128]{2,1,0:T(8,128)}), f32[32,8,128]{2,1,0:T(8,128)S(1)}, u32[]{:S(2)}, u32[]{:S(2)}) async-start(f32[32,8,128]{2,1,0:T(8,128)} %shard_map.88), calls=%async_computation | async-start | bytes 262144 | tf_op jit(solution)/shard_map/all_to_all | solution.py:368
  130.1 1.4 %copy-start.2 = (f32[8,128,384]{2,1,0:T(8,128)S(1)}, f32[8,128,384]{2,1,0:T(8,128)}, u32[]{:S(2)}) copy-start(f32[8,128,384]{2,1,0:T(8,128)} %copy-done.1) | copy-start | bytes 4718596
  131.5 1.4 %copy-start.4 = (f32[8,128,384]{2,1,0:T(8,128)S(1)}, f32[8,128,384]{2,1,0:T(8,128)}, u32[]{:S(2)}) copy-start(f32[8,128,384]{2,1,0:T(8,128)} %copy-done.3) | copy-start | bytes 4718596
where the time goes:
time: 139 us
  waiting for transfers between devices  56.6 us (41%)
  starting transfers between devices  34.1 us (25%)
  Pallas kernels  22.5 us (16%)
  local copies, waits for them, and re-layouts  13.6 us (10%)
  other arithmetic  11.1 us (8%)
    ppermute x6, waiting for transfers between devices, send(): return lax.ppermute(value, 'member', pairs)  44.2 us
    pallas_call x1, Pallas kernels, own_steps(): call(own_kernel, jax.ShapeDtypeStruct((CH, ROWS, COLS), F32), [SMEM] + [A...  12.7 us
    unnamed x26, local copies, waits for them, and re-layouts  11 us
    all_to_all x1, waiting for transfers between devices, per_device(): parts = lax.all_to_all(parts, ('lon', 'lat'), 0, 0)  10.8 us
    ppermute x6, starting transfers between devices, send(): return lax.ppermute(value, 'member', pairs)  9.96 us
    all_to_all x1, starting transfers between devices, per_device(): parts = lax.all_to_all(parts, ('lon', 'lat'), 0, 0)  9.77 us
    ppermute x1, starting transfers between devices, exchange(): lax.ppermute(c_west, both, down2)  5.34 us
    ppermute x1, starting transfers between devices, exchange(): lax.ppermute(west, 'lon', down)  5.29 us
  transfers between devices with their start and end apart: 12, of which 4 were waited for; matrix products, arithmetic and copies ran while one was open for 2% of the time, Pallas kernels for 0%

commit v1 on v0

v1 whole, which is shorter than its diff:
```python
import functools
import jax
import jax.numpy as jnp
from jax import lax
from jax.experimental import pallas as pl
from jax.experimental.pallas import tpu as pltpu
from jax.sharding import PartitionSpec as P

LEV = 5
CH = 16
FIELDS = 24
REGIONS = 16
ROWS, COLS = 128, 384
ROWS_X, COLS_X = 136, 512
HALF, HALF_X = 64, 72
HALO = 4
EPSILON = 1e-06
VMEM = pl.BlockSpec(memory_space=pltpu.VMEM)
ANY = pl.BlockSpec(memory_space=pl.ANY)
SMEM = pl.BlockSpec(memory_space=pltpu.SMEM)
F32 = jnp.float32


def call(kernel, out, in_specs, out_specs, scratch=(), flops=1 << 22, nbytes=1 << 23):
    return pl.pallas_call(
        kernel,
        out_shape=out,
        in_specs=in_specs,
        out_specs=out_specs,
        scratch_shapes=list(scratch),
        compiler_params=pltpu.CompilerParams(vmem_limit_bytes=48 << 20),
        cost_estimate=pl.CostEstimate(flops=flops, bytes_accessed=nbytes, transcendentals=0),
    )


def iota(shape, dim):
    return lax.broadcasted_iota(jnp.int32, shape, dim)


def row_slot(k):
    return (k % 8, k >= 8) if k < CH else (8 + (k - CH) % 4, k - CH >= 4)


def pack_kernel(lat, state, depth, rotation, diff, mask, west, east, rows, c_west, c_east, lo, hi, edge, sem):
    upper = lat[0] == 0
    r0 = pl.multiple_of(jnp.where(upper, ROWS - 8, 0), 8)
    tile = pl.ds(r0, 8)
    left, right, full = slice(0, 128), slice(COLS - 128, COLS), slice(0, ROWS)
    copies = []
    for i, (src, at) in enumerate(
        [(state, slice(0, CH)), (depth, CH), (rotation, CH + 1), (diff, slice(CH + 2, CH + 2 + LEV))]
    ):
        lead = (slice(None),) if src.shape[:-2] else ()
        for j, (dst, cut) in enumerate([(edge, (tile, slice(None))), (lo, (full, left)), (hi, (full, right))]):
            copies.append(pltpu.make_async_copy(src.at[lead + cut], dst.at[at], sem.at[3 * i + j]))
    for copy in copies:
        copy.start()
    last = FIELDS - 1
    lo[last] = mask[:, left].astype(F32)
    hi[last] = mask[:, right].astype(F32)
    edge[last] = mask[tile, :].astype(F32)
    for copy in copies:
        copy.wait()

    lane = iota((ROWS, 128), 1)
    w = jnp.zeros((ROWS, 128), F32)
    e = jnp.zeros((ROWS, 128), F32)
    for k in range(FIELDS):
        own = (lane >= HALO * k) & (lane < HALO * k + HALO)
        w = jnp.where(own, pltpu.roll(lo[k], HALO * k, 1) if k else lo[k], w)
        e = jnp.where(own, pltpu.roll(hi[k], HALO * k + HALO, 1), e)
    west[...] = w
    east[...] = e
    c_west[...] = west[tile, :]
    c_east[...] = east[tile, :]
    sub = iota((8, COLS), 0)
    mine = (sub >= 4) == upper
    for k in range(FIELDS):
        slot, flip = row_slot(k)
        if not flip:
            pair = k + (8 if k < CH else 4)
            rows[8 * slot : 8 * slot + 8, :] = jnp.where(mine, edge[k], pltpu.roll(edge[pair], 4, 0))


def pack(lat, state, statics):
    shapes = [(ROWS, 128), (ROWS, 128), (FIELDS * 4, COLS), (8, 128), (8, 128)]
    return call(
        pack_kernel,
        [jax.ShapeDtypeStruct(s, F32) for s in shapes],
        [SMEM] + [ANY] * 4 + [VMEM],
        [VMEM] * 5,
        [
            pltpu.VMEM((FIELDS, ROWS, 128), F32),
            pltpu.VMEM((FIELDS, ROWS, 128), F32),
            pltpu.VMEM((FIELDS, 8, COLS), F32),
            pltpu.SemaphoreType.DMA((12,)),
        ],
    )(lat, state, *statics)


def exchange(west, east, rows, c_west, c_east):
    n = lax.axis_size("lon")
    up = [(i, (i + 1) % n) for i in range(n)]
    down = [((i + 1) % n, i) for i in range(n)]
    other = [(0, 1), (1, 0)]
    both = ("lon", "lat")
    up2 = [(2 * i + j, 2 * k + 1 - j) for i, k in up for j in range(2)]
    down2 = [(2 * i + j, 2 * k + 1 - j) for i, k in down for j in range(2)]
    return (
        lax.ppermute(east, "lon", up),
        lax.ppermute(west, "lon", down),
        lax.ppermute(rows, "lat", other),
        lax.ppermute(c_east, both, up2),
        lax.ppermute(c_west, both, down2),
    )


def fill_halo(x, lat, from_west, from_east, rows, c_west, c_east):
    def margin(k, w, e):
        lane = iota(w.shape, 1)
        s = (128 - HALO * k) % 128
        e = pltpu.roll(e, s, 1) if s else e
        return jnp.where(lane < 64, e, pltpu.roll(w, (124 - HALO * k) % 128, 1))

    sub = iota((8, COLS), 0)
    got = (sub < 4) == (lat[0] == 0)
    got_c = got[:, :128]
    w, e = from_west[...], from_east[...]
    cw, ce = c_west[...], c_east[...]
    for k in range(FIELDS):
        x[k, 0:ROWS, COLS:COLS_X] = margin(k, w, e)
        j, flip = row_slot(k)
        tile = rows[8 * j : 8 * j + 8, :]
        if flip:
            tile = pltpu.roll(tile, 4, 0)
        x[k, ROWS:ROWS_X, 0:COLS] = jnp.where(got, tile, 0.0)
        x[k, ROWS:ROWS_X, COLS:COLS_X] = jnp.where(got_c, margin(k, cw, ce), 0.0)


def tile_at(t):
    return pl.ds(pl.multiple_of(t * 8, 8), 8)


def step(x, static, ub, vb, h2, store, count, tiles):
    sub = iota((8, COLS_X), 0)

    def around(t):
        return tile_at(jnp.where(t == 0, count - 1, t - 1)), tile_at(t), tile_at(jnp.where(t == count - 1, 0, t + 1))

    def north(cur, nxt):
        return pltpu.roll(jnp.where(sub == 0, nxt, cur), 7, 0)

    def south(cur, prv):
        return pltpu.roll(jnp.where(sub == 7, prv, cur), 1, 0)

    def east(cur):
        return pltpu.roll(cur, COLS_X - 1, 1)

    def west(cur):
        return pltpu.roll(cur, 1, 1)

    def sums(t, _):
        c = tile_at(t)
        u = x[1, c, :]
        v = x[1 + LEV, c, :]
        for l in range(1, LEV):
            u = u + x[1 + l, c, :]
            v = v + x[1 + LEV + l, c, :]
        ub[c, :] = east(u) - west(u)
        vb[c, :] = v
        return 0

    lax.fori_loop(0, count, sums, 0)

    def surface(t, _):
        p, c, n = around(t)
        v = vb[c, :]
        div = ub[c, :] + (north(v, vb[n, :]) - south(v, vb[p, :]))
        h2[c, :] = static[7, c, :] * (x[0, c, :] - (0.25 / LEV) * static[0, c, :] * div)
        return 0

    lax.fori_loop(0, count, surface, 0)

    def rest(t, _):
        p, c, n = around(t)
        oc = static[7, c, :]
        rot = static[1, c, :]
        h = h2[c, :]
        store(0, c, h)
        px = 0.25 * (east(h) - west(h))
        py = 0.25 * (north(h, h2[n, :]) - south(h, h2[p, :]))
        for l in range(LEV):
            k = static[2 + l, c, :]

            def near(ch):
                q = x[ch, c, :]
                return q, east(q), west(q), north(q, x[ch, n, :]), south(q, x[ch, p, :])

            q, e, w, a, b = near(1 + 2 * LEV + l)
            cx = e - w
            cy = a - b
            c0 = q + k * ((e + w) + (a + b) - 4.0 * q)
            u, e, w, a, b = near(1 + l)
            lap_u = (e + w) + (a + b) - 4.0 * u
            v, e, w, a, b = near(1 + LEV + l)
            lap_v = (e + w) + (a + b) - 4.0 * v
            u2 = oc * (u + rot * v - px - 0.1 * cx + k * lap_u)
            v2 = oc * (v - rot * u - py - 0.1 * cy + k * lap_v)
            store(1 + l, c, u2)
            store(1 + LEV + l, c, v2)
            store(1 + 2 * LEV + l, c, oc * (c0 - 0.05 * (u2 * cx + v2 * cy)))
        return 0

    lax.fori_loop(0, tiles, rest, 0)


def two_steps(x, static, y, ub, vb, h2, out):
    count = x.shape[1] // 8

    def keep(ch, c, value):
        y[ch, c, :] = value

    def give(ch, c, value):
        out[ch, c, :] = value[:, :COLS]

    step(x, static, ub, vb, h2, keep, count, count)
    step(y, static, ub, vb, h2, give, count, count - 1)


def step_scratch(rows):
    return [pltpu.VMEM((CH, rows, COLS_X), F32)] + [pltpu.VMEM((rows, COLS_X), F32)] * 3


def own_kernel(where, state, depth, rotation, diff, mask, fw, fe, rows, cw, ce, gate, out, part, x, y, ub, vb, h2, sem):
    main = (slice(0, ROWS), slice(0, COLS))
    copies = [
        pltpu.make_async_copy(state, x.at[(slice(0, CH),) + main], sem.at[0]),
        pltpu.make_async_copy(depth, x.at[(CH,) + main], sem.at[1]),
        pltpu.make_async_copy(rotation, x.at[(CH + 1,) + main], sem.at[2]),
        pltpu.make_async_copy(diff, x.at[(slice(CH + 2, CH + 2 + LEV),) + main], sem.at[3]),
    ]
    for copy in copies:
        copy.start()
    x[(FIELDS - 1,) + main] = mask[...].astype(F32)
    fill_halo(x, where, fw, fe, rows, cw, ce)
    for copy in copies:
        copy.wait()
    first = where[1] == 0
    tiles = HALF // 8
    sub = iota((8, COLS_X), 0)
    for j in range(CH, FIELDS):

        def body(t, _):
            part[j - CH, tile_at(t), :] = x[j, tile_at(t + jnp.where(first, 0, tiles)), :]
            return 0

        lax.fori_loop(0, tiles, body, 0)
        n = x[j, tile_at(jnp.where(first, tiles, 2 * tiles)), :]
        p = x[j, tile_at(jnp.where(first, 2 * tiles, tiles - 1)), :]
        part[j - CH, HALF:HALF_X, :] = jnp.where(sub < 4, n, p)
    two_steps(x, x.at[CH:FIELDS], y, ub, vb, h2, out)


def own_steps(where, state, statics, halos, gate):
    return call(
        own_kernel,
        [
            jax.ShapeDtypeStruct((CH, ROWS, COLS), F32),
            jax.ShapeDtypeStruct((FIELDS - CH, HALF_X, COLS_X), F32),
        ],
        [SMEM] + [ANY] * 4 + [VMEM] * 6 + [ANY],
        [VMEM] * 2,
        [pltpu.VMEM((FIELDS, ROWS_X, COLS_X), F32)] + step_scratch(ROWS_X) + [pltpu.SemaphoreType.DMA((4,))],
        flops=1 << 28,
    )(where, state, *statics, *halos, gate)


def control_halo_kernel(fw, fe, rows, cw, ce, out):
    out[0:64, :] = rows[0:64, :]

    def join(w, e):
        return jnp.where(iota(w.shape, 1) < 64, w, pltpu.roll(e, 64, 1))

    s = join(fw[...], fe[...])
    out[64:112, 0:128] = s[0:48]
    out[64:112, 128:256] = s[48:96]
    out[64:96, 256:384] = s[96:128]
    out[96:104, 256:384] = join(cw[...], ce[...])
    out[104:112, 256:384] = jnp.zeros((8, 128), F32)


def send(value, pairs):
    return lax.ppermute(value, "member", pairs)


def spread_halo_first(m, halos):
    own = call(control_halo_kernel, jax.ShapeDtypeStruct((112, COLS), F32), [VMEM] * 5, VMEM)(*halos)
    return jnp.where(m == 0, own, send(own, [(0, 1)]))


def spread_halo_rest(m, h):
    h = jnp.where(m < 2, h, send(h, [(0, 2), (1, 7)]))
    return jnp.where((m < 3) | (m == 7), h, send(h, [(0, 6), (1, 3), (2, 4), (7, 5)]))


def relay_kernel(where, top, low, p1, m1, gate, u, v, sem):
    m = where[2]

    def move(src, dst, i):
        copy = pltpu.make_async_copy(src, dst, sem.at[i])
        copy.start()
        copy.wait()

    @pl.when(m == 0)
    def _():
        one = pltpu.make_async_copy(low, u, sem.at[0])
        two = pltpu.make_async_copy(top, v, sem.at[1])
        one.start()
        two.start()
        one.wait()
        two.wait()

    @pl.when(m == 2)
    def _():
        move(p1, u, 0)

    @pl.when(m == 7)
    def _():
        move(m1, v, 1)


def spread_first(state):
    top, low = state[:, :HALF_X], state[:, ROWS - HALF_X :]
    return top, low, send(top, [(0, 2)]), send(low, [(0, 7)]), send(low, [(0, 1)])


def spread_rest(where, top, low, p1, m1, e0, gate):
    shape = jax.ShapeDtypeStruct((CH, HALF_X, COLS), F32)
    u, v = call(
        relay_kernel, [shape, shape], [SMEM] + [ANY] * 5, [ANY] * 2, [pltpu.SemaphoreType.DMA((2,))]
    )(where, top, low, p1, m1, gate)
    p2 = send(u, [(0, 3), (2, 4)])
    m2 = send(v, [(0, 6), (7, 5)])
    return (top, e0, p1, p2, m2, m1), u


HOLDER = ((0,), (1,), (2,), (3, 4), (5, 6), (7,))


def control_kernel(where, *refs):
    arrays, (halo, static, out, x, y, ub, vb, h2, near, strip, sem) = refs[:6], refs[6:]
    first = where[1] == 0
    m = where[2]
    for array, members in zip(arrays, HOLDER):
        for member in members:
            r0, r1 = (0, HALF) if member % 2 == 0 else (8, 0)

            @pl.when(m == member)
            def _(array=array, r0=r0, r1=r1):
                one = pltpu.make_async_copy(array.at[:, r0 : r0 + HALF, :], x.at[:, 0:HALF, 0:COLS], sem.at[0])
                two = pltpu.make_async_copy(array.at[:, r1 : r1 + 8, :], near, sem.at[1])
                one.start()
                two.start()
                one.wait()
                two.wait()

    strip[0:48, :] = halo[64:112, 0:128]
    strip[48:96, :] = halo[64:112, 128:256]
    strip[96:136, :] = halo[64:104, 256:384]

    def margin(k, s):
        lane = iota(s.shape, 1)
        return jnp.where(
            lane < 64, pltpu.roll(s, 64 - HALO * k, 1), pltpu.roll(s, 124 - HALO * k, 1)
        )

    sub = iota((8, COLS), 0)
    inner = (sub < 4) == first
    got = (sub < 4) == (where[0] == 0)
    s_main = strip[pl.ds(pl.multiple_of(jnp.where(first, 0, HALF), 8), HALF), :]
    s_near = strip[pl.ds(pl.multiple_of(jnp.where(first, HALF, HALF - 8), 8), 8), :]
    s_edge = jnp.where(inner[:, :128], s_near, jnp.where(got[:, :128], strip[ROWS:ROWS_X, :], 0.0))
    for k in range(CH):
        x[k, 0:HALF, COLS:COLS_X] = margin(k, s_main)
        x[k, HALF:HALF_X, COLS:COLS_X] = margin(k, s_edge)
        j, flip = row_slot(k)
        tile = halo[8 * j : 8 * j + 8, :]
        if flip:
            tile = pltpu.roll(tile, 4, 0)
        x[k, HALF:HALF_X, 0:COLS] = jnp.where(inner, near[k], jnp.where(got, tile, 0.0))
    two_steps(x, static, y, ub, vb, h2, out)


def control_steps(where, arrays, halo, static):
    return call(
        control_kernel,
        jax.ShapeDtypeStruct((CH, HALF, COLS), F32),
        [SMEM] + [ANY] * 6 + [VMEM] * 2,
        VMEM,
        [pltpu.VMEM((CH, HALF_X, COLS_X), F32)]
        + step_scratch(HALF_X)
        + [pltpu.VMEM((CH, 8, COLS), F32), pltpu.VMEM((ROWS_X, 128), F32), pltpu.SemaphoreType.DMA((2,))],
        flops=1 << 27,
    )(where, *arrays, halo, static)


def sums_kernel(other, where, own, control, mask, region, earlier, out):
    start = HALF // 8 * (where[1] ^ 1 if other else where[1])

    def body(t, carry):
        c, g = tile_at(t), tile_at(t + start)
        acc = None
        for k in range(CH):
            d = own[k, g, :] - control[k, c, :]
            acc = d * d if acc is None else acc + d * d
        oc = mask[g, :].astype(F32)
        cell = oc * acc
        reg = region[g, :]
        new = []
        for r in range(REGIONS):
            hit = reg == r
            s = jnp.where(hit, cell, 0.0)
            n = jnp.where(hit, oc, 0.0)
            new.append(carry[2 * r] + (s[:, :128] + s[:, 128:256] + s[:, 256:]))
            new.append(carry[2 * r + 1] + (n[:, :128] + n[:, 128:256] + n[:, 256:]))
        return tuple(new)

    zero = jnp.zeros((8, 128), F32)
    total = lax.fori_loop(0, HALF // 8, body, (zero,) * (2 * REGIONS))
    lane = iota((8, 128), 1)
    row = zero
    for r in range(REGIONS):
        for j in range(2):
            s = jnp.sum(jnp.sum(total[2 * r + j], axis=0, keepdims=True), axis=1, keepdims=True)
            row = jnp.where(lane == REGIONS * j + r, s, row)
    if other:
        row = row + earlier[...]
        for i in range(out.shape[0]):
            out[i] = row
    else:
        out[...] = row + earlier[...]


def half_sums(other, where, own, control, mask, region, earlier):
    shape = (32, 8, 128) if other else (8, 128)
    return call(
        functools.partial(sums_kernel, other), jax.ShapeDtypeStruct(shape, F32), [SMEM] + [VMEM] * 5, VMEM
    )(where, own, control, mask, region, earlier)


BLOCK = 4


def final_kernel(where, own, mine, theirs, region, parts, target, out, growth, cell):
    @pl.when(pl.program_id(0) == 0)
    def _():
        total = parts[0]
        for i in range(1, 32):
            total = total + parts[i]
        lane = iota((8, 128), 1)
        counts = jnp.where(lane < REGIONS, pltpu.roll(total, 128 - REGIONS, 1), 1.0)
        squares = jnp.where(lane < REGIONS, total, 1.0)
        g = jnp.sqrt(squares / (counts * CH) + EPSILON)
        growth[...] = g
        factor = target[...] / g

        def body(t, _):
            c = tile_at(t)
            for j in range(3):
                lanes = slice(128 * j, 128 * j + 128)
                reg = region[c, lanes]
                cell[c, lanes] = jnp.take_along_axis(factor, reg, axis=1, mode="promise_in_bounds")
            return 0

        lax.fori_loop(0, ROWS // 8, body, 0)

    start = HALF // 8 * where[1]
    for ref, s in ((mine, start), (theirs, HALF // 8 - start)):

        def body(t, _):
            c, g = tile_at(t), tile_at(t + s)
            f = cell[g, :]
            for k in range(BLOCK):
                q = ref[k, c, :]
                out[k, g, :] = q + f * (own[k, g, :] - q)
            return 0

        lax.fori_loop(0, HALF // 8, body, 0)


def rescale(where, own, mine, theirs, region, parts, target):
    target = jnp.broadcast_to(jnp.pad(target, (0, 128 - REGIONS), constant_values=1.0), (8, 128))

    def cut(rows):
        return pl.BlockSpec((BLOCK, rows, COLS), lambda i: (i, 0, 0))

    def whole(*shape):
        return pl.BlockSpec(shape, lambda i: (0,) * len(shape))

    return pl.pallas_call(
        final_kernel,
        grid=(CH // BLOCK,),
        out_shape=[jax.ShapeDtypeStruct((CH, ROWS, COLS), F32), jax.ShapeDtypeStruct((8, 128), F32)],
        in_specs=[SMEM, cut(ROWS), cut(HALF), cut(HALF), whole(ROWS, COLS), whole(32, 8, 128), whole(8, 128)],
        out_specs=[cut(ROWS), whole(8, 128)],
        scratch_shapes=[pltpu.VMEM((ROWS, COLS), F32)],
        compiler_params=pltpu.CompilerParams(vmem_limit_bytes=32 << 20),
        cost_estimate=pl.CostEstimate(flops=1 << 22, bytes_accessed=10 << 20, transcendentals=0),
    )(where, own, mine, theirs, region, parts, target)


def per_device(member_state, depth, rotation, diff, mask, region, target):
    state = member_state[0]
    statics = (depth, rotation, diff, mask)
    m = lax.axis_index("member")
    where = jnp.stack([lax.axis_index("lat"), m % 2, m]).astype(jnp.int32)
    first = spread_first(state)
    halos = exchange(*pack(where, state, statics))
    halo = spread_halo_first(m, halos)
    arrays, gate = spread_rest(where, *first, halo)
    halo = spread_halo_rest(m, halo)
    own, static = own_steps(where, state, statics, halos, gate)
    mine = control_steps(where, arrays, halo, static)
    theirs = send(mine, [(i, i ^ 1) for i in range(8)])
    parts = half_sums(False, where, own, mine, mask, region, jnp.zeros((8, 128), F32))
    parts = half_sums(True, where, own, theirs, mask, region, parts)
    parts = lax.all_to_all(parts, ("lon", "lat"), 0, 0)
    bred, growth = rescale(where, own, mine, theirs, region, parts, target)
    return bred[None], growth[:1, :REGIONS]


def solution(mesh):
    return jax.shard_map(
        per_device,
        mesh=mesh,
        in_specs=(
            P("member", None, "lat", "lon"),
            P("lat", "lon"),
            P("lat", "lon"),
            P(None, "lat", "lon"),
            P("lat", "lon"),
            P("lat", "lon"),
            P(),
        ),
        out_specs=(P("member", None, "lat", "lon"), P("member", None)),
        check_vma=False,
    )
```

time: 139 us -> 192 us (1.38); the launches traced: 139 us -> 189 us
  waiting for transfers between devices: 56.6 us -> 102 us
  Pallas kernels: 22.5 us -> 32.8 us
  other arithmetic: 11.1 us -> 1.73 us
    ppermute x6 -> x9, waiting for transfers between devices: 44.2 us -> 87.8 us  [send(): return lax.ppermute(value, 'member', pairs)]
    select_n x3, other arithmetic: 11.1 us -> 1.65 us  [the longest x1 1.61 us: spread_halo_rest(): h = jnp.where(m < 2, h, send(h, [(0, 2), (1, 7)]))]
    pallas_call x3 -> x7, Pallas kernels: 21.6 us -> 30.9 us  [the longest x1 15.3 us: own_steps(): call(own_kernel, [jax.ShapeDtypeStruct((CH, ROWS, COLS), F32), jax.ShapeD...]
    ppermute x6 -> x9, starting transfers between devices: 9.96 us -> 12.2 us  [send(): return lax.ppermute(value, 'member', pairs)]
    ppermute x1, waiting for transfers between devices: 0.01 us -> 2.24 us  [exchange(): lax.ppermute(east, 'lon', up)]
    slice x1, local copies, waits for them, and re-layouts: 2.11 us -> 4.21 us  [spread_first(): top, low = (state[:, :HALF_X], state[:, ROWS - HALF_X:])]
    unnamed x26 -> x42, local copies, waits for them, and re-layouts: 11 us -> 10.5 us
  transfers between devices with their start and end apart: 12 -> 15, of which waited for: 4 -> 5; matrix products, arithmetic and copies ran while one was open for 2% -> 1% of each run, Pallas kernels for 0% -> 10%
where the time goes in v1:
time: 192 us; the launch traced here: 189 us
  waiting for transfers between devices  102 us (53%)
  starting transfers between devices  35.8 us (19%)
  Pallas kernels  32.8 us (17%)
  local copies, waits for them, and re-layouts  15.3 us (8%)
    ppermute x9, waiting for transfers between devices, send(): return lax.ppermute(value, 'member', pairs)  87.8 us
    pallas_call x1, Pallas kernels, own_steps(): call(own_kernel, [jax.ShapeDtypeStruct((CH, ROWS, COLS), F32), jax.ShapeD...  15.3 us
    ppermute x9, starting transfers between devices, send(): return lax.ppermute(value, 'member', pairs)  12.2 us
    all_to_all x1, waiting for transfers between devices, per_device(): parts = lax.all_to_all(parts, ('lon', 'lat'), 0, 0)  10.8 us
    unnamed x42, local copies, waits for them, and re-layouts  10.5 us
    all_to_all x1, starting transfers between devices, per_device(): parts = lax.all_to_all(parts, ('lon', 'lat'), 0, 0)  9.89 us
    pallas_call x1, Pallas kernels, control_steps(): call(control_kernel, jax.ShapeDtypeStruct((CH, HALF, COLS), F32), [SMEM]...  8.32 us
    ppermute x1, starting transfers between devices, exchange(): lax.ppermute(c_west, both, down2)  5.29 us
  transfers between devices with their start and end apart: 15, of which 5 were waited for; matrix products, arithmetic and copies ran while one was open for 1% of the time, Pallas kernels for 10%

profile of v1, /device:TPU:24, one launch (start us, length us, event | category | flops | bytes accessed | tf_op | source)
XLA Modules:
  0.0 188.9 jit_solution(7259390057398011411)
XLA Ops:
  0.6 0.0 copy-start
  0.7 4.2 %fusion = (f32[16,72,384]{2,1,0:T(8,128)}, f32[16,72,384]{2,1,0:T(8,128)}) fusion(f32[16,128,384]{2,1,0:T(8,128)} %bitcast.5), kind=kLoop, calls=%fused_computation.4 | loop fusion | bytes 7077888 | tf_op jit(solution)/shard_map/slice | solution.py:333
  4.9 1.9 collective-permute-start.5
  6.7 1.9 %collective-permute-start.6 = (f32[16,72,384]{2,1,0:T(8,128)}, f32[16,72,384]{2,1,0:T(8,128)}, u32[]{:S(2)}, u32[]{:S(2)}) collective-permute-start(f32[16,72,384]{2,1,0:T(8,128)} %get-tuple-element.24.low), channel_id=1, source_target_pairs={{0,224},{1,225},{2,226},{3,227},{4,228},{5,229},{6,230},{7,231},{8... | collective-permute-start | bytes 5308424 | tf_op jit(solution)/shard_map/ppermute | solution.py:293
  8.6 0.1 pad_add_fusion.lat.where
  8.7 0.0 copy-start.6
  8.7 1.2 copy-done.6
  9.9 0.9 copy-done.11
  10.8 1.9 shard_map.86
  12.7 3.1 %collective-permute-start.2 = (f32[96,384]{1,0:T(8,128)S(1)}, f32[96,384]{1,0:T(8,128)S(1)}, u32[]{:S(2)}, u32[]{:S(2)}) collective-permute-start(f32[96,384]{1,0:T(8,128)S(1)} %get-tuple-element.15), channel_id=1, source_target_pairs={{0,1},{1,0},{2,3},{3,2},{4,5},{5,4},{6,7},{7,6},{8,9},{9,8},{10,11... | collective-permute-start | bytes 442376 | tf_op jit(solution)/shard_map/ppermute | solution.py:112
  15.8 1.1 collective-permute-start.3
  17.0 5.3 %collective-permute-start.4 = (f32[8,128]{1,0:T(8,128)S(1)}, f32[8,128]{1,0:T(8,128)S(1)}, u32[]{:S(2)}, u32[]{:S(2)}) collective-permute-start(f32[8,128]{1,0:T(8,128)S(1)} %get-tuple-element.17), channel_id=1, source_target_pairs={{2,1},{3,0},{4,3},{5,2},{6,5},{7,4},{8,7},{9,6},{10,9},{11,8},{12,... | collective-permute-start | bytes 12296 | tf_op jit(solution)/shard_map/ppermute | solution.py:114
  22.2 1.6 collective-permute-done.3.cw
  23.8 4.1 %collective-permute-start.1 = (f32[128,128]{1,0:T(8,128)S(1)}, f32[128,128]{1,0:T(8,128)S(1)}, u32[]{:S(2)}, u32[]{:S(2)}) collective-permute-start(f32[128,128]{1,0:T(8,128)S(1)} %get-tuple-element.14), channel_id=1, source_target_pairs={{2,0},{4,2},{6,4},{8,6},{10,8},{12,10},{14,12},{16,14},{18,16},{20... | collective-permute-start | bytes 196616 | tf_op jit(solution)/shard_map/ppermute | solution.py:111
  28.0 2.2 %collective-permute-done.fw = f32[128,128]{1,0:T(8,128)S(1)} collective-permute-done((f32[128,128]{1,0:T(8,128)S(1)}, f32[128,128]{1,0:T(8,128)S(1)}, u32[]{:S(2)}, u32[]{:S(2)}) %collective-permute-start) | collective-permute-done | bytes 65568 | tf_op jit(solution)/shard_map/ppermute | solution.py:110
  30.2 0.1 shard_map.87
  30.3 0.5 copy-done.16
  30.8 0.7 copy-done.13
  31.5 0.7 collective-permute-start.7
  32.2 1.9 %collective-permute-start.8 = (f32[16,72,384]{2,1,0:T(8,128)}, f32[16,72,384]{2,1,0:T(8,128)}, u32[]{:S(2)}, u32[]{:S(2)}) collective-permute-start(f32[16,72,384]{2,1,0:T(8,128)} %get-tuple-element.24.low), channel_id=1, source_target_pairs={{0,32},{1,33},{2,34},{3,35},{4,36},{5,37},{6,38},{7,39},{8,40},{9,... | collective-permute-start | bytes 5308424 | tf_op jit(solution)/shard_map/ppermute | solution.py:293
  34.1 0.0 copy-start.7
  34.1 0.0 copy-start.12
  34.2 0.6 shard_map.88
  34.8 1.3 collective-permute-start.10
  36.1 1.9 collective-permute-start.9
  37.9 1.3 collective-permute-start.11
  39.2 1.6 broadcast_select_fusion
  40.8 1.3 collective-permute-start.12
  42.1 85.6 %collective-permute-done.12 = f32[112,384]{1,0:T(8,128)S(1)} collective-permute-done((f32[112,384]{1,0:T(8,128)}, f32[112,384]{1,0:T(8,128)S(1)}, u32[]{:S(2)}, u32[]{:S(2)}) %collective-permute-start.12) | collective-permute-done | bytes 172064 | tf_op jit(solution)/shard_map/ppermute | solution.py:293
  127.8 0.9 copy-done.14
  128.7 0.8 copy-done.17
  129.6 0.8 copy-done.19
  130.4 15.3 %shard_map.89 = (f32[16,128,384]{2,1,0:T(8,128)}, f32[8,72,512]{2,1,0:T(8,128)S(1)}) custom-call(s32[3]{0:T(128)S(1)} %pad_add_fusion.lat.where, f32[16,128,384]{2,1,0:T(8,128)} %bitcast.6, f32[128,384]{1,0:T(8,128)S(1)} %copy-done.10, f32[128,384]{1,0:T(8,128)S(1)} %copy-done.12, f32[5,128,384]{2,1,0:T(8,128)S(1)} %copy-done.7, s32[128,384]{1,0:T(8,128)S(1)} %copy-done.8, ...), custom_call_target="tpu_custom_call" | custom-call | flops 268435456 | bytes 8388608 | tf_op jit(solution)/shard_map/pallas_call | solution.py:265
  145.8 0.0 copy-start.1
  145.8 8.3 %shard_map.90.control.mine = f32[16,64,384]{2,1,0:T(8,128)S(1)} custom-call(s32[3]{0:T(128)S(1)} %pad_add_fusion.lat.where, f32[16,72,384]{2,1,0:T(8,128)} %get-tuple-element.25.top.refs_0_, f32[16,72,384]{2,1,0:T(8,128)} %collective-permute-done.8.refs_1_, f32[16,72,384]{2,1,0:T(8,128)} %collective-permute-done.5.p1.refs_2_, ...), custom_call_target="tpu_custom_call" | custom-call | flops 134217728 | bytes 8388608 | tf_op jit(solution)/shard_map/pallas_call | solution.py:395
  154.1 0.1 collective-permute-start.13
  154.3 1.2 shard_map.91.earlier
  155.4 0.0 copy-start.20
  155.5 2.2 %collective-permute-done.13.control.theirs = f32[16,64,384]{2,1,0:T(8,128)S(1)} collective-permute-done((f32[16,64,384]{2,1,0:T(8,128)S(1)}, f32[16,64,384]{2,1,0:T(8,128)S(1)}, u32[]{:S(2)}, u32[]{:S(2)}) %collective-permute-start.13) | collective-permute-done | bytes 1572896 | tf_op jit(solution)/shard_map/ppermute | solution.py:293
  157.6 1.2 shard_map.92
  158.8 1.1 copy-done.4
  160.0 0.7 copy-done.15
  160.6 9.9 %all-to-all-start = ((f32[32,8,128]{2,1,0:T(8,128)}), f32[32,8,128]{2,1,0:T(8,128)S(1)}, u32[]{:S(2)}, u32[]{:S(2)}) async-start(f32[32,8,128]{2,1,0:T(8,128)} %copy-done.15), calls=%async_computation | async-start | bytes 262144 | tf_op jit(solution)/shard_map/all_to_all | solution.py:527
  170.5 10.8 %all-to-all-done.parts = f32[32,8,128]{2,1,0:T(8,128)S(1)} async-done(((f32[32,8,128]{2,1,0:T(8,128)}), f32[32,8,128]{2,1,0:T(8,128)S(1)}, u32[]{:S(2)}, u32[]{:S(2)}) %all-to-all-start) | async-done | bytes 131104 | tf_op jit(solution)/shard_map/all_to_all | solution.py:527
  181.3 1.4 copy-done.3
  182.7 1.4 copy-done.5
  184.1 4.3 %shard_map.93 = (f32[16,128,384]{2,1,0:T(8,128)}, f32[8,128]{1,0:T(8,128)S(1)}) custom-call(s32[3]{0:T(128)S(1)} %pad_add_fusion.lat.where, f32[16,128,384]{2,1,0:T(8,128)S(1)} %copy-done.1, f32[16,64,384]{2,1,0:T(8,128)S(1)} %copy-done.3, f32[16,64,384]{2,1,0:T(8,128)S(1)} %copy-done.5, s32[128,384]{1,0:T(8,128)S(1)} %copy-done.9, ...), custom_call_target="tpu_custom_call" | custom-call | flops 4194304 | bytes 10485760 | tf_op jit(solution)/shard_map/pallas_call | solution.py:500
  188.4 0.5 slice.11
  (41 shorter events, 0.1 us)
Async XLA Ops:
  0.6 8.1 %copy-start = (f32[1,16,128,384]{3,2,1,0:T(8,128)S(1)}, f32[1,16,128,384]{3,2,1,0:T(8,128)}, u32[]{:S(2)}) copy-start(f32[1,16,128,384]{3,2,1,0:T(8,128)} %param.7) | copy-start | bytes 9437188
  0.6 8.1 %copy-start.8 = (s32[128,384]{1,0:T(8,128)S(1)}, s32[128,384]{1,0:T(8,128)}, u32[]{:S(2)}) copy-start(s32[128,384]{1,0:T(8,128)} %mask.7) | copy-start | bytes 589828
  0.7 8.1 %copy-start.10 = (f32[128,384]{1,0:T(8,128)S(1)}, f32[128,384]{1,0:T(8,128)}, u32[]{:S(2)}) copy-start(f32[128,384]{1,0:T(8,128)} %depth.3) | copy-start | bytes 589828
  4.9 29.3 %collective-permute-start.5 = (f32[16,72,384]{2,1,0:T(8,128)}, f32[16,72,384]{2,1,0:T(8,128)}, u32[]{:S(2)}, u32[]{:S(2)}) collective-permute-start(f32[16,72,384]{2,1,0:T(8,128)} %get-tuple-element.25.top.refs_0_), channel_id=1, source_target_pairs={{0,64},{1,65},{2,66},{3,67},{4,68},{5,69},{6,70},{7,71},{8,72},{9,... | collective-permute-start | bytes 5308424 | tf_op jit(solution)/shard_map/ppermute | solution.py:293
  6.7 27.4 %collective-permute-start.6 = (f32[16,72,384]{2,1,0:T(8,128)}, f32[16,72,384]{2,1,0:T(8,128)}, u32[]{:S(2)}, u32[]{:S(2)}) collective-permute-start(f32[16,72,384]{2,1,0:T(8,128)} %get-tuple-element.24.low), channel_id=1, source_target_pairs={{0,224},{1,225},{2,226},{3,227},{4,228},{5,229},{6,230},{7,231},{8... | collective-permute-start | bytes 5308424 | tf_op jit(solution)/shard_map/ppermute | solution.py:293
  8.7 1.2 copy-start.6
  9.9 0.9 copy-start.11
  12.7 17.5 %collective-permute-start.2 = (f32[96,384]{1,0:T(8,128)S(1)}, f32[96,384]{1,0:T(8,128)S(1)}, u32[]{:S(2)}, u32[]{:S(2)}) collective-permute-start(f32[96,384]{1,0:T(8,128)S(1)} %get-tuple-element.15), channel_id=1, source_target_pairs={{0,1},{1,0},{2,3},{3,2},{4,5},{5,4},{6,7},{7,6},{8,9},{9,8},{10,11... | collective-permute-start | bytes 442376 | tf_op jit(solution)/shard_map/ppermute | solution.py:112
  15.8 8.0 %collective-permute-start.3 = (f32[8,128]{1,0:T(8,128)S(1)}, f32[8,128]{1,0:T(8,128)S(1)}, u32[]{:S(2)}, u32[]{:S(2)}) collective-permute-start(f32[8,128]{1,0:T(8,128)S(1)} %get-tuple-element.16), channel_id=1, source_target_pairs={{0,3},{1,2},{2,5},{3,4},{4,7},{5,6},{6,9},{7,8},{8,11},{9,10},{10,... | collective-permute-start | bytes 12296 | tf_op jit(solution)/shard_map/ppermute | solution.py:113
  17.0 6.9 %collective-permute-start.4 = (f32[8,128]{1,0:T(8,128)S(1)}, f32[8,128]{1,0:T(8,128)S(1)}, u32[]{:S(2)}, u32[]{:S(2)}) collective-permute-start(f32[8,128]{1,0:T(8,128)S(1)} %get-tuple-element.17), channel_id=1, source_target_pairs={{2,1},{3,0},{4,3},{5,2},{6,5},{7,4},{8,7},{9,6},{10,9},{11,8},{12,... | collective-permute-start | bytes 12296 | tf_op jit(solution)/shard_map/ppermute | solution.py:114
  23.8 6.4 %collective-permute-start = (f32[128,128]{1,0:T(8,128)S(1)}, f32[128,128]{1,0:T(8,128)S(1)}, u32[]{:S(2)}, u32[]{:S(2)}) collective-permute-start(f32[128,128]{1,0:T(8,128)S(1)} %get-tuple-element.13), channel_id=1, source_target_pairs={{0,2},{2,4},{4,6},{6,8},{8,10},{10,12},{12,14},{14,16},{16,18},{18... | collective-permute-start | bytes 196616 | tf_op jit(solution)/shard_map/ppermute | solution.py:110
  23.8 6.4 %collective-permute-start.1 = (f32[128,128]{1,0:T(8,128)S(1)}, f32[128,128]{1,0:T(8,128)S(1)}, u32[]{:S(2)}, u32[]{:S(2)}) collective-permute-start(f32[128,128]{1,0:T(8,128)S(1)} %get-tuple-element.14), channel_id=1, source_target_pairs={{2,0},{4,2},{6,4},{8,6},{10,8},{12,10},{14,12},{16,14},{18,16},{20... | collective-permute-start | bytes 196616 | tf_op jit(solution)/shard_map/ppermute | solution.py:111
  30.2 0.6 copy-start.16
  30.2 1.9 %copy-start.18 = (f32[128,128]{1,0:T(8,128)}, f32[128,128]{1,0:T(8,128)S(1)}, u32[]{:S(2)}) copy-start(f32[128,128]{1,0:T(8,128)S(1)} %collective-permute-done.1.fe) | copy-start | bytes 196612
  30.8 0.7 copy-start.13
  31.5 2.6 %collective-permute-start.7 = (f32[112,384]{1,0:T(8,128)S(1)}, f32[112,384]{1,0:T(8,128)S(1)}, u32[]{:S(2)}, u32[]{:S(2)}) collective-permute-start(f32[112,384]{1,0:T(8,128)S(1)} %shard_map.87), channel_id=1, source_target_pairs={{0,32},{1,33},{2,34},{3,35},{4,36},{5,37},{6,38},{7,39},{8,40},{9,... | collective-permute-start | bytes 516104 | tf_op jit(solution)/shard_map/ppermute | solution.py:293
  32.2 113.6 %collective-permute-start.8 = (f32[16,72,384]{2,1,0:T(8,128)}, f32[16,72,384]{2,1,0:T(8,128)}, u32[]{:S(2)}, u32[]{:S(2)}) collective-permute-start(f32[16,72,384]{2,1,0:T(8,128)} %get-tuple-element.24.low), channel_id=1, source_target_pairs={{0,32},{1,33},{2,34},{3,35},{4,36},{5,37},{6,38},{7,39},{8,40},{9,... | collective-permute-start | bytes 5308424 | tf_op jit(solution)/shard_map/ppermute | solution.py:293
  34.1 93.7 %copy-start.7 = (f32[5,128,384]{2,1,0:T(8,128)S(1)}, f32[5,128,384]{2,1,0:T(8,128)}, u32[]{:S(2)}) copy-start(f32[5,128,384]{2,1,0:T(8,128)} %diff.3) | copy-start | bytes 2949124
  34.1 93.7 %copy-start.12 = (f32[128,384]{1,0:T(8,128)S(1)}, f32[128,384]{1,0:T(8,128)}, u32[]{:S(2)}) copy-start(f32[128,384]{1,0:T(8,128)} %rotation.3) | copy-start | bytes 589828
  34.8 111.0 %collective-permute-start.10 = (f32[16,72,384]{2,1,0:T(8,128)}, f32[16,72,384]{2,1,0:T(8,128)}, u32[]{:S(2)}, u32[]{:S(2)}) collective-permute-start(f32[16,72,384]{2,1,0:T(8,128)} %get-tuple-element.20), channel_id=1, source_target_pairs={{0,192},{224,160},{1,193},{225,161},{2,194},{226,162},{3,195},{227... | collective-permute-start | bytes 5308424 | tf_op jit(solution)/shard_map/ppermute | solution.py:293
  36.1 109.7 %collective-permute-start.9 = (f32[16,72,384]{2,1,0:T(8,128)S(1)}, f32[16,72,384]{2,1,0:T(8,128)}, u32[]{:S(2)}, u32[]{:S(2)}) collective-permute-start(f32[16,72,384]{2,1,0:T(8,128)S(1)} %get-tuple-element.18.gate), channel_id=1, source_target_pairs={{0,96},{64,128},{1,97},{65,129},{2,98},{66,130},{3,99},{67,131},{4... | collective-permute-start | bytes 5308424 | tf_op jit(solution)/shard_map/ppermute | solution.py:293
  37.9 1.3 collective-permute-start.11
  40.8 86.9 %collective-permute-start.12 = (f32[112,384]{1,0:T(8,128)}, f32[112,384]{1,0:T(8,128)S(1)}, u32[]{:S(2)}, u32[]{:S(2)}) collective-permute-start(f32[112,384]{1,0:T(8,128)} %broadcast_select_fusion), channel_id=1, source_target_pairs={{0,192},{32,96},{64,128},{224,160},{1,193},{33,97},{65,129},{225,1... | collective-permute-start | bytes 516104 | tf_op jit(solution)/shard_map/ppermute | solution.py:293
  127.8 0.9 copy-start.14
  128.7 0.8 copy-start.17
  129.6 0.8 copy-start.19
  145.8 8.5 %copy-start.1 = (f32[16,128,384]{2,1,0:T(8,128)S(1)}, f32[16,128,384]{2,1,0:T(8,128)}, u32[]{:S(2)}) copy-start(f32[16,128,384]{2,1,0:T(8,128)} %get-tuple-element.19.own) | copy-start | bytes 9437188
  145.8 8.5 %copy-start.9 = (s32[128,384]{1,0:T(8,128)S(1)}, s32[128,384]{1,0:T(8,128)}, u32[]{:S(2)}) copy-start(s32[128,384]{1,0:T(8,128)} %region.5) | copy-start | bytes 589828
  154.1 1.3 copy-start.2
  154.1 3.5 %collective-permute-start.13 = (f32[16,64,384]{2,1,0:T(8,128)S(1)}, f32[16,64,384]{2,1,0:T(8,128)S(1)}, u32[]{:S(2)}, u32[]{:S(2)}) collective-permute-start(f32[16,64,384]{2,1,0:T(8,128)S(1)} %shard_map.90.control.mine), channel_id=1, source_target_pairs={{0,32},{32,0},{64,96},{96,64},{128,160},{160,128},{192,224},{224,1... | collective-permute-start | bytes 4718600 | tf_op jit(solution)/shard_map/ppermute | solution.py:293
  155.4 15.1 %copy-start.20 = (f32[16]{0:T(128)S(1)}, f32[16]{0:T(128)}, u32[]{:S(2)}) copy-start(f32[16]{0:T(128)} %param.13) | copy-start | bytes 196
  158.8 1.1 copy-start.4
  160.0 0.7 copy-start.15
  160.6 20.7 %all-to-all-start = ((f32[32,8,128]{2,1,0:T(8,128)}), f32[32,8,128]{2,1,0:T(8,128)S(1)}, u32[]{:S(2)}, u32[]{:S(2)}) async-start(f32[32,8,128]{2,1,0:T(8,128)} %copy-done.15), calls=%async_computation | async-start | bytes 262144 | tf_op jit(solution)/shard_map/all_to_all | solution.py:527
  181.3 1.4 copy-start.3
  182.7 1.4 copy-start.5

commit v2 on v1

--- a/solution.py
+++ b/solution.py
@@ -276,69 +276,77 @@
 
 
 def control_halo_kernel(fw, fe, rows, cw, ce, out):
-    out[0:64, :] = rows[0:64, :]
-
-    def join(w, e):
-        return jnp.where(iota(w.shape, 1) < 64, w, pltpu.roll(e, 64, 1))
-
-    s = join(fw[...], fe[...])
-    out[64:112, 0:128] = s[0:48]
-    out[64:112, 128:256] = s[48:96]
-    out[64:96, 256:384] = s[96:128]
-    out[96:104, 256:384] = join(cw[...], ce[...])
-    out[104:112, 256:384] = jnp.zeros((8, 128), F32)
+    for k in range(8):
+        out[k] = rows[8 * k : 8 * k + 8, :]
+    for i in range(18):
+        out[8 + i // 3, :, 128 * (i % 3) : 128 * (i % 3) + 128] = jnp.zeros((8, 128), F32)
+    lane = iota((8, 128), 1)
+    for i in range(17):
+        r = slice(8 * i, 8 * i + 8)
+        w, e = (fw[r, :], fe[r, :]) if i < 16 else (cw[...], ce[...])
+        s = jnp.where(lane < 64, w, pltpu.roll(e, 64, 1))
+        out[8 + i // 3, :, 128 * (i % 3) : 128 * (i % 3) + 128] = s
+    out[14:16] = jnp.zeros((2, 8, COLS), F32)
 
 
 def send(value, pairs):
     return lax.ppermute(value, "member", pairs)
 
 
-def spread_halo_first(m, halos):
-    own = call(control_halo_kernel, jax.ShapeDtypeStruct((112, COLS), F32), [VMEM] * 5, VMEM)(*halos)
-    return jnp.where(m == 0, own, send(own, [(0, 1)]))
-
-
-def spread_halo_rest(m, h):
-    h = jnp.where(m < 2, h, send(h, [(0, 2), (1, 7)]))
-    return jnp.where((m < 3) | (m == 7), h, send(h, [(0, 6), (1, 3), (2, 4), (7, 5)]))
-
-
-def relay_kernel(where, top, low, p1, m1, gate, u, v, sem):
-    m = where[2]
-
-    def move(src, dst, i):
-        copy = pltpu.make_async_copy(src, dst, sem.at[i])
-        copy.start()
-        copy.wait()
-
-    @pl.when(m == 0)
+def cut_kernel(where, state, top, low, sem):
+    @pl.when(where[2] == 0)
     def _():
-        one = pltpu.make_async_copy(low, u, sem.at[0])
-        two = pltpu.make_async_copy(top, v, sem.at[1])
+        one = pltpu.make_async_copy(state.at[:, 0:HALF_X, :], top, sem.at[0])
+        two = pltpu.make_async_copy(state.at[:, ROWS - HALF_X : ROWS, :], low, sem.at[1])
         one.start()
         two.start()
         one.wait()
         two.wait()
 
+
+def spread_first(where, state):
+    shape = jax.ShapeDtypeStruct((CH, HALF_X, COLS), F32)
+    top, low = call(cut_kernel, [shape, shape], [SMEM, ANY], [VMEM] * 2, [pltpu.SemaphoreType.DMA((2,))])(where, state)
+    return top, low, send(top, [(0, 2)]), send(low, [(0, 7)]), send(low, [(0, 1)])
+
+
+def spread_halo(m, halos):
+    own = call(control_halo_kernel, jax.ShapeDtypeStruct((CH, 8, COLS), F32), [VMEM] * 5, VMEM)(*halos)
+    h = jnp.where(m == 0, own, send(own, [(0, 1)]))
+    return jnp.where(m < 2, h, send(h, [(0, 2), (1, 7)]))
+
+
+def relay_kernel(where, top, low, p1, m1, halo, u, v, sem):
+    m = where[2]
+
+    def move(pairs):
+        copies = []
+        for i, (src, dst) in enumerate(pairs):
+            copies.append(pltpu.make_async_copy(src, dst.at[:, 0:HALF_X, :], sem.at[2 * i]))
+            copies.append(pltpu.make_async_copy(halo, dst.at[:, HALF_X : HALF_X + 8, :], sem.at[2 * i + 1]))
+        for copy in copies:
+            copy.start()
+        for copy in copies:
+            copy.wait()
+
+    @pl.when(m == 0)
+    def _():
+        move([(low, u), (top, v)])
+
     @pl.when(m == 2)
     def _():
-        move(p1, u, 0)
+        move([(p1, u)])
 
     @pl.when(m == 7)
     def _():
-        move(m1, v, 1)
-
-
-def spread_first(state):
-    top, low = state[:, :HALF_X], state[:, ROWS - HALF_X :]
-    return top, low, send(top, [(0, 2)]), send(low, [(0, 7)]), send(low, [(0, 1)])
-
-
-def spread_rest(where, top, low, p1, m1, e0, gate):
-    shape = jax.ShapeDtypeStruct((CH, HALF_X, COLS), F32)
+        move([(m1, v)])
+
+
+def spread_rest(where, top, low, p1, m1, e0, halo):
+    shape = jax.ShapeDtypeStruct((CH, HALF_X + 8, COLS), F32)
     u, v = call(
-        relay_kernel, [shape, shape], [SMEM] + [ANY] * 5, [ANY] * 2, [pltpu.SemaphoreType.DMA((2,))]
-    )(where, top, low, p1, m1, gate)
+        relay_kernel, [shape, shape], [SMEM] + [ANY] * 5, [VMEM] * 2, [pltpu.SemaphoreType.DMA((4,))]
+    )(where, top, low, p1, m1, halo)
     p2 = send(u, [(0, 3), (2, 4)])
     m2 = send(v, [(0, 6), (7, 5)])
     return (top, e0, p1, p2, m2, m1), u
@@ -348,7 +356,7 @@
 
 
 def control_kernel(where, *refs):
-    arrays, (halo, static, out, x, y, ub, vb, h2, near, strip, sem) = refs[:6], refs[6:]
+    arrays, (early, static, out, x, y, ub, vb, h2, near, halo, strip, sem) = refs[:6], refs[6:]
     first = where[1] == 0
     m = where[2]
     for array, members in zip(arrays, HOLDER):
@@ -359,14 +367,18 @@
             def _(array=array, r0=r0, r1=r1):
                 one = pltpu.make_async_copy(array.at[:, r0 : r0 + HALF, :], x.at[:, 0:HALF, 0:COLS], sem.at[0])
                 two = pltpu.make_async_copy(array.at[:, r1 : r1 + 8, :], near, sem.at[1])
+                rides = array.shape[1] > HALF_X
+                source = array.at[:, HALF_X : HALF_X + 8, :] if rides else early
+                three = pltpu.make_async_copy(source, halo, sem.at[2])
                 one.start()
                 two.start()
+                three.start()
                 one.wait()
                 two.wait()
-
-    strip[0:48, :] = halo[64:112, 0:128]
-    strip[48:96, :] = halo[64:112, 128:256]
-    strip[96:136, :] = halo[64:104, 256:384]
+                three.wait()
+
+    for i in range(17):
+        strip[8 * i : 8 * i + 8, :] = halo[8 + i // 3, :, 128 * (i % 3) : 128 * (i % 3) + 128]
 
     def margin(k, s):
         lane = iota(s.shape, 1)
@@ -384,7 +396,7 @@
         x[k, 0:HALF, COLS:COLS_X] = margin(k, s_main)
         x[k, HALF:HALF_X, COLS:COLS_X] = margin(k, s_edge)
         j, flip = row_slot(k)
-        tile = halo[8 * j : 8 * j + 8, :]
+        tile = halo[j]
         if flip:
             tile = pltpu.roll(tile, 4, 0)
         x[k, HALF:HALF_X, 0:COLS] = jnp.where(inner, near[k], jnp.where(got, tile, 0.0))
@@ -395,11 +407,12 @@
     return call(
         control_kernel,
         jax.ShapeDtypeStruct((CH, HALF, COLS), F32),
-        [SMEM] + [ANY] * 6 + [VMEM] * 2,
+        [SMEM] + [ANY] * 7 + [VMEM],
         VMEM,
         [pltpu.VMEM((CH, HALF_X, COLS_X), F32)]
         + step_scratch(HALF_X)
-        + [pltpu.VMEM((CH, 8, COLS), F32), pltpu.VMEM((ROWS_X, 128), F32), pltpu.SemaphoreType.DMA((2,))],
+        + [pltpu.VMEM((CH, 8, COLS), F32)] * 2
+        + [pltpu.VMEM((ROWS_X, 128), F32), pltpu.SemaphoreType.DMA((3,))],
         flops=1 << 27,
     )(where, *arrays, halo, static)
 
@@ -514,11 +527,10 @@
     statics = (depth, rotation, diff, mask)
     m = lax.axis_index("member")
     where = jnp.stack([lax.axis_index("lat"), m % 2, m]).astype(jnp.int32)
-    first = spread_first(state)
+    first = spread_first(where, state)
     halos = exchange(*pack(where, state, statics))
-    halo = spread_halo_first(m, halos)
+    halo = spread_halo(m, halos)
     arrays, gate = spread_rest(where, *first, halo)
-    halo = spread_halo_rest(m, halo)
     own, static = own_steps(where, state, statics, halos, gate)
     mine = control_steps(where, arrays, halo, static)
     theirs = send(mine, [(i, i ^ 1) for i in range(8)])

time: 192 us -> 117 us (0.61); the launches traced: 189 us -> 116 us
  waiting for transfers between devices: 102 us -> 33.8 us
  Pallas kernels: 32.8 us -> 37 us
  starting transfers between devices: 35.8 us -> 32.2 us
  local copies, waits for them, and re-layouts: 15.3 us -> 12 us
    ppermute x9 -> x8, waiting for transfers between devices: 87.8 us -> 19.3 us  [send(): return lax.ppermute(value, 'member', pairs)]
    pallas_call x2 -> x3, Pallas kernels: 0.66 us -> 4.93 us  [the longest x1 2.47 us: spread_rest(): call(relay_kernel, [shape, shape], [SMEM] + [ANY] * 5, [VMEM] * 2, [pltpu...]
    slice x1 -> x0, local copies, waits for them, and re-layouts: 4.21 us -> none  [spread_first(): top, low = (state[:, :HALF_X], state[:, ROWS - HALF_X:])]
    ppermute x9 -> x8, starting transfers between devices: 12.2 us -> 8.14 us  [send(): return lax.ppermute(value, 'member', pairs)]
  transfers between devices with their start and end apart: 15 -> 14, of which waited for: 5 -> 5; matrix products, arithmetic and copies ran while one was open for 1% -> 0% of each run, Pallas kernels for 10% -> 16%
where the time goes in v2:
time: 117 us; the launch traced here: 116 us
  Pallas kernels  37 us (32%)
  waiting for transfers between devices  33.8 us (29%)
  starting transfers between devices  32.2 us (28%)
  local copies, waits for them, and re-layouts  12 us (10%)
    ppermute x8, waiting for transfers between devices, send(): return lax.ppermute(value, 'member', pairs)  19.3 us
    pallas_call x1, Pallas kernels, own_steps(): call(own_kernel, [jax.ShapeDtypeStruct((CH, ROWS, COLS), F32), jax.ShapeD...  15.3 us
    unnamed x42, local copies, waits for them, and re-layouts  11.4 us
    all_to_all x1, waiting for transfers between devices, per_device(): parts = lax.all_to_all(parts, ('lon', 'lat'), 0, 0)  10.8 us
    all_to_all x1, starting transfers between devices, per_device(): parts = lax.all_to_all(parts, ('lon', 'lat'), 0, 0)  10.4 us
    pallas_call x1, Pallas kernels, control_steps(): call(control_kernel, jax.ShapeDtypeStruct((CH, HALF, COLS), F32), [SMEM]...  8.28 us
    ppermute x8, starting transfers between devices, send(): return lax.ppermute(value, 'member', pairs)  8.14 us
    ppermute x1, starting transfers between devices, exchange(): lax.ppermute(c_west, both, down2)  5.29 us
  transfers between devices with their start and end apart: 14, of which 5 were waited for; matrix products, arithmetic and copies ran while one was open for 0% of the time, Pallas kernels for 16%

profile of v2, /device:TPU:24, one launch (start us, length us, event | category | flops | bytes accessed | tf_op | source)
XLA Modules:
  0.0 116.2 jit_solution(7131546458065504464)
XLA Ops:
  0.6 0.0 copy-start
  0.7 0.1 pad_add_fusion.lat.where
  0.7 2.4 %shard_map.87 = (f32[16,72,384]{2,1,0:T(8,128)}, f32[16,72,384]{2,1,0:T(8,128)}) custom-call(s32[3]{0:T(128)S(1)} %pad_add_fusion.lat.where, f32[16,128,384]{2,1,0:T(8,128)} %bitcast.5), custom_call_target="tpu_custom_call" | custom-call | flops 4194304 | bytes 8388608 | tf_op jit(solution)/shard_map/pallas_call | solution.py:309
  3.1 1.9 %collective-permute-start.5 = (f32[16,72,384]{2,1,0:T(8,128)}, f32[16,72,384]{2,1,0:T(8,128)}, u32[]{:S(2)}, u32[]{:S(2)}) collective-permute-start(f32[16,72,384]{2,1,0:T(8,128)} %get-tuple-element.20.top.refs_0_), channel_id=1, source_target_pairs={{0,64},{1,65},{2,66},{3,67},{4,68},{5,69},{6,70},{7,71},{8,72},{9,... | collective-permute-start | bytes 5308424 | tf_op jit(solution)/shard_map/ppermute | solution.py:293
  5.0 2.0 %collective-permute-start.6 = (f32[16,72,384]{2,1,0:T(8,128)}, f32[16,72,384]{2,1,0:T(8,128)}, u32[]{:S(2)}, u32[]{:S(2)}) collective-permute-start(f32[16,72,384]{2,1,0:T(8,128)} %get-tuple-element.21.low), channel_id=1, source_target_pairs={{0,224},{1,225},{2,226},{3,227},{4,228},{5,229},{6,230},{7,231},{8... | collective-permute-start | bytes 5308424 | tf_op jit(solution)/shard_map/ppermute | solution.py:293
  7.0 1.2 %copy-done.6 = f32[5,128,384]{2,1,0:T(8,128)S(1)} copy-done((f32[5,128,384]{2,1,0:T(8,128)S(1)}, f32[5,128,384]{2,1,0:T(8,128)}, u32[]{:S(2)}) %copy-start.6) | copy-done | bytes 983064
  8.2 0.9 copy-done.8
  9.1 0.9 copy-done.12
  10.0 0.9 copy-done.14
  10.9 1.9 %shard_map.86 = (f32[128,128]{1,0:T(8,128)S(1)}, f32[128,128]{1,0:T(8,128)S(1)}, f32[96,384]{1,0:T(8,128)S(1)}, f32[8,128]{1,0:T(8,128)S(1)}, f32[8,128]{1,0:T(8,128)S(1)}) custom-call(s32[3]{0:T(128)S(1)} %pad_add_fusion.lat.where, f32[16,128,384]{2,1,0:T(8,128)S(1)} %bitcast.7, f32[128,384]{1,0:T(8,128)S(1)} %copy-done.12, f32[128,384]{1,0:T(8,128)S(1)} %copy-done.14, ...), custom_call_target="tpu_custom_call" | custom-call | flops 4194304 | bytes 8388608 | tf_op jit(solution)/shard_map/pallas_call | solution.py:87
  12.8 3.1 %collective-permute-start.2 = (f32[96,384]{1,0:T(8,128)S(1)}, f32[96,384]{1,0:T(8,128)S(1)}, u32[]{:S(2)}, u32[]{:S(2)}) collective-permute-start(f32[96,384]{1,0:T(8,128)S(1)} %get-tuple-element.17), channel_id=1, source_target_pairs={{0,1},{1,0},{2,3},{3,2},{4,5},{5,4},{6,7},{7,6},{8,9},{9,8},{10,11... | collective-permute-start | bytes 442376 | tf_op jit(solution)/shard_map/ppermute | solution.py:112
  15.9 1.1 collective-permute-start.3
  17.1 5.3 %collective-permute-start.4 = (f32[8,128]{1,0:T(8,128)S(1)}, f32[8,128]{1,0:T(8,128)S(1)}, u32[]{:S(2)}, u32[]{:S(2)}) collective-permute-start(f32[8,128]{1,0:T(8,128)S(1)} %get-tuple-element.19), channel_id=1, source_target_pairs={{2,1},{3,0},{4,3},{5,2},{6,5},{7,4},{8,7},{9,6},{10,9},{11,8},{12,... | collective-permute-start | bytes 12296 | tf_op jit(solution)/shard_map/ppermute | solution.py:114
  22.4 1.6 %collective-permute-done.3.cw = f32[8,128]{1,0:T(8,128)S(1)} collective-permute-done((f32[8,128]{1,0:T(8,128)S(1)}, f32[8,128]{1,0:T(8,128)S(1)}, u32[]{:S(2)}, u32[]{:S(2)}) %collective-permute-start.3) | collective-permute-done | bytes 4128 | tf_op jit(solution)/shard_map/ppermute | solution.py:113
  23.9 4.1 %collective-permute-start.1 = (f32[128,128]{1,0:T(8,128)S(1)}, f32[128,128]{1,0:T(8,128)S(1)}, u32[]{:S(2)}, u32[]{:S(2)}) collective-permute-start(f32[128,128]{1,0:T(8,128)S(1)} %get-tuple-element.16), channel_id=1, source_target_pairs={{2,0},{4,2},{6,4},{8,6},{10,8},{12,10},{14,12},{16,14},{18,16},{20... | collective-permute-start | bytes 196616 | tf_op jit(solution)/shard_map/ppermute | solution.py:111
  28.1 2.2 %collective-permute-done.fw = f32[128,128]{1,0:T(8,128)S(1)} collective-permute-done((f32[128,128]{1,0:T(8,128)S(1)}, f32[128,128]{1,0:T(8,128)S(1)}, u32[]{:S(2)}, u32[]{:S(2)}) %collective-permute-start) | collective-permute-done | bytes 65568 | tf_op jit(solution)/shard_map/ppermute | solution.py:110
  30.3 0.0 collective-permute-done.1.fe
  30.3 0.0 collective-permute-done.2.rows
  30.3 0.1 shard_map.88
  30.4 0.7 collective-permute-start.7
  31.1 0.7 collective-permute-start.8
  31.9 0.0 copy-start.7
  31.9 0.0 copy-start.9
  31.9 0.0 copy-start.13
  31.9 0.0 copy-start.15
  31.9 2.5 %shard_map.89 = (f32[16,80,384]{2,1,0:T(8,128)}, f32[16,80,384]{2,1,0:T(8,128)}) custom-call(s32[3]{0:T(128)S(1)} %pad_add_fusion.lat.where, f32[16,72,384]{2,1,0:T(8,128)} %get-tuple-element.20.top.refs_0_, f32[16,72,384]{2,1,0:T(8,128)} %get-tuple-element.21.low, f32[16,72,384]{2,1,0:T(8,128)} %collective-permute-done.5.p1.refs_2_, ...), custom_call_target="tpu_custom_call" | custom-call | flops 4194304 | bytes 8388608 | tf_op jit(solution)/shard_map/pallas_call | solution.py:347
  34.4 0.8 collective-permute-start.10
  35.2 1.3 %collective-permute-start.11 = (f32[16,80,384]{2,1,0:T(8,128)}, f32[16,80,384]{2,1,0:T(8,128)S(1)}, u32[]{:S(2)}, u32[]{:S(2)}) collective-permute-start(f32[16,80,384]{2,1,0:T(8,128)} %get-tuple-element.24), channel_id=1, source_target_pairs={{0,192},{224,160},{1,193},{225,161},{2,194},{226,162},{3,195},{227... | collective-permute-start | bytes 5898248 | tf_op jit(solution)/shard_map/ppermute | solution.py:293
  36.5 0.8 collective-permute-start.9
  37.3 1.5 %copy-done.10 = f32[16,80,384]{2,1,0:T(8,128)S(1)} copy-done((f32[16,80,384]{2,1,0:T(8,128)S(1)}, f32[16,80,384]{2,1,0:T(8,128)}, u32[]{:S(2)}) %copy-start.10) | copy-done | bytes 1966104
  38.9 15.3 %shard_map.90 = (f32[16,128,384]{2,1,0:T(8,128)}, f32[8,72,512]{2,1,0:T(8,128)S(1)}) custom-call(s32[3]{0:T(128)S(1)} %pad_add_fusion.lat.where, f32[16,128,384]{2,1,0:T(8,128)} %bitcast.6, f32[128,384]{1,0:T(8,128)S(1)} %copy-done.13, f32[128,384]{1,0:T(8,128)S(1)} %copy-done.15, f32[5,128,384]{2,1,0:T(8,128)S(1)} %copy-done.7, s32[128,384]{1,0:T(8,128)S(1)} %copy-done.9, ...), custom_call_target="tpu_custom_call" | custom-call | flops 268435456 | bytes 8388608 | tf_op jit(solution)/shard_map/pallas_call | solution.py:265
  54.2 17.1 %collective-permute-done.11.refs_4_ = f32[16,80,384]{2,1,0:T(8,128)S(1)} collective-permute-done((f32[16,80,384]{2,1,0:T(8,128)}, f32[16,80,384]{2,1,0:T(8,128)S(1)}, u32[]{:S(2)}, u32[]{:S(2)}) %collective-permute-start.11) | collective-permute-done | bytes 1966112 | tf_op jit(solution)/shard_map/ppermute | solution.py:293
  71.3 1.3 %copy-done.18 = f32[16,80,384]{2,1,0:T(8,128)} copy-done((f32[16,80,384]{2,1,0:T(8,128)}, f32[16,80,384]{2,1,0:T(8,128)S(1)}, u32[]{:S(2)}) %copy-start.18) | copy-done | bytes 1966104
  72.6 8.3 %shard_map.91.control.mine = f32[16,64,384]{2,1,0:T(8,128)S(1)} custom-call(s32[3]{0:T(128)S(1)} %pad_add_fusion.lat.where, f32[16,72,384]{2,1,0:T(8,128)} %get-tuple-element.20.top.refs_0_, f32[16,72,384]{2,1,0:T(8,128)} %copy-done.19, f32[16,72,384]{2,1,0:T(8,128)} %collective-permute-done.5.p1.refs_2_, f32[16,80,384]{2,1,0:T(8,128)} %copy-done.17, ...), custom_call_target="tpu_custom_call" | custom-call | flops 134217728 | bytes 8388608 | tf_op jit(solution)/shard_map/pallas_call | solution.py:407
  80.9 0.1 collective-permute-start.12
  81.0 1.2 shard_map.92.earlier
  82.2 0.0 copy-start.20
  82.2 2.2 %collective-permute-done.12.control.theirs = f32[16,64,384]{2,1,0:T(8,128)S(1)} collective-permute-done((f32[16,64,384]{2,1,0:T(8,128)S(1)}, f32[16,64,384]{2,1,0:T(8,128)S(1)}, u32[]{:S(2)}, u32[]{:S(2)}) %collective-permute-start.12) | collective-permute-done | bytes 1572896 | tf_op jit(solution)/shard_map/ppermute | solution.py:293
  84.4 1.2 %shard_map.93 = f32[32,8,128]{2,1,0:T(8,128)S(1)} custom-call(s32[3]{0:T(128)S(1)} %pad_add_fusion.lat.where, f32[16,128,384]{2,1,0:T(8,128)S(1)} %copy-done.1, f32[16,64,384]{2,1,0:T(8,128)S(1)} %collective-permute-done.12.control.theirs, s32[128,384]{1,0:T(8,128)S(1)} %copy-done.9, s32[128,384]{1,0:T(8,128)S(1)} %copy-done.11, f32[8,128]{1,0:T(8,128)S(1)} %shard_map.92.earlier), custom_call_target="tpu_custom_call" | custom-call | flops 4194304 | bytes 8388608 | tf_op jit(solution)/shard_map/pallas_call | solution.py:459
  85.6 0.0 copy-start.4
  85.6 1.1 copy-done.4
  86.7 0.6 copy-done.16
  87.3 10.4 %all-to-all-start = ((f32[32,8,128]{2,1,0:T(8,128)}), f32[32,8,128]{2,1,0:T(8,128)S(1)}, u32[]{:S(2)}, u32[]{:S(2)}) async-start(f32[32,8,128]{2,1,0:T(8,128)} %copy-done.16), calls=%async_computation | async-start | bytes 262144 | tf_op jit(solution)/shard_map/all_to_all | solution.py:539
  97.8 10.8 %all-to-all-done.parts = f32[32,8,128]{2,1,0:T(8,128)S(1)} async-done(((f32[32,8,128]{2,1,0:T(8,128)}), f32[32,8,128]{2,1,0:T(8,128)S(1)}, u32[]{:S(2)}, u32[]{:S(2)}) %all-to-all-start) | async-done | bytes 131104 | tf_op jit(solution)/shard_map/all_to_all | solution.py:539
  108.5 1.4 %copy-done.3 = f32[16,64,384]{2,1,0:T(8,128)S(1)} copy-done((f32[16,64,384]{2,1,0:T(8,128)S(1)}, f32[16,64,384]{2,1,0:T(8,128)}, u32[]{:S(2)}) %copy-start.3) | copy-done | bytes 1572888
  110.0 1.4 %copy-done.5 = f32[16,64,384]{2,1,0:T(8,128)S(1)} copy-done((f32[16,64,384]{2,1,0:T(8,128)S(1)}, f32[16,64,384]{2,1,0:T(8,128)}, u32[]{:S(2)}) %copy-start.5) | copy-done | bytes 1572888
  111.4 4.3 %shard_map.94 = (f32[16,128,384]{2,1,0:T(8,128)}, f32[8,128]{1,0:T(8,128)S(1)}) custom-call(s32[3]{0:T(128)S(1)} %pad_add_fusion.lat.where, f32[16,128,384]{2,1,0:T(8,128)S(1)} %copy-done.1, f32[16,64,384]{2,1,0:T(8,128)S(1)} %copy-done.3, f32[16,64,384]{2,1,0:T(8,128)S(1)} %copy-done.5, s32[128,384]{1,0:T(8,128)S(1)} %copy-done.11, ...), custom_call_target="tpu_custom_call" | custom-call | flops 4194304 | bytes 10485760 | tf_op jit(solution)/shard_map/pallas_call | solution.py:513
  115.7 0.5 slice.3
  (38 shorter events, 0.1 us)
Async XLA Ops:
  0.6 6.3 %copy-start = (f32[1,16,128,384]{3,2,1,0:T(8,128)S(1)}, f32[1,16,128,384]{3,2,1,0:T(8,128)}, u32[]{:S(2)}) copy-start(f32[1,16,128,384]{3,2,1,0:T(8,128)} %param.7) | copy-start | bytes 9437188
  3.1 28.8 %collective-permute-start.5 = (f32[16,72,384]{2,1,0:T(8,128)}, f32[16,72,384]{2,1,0:T(8,128)}, u32[]{:S(2)}, u32[]{:S(2)}) collective-permute-start(f32[16,72,384]{2,1,0:T(8,128)} %get-tuple-element.20.top.refs_0_), channel_id=1, source_target_pairs={{0,64},{1,65},{2,66},{3,67},{4,68},{5,69},{6,70},{7,71},{8,72},{9,... | collective-permute-start | bytes 5308424 | tf_op jit(solution)/shard_map/ppermute | solution.py:293
  5.0 26.9 %collective-permute-start.6 = (f32[16,72,384]{2,1,0:T(8,128)}, f32[16,72,384]{2,1,0:T(8,128)}, u32[]{:S(2)}, u32[]{:S(2)}) collective-permute-start(f32[16,72,384]{2,1,0:T(8,128)} %get-tuple-element.21.low), channel_id=1, source_target_pairs={{0,224},{1,225},{2,226},{3,227},{4,228},{5,229},{6,230},{7,231},{8... | collective-permute-start | bytes 5308424 | tf_op jit(solution)/shard_map/ppermute | solution.py:293
  7.0 1.2 %copy-start.6 = (f32[5,128,384]{2,1,0:T(8,128)S(1)}, f32[5,128,384]{2,1,0:T(8,128)}, u32[]{:S(2)}) copy-start(f32[5,128,384]{2,1,0:T(8,128)} %diff.3) | copy-start | bytes 2949124
  8.2 0.9 copy-start.8
  9.1 0.9 copy-start.12
  10.0 0.9 copy-start.14
  12.8 17.5 %collective-permute-start.2 = (f32[96,384]{1,0:T(8,128)S(1)}, f32[96,384]{1,0:T(8,128)S(1)}, u32[]{:S(2)}, u32[]{:S(2)}) collective-permute-start(f32[96,384]{1,0:T(8,128)S(1)} %get-tuple-element.17), channel_id=1, source_target_pairs={{0,1},{1,0},{2,3},{3,2},{4,5},{5,4},{6,7},{7,6},{8,9},{9,8},{10,11... | collective-permute-start | bytes 442376 | tf_op jit(solution)/shard_map/ppermute | solution.py:112
  15.9 8.0 %collective-permute-start.3 = (f32[8,128]{1,0:T(8,128)S(1)}, f32[8,128]{1,0:T(8,128)S(1)}, u32[]{:S(2)}, u32[]{:S(2)}) collective-permute-start(f32[8,128]{1,0:T(8,128)S(1)} %get-tuple-element.18), channel_id=1, source_target_pairs={{0,3},{1,2},{2,5},{3,4},{4,7},{5,6},{6,9},{7,8},{8,11},{9,10},{10,... | collective-permute-start | bytes 12296 | tf_op jit(solution)/shard_map/ppermute | solution.py:113
  17.1 6.9 %collective-permute-start.4 = (f32[8,128]{1,0:T(8,128)S(1)}, f32[8,128]{1,0:T(8,128)S(1)}, u32[]{:S(2)}, u32[]{:S(2)}) collective-permute-start(f32[8,128]{1,0:T(8,128)S(1)} %get-tuple-element.19), channel_id=1, source_target_pairs={{2,1},{3,0},{4,3},{5,2},{6,5},{7,4},{8,7},{9,6},{10,9},{11,8},{12,... | collective-permute-start | bytes 12296 | tf_op jit(solution)/shard_map/ppermute | solution.py:114
  23.9 6.4 %collective-permute-start = (f32[128,128]{1,0:T(8,128)S(1)}, f32[128,128]{1,0:T(8,128)S(1)}, u32[]{:S(2)}, u32[]{:S(2)}) collective-permute-start(f32[128,128]{1,0:T(8,128)S(1)} %get-tuple-element.15), channel_id=1, source_target_pairs={{0,2},{2,4},{4,6},{6,8},{8,10},{10,12},{12,14},{14,16},{16,18},{18... | collective-permute-start | bytes 196616 | tf_op jit(solution)/shard_map/ppermute | solution.py:110
  23.9 6.4 %collective-permute-start.1 = (f32[128,128]{1,0:T(8,128)S(1)}, f32[128,128]{1,0:T(8,128)S(1)}, u32[]{:S(2)}, u32[]{:S(2)}) collective-permute-start(f32[128,128]{1,0:T(8,128)S(1)} %get-tuple-element.16), channel_id=1, source_target_pairs={{2,0},{4,2},{6,4},{8,6},{10,8},{12,10},{14,12},{16,14},{18,16},{20... | collective-permute-start | bytes 196616 | tf_op jit(solution)/shard_map/ppermute | solution.py:111
  30.4 0.7 collective-permute-start.7
  31.1 0.7 collective-permute-start.8
  31.9 5.4 %copy-start.7 = (f32[5,128,384]{2,1,0:T(8,128)S(1)}, f32[5,128,384]{2,1,0:T(8,128)}, u32[]{:S(2)}) copy-start(f32[5,128,384]{2,1,0:T(8,128)} %diff.3) | copy-start | bytes 2949124
  31.9 5.4 %copy-start.9 = (s32[128,384]{1,0:T(8,128)S(1)}, s32[128,384]{1,0:T(8,128)}, u32[]{:S(2)}) copy-start(s32[128,384]{1,0:T(8,128)} %mask.7) | copy-start | bytes 589828
  31.9 5.4 %copy-start.13 = (f32[128,384]{1,0:T(8,128)S(1)}, f32[128,384]{1,0:T(8,128)}, u32[]{:S(2)}) copy-start(f32[128,384]{1,0:T(8,128)} %depth.3) | copy-start | bytes 589828
  31.9 5.4 %copy-start.15 = (f32[128,384]{1,0:T(8,128)S(1)}, f32[128,384]{1,0:T(8,128)}, u32[]{:S(2)}) copy-start(f32[128,384]{1,0:T(8,128)} %rotation.3) | copy-start | bytes 589828
  34.4 19.8 %collective-permute-start.10 = (f32[16,80,384]{2,1,0:T(8,128)}, f32[16,80,384]{2,1,0:T(8,128)S(1)}, u32[]{:S(2)}, u32[]{:S(2)}) collective-permute-start(f32[16,80,384]{2,1,0:T(8,128)} %get-tuple-element.22.gate), channel_id=1, source_target_pairs={{0,96},{64,128},{1,97},{65,129},{2,98},{66,130},{3,99},{67,131},{4... | collective-permute-start | bytes 5898248 | tf_op jit(solution)/shard_map/ppermute | solution.py:293
  35.2 36.1 %collective-permute-start.11 = (f32[16,80,384]{2,1,0:T(8,128)}, f32[16,80,384]{2,1,0:T(8,128)S(1)}, u32[]{:S(2)}, u32[]{:S(2)}) collective-permute-start(f32[16,80,384]{2,1,0:T(8,128)} %get-tuple-element.24), channel_id=1, source_target_pairs={{0,192},{224,160},{1,193},{225,161},{2,194},{226,162},{3,195},{227... | collective-permute-start | bytes 5898248 | tf_op jit(solution)/shard_map/ppermute | solution.py:293
  36.5 17.7 %collective-permute-start.9 = (f32[16,72,384]{2,1,0:T(8,128)}, f32[16,72,384]{2,1,0:T(8,128)S(1)}, u32[]{:S(2)}, u32[]{:S(2)}) collective-permute-start(f32[16,72,384]{2,1,0:T(8,128)} %get-tuple-element.21.low), channel_id=1, source_target_pairs={{0,32},{1,33},{2,34},{3,35},{4,36},{5,37},{6,38},{7,39},{8,40},{9,... | collective-permute-start | bytes 5308424 | tf_op jit(solution)/shard_map/ppermute | solution.py:293
  37.3 1.5 %copy-start.10 = (f32[16,80,384]{2,1,0:T(8,128)S(1)}, f32[16,80,384]{2,1,0:T(8,128)}, u32[]{:S(2)}) copy-start(f32[16,80,384]{2,1,0:T(8,128)} %get-tuple-element.22.gate) | copy-start | bytes 5898244
  54.2 17.1 %copy-start.19 = (f32[16,72,384]{2,1,0:T(8,128)}, f32[16,72,384]{2,1,0:T(8,128)S(1)}, u32[]{:S(2)}) copy-start(f32[16,72,384]{2,1,0:T(8,128)S(1)} %collective-permute-done.9.refs_1_) | copy-start | bytes 5308420
  54.2 17.1 %copy-start.17 = (f32[16,80,384]{2,1,0:T(8,128)}, f32[16,80,384]{2,1,0:T(8,128)S(1)}, u32[]{:S(2)}) copy-start(f32[16,80,384]{2,1,0:T(8,128)S(1)} %collective-permute-done.10.refs_3_) | copy-start | bytes 5898244
  71.3 1.3 %copy-start.18 = (f32[16,80,384]{2,1,0:T(8,128)}, f32[16,80,384]{2,1,0:T(8,128)S(1)}, u32[]{:S(2)}) copy-start(f32[16,80,384]{2,1,0:T(8,128)S(1)} %collective-permute-done.11.refs_4_) | copy-start | bytes 5898244
  72.6 8.4 %copy-start.1 = (f32[16,128,384]{2,1,0:T(8,128)S(1)}, f32[16,128,384]{2,1,0:T(8,128)}, u32[]{:S(2)}) copy-start(f32[16,128,384]{2,1,0:T(8,128)} %get-tuple-element.23.own) | copy-start | bytes 9437188
  72.6 8.4 %copy-start.11 = (s32[128,384]{1,0:T(8,128)S(1)}, s32[128,384]{1,0:T(8,128)}, u32[]{:S(2)}) copy-start(s32[128,384]{1,0:T(8,128)} %region.5) | copy-start | bytes 589828
  80.9 1.3 %copy-start.2 = (f32[16,64,384]{2,1,0:T(8,128)}, f32[16,64,384]{2,1,0:T(8,128)S(1)}, u32[]{:S(2)}) copy-start(f32[16,64,384]{2,1,0:T(8,128)S(1)} %shard_map.91.control.mine) | copy-start | bytes 4718596
  80.9 3.5 %collective-permute-start.12 = (f32[16,64,384]{2,1,0:T(8,128)S(1)}, f32[16,64,384]{2,1,0:T(8,128)S(1)}, u32[]{:S(2)}, u32[]{:S(2)}) collective-permute-start(f32[16,64,384]{2,1,0:T(8,128)S(1)} %shard_map.91.control.mine), channel_id=1, source_target_pairs={{0,32},{32,0},{64,96},{96,64},{128,160},{160,128},{192,224},{224,1... | collective-permute-start | bytes 4718600 | tf_op jit(solution)/shard_map/ppermute | solution.py:293
  82.2 15.6 %copy-start.20 = (f32[16]{0:T(128)S(1)}, f32[16]{0:T(128)}, u32[]{:S(2)}) copy-start(f32[16]{0:T(128)} %param.13) | copy-start | bytes 196
  85.6 1.1 copy-start.4
  86.7 0.7 copy-start.16
  87.3 21.2 %all-to-all-start = ((f32[32,8,128]{2,1,0:T(8,128)}), f32[32,8,128]{2,1,0:T(8,128)S(1)}, u32[]{:S(2)}, u32[]{:S(2)}) async-start(f32[32,8,128]{2,1,0:T(8,128)} %copy-done.16), calls=%async_computation | async-start | bytes 262144 | tf_op jit(solution)/shard_map/all_to_all | solution.py:539
  108.5 1.4 %copy-start.3 = (f32[16,64,384]{2,1,0:T(8,128)S(1)}, f32[16,64,384]{2,1,0:T(8,128)}, u32[]{:S(2)}) copy-start(f32[16,64,384]{2,1,0:T(8,128)} %copy-done.2) | copy-start | bytes 4718596
  110.0 1.4 %copy-start.5 = (f32[16,64,384]{2,1,0:T(8,128)S(1)}, f32[16,64,384]{2,1,0:T(8,128)}, u32[]{:S(2)}) copy-start(f32[16,64,384]{2,1,0:T(8,128)} %copy-done.4) | copy-start | bytes 4718596

commit v3 on v2

--- a/solution.py
+++ b/solution.py
@@ -18,17 +18,18 @@
 VMEM = pl.BlockSpec(memory_space=pltpu.VMEM)
 ANY = pl.BlockSpec(memory_space=pl.ANY)
 SMEM = pl.BlockSpec(memory_space=pltpu.SMEM)
+HBM = pl.BlockSpec(memory_space=pltpu.HBM)
 F32 = jnp.float32
 
 
-def call(kernel, out, in_specs, out_specs, scratch=(), flops=1 << 22, nbytes=1 << 23):
+def call(kernel, out, in_specs, out_specs, scratch=(), flops=1 << 22, nbytes=1 << 23, mib=12):
     return pl.pallas_call(
         kernel,
         out_shape=out,
         in_specs=in_specs,
         out_specs=out_specs,
         scratch_shapes=list(scratch),
-        compiler_params=pltpu.CompilerParams(vmem_limit_bytes=48 << 20),
+        compiler_params=pltpu.CompilerParams(vmem_limit_bytes=mib << 20),
         cost_estimate=pl.CostEstimate(flops=flops, bytes_accessed=nbytes, transcendentals=0),
     )
 
@@ -41,7 +42,7 @@
     return (k % 8, k >= 8) if k < CH else (8 + (k - CH) % 4, k - CH >= 4)
 
 
-def pack_kernel(lat, state, depth, rotation, diff, mask, west, east, rows, c_west, c_east, lo, hi, edge, sem):
+def pack_kernel(lat, state, depth, rotation, diff, mask, west, east, rows, c_west, c_east, lo, hi, edge, land, sem):
     upper = lat[0] == 0
     r0 = pl.multiple_of(jnp.where(upper, ROWS - 8, 0), 8)
     tile = pl.ds(r0, 8)
@@ -53,14 +54,15 @@
         lead = (slice(None),) if src.shape[:-2] else ()
         for j, (dst, cut) in enumerate([(edge, (tile, slice(None))), (lo, (full, left)), (hi, (full, right))]):
             copies.append(pltpu.make_async_copy(src.at[lead + cut], dst.at[at], sem.at[3 * i + j]))
+    copies.append(pltpu.make_async_copy(mask, land, sem.at[12]))
     for copy in copies:
         copy.start()
-    last = FIELDS - 1
-    lo[last] = mask[:, left].astype(F32)
-    hi[last] = mask[:, right].astype(F32)
-    edge[last] = mask[tile, :].astype(F32)
     for copy in copies:
         copy.wait()
+    last = FIELDS - 1
+    lo[last] = land[:, left].astype(F32)
+    hi[last] = land[:, right].astype(F32)
+    edge[last] = land[tile, :].astype(F32)
 
     lane = iota((ROWS, 128), 1)
     w = jnp.zeros((ROWS, 128), F32)
@@ -87,14 +89,16 @@
     return call(
         pack_kernel,
         [jax.ShapeDtypeStruct(s, F32) for s in shapes],
-        [SMEM] + [ANY] * 4 + [VMEM],
+        [SMEM] + [HBM] * 5,
         [VMEM] * 5,
         [
             pltpu.VMEM((FIELDS, ROWS, 128), F32),
             pltpu.VMEM((FIELDS, ROWS, 128), F32),
             pltpu.VMEM((FIELDS, 8, COLS), F32),
-            pltpu.SemaphoreType.DMA((12,)),
+            pltpu.VMEM((ROWS, COLS), jnp.int32),
+            pltpu.SemaphoreType.DMA((13,)),
         ],
+        mib=62,
     )(lat, state, *statics)
 
 
@@ -231,7 +235,7 @@
     return [pltpu.VMEM((CH, rows, COLS_X), F32)] + [pltpu.VMEM((rows, COLS_X), F32)] * 3
 
 
-def own_kernel(where, state, depth, rotation, diff, mask, fw, fe, rows, cw, ce, gate, out, part, x, y, ub, vb, h2, sem):
+def own_kernel(where, state, depth, rotation, diff, mask, fw, fe, rows, cw, ce, gate, out, part, x, land, y, ub, vb, h2, sem):
     main = (slice(0, ROWS), slice(0, COLS))
     copies = [
         pltpu.make_async_copy(state, x.at[(slice(0, CH),) + main], sem.at[0]),
@@ -239,12 +243,13 @@
         pltpu.make_async_copy(rotation, x.at[(CH + 1,) + main], sem.at[2]),
         pltpu.make_async_copy(diff, x.at[(slice(CH + 2, CH + 2 + LEV),) + main], sem.at[3]),
     ]
+    copies.append(pltpu.make_async_copy(mask, land, sem.at[4]))
     for copy in copies:
         copy.start()
-    x[(FIELDS - 1,) + main] = mask[...].astype(F32)
     fill_halo(x, where, fw, fe, rows, cw, ce)
     for copy in copies:
         copy.wait()
+    x[(FIELDS - 1,) + main] = land[...].astype(F32)
     first = where[1] == 0
     tiles = HALF // 8
     sub = iota((8, COLS_X), 0)
@@ -268,10 +273,13 @@
             jax.ShapeDtypeStruct((CH, ROWS, COLS), F32),
             jax.ShapeDtypeStruct((FIELDS - CH, HALF_X, COLS_X), F32),
         ],
-        [SMEM] + [ANY] * 4 + [VMEM] * 6 + [ANY],
+        [SMEM] + [HBM] * 5 + [VMEM] * 5 + [HBM],
         [VMEM] * 2,
-        [pltpu.VMEM((FIELDS, ROWS_X, COLS_X), F32)] + step_scratch(ROWS_X) + [pltpu.SemaphoreType.DMA((4,))],
+        [pltpu.VMEM((FIELDS, ROWS_X, COLS_X), F32), pltpu.VMEM((ROWS, COLS), jnp.int32)]
+        + step_scratch(ROWS_X)
+        + [pltpu.SemaphoreType.DMA((5,))],
         flops=1 << 28,
+        mib=28,
     )(where, state, *statics, *halos, gate)
 
 
@@ -293,40 +301,57 @@
     return lax.ppermute(value, "member", pairs)
 
 
-def cut_kernel(where, state, top, low, sem):
+CHUNKS = 4
+
+
+def staged(copies, buffer, sem):
+    n = CH // CHUNKS
+    both = []
+    for i, (src, dst) in enumerate(copies):
+        for j in range(CHUNKS):
+            ch, s = slice(n * j, n * j + n), CHUNKS * i + j
+            one = pltpu.make_async_copy(src.at[ch], buffer.at[i, ch], sem.at[2 * s])
+            both.append((one, pltpu.make_async_copy(buffer.at[i, ch], dst.at[ch, 0:HALF_X, :], sem.at[2 * s + 1])))
+            one.start()
+    for one, two in both:
+        one.wait()
+        two.start()
+    for one, two in both:
+        two.wait()
+
+
+STAGE = [pltpu.VMEM((2, CH, HALF_X, COLS), F32), pltpu.SemaphoreType.DMA((4 * CHUNKS,))]
+
+
+def cut_kernel(where, state, top, low, buffer, sem):
     @pl.when(where[2] == 0)
     def _():
-        one = pltpu.make_async_copy(state.at[:, 0:HALF_X, :], top, sem.at[0])
-        two = pltpu.make_async_copy(state.at[:, ROWS - HALF_X : ROWS, :], low, sem.at[1])
-        one.start()
-        two.start()
-        one.wait()
-        two.wait()
+        staged(
+            [(state.at[:, 0:HALF_X, :], top), (state.at[:, ROWS - HALF_X : ROWS, :], low)], buffer, sem
+        )
 
 
 def spread_first(where, state):
     shape = jax.ShapeDtypeStruct((CH, HALF_X, COLS), F32)
-    top, low = call(cut_kernel, [shape, shape], [SMEM, ANY], [VMEM] * 2, [pltpu.SemaphoreType.DMA((2,))])(where, state)
-    return top, low, send(top, [(0, 2)]), send(low, [(0, 7)]), send(low, [(0, 1)])
-
-
-def spread_halo(m, halos):
-    own = call(control_halo_kernel, jax.ShapeDtypeStruct((CH, 8, COLS), F32), [VMEM] * 5, VMEM)(*halos)
-    h = jnp.where(m == 0, own, send(own, [(0, 1)]))
-    return jnp.where(m < 2, h, send(h, [(0, 2), (1, 7)]))
-
-
-def relay_kernel(where, top, low, p1, m1, halo, u, v, sem):
+    top, low = call(cut_kernel, [shape, shape], [SMEM, HBM], [HBM] * 2, STAGE, mib=62)(where, state)
+    return top, low, send(top, [(0, 2)]), send(low, [(0, 7)])
+
+
+def relay_kernel(where, top, low, p1, m1, halo, u, v, buffer, sem, ride, ride_sem):
     m = where[2]
 
     def move(pairs):
-        copies = []
-        for i, (src, dst) in enumerate(pairs):
-            copies.append(pltpu.make_async_copy(src, dst.at[:, 0:HALF_X, :], sem.at[2 * i]))
-            copies.append(pltpu.make_async_copy(halo, dst.at[:, HALF_X : HALF_X + 8, :], sem.at[2 * i + 1]))
-        for copy in copies:
+        one = pltpu.make_async_copy(halo, ride, ride_sem.at[0])
+        one.start()
+        one.wait()
+        more = [
+            pltpu.make_async_copy(ride, dst.at[:, HALF_X : HALF_X + 8, :], ride_sem.at[1 + i])
+            for i, (_, dst) in enumerate(pairs)
+        ]
+        for copy in more:
             copy.start()
-        for copy in copies:
+        staged(pairs, buffer, sem)
+        for copy in more:
             copy.wait()
 
     @pl.when(m == 0)
@@ -342,14 +367,22 @@
         move([(m1, v)])
 
 
-def spread_rest(where, top, low, p1, m1, e0, halo):
+def spread_rest(where, top, low, p1, m1, halo):
+    m = where[2]
+    for_two, for_seven = send(halo, [(0, 2)]), send(halo, [(0, 7)])
+    halo = jnp.where(m == 2, for_two, jnp.where(m == 7, for_seven, halo))
     shape = jax.ShapeDtypeStruct((CH, HALF_X + 8, COLS), F32)
     u, v = call(
-        relay_kernel, [shape, shape], [SMEM] + [ANY] * 5, [VMEM] * 2, [pltpu.SemaphoreType.DMA((4,))]
+        relay_kernel,
+        [shape, shape],
+        [SMEM] + [HBM] * 4 + [ANY],
+        [HBM] * 2,
+        STAGE + [pltpu.VMEM((CH, 8, COLS), F32), pltpu.SemaphoreType.DMA((3,))],
     )(where, top, low, p1, m1, halo)
     p2 = send(u, [(0, 3), (2, 4)])
     m2 = send(v, [(0, 6), (7, 5)])
-    return (top, e0, p1, p2, m2, m1), u
+    e0 = send(u, [(0, 1)])
+    return (top, e0, p1, p2, m2, m1), halo, u
 
 
 HOLDER = ((0,), (1,), (2,), (3, 4), (5, 6), (7,))
@@ -407,17 +440,18 @@
     return call(
         control_kernel,
         jax.ShapeDtypeStruct((CH, HALF, COLS), F32),
-        [SMEM] + [ANY] * 7 + [VMEM],
+        [SMEM] + [HBM] * 6 + [ANY, VMEM],
         VMEM,
         [pltpu.VMEM((CH, HALF_X, COLS_X), F32)]
         + step_scratch(HALF_X)
         + [pltpu.VMEM((CH, 8, COLS), F32)] * 2
         + [pltpu.VMEM((ROWS_X, 128), F32), pltpu.SemaphoreType.DMA((3,))],
         flops=1 << 27,
+        mib=16,
     )(where, *arrays, halo, static)
 
 
-def sums_kernel(other, where, own, control, mask, region, earlier, out):
+def sums_kernel(other, where, own, control, mask, region, earlier, out, *copy):
     start = HALF // 8 * (where[1] ^ 1 if other else where[1])
 
     def body(t, carry):
@@ -448,8 +482,12 @@
             row = jnp.where(lane == REGIONS * j + r, s, row)
     if other:
         row = row + earlier[...]
+        copies, sem = copy
         for i in range(out.shape[0]):
-            out[i] = row
+            copies[i] = row
+        move = pltpu.make_async_copy(copies, out, sem.at[0])
+        move.start()
+        move.wait()
     else:
         out[...] = row + earlier[...]
 
@@ -457,7 +495,12 @@
 def half_sums(other, where, own, control, mask, region, earlier):
     shape = (32, 8, 128) if other else (8, 128)
     return call(
-        functools.partial(sums_kernel, other), jax.ShapeDtypeStruct(shape, F32), [SMEM] + [VMEM] * 5, VMEM
+        functools.partial(sums_kernel, other),
+        jax.ShapeDtypeStruct(shape, F32),
+        [SMEM] + [VMEM] * 5,
+        HBM if other else VMEM,
+        [pltpu.VMEM(shape, F32), pltpu.SemaphoreType.DMA((1,))] if other else (),
+        mib=4,
     )(where, own, control, mask, region, earlier)
 
 
@@ -474,7 +517,7 @@
         counts = jnp.where(lane < REGIONS, pltpu.roll(total, 128 - REGIONS, 1), 1.0)
         squares = jnp.where(lane < REGIONS, total, 1.0)
         g = jnp.sqrt(squares / (counts * CH) + EPSILON)
-        growth[...] = g
+        growth[...] = g[0:1, 0:REGIONS]
         factor = target[...] / g
 
         def body(t, _):
@@ -488,14 +531,15 @@
         lax.fori_loop(0, ROWS // 8, body, 0)
 
     start = HALF // 8 * where[1]
+    lead = pl.program_id(0) * BLOCK
     for ref, s in ((mine, start), (theirs, HALF // 8 - start)):
 
         def body(t, _):
             c, g = tile_at(t), tile_at(t + s)
             f = cell[g, :]
             for k in range(BLOCK):
-                q = ref[k, c, :]
-                out[k, g, :] = q + f * (own[k, g, :] - q)
+                q = ref[lead + k, c, :]
+                out[k, g, :] = q + f * (own[lead + k, g, :] - q)
             return 0
 
         lax.fori_loop(0, HALF // 8, body, 0)
@@ -504,20 +548,16 @@
 def rescale(where, own, mine, theirs, region, parts, target):
     target = jnp.broadcast_to(jnp.pad(target, (0, 128 - REGIONS), constant_values=1.0), (8, 128))
 
-    def cut(rows):
-        return pl.BlockSpec((BLOCK, rows, COLS), lambda i: (i, 0, 0))
-
-    def whole(*shape):
-        return pl.BlockSpec(shape, lambda i: (0,) * len(shape))
-
+    cut = pl.BlockSpec((BLOCK, ROWS, COLS), lambda i: (i, 0, 0))
+    row = pl.BlockSpec((1, REGIONS), lambda i: (0, 0))
     return pl.pallas_call(
         final_kernel,
         grid=(CH // BLOCK,),
-        out_shape=[jax.ShapeDtypeStruct((CH, ROWS, COLS), F32), jax.ShapeDtypeStruct((8, 128), F32)],
-        in_specs=[SMEM, cut(ROWS), cut(HALF), cut(HALF), whole(ROWS, COLS), whole(32, 8, 128), whole(8, 128)],
-        out_specs=[cut(ROWS), whole(8, 128)],
+        out_shape=[jax.ShapeDtypeStruct((CH, ROWS, COLS), F32), jax.ShapeDtypeStruct((1, REGIONS), F32)],
+        in_specs=[SMEM] + [VMEM] * 6,
+        out_specs=[cut, row],
         scratch_shapes=[pltpu.VMEM((ROWS, COLS), F32)],
-        compiler_params=pltpu.CompilerParams(vmem_limit_bytes=32 << 20),
+        compiler_params=pltpu.CompilerParams(vmem_limit_bytes=8 << 20),
         cost_estimate=pl.CostEstimate(flops=1 << 22, bytes_accessed=10 << 20, transcendentals=0),
     )(where, own, mine, theirs, region, parts, target)
 
@@ -529,8 +569,8 @@
     where = jnp.stack([lax.axis_index("lat"), m % 2, m]).astype(jnp.int32)
     first = spread_first(where, state)
     halos = exchange(*pack(where, state, statics))
-    halo = spread_halo(m, halos)
-    arrays, gate = spread_rest(where, *first, halo)
+    halo = call(control_halo_kernel, jax.ShapeDtypeStruct((CH, 8, COLS), F32), [VMEM] * 5, VMEM)(*halos)
+    arrays, halo, gate = spread_rest(where, *first, halo)
     own, static = own_steps(where, state, statics, halos, gate)
     mine = control_steps(where, arrays, halo, static)
     theirs = send(mine, [(i, i ^ 1) for i in range(8)])
@@ -538,7 +578,7 @@
     parts = half_sums(True, where, own, theirs, mask, region, parts)
     parts = lax.all_to_all(parts, ("lon", "lat"), 0, 0)
     bred, growth = rescale(where, own, mine, theirs, region, parts, target)
-    return bred[None], growth[:1, :REGIONS]
+    return bred[None], growth
 
 
 def solution(mesh):

time: 117 us -> 112 us (0.957)
  local copies, waits for them, and re-layouts: 12 us -> 6.89 us
  Pallas kernels: 37 us -> 33.3 us
  waiting for transfers between devices: 33.8 us -> 37.5 us
    unnamed x42 -> x36, local copies, waits for them, and re-layouts: 11.4 us -> 6.88 us
    pallas_call x3, Pallas kernels: 4.93 us -> 1.65 us  [the longest x1 0.84 us: spread_first(): call(cut_kernel, [shape, shape], [SMEM, HBM], [HBM] * 2, STAGE, mib=62)]
    ppermute x8, waiting for transfers between devices: 19.3 us -> 22.5 us  [send(): return lax.ppermute(value, 'member', pairs)]
    pallas_call x1, Pallas kernels: 1.85 us -> 4.42 us  [pack(): call(pack_kernel, [jax.ShapeDtypeStruct(s, F32) for s in shapes], [SMEM]...]
    pallas_call x1, Pallas kernels: 15.3 us -> 13.6 us  [own_steps(): call(own_kernel, [jax.ShapeDtypeStruct((CH, ROWS, COLS), F32), jax.ShapeD...]
    pallas_call x1, Pallas kernels: 8.28 us -> 6.77 us  [control_steps(): call(control_kernel, jax.ShapeDtypeStruct((CH, HALF, COLS), F32), [SMEM]...]
  transfers between devices with their start and end apart: 14 -> 14, of which waited for: 5 -> 5; matrix products, arithmetic and copies ran while one was open for 0% -> 0% of each run, Pallas kernels for 16% -> 17%
where the time goes in v3:
time: 112 us
  waiting for transfers between devices  37.5 us (33%)
  Pallas kernels  33.3 us (30%)
  starting transfers between devices  32.4 us (29%)
  local copies, waits for them, and re-layouts  6.89 us (6%)
    ppermute x8, waiting for transfers between devices, send(): return lax.ppermute(value, 'member', pairs)  22.5 us
    pallas_call x1, Pallas kernels, own_steps(): call(own_kernel, [jax.ShapeDtypeStruct((CH, ROWS, COLS), F32), jax.ShapeD...  13.6 us
    all_to_all x1, waiting for transfers between devices, per_device(): parts = lax.all_to_all(parts, ('lon', 'lat'), 0, 0)  10.8 us
    all_to_all x1, starting transfers between devices, per_device(): parts = lax.all_to_all(parts, ('lon', 'lat'), 0, 0)  10.4 us
    ppermute x8, starting transfers between devices, send(): return lax.ppermute(value, 'member', pairs)  8.33 us
    unnamed x36, local copies, waits for them, and re-layouts  6.88 us
    pallas_call x1, Pallas kernels, control_steps(): call(control_kernel, jax.ShapeDtypeStruct((CH, HALF, COLS), F32), [SMEM]...  6.77 us
    ppermute x1, starting transfers between devices, exchange(): lax.ppermute(c_west, both, down2)  5.29 us
  transfers between devices with their start and end apart: 14, of which 5 were waited for; matrix products, arithmetic and copies ran while one was open for 0% of the time, Pallas kernels for 17%

profile of v3, /device:TPU:24, one launch (start us, length us, event | category | flops | bytes accessed | tf_op | source)
XLA Modules:
  0.0 111.8 jit_solution(13872171482979418488)
XLA Ops:
  0.6 0.7 pad_add_fusion.lat.where
  1.3 0.8 shard_map.87
  2.1 1.9 %collective-permute-start.5 = (f32[16,72,384]{2,1,0:T(8,128)}, f32[16,72,384]{2,1,0:T(8,128)}, u32[]{:S(2)}, u32[]{:S(2)}) collective-permute-start(f32[16,72,384]{2,1,0:T(8,128)} %get-tuple-element.20.top.refs_0_), channel_id=1, source_target_pairs={{0,64},{1,65},{2,66},{3,67},{4,68},{5,69},{6,70},{7,71},{8,72},{9,... | collective-permute-start | bytes 5308424 | tf_op jit(solution)/shard_map/ppermute | solution.py:301
  4.1 2.0 %collective-permute-start.6 = (f32[16,72,384]{2,1,0:T(8,128)}, f32[16,72,384]{2,1,0:T(8,128)}, u32[]{:S(2)}, u32[]{:S(2)}) collective-permute-start(f32[16,72,384]{2,1,0:T(8,128)} %get-tuple-element.21.low), channel_id=1, source_target_pairs={{0,224},{1,225},{2,226},{3,227},{4,228},{5,229},{6,230},{7,231},{8... | collective-permute-start | bytes 5308424 | tf_op jit(solution)/shard_map/ppermute | solution.py:301
  6.0 4.4 %shard_map.86 = (f32[128,128]{1,0:T(8,128)}, f32[128,128]{1,0:T(8,128)}, f32[96,384]{1,0:T(8,128)}, f32[8,128]{1,0:T(8,128)}, f32[8,128]{1,0:T(8,128)}) custom-call(s32[3]{0:T(128)} %pad_add_fusion.lat.where, f32[16,128,384]{2,1,0:T(8,128)} %bitcast.6, f32[128,384]{1,0:T(8,128)} %depth.3, f32[128,384]{1,0:T(8,128)} %rotation.3, f32[5,128,384]{2,1,0:T(8,128)} %diff.3, ...), custom_call_target="tpu_custom_call" | custom-call | flops 4194304 | bytes 8388608 | tf_op jit(solution)/shard_map/pallas_call | solution.py:89
  10.5 3.1 %collective-permute-start.2 = (f32[96,384]{1,0:T(8,128)}, f32[96,384]{1,0:T(8,128)S(1)}, u32[]{:S(2)}, u32[]{:S(2)}) collective-permute-start(f32[96,384]{1,0:T(8,128)} %get-tuple-element.17), channel_id=1, source_target_pairs={{0,1},{1,0},{2,3},{3,2},{4,5},{5,4},{6,7},{7,6},{8,9},{9,8},{10,11... | collective-permute-start | bytes 442376 | tf_op jit(solution)/shard_map/ppermute | solution.py:116
  13.6 1.1 %collective-permute-start.3 = (f32[8,128]{1,0:T(8,128)}, f32[8,128]{1,0:T(8,128)S(1)}, u32[]{:S(2)}, u32[]{:S(2)}) collective-permute-start(f32[8,128]{1,0:T(8,128)} %get-tuple-element.18), channel_id=1, source_target_pairs={{0,3},{1,2},{2,5},{3,4},{4,7},{5,6},{6,9},{7,8},{8,11},{9,10},{10,... | collective-permute-start | bytes 12296 | tf_op jit(solution)/shard_map/ppermute | solution.py:117
  14.7 5.3 %collective-permute-start.4 = (f32[8,128]{1,0:T(8,128)}, f32[8,128]{1,0:T(8,128)S(1)}, u32[]{:S(2)}, u32[]{:S(2)}) collective-permute-start(f32[8,128]{1,0:T(8,128)} %get-tuple-element.19), channel_id=1, source_target_pairs={{2,1},{3,0},{4,3},{5,2},{6,5},{7,4},{8,7},{9,6},{10,9},{11,8},{12,... | collective-permute-start | bytes 12296 | tf_op jit(solution)/shard_map/ppermute | solution.py:118
  20.0 1.8 %collective-permute-done.3.cw = f32[8,128]{1,0:T(8,128)S(1)} collective-permute-done((f32[8,128]{1,0:T(8,128)}, f32[8,128]{1,0:T(8,128)S(1)}, u32[]{:S(2)}, u32[]{:S(2)}) %collective-permute-start.3) | collective-permute-done | bytes 4128 | tf_op jit(solution)/shard_map/ppermute | solution.py:117
  21.8 0.0 collective-permute-start
  21.8 0.0 collective-permute-done.4.ce
  21.8 4.1 %collective-permute-start.1 = (f32[128,128]{1,0:T(8,128)}, f32[128,128]{1,0:T(8,128)S(1)}, u32[]{:S(2)}, u32[]{:S(2)}) collective-permute-start(f32[128,128]{1,0:T(8,128)} %get-tuple-element.16), channel_id=1, source_target_pairs={{2,0},{4,2},{6,4},{8,6},{10,8},{12,10},{14,12},{16,14},{18,16},{20... | collective-permute-start | bytes 196616 | tf_op jit(solution)/shard_map/ppermute | solution.py:115
  25.9 2.4 %collective-permute-done.fw = f32[128,128]{1,0:T(8,128)S(1)} collective-permute-done((f32[128,128]{1,0:T(8,128)}, f32[128,128]{1,0:T(8,128)S(1)}, u32[]{:S(2)}, u32[]{:S(2)}) %collective-permute-start) | collective-permute-done | bytes 65568 | tf_op jit(solution)/shard_map/ppermute | solution.py:114
  28.4 0.0 collective-permute-done.1.fe
  28.4 0.0 collective-permute-done.2.rows
  28.4 0.1 shard_map.88
  28.5 0.5 copy-done.14
  29.0 0.7 collective-permute-start.7
  29.7 0.7 collective-permute-start.8
  30.4 0.0 collective-permute-done.8
  30.4 0.0 copy-start.11
  30.4 0.0 copy-start.12
  30.5 0.0 copy-start
  30.5 0.0 copy-start.7
  30.5 0.0 copy-start.8
  30.5 0.0 collective-permute-done.5.p1.refs_2_
  30.6 1.6 %copy-done.10 = f32[16,72,384]{2,1,0:T(8,128)S(1)} copy-done((f32[16,72,384]{2,1,0:T(8,128)S(1)}, f32[16,72,384]{2,1,0:T(8,128)}, u32[]{:S(2)}) %copy-start.10) | copy-done | bytes 1769496
  32.2 0.7 shard_map.89
  32.9 0.8 collective-permute-start.10
  33.7 0.0 copy-start.4
  33.7 1.4 %collective-permute-start.11 = (f32[16,80,384]{2,1,0:T(8,128)S(1)}, f32[16,80,384]{2,1,0:T(8,128)S(1)}, u32[]{:S(2)}, u32[]{:S(2)}) collective-permute-start(f32[16,80,384]{2,1,0:T(8,128)S(1)} %get-tuple-element.24), channel_id=1, source_target_pairs={{0,192},{224,160},{1,193},{225,161},{2,194},{226,162},{3,195},{227... | collective-permute-start | bytes 5898248 | tf_op jit(solution)/shard_map/ppermute | solution.py:301
  35.2 0.8 collective-permute-start.9
  36.0 13.6 %shard_map.90 = (f32[16,128,384]{2,1,0:T(8,128)S(1)}, f32[8,72,512]{2,1,0:T(8,128)S(1)}) custom-call(s32[3]{0:T(128)S(1)} %copy-done.16, f32[16,128,384]{2,1,0:T(8,128)S(1)} %bitcast.7, f32[128,384]{1,0:T(8,128)S(1)} %copy-done.11, f32[128,384]{1,0:T(8,128)S(1)} %copy-done.12, f32[5,128,384]{2,1,0:T(8,128)S(1)} %copy-done.7, s32[128,384]{1,0:T(8,128)S(1)} %copy-done.8, ...), custom_call_target="tpu_custom_call" | custom-call | flops 268435456 | bytes 8388608 | tf_op jit(solution)/shard_map/pallas_call | solution.py:270
  49.7 20.3 %collective-permute-done.11.refs_4_ = f32[16,80,384]{2,1,0:T(8,128)S(1)} collective-permute-done((f32[16,80,384]{2,1,0:T(8,128)S(1)}, f32[16,80,384]{2,1,0:T(8,128)S(1)}, u32[]{:S(2)}, u32[]{:S(2)}) %collective-permute-start.11) | collective-permute-done | bytes 1966112 | tf_op jit(solution)/shard_map/ppermute | solution.py:301
  69.9 6.8 %shard_map.91.control.mine = f32[16,64,384]{2,1,0:T(8,128)S(1)} custom-call(s32[3]{0:T(128)S(1)} %copy-done.16, f32[16,72,384]{2,1,0:T(8,128)S(1)} %copy-done.4, f32[16,80,384]{2,1,0:T(8,128)S(1)} %collective-permute-done.9.refs_1_, f32[16,72,384]{2,1,0:T(8,128)} %collective-permute-done.5.p1.refs_2_, f32[16,80,384]{2,1,0:T(8,128)S(1)} %collective-permute-done.10.refs_3_, ...), custom_call_target="tpu_custom_call" | custom-call | flops 134217728 | bytes 8388608 | tf_op jit(solution)/shard_map/pallas_call | solution.py:440
  76.7 0.0 copy-start.1
  76.7 0.1 collective-permute-start.12
  76.8 1.2 %shard_map.92.earlier = f32[8,128]{1,0:T(8,128)S(1)} custom-call(s32[3]{0:T(128)S(1)} %copy-done.16, f32[16,128,384]{2,1,0:T(8,128)S(1)} %get-tuple-element.23.own, f32[16,64,384]{2,1,0:T(8,128)S(1)} %shard_map.91.control.mine, s32[128,384]{1,0:T(8,128)S(1)} %copy-done.8, s32[128,384]{1,0:T(8,128)S(1)} %copy-done.9, f32[8,128]{1,0:T(8,128)S(1)} %broadcast_in_dim.9.earlier), custom_call_target="tpu_custom_call" | custom-call | flops 4194304 | bytes 8388608 | tf_op jit(solution)/shard_map/pallas_call | solution.py:497
  78.0 0.0 copy-start.17
  78.0 2.2 %collective-permute-done.12.control.theirs = f32[16,64,384]{2,1,0:T(8,128)S(1)} collective-permute-done((f32[16,64,384]{2,1,0:T(8,128)S(1)}, f32[16,64,384]{2,1,0:T(8,128)S(1)}, u32[]{:S(2)}, u32[]{:S(2)}) %collective-permute-start.12) | collective-permute-done | bytes 1572896 | tf_op jit(solution)/shard_map/ppermute | solution.py:301
  80.2 1.3 %shard_map.93 = f32[32,8,128]{2,1,0:T(8,128)S(1)} custom-call(s32[3]{0:T(128)S(1)} %copy-done.16, f32[16,128,384]{2,1,0:T(8,128)S(1)} %get-tuple-element.23.own, f32[16,64,384]{2,1,0:T(8,128)S(1)} %collective-permute-done.12.control.theirs, s32[128,384]{1,0:T(8,128)S(1)} %copy-done.8, s32[128,384]{1,0:T(8,128)S(1)} %copy-done.9, f32[8,128]{1,0:T(8,128)S(1)} %shard_map.92.earlier), custom_call_target="tpu_custom_call" | custom-call | flops 4194304 | bytes 8388608 | tf_op jit(solution)/shard_map/pallas_call | solution.py:497
  81.6 1.2 %copy-done.5 = f32[16,64,384]{2,1,0:T(8,128)} copy-done((f32[16,64,384]{2,1,0:T(8,128)}, f32[16,64,384]{2,1,0:T(8,128)S(1)}, u32[]{:S(2)}) %copy-start.5) | copy-done | bytes 1572888
  82.8 0.6 copy-done.13
  83.4 10.4 %all-to-all-start = ((f32[32,8,128]{2,1,0:T(8,128)}), f32[32,8,128]{2,1,0:T(8,128)S(1)}, u32[]{:S(2)}, u32[]{:S(2)}) async-start(f32[32,8,128]{2,1,0:T(8,128)} %copy-done.13), calls=%async_computation | async-start | bytes 262144 | tf_op jit(solution)/shard_map/all_to_all | solution.py:579
  93.9 10.8 %all-to-all-done.parts = f32[32,8,128]{2,1,0:T(8,128)S(1)} async-done(((f32[32,8,128]{2,1,0:T(8,128)}), f32[32,8,128]{2,1,0:T(8,128)S(1)}, u32[]{:S(2)}, u32[]{:S(2)}) %all-to-all-start) | async-done | bytes 131104 | tf_op jit(solution)/shard_map/all_to_all | solution.py:579
  104.6 1.4 %copy-done.2 = f32[16,64,384]{2,1,0:T(8,128)S(1)} copy-done((f32[16,64,384]{2,1,0:T(8,128)S(1)}, f32[16,64,384]{2,1,0:T(8,128)}, u32[]{:S(2)}) %copy-start.2) | copy-done | bytes 1572888
  106.1 1.4 %copy-done.6 = f32[16,64,384]{2,1,0:T(8,128)S(1)} copy-done((f32[16,64,384]{2,1,0:T(8,128)S(1)}, f32[16,64,384]{2,1,0:T(8,128)}, u32[]{:S(2)}) %copy-start.6) | copy-done | bytes 1572888
  107.5 4.4 %shard_map.94 = (f32[16,128,384]{2,1,0:T(8,128)}, f32[1,16]{1,0:T(1,128)}) custom-call(s32[3]{0:T(128)S(1)} %copy-done.16, f32[16,128,384]{2,1,0:T(8,128)S(1)} %get-tuple-element.23.own, f32[16,64,384]{2,1,0:T(8,128)S(1)} %copy-done.2, f32[16,64,384]{2,1,0:T(8,128)S(1)} %copy-done.6, s32[128,384]{1,0:T(8,128)S(1)} %copy-done.9, ...), custom_call_target="tpu_custom_call" | custom-call | flops 4194304 | bytes 10485760 | tf_op jit(solution)/shard_map/pallas_call | solution.py:553
  (30 shorter events, 0.1 us)
Async XLA Ops:
  2.1 28.4 %collective-permute-start.5 = (f32[16,72,384]{2,1,0:T(8,128)}, f32[16,72,384]{2,1,0:T(8,128)}, u32[]{:S(2)}, u32[]{:S(2)}) collective-permute-start(f32[16,72,384]{2,1,0:T(8,128)} %get-tuple-element.20.top.refs_0_), channel_id=1, source_target_pairs={{0,64},{1,65},{2,66},{3,67},{4,68},{5,69},{6,70},{7,71},{8,72},{9,... | collective-permute-start | bytes 5308424 | tf_op jit(solution)/shard_map/ppermute | solution.py:301
  4.1 26.5 %copy-start.3 = (f32[16,72,384]{2,1,0:T(8,128)S(1)}, f32[16,72,384]{2,1,0:T(8,128)}, u32[]{:S(2)}) copy-start(f32[16,72,384]{2,1,0:T(8,128)} %get-tuple-element.20.top.refs_0_) | copy-start | bytes 5308420
  4.1 26.5 %copy-start.16 = (s32[3]{0:T(128)S(1)}, s32[3]{0:T(128)}, u32[]{:S(2)}) copy-start(s32[3]{0:T(128)} %pad_add_fusion.lat.where) | copy-start | bytes 40
  4.1 26.5 %collective-permute-start.6 = (f32[16,72,384]{2,1,0:T(8,128)}, f32[16,72,384]{2,1,0:T(8,128)}, u32[]{:S(2)}, u32[]{:S(2)}) collective-permute-start(f32[16,72,384]{2,1,0:T(8,128)} %get-tuple-element.21.low), channel_id=1, source_target_pairs={{0,224},{1,225},{2,226},{3,227},{4,228},{5,229},{6,230},{7,231},{8... | collective-permute-start | bytes 5308424 | tf_op jit(solution)/shard_map/ppermute | solution.py:301
  10.5 17.9 %collective-permute-start.2 = (f32[96,384]{1,0:T(8,128)}, f32[96,384]{1,0:T(8,128)S(1)}, u32[]{:S(2)}, u32[]{:S(2)}) collective-permute-start(f32[96,384]{1,0:T(8,128)} %get-tuple-element.17), channel_id=1, source_target_pairs={{0,1},{1,0},{2,3},{3,2},{4,5},{5,4},{6,7},{7,6},{8,9},{9,8},{10,11... | collective-permute-start | bytes 442376 | tf_op jit(solution)/shard_map/ppermute | solution.py:116
  13.6 8.2 %collective-permute-start.3 = (f32[8,128]{1,0:T(8,128)}, f32[8,128]{1,0:T(8,128)S(1)}, u32[]{:S(2)}, u32[]{:S(2)}) collective-permute-start(f32[8,128]{1,0:T(8,128)} %get-tuple-element.18), channel_id=1, source_target_pairs={{0,3},{1,2},{2,5},{3,4},{4,7},{5,6},{6,9},{7,8},{8,11},{9,10},{10,... | collective-permute-start | bytes 12296 | tf_op jit(solution)/shard_map/ppermute | solution.py:117
  14.7 7.1 %collective-permute-start.4 = (f32[8,128]{1,0:T(8,128)}, f32[8,128]{1,0:T(8,128)S(1)}, u32[]{:S(2)}, u32[]{:S(2)}) collective-permute-start(f32[8,128]{1,0:T(8,128)} %get-tuple-element.19), channel_id=1, source_target_pairs={{2,1},{3,0},{4,3},{5,2},{6,5},{7,4},{8,7},{9,6},{10,9},{11,8},{12,... | collective-permute-start | bytes 12296 | tf_op jit(solution)/shard_map/ppermute | solution.py:118
  21.8 6.6 %collective-permute-start = (f32[128,128]{1,0:T(8,128)}, f32[128,128]{1,0:T(8,128)S(1)}, u32[]{:S(2)}, u32[]{:S(2)}) collective-permute-start(f32[128,128]{1,0:T(8,128)} %get-tuple-element.15), channel_id=1, source_target_pairs={{0,2},{2,4},{4,6},{6,8},{8,10},{10,12},{12,14},{14,16},{16,18},{18... | collective-permute-start | bytes 196616 | tf_op jit(solution)/shard_map/ppermute | solution.py:114
  21.8 6.6 %collective-permute-start.1 = (f32[128,128]{1,0:T(8,128)}, f32[128,128]{1,0:T(8,128)S(1)}, u32[]{:S(2)}, u32[]{:S(2)}) collective-permute-start(f32[128,128]{1,0:T(8,128)} %get-tuple-element.16), channel_id=1, source_target_pairs={{2,0},{4,2},{6,4},{8,6},{10,8},{12,10},{14,12},{16,14},{18,16},{20... | collective-permute-start | bytes 196616 | tf_op jit(solution)/shard_map/ppermute | solution.py:115
  28.4 0.6 copy-start.14
  29.0 1.4 %collective-permute-start.7 = (f32[16,8,384]{2,1,0:T(8,128)S(1)}, f32[16,8,384]{2,1,0:T(8,128)S(1)}, u32[]{:S(2)}, u32[]{:S(2)}) collective-permute-start(f32[16,8,384]{2,1,0:T(8,128)S(1)} %shard_map.88), channel_id=1, source_target_pairs={{0,64},{1,65},{2,66},{3,67},{4,68},{5,69},{6,70},{7,71},{8,72},{9,... | collective-permute-start | bytes 589832 | tf_op jit(solution)/shard_map/ppermute | solution.py:301
  29.7 0.7 collective-permute-start.8
  30.4 5.6 %copy-start.11 = (f32[128,384]{1,0:T(8,128)S(1)}, f32[128,384]{1,0:T(8,128)}, u32[]{:S(2)}) copy-start(f32[128,384]{1,0:T(8,128)} %depth.3) | copy-start | bytes 589828
  30.4 5.5 %copy-start.12 = (f32[128,384]{1,0:T(8,128)S(1)}, f32[128,384]{1,0:T(8,128)}, u32[]{:S(2)}) copy-start(f32[128,384]{1,0:T(8,128)} %rotation.3) | copy-start | bytes 589828
  30.4 5.5 %copy-start.15 = (f32[128,128]{1,0:T(8,128)S(1)}, f32[128,128]{1,0:T(8,128)}, u32[]{:S(2)}) copy-start(f32[128,128]{1,0:T(8,128)} %copy-done.14) | copy-start | bytes 196612
  30.5 5.5 %copy-start = (f32[1,16,128,384]{3,2,1,0:T(8,128)S(1)}, f32[1,16,128,384]{3,2,1,0:T(8,128)}, u32[]{:S(2)}) copy-start(f32[1,16,128,384]{3,2,1,0:T(8,128)} %param.7) | copy-start | bytes 9437188
  30.5 5.5 %copy-start.7 = (f32[5,128,384]{2,1,0:T(8,128)S(1)}, f32[5,128,384]{2,1,0:T(8,128)}, u32[]{:S(2)}) copy-start(f32[5,128,384]{2,1,0:T(8,128)} %diff.3) | copy-start | bytes 2949124
  30.5 5.5 %copy-start.8 = (s32[128,384]{1,0:T(8,128)S(1)}, s32[128,384]{1,0:T(8,128)}, u32[]{:S(2)}) copy-start(s32[128,384]{1,0:T(8,128)} %mask.7) | copy-start | bytes 589828
  30.6 1.6 %copy-start.10 = (f32[16,72,384]{2,1,0:T(8,128)S(1)}, f32[16,72,384]{2,1,0:T(8,128)}, u32[]{:S(2)}) copy-start(f32[16,72,384]{2,1,0:T(8,128)} %get-tuple-element.21.low) | copy-start | bytes 5308420
  32.9 16.7 %collective-permute-start.10 = (f32[16,80,384]{2,1,0:T(8,128)S(1)}, f32[16,80,384]{2,1,0:T(8,128)S(1)}, u32[]{:S(2)}, u32[]{:S(2)}) collective-permute-start(f32[16,80,384]{2,1,0:T(8,128)S(1)} %get-tuple-element.22.gate), channel_id=1, source_target_pairs={{0,96},{64,128},{1,97},{65,129},{2,98},{66,130},{3,99},{67,131},{4... | collective-permute-start | bytes 5898248 | tf_op jit(solution)/shard_map/ppermute | solution.py:301
  33.7 36.2 %copy-start.4 = (f32[16,72,384]{2,1,0:T(8,128)S(1)}, f32[16,72,384]{2,1,0:T(8,128)}, u32[]{:S(2)}) copy-start(f32[16,72,384]{2,1,0:T(8,128)} %get-tuple-element.20.top.refs_0_) | copy-start | bytes 5308420
  33.7 36.2 %collective-permute-start.11 = (f32[16,80,384]{2,1,0:T(8,128)S(1)}, f32[16,80,384]{2,1,0:T(8,128)S(1)}, u32[]{:S(2)}, u32[]{:S(2)}) collective-permute-start(f32[16,80,384]{2,1,0:T(8,128)S(1)} %get-tuple-element.24), channel_id=1, source_target_pairs={{0,192},{224,160},{1,193},{225,161},{2,194},{226,162},{3,195},{227... | collective-permute-start | bytes 5898248 | tf_op jit(solution)/shard_map/ppermute | solution.py:301
  35.2 34.8 %collective-permute-start.9 = (f32[16,80,384]{2,1,0:T(8,128)S(1)}, f32[16,80,384]{2,1,0:T(8,128)S(1)}, u32[]{:S(2)}, u32[]{:S(2)}) collective-permute-start(f32[16,80,384]{2,1,0:T(8,128)S(1)} %get-tuple-element.22.gate), channel_id=1, source_target_pairs={{0,32},{1,33},{2,34},{3,35},{4,36},{5,37},{6,38},{7,39},{8,40},{9,... | collective-permute-start | bytes 5898248 | tf_op jit(solution)/shard_map/ppermute | solution.py:301
  69.9 6.9 %copy-start.9 = (s32[128,384]{1,0:T(8,128)S(1)}, s32[128,384]{1,0:T(8,128)}, u32[]{:S(2)}) copy-start(s32[128,384]{1,0:T(8,128)} %region.5) | copy-start | bytes 589828
  76.7 1.3 %copy-start.1 = (f32[16,64,384]{2,1,0:T(8,128)}, f32[16,64,384]{2,1,0:T(8,128)S(1)}, u32[]{:S(2)}) copy-start(f32[16,64,384]{2,1,0:T(8,128)S(1)} %shard_map.91.control.mine) | copy-start | bytes 4718596
  76.7 3.5 %collective-permute-start.12 = (f32[16,64,384]{2,1,0:T(8,128)S(1)}, f32[16,64,384]{2,1,0:T(8,128)S(1)}, u32[]{:S(2)}, u32[]{:S(2)}) collective-permute-start(f32[16,64,384]{2,1,0:T(8,128)S(1)} %shard_map.91.control.mine), channel_id=1, source_target_pairs={{0,32},{32,0},{64,96},{96,64},{128,160},{160,128},{192,224},{224,1... | collective-permute-start | bytes 4718600 | tf_op jit(solution)/shard_map/ppermute | solution.py:301
  78.0 15.8 %copy-start.17 = (f32[16]{0:T(128)S(1)}, f32[16]{0:T(128)}, u32[]{:S(2)}) copy-start(f32[16]{0:T(128)} %param.13) | copy-start | bytes 196
  81.6 1.2 %copy-start.5 = (f32[16,64,384]{2,1,0:T(8,128)}, f32[16,64,384]{2,1,0:T(8,128)S(1)}, u32[]{:S(2)}) copy-start(f32[16,64,384]{2,1,0:T(8,128)S(1)} %collective-permute-done.12.control.theirs) | copy-start | bytes 4718596
  82.8 0.7 copy-start.13
  83.4 21.2 %all-to-all-start = ((f32[32,8,128]{2,1,0:T(8,128)}), f32[32,8,128]{2,1,0:T(8,128)S(1)}, u32[]{:S(2)}, u32[]{:S(2)}) async-start(f32[32,8,128]{2,1,0:T(8,128)} %copy-done.13), calls=%async_computation | async-start | bytes 262144 | tf_op jit(solution)/shard_map/all_to_all | solution.py:579
  104.6 1.4 %copy-start.2 = (f32[16,64,384]{2,1,0:T(8,128)S(1)}, f32[16,64,384]{2,1,0:T(8,128)}, u32[]{:S(2)}) copy-start(f32[16,64,384]{2,1,0:T(8,128)} %copy-done.1) | copy-start | bytes 4718596
  106.1 1.4 %copy-start.6 = (f32[16,64,384]{2,1,0:T(8,128)S(1)}, f32[16,64,384]{2,1,0:T(8,128)}, u32[]{:S(2)}) copy-start(f32[16,64,384]{2,1,0:T(8,128)} %copy-done.5) | copy-start | bytes 4718596

commit v4 on v3

--- a/solution.py
+++ b/solution.py
@@ -22,13 +22,14 @@
 F32 = jnp.float32
 
 
-def call(kernel, out, in_specs, out_specs, scratch=(), flops=1 << 22, nbytes=1 << 23, mib=12):
+def call(kernel, out, in_specs, out_specs, scratch=(), flops=1 << 22, nbytes=1 << 23, mib=12, aliases=None):
     return pl.pallas_call(
         kernel,
-        out_shape=out,
+        out_shape=[jax.ShapeDtypeStruct(o.shape, o.dtype) for o in out] if isinstance(out, list) else out,
         in_specs=in_specs,
         out_specs=out_specs,
         scratch_shapes=list(scratch),
+        input_output_aliases=aliases or {},
         compiler_params=pltpu.CompilerParams(vmem_limit_bytes=mib << 20),
         cost_estimate=pl.CostEstimate(flops=flops, bytes_accessed=nbytes, transcendentals=0),
     )
@@ -279,7 +280,7 @@
         + step_scratch(ROWS_X)
         + [pltpu.SemaphoreType.DMA((5,))],
         flops=1 << 28,
-        mib=28,
+        mib=60,
     )(where, state, *statics, *halos, gate)
 
 
@@ -323,7 +324,7 @@
 STAGE = [pltpu.VMEM((2, CH, HALF_X, COLS), F32), pltpu.SemaphoreType.DMA((4 * CHUNKS,))]
 
 
-def cut_kernel(where, state, top, low, buffer, sem):
+def cut_kernel(where, state, low, top, buffer, sem):
     @pl.when(where[2] == 0)
     def _():
         staged(
@@ -333,63 +334,41 @@
 
 def spread_first(where, state):
     shape = jax.ShapeDtypeStruct((CH, HALF_X, COLS), F32)
-    top, low = call(cut_kernel, [shape, shape], [SMEM, HBM], [HBM] * 2, STAGE, mib=62)(where, state)
-    return top, low, send(top, [(0, 2)]), send(low, [(0, 7)])
-
-
-def relay_kernel(where, top, low, p1, m1, halo, u, v, buffer, sem, ride, ride_sem):
-    m = where[2]
-
-    def move(pairs):
-        one = pltpu.make_async_copy(halo, ride, ride_sem.at[0])
-        one.start()
-        one.wait()
-        more = [
-            pltpu.make_async_copy(ride, dst.at[:, HALF_X : HALF_X + 8, :], ride_sem.at[1 + i])
-            for i, (_, dst) in enumerate(pairs)
-        ]
-        for copy in more:
-            copy.start()
-        staged(pairs, buffer, sem)
-        for copy in more:
-            copy.wait()
-
-    @pl.when(m == 0)
+    low, top = call(cut_kernel, [shape, shape], [SMEM, HBM], [HBM] * 2, STAGE, mib=62)(where, state)
+    return low, top, send(top, [(0, 2)]), send(low, [(0, 7)])
+
+
+def relay_kernel(where, u, v, p1, m1, gate, u_out, v_out, buffer, sem):
+    @pl.when(where[2] == 2)
     def _():
-        move([(low, u), (top, v)])
-
-    @pl.when(m == 2)
+        staged([(p1, u_out)], buffer, sem)
+
+    @pl.when(where[2] == 7)
     def _():
-        move([(p1, u)])
-
-    @pl.when(m == 7)
-    def _():
-        move([(m1, v)])
-
-
-def spread_rest(where, top, low, p1, m1, halo):
+        staged([(m1, v_out)], buffer, sem)
+
+
+def spread_rest(where, u, v, p1, m1, halo):
     m = where[2]
     for_two, for_seven = send(halo, [(0, 2)]), send(halo, [(0, 7)])
-    halo = jnp.where(m == 2, for_two, jnp.where(m == 7, for_seven, halo))
-    shape = jax.ShapeDtypeStruct((CH, HALF_X + 8, COLS), F32)
+    known = jnp.where(m == 2, for_two, jnp.where(m == 7, for_seven, halo))
     u, v = call(
-        relay_kernel,
-        [shape, shape],
-        [SMEM] + [HBM] * 4 + [ANY],
-        [HBM] * 2,
-        STAGE + [pltpu.VMEM((CH, 8, COLS), F32), pltpu.SemaphoreType.DMA((3,))],
-    )(where, top, low, p1, m1, halo)
+        relay_kernel, [u, v], [SMEM] + [HBM] * 4 + [ANY], [HBM] * 2, STAGE, mib=60, aliases={1: 0, 2: 1}
+    )(where, u, v, p1, m1, known)
     p2 = send(u, [(0, 3), (2, 4)])
     m2 = send(v, [(0, 6), (7, 5)])
     e0 = send(u, [(0, 1)])
-    return (top, e0, p1, p2, m2, m1), halo, u
+    on = send(known, [(0, 1), (2, 4), (7, 5)])
+    across = send(known, [(2, 3), (7, 6)])
+    return (v, e0, p1, p2, m2, m1), (known, on, across), u
 
 
 HOLDER = ((0,), (1,), (2,), (3, 4), (5, 6), (7,))
+HALO_HOLDER = (0, 1, 0, 2, 1, 1, 2, 0)
 
 
 def control_kernel(where, *refs):
-    arrays, (early, static, out, x, y, ub, vb, h2, near, halo, strip, sem) = refs[:6], refs[6:]
+    arrays, halos, (static, out, x, y, ub, vb, h2, near, halo, strip, sem) = refs[:6], refs[6:9], refs[9:]
     first = where[1] == 0
     m = where[2]
     for array, members in zip(arrays, HOLDER):
@@ -397,11 +376,9 @@
             r0, r1 = (0, HALF) if member % 2 == 0 else (8, 0)
 
             @pl.when(m == member)
-            def _(array=array, r0=r0, r1=r1):
+            def _(array=array, r0=r0, r1=r1, source=halos[HALO_HOLDER[member]]):
                 one = pltpu.make_async_copy(array.at[:, r0 : r0 + HALF, :], x.at[:, 0:HALF, 0:COLS], sem.at[0])
                 two = pltpu.make_async_copy(array.at[:, r1 : r1 + 8, :], near, sem.at[1])
-                rides = array.shape[1] > HALF_X
-                source = array.at[:, HALF_X : HALF_X + 8, :] if rides else early
                 three = pltpu.make_async_copy(source, halo, sem.at[2])
                 one.start()
                 two.start()
@@ -436,33 +413,54 @@
     two_steps(x, static, y, ub, vb, h2, out)
 
 
-def control_steps(where, arrays, halo, static):
+def control_steps(where, arrays, halos, static):
     return call(
         control_kernel,
         jax.ShapeDtypeStruct((CH, HALF, COLS), F32),
-        [SMEM] + [HBM] * 6 + [ANY, VMEM],
+        [SMEM] + [HBM] * 6 + [ANY] * 3 + [VMEM],
         VMEM,
         [pltpu.VMEM((CH, HALF_X, COLS_X), F32)]
         + step_scratch(HALF_X)
         + [pltpu.VMEM((CH, 8, COLS), F32)] * 2
         + [pltpu.VMEM((ROWS_X, 128), F32), pltpu.SemaphoreType.DMA((3,))],
         flops=1 << 27,
-        mib=16,
-    )(where, *arrays, halo, static)
-
-
-def sums_kernel(other, where, own, control, mask, region, earlier, out, *copy):
-    start = HALF // 8 * (where[1] ^ 1 if other else where[1])
+        mib=60,
+    )(where, *arrays, *halos, static)
+
+
+def half_rows(where, other):
+    return pl.multiple_of(HALF * (where[1] ^ 1 if other else where[1]), 8)
+
+
+PARTS = 2
+
+
+def sums_kernel(other, where, own, control, mask, region, earlier, out, a, b, land, reg_all, rows, sem):
+    start = half_rows(where, other)
+    n = HALF // PARTS
+    copies = []
+    for i in range(PARTS):
+        at = slice(n * i, n * i + n)
+        here = pl.ds(start + n * i, n)
+        pairs = [
+            (own.at[:, here, :], a.at[:, at, :]),
+            (control.at[:, at, :], b.at[:, at, :]),
+            (mask.at[here, :], land.at[at, :]),
+            (region.at[here, :], reg_all.at[at, :]),
+        ]
+        copies.append([pltpu.make_async_copy(*pair, sem.at[4 * i + k]) for k, pair in enumerate(pairs)])
+        for copy in copies[-1]:
+            copy.start()
 
     def body(t, carry):
-        c, g = tile_at(t), tile_at(t + start)
+        c = tile_at(t)
         acc = None
         for k in range(CH):
-            d = own[k, g, :] - control[k, c, :]
+            d = a[k, c, :] - b[k, c, :]
             acc = d * d if acc is None else acc + d * d
-        oc = mask[g, :].astype(F32)
+        oc = land[c, :].astype(F32)
         cell = oc * acc
-        reg = region[g, :]
+        reg = reg_all[c, :]
         new = []
         for r in range(REGIONS):
             hit = reg == r
@@ -473,38 +471,43 @@
         return tuple(new)
 
     zero = jnp.zeros((8, 128), F32)
-    total = lax.fori_loop(0, HALF // 8, body, (zero,) * (2 * REGIONS))
+    total = (zero,) * (2 * REGIONS)
+    for i in range(PARTS):
+        for copy in copies[i]:
+            copy.wait()
+        total = lax.fori_loop(n // 8 * i, n // 8 * (i + 1), body, total)
     lane = iota((8, 128), 1)
     row = zero
     for r in range(REGIONS):
         for j in range(2):
             s = jnp.sum(jnp.sum(total[2 * r + j], axis=0, keepdims=True), axis=1, keepdims=True)
             row = jnp.where(lane == REGIONS * j + r, s, row)
-    if other:
-        row = row + earlier[...]
-        copies, sem = copy
-        for i in range(out.shape[0]):
-            copies[i] = row
-        move = pltpu.make_async_copy(copies, out, sem.at[0])
-        move.start()
-        move.wait()
-    else:
-        out[...] = row + earlier[...]
+    row = row + earlier[...]
+    if not other:
+        out[...] = row
+        return
+    for i in range(out.shape[0]):
+        rows[i] = row
+    move = pltpu.make_async_copy(rows, out, sem.at[0])
+    move.start()
+    move.wait()
 
 
 def half_sums(other, where, own, control, mask, region, earlier):
     shape = (32, 8, 128) if other else (8, 128)
+    cells = pltpu.VMEM((HALF, COLS), jnp.int32)
     return call(
         functools.partial(sums_kernel, other),
         jax.ShapeDtypeStruct(shape, F32),
-        [SMEM] + [VMEM] * 5,
+        [SMEM] + [HBM] * 4 + [VMEM],
         HBM if other else VMEM,
-        [pltpu.VMEM(shape, F32), pltpu.SemaphoreType.DMA((1,))] if other else (),
-        mib=4,
+        [pltpu.VMEM((CH, HALF, COLS), F32)] * 2
+        + [cells, cells, pltpu.VMEM((32, 8, 128), F32), pltpu.SemaphoreType.DMA((4 * PARTS,))],
+        mib=56,
     )(where, own, control, mask, region, earlier)
 
 
-BLOCK = 4
+BLOCK = 2
 
 
 def final_kernel(where, own, mine, theirs, region, parts, target, out, growth, cell):
@@ -531,15 +534,14 @@
         lax.fori_loop(0, ROWS // 8, body, 0)
 
     start = HALF // 8 * where[1]
-    lead = pl.program_id(0) * BLOCK
     for ref, s in ((mine, start), (theirs, HALF // 8 - start)):
 
         def body(t, _):
             c, g = tile_at(t), tile_at(t + s)
             f = cell[g, :]
             for k in range(BLOCK):
-                q = ref[lead + k, c, :]
-                out[k, g, :] = q + f * (own[lead + k, g, :] - q)
+                q = ref[k, c, :]
+                out[k, g, :] = q + f * (own[k, g, :] - q)
             return 0
 
         lax.fori_loop(0, HALF // 8, body, 0)
@@ -548,16 +550,18 @@
 def rescale(where, own, mine, theirs, region, parts, target):
     target = jnp.broadcast_to(jnp.pad(target, (0, 128 - REGIONS), constant_values=1.0), (8, 128))
 
-    cut = pl.BlockSpec((BLOCK, ROWS, COLS), lambda i: (i, 0, 0))
+    def cut(rows):
+        return pl.BlockSpec((BLOCK, rows, COLS), lambda i: (i, 0, 0))
+
     row = pl.BlockSpec((1, REGIONS), lambda i: (0, 0))
     return pl.pallas_call(
         final_kernel,
         grid=(CH // BLOCK,),
         out_shape=[jax.ShapeDtypeStruct((CH, ROWS, COLS), F32), jax.ShapeDtypeStruct((1, REGIONS), F32)],
-        in_specs=[SMEM] + [VMEM] * 6,
-        out_specs=[cut, row],
+        in_specs=[SMEM, cut(ROWS), cut(HALF), cut(HALF)] + [VMEM] * 3,
+        out_specs=[cut(ROWS), row],
         scratch_shapes=[pltpu.VMEM((ROWS, COLS), F32)],
-        compiler_params=pltpu.CompilerParams(vmem_limit_bytes=8 << 20),
+        compiler_params=pltpu.CompilerParams(vmem_limit_bytes=62 << 20),
         cost_estimate=pl.CostEstimate(flops=1 << 22, bytes_accessed=10 << 20, transcendentals=0),
     )(where, own, mine, theirs, region, parts, target)
 
@@ -570,9 +574,9 @@
     first = spread_first(where, state)
     halos = exchange(*pack(where, state, statics))
     halo = call(control_halo_kernel, jax.ShapeDtypeStruct((CH, 8, COLS), F32), [VMEM] * 5, VMEM)(*halos)
-    arrays, halo, gate = spread_rest(where, *first, halo)
+    arrays, control_halos, gate = spread_rest(where, *first, halo)
     own, static = own_steps(where, state, statics, halos, gate)
-    mine = control_steps(where, arrays, halo, static)
+    mine = control_steps(where, arrays, control_halos, static)
     theirs = send(mine, [(i, i ^ 1) for i in range(8)])
     parts = half_sums(False, where, own, mine, mask, region, jnp.zeros((8, 128), F32))
     parts = half_sums(True, where, own, theirs, mask, region, parts)

time: 112 us -> 121 us (1.080); the launches traced: 112 us -> 119 us
  Pallas kernels: 33.3 us -> 48.7 us
  waiting for transfers between devices: 37.5 us -> 27.1 us
  starting transfers between devices: 32.4 us -> 37.1 us
  local copies, waits for them, and re-layouts: 6.89 us -> 3.73 us
    ppermute x8 -> x10, waiting for transfers between devices: 22.5 us -> 12.3 us  [send(): return lax.ppermute(value, 'member', pairs)]
    pallas_call x2, Pallas kernels: 2.51 us -> 7.32 us  [half_sums(): call(functools.partial(sums_kernel, other), jax.ShapeDtypeStruct(shape, F...]
    ppermute x8 -> x10, starting transfers between devices: 8.33 us -> 13 us  [send(): return lax.ppermute(value, 'member', pairs)]
    pallas_call x1, Pallas kernels: 4.36 us -> 8.73 us  [rescale(): pl.pallas_call(final_kernel, grid=(CH // BLOCK,), out_shape=[jax.ShapeDty...]
    unnamed x36 -> x26, local copies, waits for them, and re-layouts: 6.88 us -> 2.52 us
    pallas_call x1, Pallas kernels: 6.77 us -> 10 us  [control_steps(): call(control_kernel, jax.ShapeDtypeStruct((CH, HALF, COLS), F32), [SMEM]...]
    pallas_call x1, Pallas kernels: 13.6 us -> 16.4 us  [own_steps(): call(own_kernel, [jax.ShapeDtypeStruct((CH, ROWS, COLS), F32), jax.ShapeD...]
  transfers between devices with their start and end apart: 14 -> 16, of which waited for: 5 -> 4; matrix products, arithmetic and copies ran while one was open for 0% -> 1% of each run, Pallas kernels for 17% -> 21%
where the time goes in v4:
time: 121 us; the launch traced here: 119 us
  Pallas kernels  48.7 us (40%)
  starting transfers between devices  37.1 us (31%)
  waiting for transfers between devices  27.1 us (22%)
  local copies, waits for them, and re-layouts  3.73 us (3%)
  other arithmetic  1.27 us (1%)
    pallas_call x1, Pallas kernels, own_steps(): call(own_kernel, [jax.ShapeDtypeStruct((CH, ROWS, COLS), F32), jax.ShapeD...  16.4 us
    ppermute x10, starting transfers between devices, send(): return lax.ppermute(value, 'member', pairs)  13 us
    ppermute x10, waiting for transfers between devices, send(): return lax.ppermute(value, 'member', pairs)  12.3 us
    all_to_all x1, waiting for transfers between devices, per_device(): parts = lax.all_to_all(parts, ('lon', 'lat'), 0, 0)  10.6 us
    all_to_all x1, starting transfers between devices, per_device(): parts = lax.all_to_all(parts, ('lon', 'lat'), 0, 0)  10.4 us
    pallas_call x1, Pallas kernels, control_steps(): call(control_kernel, jax.ShapeDtypeStruct((CH, HALF, COLS), F32), [SMEM]...  10 us
    pallas_call x1, Pallas kernels, rescale(): pl.pallas_call(final_kernel, grid=(CH // BLOCK,), out_shape=[jax.ShapeDty...  8.73 us
    pallas_call x2, Pallas kernels, half_sums(): call(functools.partial(sums_kernel, other), jax.ShapeDtypeStruct(shape, F...  7.32 us
  transfers between devices with their start and end apart: 16, of which 4 were waited for; matrix products, arithmetic and copies ran while one was open for 1% of the time, Pallas kernels for 21%

profile of v4, /device:TPU:24, one launch (start us, length us, event | category | flops | bytes accessed | tf_op | source)
XLA Modules:
  0.0 118.8 jit_solution(14403979638752757730)
XLA Ops:
  0.6 0.6 pad_add_fusion.lat.where
  1.2 0.8 shard_map.87
  2.0 0.8 collective-permute-start.5
  2.8 1.9 %collective-permute-start.6 = (f32[16,72,384]{2,1,0:T(8,128)}, f32[16,72,384]{2,1,0:T(8,128)}, u32[]{:S(2)}, u32[]{:S(2)}) collective-permute-start(f32[16,72,384]{2,1,0:T(8,128)} %get-tuple-element.20.u), channel_id=1, source_target_pairs={{0,224},{1,225},{2,226},{3,227},{4,228},{5,229},{6,230},{7,231},{8... | collective-permute-start | bytes 5308424 | tf_op jit(solution)/shard_map/ppermute | solution.py:302
  4.7 4.4 %shard_map.86 = (f32[128,128]{1,0:T(8,128)}, f32[128,128]{1,0:T(8,128)}, f32[96,384]{1,0:T(8,128)}, f32[8,128]{1,0:T(8,128)}, f32[8,128]{1,0:T(8,128)}) custom-call(s32[3]{0:T(128)} %pad_add_fusion.lat.where, f32[16,128,384]{2,1,0:T(8,128)} %bitcast.6, f32[128,384]{1,0:T(8,128)} %depth.3, f32[128,384]{1,0:T(8,128)} %rotation.3, f32[5,128,384]{2,1,0:T(8,128)} %diff.3, ...), custom_call_target="tpu_custom_call" | custom-call | flops 4194304 | bytes 8388608 | tf_op jit(solution)/shard_map/pallas_call | solution.py:90
  9.1 3.1 %collective-permute-start.2 = (f32[96,384]{1,0:T(8,128)}, f32[96,384]{1,0:T(8,128)S(1)}, u32[]{:S(2)}, u32[]{:S(2)}) collective-permute-start(f32[96,384]{1,0:T(8,128)} %get-tuple-element.17), channel_id=1, source_target_pairs={{0,1},{1,0},{2,3},{3,2},{4,5},{5,4},{6,7},{7,6},{8,9},{9,8},{10,11... | collective-permute-start | bytes 442376 | tf_op jit(solution)/shard_map/ppermute | solution.py:117
  12.2 1.1 collective-permute-start.3
  13.4 5.3 %collective-permute-start.4 = (f32[8,128]{1,0:T(8,128)}, f32[8,128]{1,0:T(8,128)S(1)}, u32[]{:S(2)}, u32[]{:S(2)}) collective-permute-start(f32[8,128]{1,0:T(8,128)} %get-tuple-element.19), channel_id=1, source_target_pairs={{2,1},{3,0},{4,3},{5,2},{6,5},{7,4},{8,7},{9,6},{10,9},{11,8},{12,... | collective-permute-start | bytes 12296 | tf_op jit(solution)/shard_map/ppermute | solution.py:119
  18.7 1.8 %collective-permute-done.3.cw = f32[8,128]{1,0:T(8,128)S(1)} collective-permute-done((f32[8,128]{1,0:T(8,128)}, f32[8,128]{1,0:T(8,128)S(1)}, u32[]{:S(2)}, u32[]{:S(2)}) %collective-permute-start.3) | collective-permute-done | bytes 4128 | tf_op jit(solution)/shard_map/ppermute | solution.py:118
  20.5 0.0 collective-permute-start
  20.5 0.0 collective-permute-done.4.ce
  20.5 4.1 %collective-permute-start.1 = (f32[128,128]{1,0:T(8,128)}, f32[128,128]{1,0:T(8,128)S(1)}, u32[]{:S(2)}, u32[]{:S(2)}) collective-permute-start(f32[128,128]{1,0:T(8,128)} %get-tuple-element.16), channel_id=1, source_target_pairs={{2,0},{4,2},{6,4},{8,6},{10,8},{12,10},{14,12},{16,14},{18,16},{20... | collective-permute-start | bytes 196616 | tf_op jit(solution)/shard_map/ppermute | solution.py:116
  24.6 2.4 %collective-permute-done.fw = f32[128,128]{1,0:T(8,128)S(1)} collective-permute-done((f32[128,128]{1,0:T(8,128)}, f32[128,128]{1,0:T(8,128)S(1)}, u32[]{:S(2)}, u32[]{:S(2)}) %collective-permute-start) | collective-permute-done | bytes 65568 | tf_op jit(solution)/shard_map/ppermute | solution.py:115
  27.1 0.0 collective-permute-done.1.fe
  27.1 0.0 collective-permute-done.2.rows
  27.1 0.1 shard_map.88
  27.2 0.7 collective-permute-start.7
  27.9 0.7 collective-permute-start.8
  28.5 0.0 collective-permute-done.7
  28.6 0.0 collective-permute-done.8
  28.6 0.7 select_select_fusion.gate.refs_6_
  29.3 0.0 collective-permute-done.5.p1.refs_2_
  29.3 0.0 collective-permute-done.6.m1.refs_5_
  29.3 1.3 %copy-done.5 = f32[16,72,384]{2,1,0:T(8,128)} copy-done((f32[16,72,384]{2,1,0:T(8,128)}, f32[16,72,384]{2,1,0:T(8,128)S(1)}, u32[]{:S(2)}) %copy-start.5) | copy-done | bytes 1769496
  30.6 0.8 shard_map.89
  31.5 0.8 collective-permute-start.9
  32.3 0.8 collective-permute-start.10
  33.0 1.3 %collective-permute-start.11 = (f32[16,72,384]{2,1,0:T(8,128)}, f32[16,72,384]{2,1,0:T(8,128)}, u32[]{:S(2)}, u32[]{:S(2)}) collective-permute-start(f32[16,72,384]{2,1,0:T(8,128)} %get-tuple-element.24.refs_0_), channel_id=1, source_target_pairs={{0,192},{224,160},{1,193},{225,161},{2,194},{226,162},{3,195},{227... | collective-permute-start | bytes 5308424 | tf_op jit(solution)/shard_map/ppermute | solution.py:302
  34.3 0.7 collective-permute-start.12
  35.0 1.3 %collective-permute-start.13 = (f32[16,8,384]{2,1,0:T(8,128)S(1)}, f32[16,8,384]{2,1,0:T(8,128)}, u32[]{:S(2)}, u32[]{:S(2)}) collective-permute-start(f32[16,8,384]{2,1,0:T(8,128)S(1)} %copy-done.9), channel_id=1, source_target_pairs={{64,96},{224,192},{65,97},{225,193},{66,98},{226,194},{67,99},{227... | collective-permute-start | bytes 589832 | tf_op jit(solution)/shard_map/ppermute | solution.py:302
  36.3 16.4 %shard_map.90 = (f32[16,128,384]{2,1,0:T(8,128)}, f32[8,72,512]{2,1,0:T(8,128)}) custom-call(s32[3]{0:T(128)} %pad_add_fusion.lat.where, f32[16,128,384]{2,1,0:T(8,128)} %bitcast.7, f32[128,384]{1,0:T(8,128)} %depth.3, f32[128,384]{1,0:T(8,128)} %rotation.3, f32[5,128,384]{2,1,0:T(8,128)} %diff.3, s32[128,384]{1,0:T(8,128)} %mask.7, f32[128,128]{1,0:T(8,128)} %copy-done.1, ...), custom_call_target="tpu_custom_call" | custom-call | flops 268435456 | bytes 8388608 | tf_op jit(solution)/shard_map/pallas_call | solution.py:271
  52.7 0.0 collective-permute-done.12.refs_7_
  52.8 0.0 collective-permute-done.13.refs_8_
  52.8 0.0 collective-permute-done.9.refs_1_
  52.8 0.0 copy-start.8
  52.8 12.2 %collective-permute-done.11.refs_4_ = f32[16,72,384]{2,1,0:T(8,128)} collective-permute-done((f32[16,72,384]{2,1,0:T(8,128)}, f32[16,72,384]{2,1,0:T(8,128)}, u32[]{:S(2)}, u32[]{:S(2)}) %collective-permute-start.11) | collective-permute-done | bytes 1769504 | tf_op jit(solution)/shard_map/ppermute | solution.py:302
  65.1 10.0 %shard_map.91.control.mine = f32[16,64,384]{2,1,0:T(8,128)} custom-call(s32[3]{0:T(128)} %pad_add_fusion.lat.where, f32[16,72,384]{2,1,0:T(8,128)} %get-tuple-element.24.refs_0_, f32[16,72,384]{2,1,0:T(8,128)} %copy-done.7, f32[16,72,384]{2,1,0:T(8,128)} %copy-done.5, f32[16,72,384]{2,1,0:T(8,128)} %copy-done.8, ...), custom_call_target="tpu_custom_call" | custom-call | flops 134217728 | bytes 8388608 | tf_op jit(solution)/shard_map/pallas_call | solution.py:417
  75.1 4.2 %collective-permute-start.14 = (f32[16,64,384]{2,1,0:T(8,128)}, f32[16,64,384]{2,1,0:T(8,128)S(1)}, u32[]{:S(2)}, u32[]{:S(2)}) collective-permute-start(f32[16,64,384]{2,1,0:T(8,128)} %shard_map.91.control.mine), channel_id=1, source_target_pairs={{0,32},{32,0},{64,96},{96,64},{128,160},{160,128},{192,224},{224,1... | collective-permute-start | bytes 4718600 | tf_op jit(solution)/shard_map/ppermute | solution.py:302
  79.3 0.6 broadcast_in_dim.9.earlier
  79.9 3.7 %shard_map.92.earlier = f32[8,128]{1,0:T(8,128)} custom-call(s32[3]{0:T(128)} %pad_add_fusion.lat.where, f32[16,128,384]{2,1,0:T(8,128)} %get-tuple-element.23.own, f32[16,64,384]{2,1,0:T(8,128)} %shard_map.91.control.mine, s32[128,384]{1,0:T(8,128)} %mask.7, s32[128,384]{1,0:T(8,128)} %region.5, f32[8,128]{1,0:T(8,128)} %broadcast_in_dim.9.earlier), custom_call_target="tpu_custom_call" | custom-call | flops 4194304 | bytes 8388608 | tf_op jit(solution)/shard_map/pallas_call | solution.py:499
  83.5 0.0 copy-start.12
  83.6 1.1 copy-done.6
  84.7 3.7 %shard_map.93 = f32[32,8,128]{2,1,0:T(8,128)} custom-call(s32[3]{0:T(128)} %pad_add_fusion.lat.where, f32[16,128,384]{2,1,0:T(8,128)} %get-tuple-element.23.own, f32[16,64,384]{2,1,0:T(8,128)} %copy-done.6, s32[128,384]{1,0:T(8,128)} %mask.7, s32[128,384]{1,0:T(8,128)} %region.5, f32[8,128]{1,0:T(8,128)} %shard_map.92.earlier), custom_call_target="tpu_custom_call" | custom-call | flops 4194304 | bytes 8388608 | tf_op jit(solution)/shard_map/pallas_call | solution.py:499
  88.4 10.4 %all-to-all-start = ((f32[32,8,128]{2,1,0:T(8,128)}), f32[32,8,128]{2,1,0:T(8,128)S(1)}, u32[]{:S(2)}, u32[]{:S(2)}) async-start(f32[32,8,128]{2,1,0:T(8,128)} %shard_map.93), calls=%async_computation | async-start | bytes 262144 | tf_op jit(solution)/shard_map/all_to_all | solution.py:583
  98.8 10.6 %all-to-all-done.parts = f32[32,8,128]{2,1,0:T(8,128)S(1)} async-done(((f32[32,8,128]{2,1,0:T(8,128)}), f32[32,8,128]{2,1,0:T(8,128)S(1)}, u32[]{:S(2)}, u32[]{:S(2)}) %all-to-all-start) | async-done | bytes 131104 | tf_op jit(solution)/shard_map/all_to_all | solution.py:583
  109.4 0.6 broadcast_in_dim.10.target
  110.0 0.0 copy-done.10
  110.1 8.7 %shard_map.94 = (f32[16,128,384]{2,1,0:T(8,128)}, f32[1,16]{1,0:T(1,128)}) custom-call(s32[3]{0:T(128)} %pad_add_fusion.lat.where, f32[16,128,384]{2,1,0:T(8,128)} %get-tuple-element.23.own, f32[16,64,384]{2,1,0:T(8,128)} %shard_map.91.control.mine, f32[16,64,384]{2,1,0:T(8,128)} %copy-done.6, s32[128,384]{1,0:T(8,128)} %region.5, f32[32,8,128]{2,1,0:T(8,128)} %copy-done.10, ...), custom_call_target="tpu_custom_call" | custom-call | flops 4194304 | bytes 10485760 | tf_op jit(solution)/shard_map/pallas_call | solution.py:557
  (24 shorter events, 0.1 us)
Async XLA Ops:
  2.0 27.2 %collective-permute-start.5 = (f32[16,72,384]{2,1,0:T(8,128)}, f32[16,72,384]{2,1,0:T(8,128)S(1)}, u32[]{:S(2)}, u32[]{:S(2)}) collective-permute-start(f32[16,72,384]{2,1,0:T(8,128)} %get-tuple-element.21.v), channel_id=1, source_target_pairs={{0,64},{1,65},{2,66},{3,67},{4,68},{5,69},{6,70},{7,71},{8,72},{9,... | collective-permute-start | bytes 5308424 | tf_op jit(solution)/shard_map/ppermute | solution.py:302
  2.8 26.5 %collective-permute-start.6 = (f32[16,72,384]{2,1,0:T(8,128)}, f32[16,72,384]{2,1,0:T(8,128)}, u32[]{:S(2)}, u32[]{:S(2)}) collective-permute-start(f32[16,72,384]{2,1,0:T(8,128)} %get-tuple-element.20.u), channel_id=1, source_target_pairs={{0,224},{1,225},{2,226},{3,227},{4,228},{5,229},{6,230},{7,231},{8... | collective-permute-start | bytes 5308424 | tf_op jit(solution)/shard_map/ppermute | solution.py:302
  9.1 17.9 %collective-permute-start.2 = (f32[96,384]{1,0:T(8,128)}, f32[96,384]{1,0:T(8,128)S(1)}, u32[]{:S(2)}, u32[]{:S(2)}) collective-permute-start(f32[96,384]{1,0:T(8,128)} %get-tuple-element.17), channel_id=1, source_target_pairs={{0,1},{1,0},{2,3},{3,2},{4,5},{5,4},{6,7},{7,6},{8,9},{9,8},{10,11... | collective-permute-start | bytes 442376 | tf_op jit(solution)/shard_map/ppermute | solution.py:117
  12.2 8.2 %collective-permute-start.3 = (f32[8,128]{1,0:T(8,128)}, f32[8,128]{1,0:T(8,128)S(1)}, u32[]{:S(2)}, u32[]{:S(2)}) collective-permute-start(f32[8,128]{1,0:T(8,128)} %get-tuple-element.18), channel_id=1, source_target_pairs={{0,3},{1,2},{2,5},{3,4},{4,7},{5,6},{6,9},{7,8},{8,11},{9,10},{10,... | collective-permute-start | bytes 12296 | tf_op jit(solution)/shard_map/ppermute | solution.py:118
  13.4 7.1 %collective-permute-start.4 = (f32[8,128]{1,0:T(8,128)}, f32[8,128]{1,0:T(8,128)S(1)}, u32[]{:S(2)}, u32[]{:S(2)}) collective-permute-start(f32[8,128]{1,0:T(8,128)} %get-tuple-element.19), channel_id=1, source_target_pairs={{2,1},{3,0},{4,3},{5,2},{6,5},{7,4},{8,7},{9,6},{10,9},{11,8},{12,... | collective-permute-start | bytes 12296 | tf_op jit(solution)/shard_map/ppermute | solution.py:119
  20.5 10.9 %copy-start.3 = (f32[8,128]{1,0:T(8,128)}, f32[8,128]{1,0:T(8,128)S(1)}, u32[]{:S(2)}) copy-start(f32[8,128]{1,0:T(8,128)S(1)} %collective-permute-done.3.cw) | copy-start | bytes 12292
  20.5 6.6 %collective-permute-start = (f32[128,128]{1,0:T(8,128)}, f32[128,128]{1,0:T(8,128)S(1)}, u32[]{:S(2)}, u32[]{:S(2)}) collective-permute-start(f32[128,128]{1,0:T(8,128)} %get-tuple-element.15), channel_id=1, source_target_pairs={{0,2},{2,4},{4,6},{6,8},{8,10},{10,12},{12,14},{14,16},{16,18},{18... | collective-permute-start | bytes 196616 | tf_op jit(solution)/shard_map/ppermute | solution.py:115
  20.5 10.9 %copy-start.4 = (f32[8,128]{1,0:T(8,128)}, f32[8,128]{1,0:T(8,128)S(1)}, u32[]{:S(2)}) copy-start(f32[8,128]{1,0:T(8,128)S(1)} %collective-permute-done.4.ce) | copy-start | bytes 12292
  20.5 6.6 %collective-permute-start.1 = (f32[128,128]{1,0:T(8,128)}, f32[128,128]{1,0:T(8,128)S(1)}, u32[]{:S(2)}, u32[]{:S(2)}) collective-permute-start(f32[128,128]{1,0:T(8,128)} %get-tuple-element.16), channel_id=1, source_target_pairs={{2,0},{4,2},{6,4},{8,6},{10,8},{12,10},{14,12},{16,14},{18,16},{20... | collective-permute-start | bytes 196616 | tf_op jit(solution)/shard_map/ppermute | solution.py:116
  27.1 4.4 %copy-start.1 = (f32[128,128]{1,0:T(8,128)}, f32[128,128]{1,0:T(8,128)S(1)}, u32[]{:S(2)}) copy-start(f32[128,128]{1,0:T(8,128)S(1)} %collective-permute-done.fw) | copy-start | bytes 196612
  27.1 4.4 %copy-start.2 = (f32[128,128]{1,0:T(8,128)}, f32[128,128]{1,0:T(8,128)S(1)}, u32[]{:S(2)}) copy-start(f32[128,128]{1,0:T(8,128)S(1)} %collective-permute-done.1.fe) | copy-start | bytes 196612
  27.1 4.4 %copy-start = (f32[96,384]{1,0:T(8,128)}, f32[96,384]{1,0:T(8,128)S(1)}, u32[]{:S(2)}) copy-start(f32[96,384]{1,0:T(8,128)S(1)} %collective-permute-done.2.rows) | copy-start | bytes 442372
  27.2 1.4 %collective-permute-start.7 = (f32[16,8,384]{2,1,0:T(8,128)S(1)}, f32[16,8,384]{2,1,0:T(8,128)S(1)}, u32[]{:S(2)}, u32[]{:S(2)}) collective-permute-start(f32[16,8,384]{2,1,0:T(8,128)S(1)} %shard_map.88), channel_id=1, source_target_pairs={{0,64},{1,65},{2,66},{3,67},{4,68},{5,69},{6,70},{7,71},{8,72},{9,... | collective-permute-start | bytes 589832 | tf_op jit(solution)/shard_map/ppermute | solution.py:302
  27.9 0.7 collective-permute-start.8
  29.3 5.1 %copy-start.9 = (f32[16,8,384]{2,1,0:T(8,128)S(1)}, f32[16,8,384]{2,1,0:T(8,128)}, u32[]{:S(2)}) copy-start(f32[16,8,384]{2,1,0:T(8,128)} %select_select_fusion.gate.refs_6_) | copy-start | bytes 589828
  29.3 1.3 %copy-start.5 = (f32[16,72,384]{2,1,0:T(8,128)}, f32[16,72,384]{2,1,0:T(8,128)S(1)}, u32[]{:S(2)}) copy-start(f32[16,72,384]{2,1,0:T(8,128)S(1)} %collective-permute-done.5.p1.refs_2_) | copy-start | bytes 5308420
  31.5 21.3 %collective-permute-start.9 = (f32[16,72,384]{2,1,0:T(8,128)}, f32[16,72,384]{2,1,0:T(8,128)S(1)}, u32[]{:S(2)}, u32[]{:S(2)}) collective-permute-start(f32[16,72,384]{2,1,0:T(8,128)} %get-tuple-element.22.gate), channel_id=1, source_target_pairs={{0,32},{1,33},{2,34},{3,35},{4,36},{5,37},{6,38},{7,39},{8,40},{9,... | collective-permute-start | bytes 5308424 | tf_op jit(solution)/shard_map/ppermute | solution.py:302
  32.3 20.5 %collective-permute-start.10 = (f32[16,72,384]{2,1,0:T(8,128)}, f32[16,72,384]{2,1,0:T(8,128)S(1)}, u32[]{:S(2)}, u32[]{:S(2)}) collective-permute-start(f32[16,72,384]{2,1,0:T(8,128)} %get-tuple-element.22.gate), channel_id=1, source_target_pairs={{0,96},{64,128},{1,97},{65,129},{2,98},{66,130},{3,99},{67,131},{4... | collective-permute-start | bytes 5308424 | tf_op jit(solution)/shard_map/ppermute | solution.py:302
  33.0 32.0 %collective-permute-start.11 = (f32[16,72,384]{2,1,0:T(8,128)}, f32[16,72,384]{2,1,0:T(8,128)}, u32[]{:S(2)}, u32[]{:S(2)}) collective-permute-start(f32[16,72,384]{2,1,0:T(8,128)} %get-tuple-element.24.refs_0_), channel_id=1, source_target_pairs={{0,192},{224,160},{1,193},{225,161},{2,194},{226,162},{3,195},{227... | collective-permute-start | bytes 5308424 | tf_op jit(solution)/shard_map/ppermute | solution.py:302
  34.3 18.4 %collective-permute-start.12 = (f32[16,8,384]{2,1,0:T(8,128)S(1)}, f32[16,8,384]{2,1,0:T(8,128)S(1)}, u32[]{:S(2)}, u32[]{:S(2)}) collective-permute-start(f32[16,8,384]{2,1,0:T(8,128)S(1)} %copy-done.9), channel_id=1, source_target_pairs={{0,32},{64,128},{224,160},{1,33},{65,129},{225,161},{2,34},{66,130... | collective-permute-start | bytes 589832 | tf_op jit(solution)/shard_map/ppermute | solution.py:302
  35.0 17.7 %collective-permute-start.13 = (f32[16,8,384]{2,1,0:T(8,128)S(1)}, f32[16,8,384]{2,1,0:T(8,128)}, u32[]{:S(2)}, u32[]{:S(2)}) collective-permute-start(f32[16,8,384]{2,1,0:T(8,128)S(1)} %copy-done.9), channel_id=1, source_target_pairs={{64,96},{224,192},{65,97},{225,193},{66,98},{226,194},{67,99},{227... | collective-permute-start | bytes 589832 | tf_op jit(solution)/shard_map/ppermute | solution.py:302
  52.8 12.3 %copy-start.11 = (f32[16,8,384]{2,1,0:T(8,128)}, f32[16,8,384]{2,1,0:T(8,128)S(1)}, u32[]{:S(2)}) copy-start(f32[16,8,384]{2,1,0:T(8,128)S(1)} %collective-permute-done.12.refs_7_) | copy-start | bytes 589828
  52.8 12.3 %copy-start.7 = (f32[16,72,384]{2,1,0:T(8,128)}, f32[16,72,384]{2,1,0:T(8,128)S(1)}, u32[]{:S(2)}) copy-start(f32[16,72,384]{2,1,0:T(8,128)S(1)} %collective-permute-done.9.refs_1_) | copy-start | bytes 5308420
  52.8 12.3 %copy-start.8 = (f32[16,72,384]{2,1,0:T(8,128)}, f32[16,72,384]{2,1,0:T(8,128)S(1)}, u32[]{:S(2)}) copy-start(f32[16,72,384]{2,1,0:T(8,128)S(1)} %collective-permute-done.10.refs_3_) | copy-start | bytes 5308420
  75.1 8.4 %collective-permute-start.14 = (f32[16,64,384]{2,1,0:T(8,128)}, f32[16,64,384]{2,1,0:T(8,128)S(1)}, u32[]{:S(2)}, u32[]{:S(2)}) collective-permute-start(f32[16,64,384]{2,1,0:T(8,128)} %shard_map.91.control.mine), channel_id=1, source_target_pairs={{0,32},{32,0},{64,96},{96,64},{128,160},{160,128},{192,224},{224,1... | collective-permute-start | bytes 4718600 | tf_op jit(solution)/shard_map/ppermute | solution.py:302
  83.5 15.3 %copy-start.12 = (f32[16]{0:T(128)S(1)}, f32[16]{0:T(128)}, u32[]{:S(2)}) copy-start(f32[16]{0:T(128)} %param.13) | copy-start | bytes 196
  83.6 1.2 copy-start.6
  88.4 21.0 %all-to-all-start = ((f32[32,8,128]{2,1,0:T(8,128)}), f32[32,8,128]{2,1,0:T(8,128)S(1)}, u32[]{:S(2)}, u32[]{:S(2)}) async-start(f32[32,8,128]{2,1,0:T(8,128)} %shard_map.93), calls=%async_computation | async-start | bytes 262144 | tf_op jit(solution)/shard_map/all_to_all | solution.py:583
  109.4 0.7 copy-start.10

commit v5 on v3

--- a/solution.py
+++ b/solution.py
@@ -42,41 +42,28 @@
     return (k % 8, k >= 8) if k < CH else (8 + (k - CH) % 4, k - CH >= 4)
 
 
-def pack_kernel(lat, state, depth, rotation, diff, mask, west, east, rows, c_west, c_east, lo, hi, edge, land, sem):
-    upper = lat[0] == 0
-    r0 = pl.multiple_of(jnp.where(upper, ROWS - 8, 0), 8)
-    tile = pl.ds(r0, 8)
-    left, right, full = slice(0, 128), slice(COLS - 128, COLS), slice(0, ROWS)
-    copies = []
-    for i, (src, at) in enumerate(
-        [(state, slice(0, CH)), (depth, CH), (rotation, CH + 1), (diff, slice(CH + 2, CH + 2 + LEV))]
-    ):
+def sources(state, depth, rotation, diff, mask):
+    return [(state, slice(0, CH)), (depth, CH), (rotation, CH + 1), (diff, slice(CH + 2, CH + 2 + LEV))]
+
+
+def fetch(fields, mask, cuts, land, land_cut, sem):
+    copies = [pltpu.make_async_copy(mask.at[land_cut], land, sem.at[0])]
+    for src, at in fields:
         lead = (slice(None),) if src.shape[:-2] else ()
-        for j, (dst, cut) in enumerate([(edge, (tile, slice(None))), (lo, (full, left)), (hi, (full, right))]):
-            copies.append(pltpu.make_async_copy(src.at[lead + cut], dst.at[at], sem.at[3 * i + j]))
-    copies.append(pltpu.make_async_copy(mask, land, sem.at[12]))
+        for dst, cut in cuts:
+            copies.append(pltpu.make_async_copy(src.at[lead + cut], dst.at[at], sem.at[len(copies)]))
     for copy in copies:
         copy.start()
     for copy in copies:
         copy.wait()
-    last = FIELDS - 1
-    lo[last] = land[:, left].astype(F32)
-    hi[last] = land[:, right].astype(F32)
-    edge[last] = land[tile, :].astype(F32)
-
-    lane = iota((ROWS, 128), 1)
-    w = jnp.zeros((ROWS, 128), F32)
-    e = jnp.zeros((ROWS, 128), F32)
-    for k in range(FIELDS):
-        own = (lane >= HALO * k) & (lane < HALO * k + HALO)
-        w = jnp.where(own, pltpu.roll(lo[k], HALO * k, 1) if k else lo[k], w)
-        e = jnp.where(own, pltpu.roll(hi[k], HALO * k + HALO, 1), e)
-    west[...] = w
-    east[...] = e
-    c_west[...] = west[tile, :]
-    c_east[...] = east[tile, :]
-    sub = iota((8, COLS), 0)
-    mine = (sub >= 4) == upper
+
+
+def rows_kernel(lat, state, depth, rotation, diff, mask, rows, edge, land, sem):
+    upper = lat[0] == 0
+    cut = (pl.ds(pl.multiple_of(jnp.where(upper, ROWS - 8, 0), 8), 8), slice(None))
+    fetch(sources(state, depth, rotation, diff, mask), mask, [(edge, cut)], land, cut, sem)
+    edge[FIELDS - 1] = land[...].astype(F32)
+    mine = (iota((8, COLS), 0) >= 4) == upper
     for k in range(FIELDS):
         slot, flip = row_slot(k)
         if not flip:
@@ -84,61 +71,88 @@
             rows[8 * slot : 8 * slot + 8, :] = jnp.where(mine, edge[k], pltpu.roll(edge[pair], 4, 0))
 
 
-def pack(lat, state, statics):
-    shapes = [(ROWS, 128), (ROWS, 128), (FIELDS * 4, COLS), (8, 128), (8, 128)]
-    return call(
-        pack_kernel,
-        [jax.ShapeDtypeStruct(s, F32) for s in shapes],
-        [SMEM] + [HBM] * 5,
-        [VMEM] * 5,
-        [
-            pltpu.VMEM((FIELDS, ROWS, 128), F32),
-            pltpu.VMEM((FIELDS, ROWS, 128), F32),
-            pltpu.VMEM((FIELDS, 8, COLS), F32),
-            pltpu.VMEM((ROWS, COLS), jnp.int32),
-            pltpu.SemaphoreType.DMA((13,)),
-        ],
-        mib=62,
-    )(lat, state, *statics)
-
-
-def exchange(west, east, rows, c_west, c_east):
+def put(k, a, b, w, e):
+    lane = iota(w.shape, 1)
+    own = (lane >= HALO * k) & (lane < HALO * k + HALO)
+    w = jnp.where(own, pltpu.roll(a, HALO * k, 1) if k else a, w)
+    return w, jnp.where(own, pltpu.roll(b, HALO * k + HALO, 1), e)
+
+
+LEFT, RIGHT = slice(0, 128), slice(COLS - 128, COLS)
+
+
+def strips_kernel(state, depth, rotation, diff, mask, west, east, lo, hi, land, sem):
+    full = slice(None)
+    cuts = [(lo, (full, LEFT)), (hi, (full, RIGHT))]
+    fetch(sources(state, depth, rotation, diff, mask), mask, cuts, land, (full, full), sem)
+    lo[FIELDS - 1] = land[:, LEFT].astype(F32)
+    hi[FIELDS - 1] = land[:, RIGHT].astype(F32)
+    w = e = jnp.zeros((ROWS, 128), F32)
+    for k in range(FIELDS):
+        w, e = put(k, lo[k], hi[k], w, e)
+    west[...] = w
+    east[...] = e
+
+
+def corners_kernel(lat, rows, west, east, west_out, east_out):
+    got = (iota((8, 128), 0) < 4) == (lat[0] == 0)
+    w = e = jnp.zeros((8, 128), F32)
+    for k in range(FIELDS):
+        slot, flip = row_slot(k)
+        a, b = rows[8 * slot : 8 * slot + 8, LEFT], rows[8 * slot : 8 * slot + 8, RIGHT]
+        if flip:
+            a, b = pltpu.roll(a, 4, 0), pltpu.roll(b, 4, 0)
+        w, e = put(k, a, b, w, e)
+    west_out[0:ROWS, :] = west[...]
+    east_out[0:ROWS, :] = east[...]
+    west_out[ROWS:ROWS_X, :] = jnp.where(got, w, 0.0)
+    east_out[ROWS:ROWS_X, :] = jnp.where(got, e, 0.0)
+
+
+def exchange(where, state, statics):
     n = lax.axis_size("lon")
     up = [(i, (i + 1) % n) for i in range(n)]
     down = [((i + 1) % n, i) for i in range(n)]
-    other = [(0, 1), (1, 0)]
-    both = ("lon", "lat")
-    up2 = [(2 * i + j, 2 * k + 1 - j) for i, k in up for j in range(2)]
-    down2 = [(2 * i + j, 2 * k + 1 - j) for i, k in down for j in range(2)]
-    return (
-        lax.ppermute(east, "lon", up),
-        lax.ppermute(west, "lon", down),
-        lax.ppermute(rows, "lat", other),
-        lax.ppermute(c_east, both, up2),
-        lax.ppermute(c_west, both, down2),
+
+    def shape(*dims):
+        return jax.ShapeDtypeStruct(dims, F32)
+
+    rows = call(
+        rows_kernel,
+        shape(FIELDS * 4, COLS),
+        [SMEM] + [HBM] * 5,
+        VMEM,
+        [pltpu.VMEM((FIELDS, 8, COLS), F32), pltpu.VMEM((8, COLS), jnp.int32), pltpu.SemaphoreType.DMA((5,))],
+        mib=62,
+    )(where, state, *statics)
+    rows = lax.ppermute(rows, "lat", [(0, 1), (1, 0)])
+    strip = pltpu.VMEM((FIELDS, ROWS, 128), F32)
+    west, east = call(
+        strips_kernel,
+        [shape(ROWS, 128)] * 2,
+        [HBM] * 5,
+        [VMEM] * 2,
+        [strip, strip, pltpu.VMEM((ROWS, COLS), jnp.int32), pltpu.SemaphoreType.DMA((9,))],
+        mib=60,
+    )(state, *statics)
+    west, east = call(corners_kernel, [shape(ROWS_X, 128)] * 2, [SMEM] + [VMEM] * 3, [VMEM] * 2)(
+        where, rows, west, east
     )
-
-
-def fill_halo(x, lat, from_west, from_east, rows, c_west, c_east):
-    def margin(k, w, e):
-        lane = iota(w.shape, 1)
-        s = (128 - HALO * k) % 128
-        e = pltpu.roll(e, s, 1) if s else e
-        return jnp.where(lane < 64, e, pltpu.roll(w, (124 - HALO * k) % 128, 1))
-
-    sub = iota((8, COLS), 0)
-    got = (sub < 4) == (lat[0] == 0)
-    got_c = got[:, :128]
+    return lax.ppermute(east, "lon", up), lax.ppermute(west, "lon", down), rows
+
+
+def fill_halo(x, lat, from_west, from_east, rows):
+    lane = iota((ROWS_X, 128), 1)
+    got = (iota((8, COLS), 0) < 4) == (lat[0] == 0)
     w, e = from_west[...], from_east[...]
-    cw, ce = c_west[...], c_east[...]
     for k in range(FIELDS):
-        x[k, 0:ROWS, COLS:COLS_X] = margin(k, w, e)
+        a = pltpu.roll(e, (128 - HALO * k) % 128, 1) if k else e
+        x[k, :, COLS:COLS_X] = jnp.where(lane < 64, a, pltpu.roll(w, (124 - HALO * k) % 128, 1))
         j, flip = row_slot(k)
         tile = rows[8 * j : 8 * j + 8, :]
         if flip:
             tile = pltpu.roll(tile, 4, 0)
         x[k, ROWS:ROWS_X, 0:COLS] = jnp.where(got, tile, 0.0)
-        x[k, ROWS:ROWS_X, COLS:COLS_X] = jnp.where(got_c, margin(k, cw, ce), 0.0)
 
 
 def tile_at(t):
@@ -235,7 +249,7 @@
     return [pltpu.VMEM((CH, rows, COLS_X), F32)] + [pltpu.VMEM((rows, COLS_X), F32)] * 3
 
 
-def own_kernel(where, state, depth, rotation, diff, mask, fw, fe, rows, cw, ce, gate, out, part, x, land, y, ub, vb, h2, sem):
+def own_kernel(where, state, depth, rotation, diff, mask, fw, fe, rows, gate, out, part, x, land, y, ub, vb, h2, sem):
     main = (slice(0, ROWS), slice(0, COLS))
     copies = [
         pltpu.make_async_copy(state, x.at[(slice(0, CH),) + main], sem.at[0]),
@@ -246,7 +260,7 @@
     copies.append(pltpu.make_async_copy(mask, land, sem.at[4]))
     for copy in copies:
         copy.start()
-    fill_halo(x, where, fw, fe, rows, cw, ce)
+    fill_halo(x, where, fw, fe, rows)
     for copy in copies:
         copy.wait()
     x[(FIELDS - 1,) + main] = land[...].astype(F32)
@@ -273,7 +287,7 @@
             jax.ShapeDtypeStruct((CH, ROWS, COLS), F32),
             jax.ShapeDtypeStruct((FIELDS - CH, HALF_X, COLS_X), F32),
         ],
-        [SMEM] + [HBM] * 5 + [VMEM] * 5 + [HBM],
+        [SMEM] + [HBM] * 5 + [VMEM] * 3 + [HBM],
         [VMEM] * 2,
         [pltpu.VMEM((FIELDS, ROWS_X, COLS_X), F32), pltpu.VMEM((ROWS, COLS), jnp.int32)]
         + step_scratch(ROWS_X)
@@ -283,7 +297,7 @@
     )(where, state, *statics, *halos, gate)
 
 
-def control_halo_kernel(fw, fe, rows, cw, ce, out):
+def control_halo_kernel(fw, fe, rows, out):
     for k in range(8):
         out[k] = rows[8 * k : 8 * k + 8, :]
     for i in range(18):
@@ -291,8 +305,7 @@
     lane = iota((8, 128), 1)
     for i in range(17):
         r = slice(8 * i, 8 * i + 8)
-        w, e = (fw[r, :], fe[r, :]) if i < 16 else (cw[...], ce[...])
-        s = jnp.where(lane < 64, w, pltpu.roll(e, 64, 1))
+        s = jnp.where(lane < 64, fw[r, :], pltpu.roll(fe[r, :], 64, 1))
         out[8 + i // 3, :, 128 * (i % 3) : 128 * (i % 3) + 128] = s
     out[14:16] = jnp.zeros((2, 8, COLS), F32)
 
@@ -568,8 +581,8 @@
     m = lax.axis_index("member")
     where = jnp.stack([lax.axis_index("lat"), m % 2, m]).astype(jnp.int32)
     first = spread_first(where, state)
-    halos = exchange(*pack(where, state, statics))
-    halo = call(control_halo_kernel, jax.ShapeDtypeStruct((CH, 8, COLS), F32), [VMEM] * 5, VMEM)(*halos)
+    halos = exchange(where, state, statics)
+    halo = call(control_halo_kernel, jax.ShapeDtypeStruct((CH, 8, COLS), F32), [VMEM] * 3, VMEM)(*halos)
     arrays, halo, gate = spread_rest(where, *first, halo)
     own, static = own_steps(where, state, statics, halos, gate)
     mine = control_steps(where, arrays, halo, static)

time: 112 us -> 113 us (level)
  starting transfers between devices: 32.4 us -> 28.1 us
  Pallas kernels: 33.3 us -> 36.2 us
  local copies, waits for them, and re-layouts: 6.89 us -> 8.61 us
    ppermute x3 -> x1, starting transfers between devices: 9.55 us -> 3.11 us  [exchange(): rows = lax.ppermute(rows, 'lat', [(0, 1), (1, 0)])]
    pallas_call x1 -> x3, Pallas kernels: 4.42 us -> 6.51 us  [the longest x1 3.52 us: exchange(): call(strips_kernel, [shape(ROWS, 128)] * 2, [HBM] * 5, [VMEM] * 2, [strip...]
    unnamed x36 -> x52, local copies, waits for them, and re-layouts: 6.88 us -> 8.6 us
    ppermute x1, starting transfers between devices: 0.01 us -> 1.57 us  [exchange(): lax.ppermute(east, 'lon', up)]
    ppermute x3 -> x1, waiting for transfers between devices: 1.8 us -> 0.31 us  [exchange(): rows = lax.ppermute(rows, 'lat', [(0, 1), (1, 0)])]
    ppermute x1, starting transfers between devices: 4.13 us -> 5.38 us  [exchange(): lax.ppermute(west, 'lon', down)]
  transfers between devices with their start and end apart: 14 -> 12, of which waited for: 5 -> 5; matrix products, arithmetic and copies ran while one was open for 0% -> 1% of each run, Pallas kernels for 17% -> 20%
where the time goes in v5:
time: 113 us; the launch traced here: 112 us
  waiting for transfers between devices  36.7 us (32%)
  Pallas kernels  36.2 us (32%)
  starting transfers between devices  28.1 us (25%)
  local copies, waits for them, and re-layouts  8.61 us (8%)
  other arithmetic  1.68 us (1%)
    ppermute x8, waiting for transfers between devices, send(): return lax.ppermute(value, 'member', pairs)  23.4 us
    pallas_call x1, Pallas kernels, own_steps(): call(own_kernel, [jax.ShapeDtypeStruct((CH, ROWS, COLS), F32), jax.ShapeD...  13.6 us
    all_to_all x1, waiting for transfers between devices, per_device(): parts = lax.all_to_all(parts, ('lon', 'lat'), 0, 0)  10.8 us
    all_to_all x1, starting transfers between devices, per_device(): parts = lax.all_to_all(parts, ('lon', 'lat'), 0, 0)  9.48 us
    ppermute x8, starting transfers between devices, send(): return lax.ppermute(value, 'member', pairs)  8.6 us
    unnamed x52, local copies, waits for them, and re-layouts  8.6 us
    pallas_call x1, Pallas kernels, control_steps(): call(control_kernel, jax.ShapeDtypeStruct((CH, HALF, COLS), F32), [SMEM]...  6.86 us
    ppermute x1, starting transfers between devices, exchange(): lax.ppermute(west, 'lon', down)  5.38 us
  transfers between devices with their start and end apart: 12, of which 5 were waited for; matrix products, arithmetic and copies ran while one was open for 1% of the time, Pallas kernels for 20%

profile of v5, /device:TPU:24, one launch (start us, length us, event | category | flops | bytes accessed | tf_op | source)
XLA Modules:
  0.0 112.4 jit_solution(12385018427835534625)
XLA Ops:
  0.6 0.7 pad_add_fusion.lat.where
  1.3 0.8 shard_map.89
  2.1 0.8 collective-permute-start.3
  2.9 1.9 %collective-permute-start.4 = (f32[16,72,384]{2,1,0:T(8,128)}, f32[16,72,384]{2,1,0:T(8,128)}, u32[]{:S(2)}, u32[]{:S(2)}) collective-permute-start(f32[16,72,384]{2,1,0:T(8,128)} %get-tuple-element.19.low), channel_id=1, source_target_pairs={{0,224},{1,225},{2,226},{3,227},{4,228},{5,229},{6,230},{7,231},{8... | collective-permute-start | bytes 5308424 | tf_op jit(solution)/shard_map/ppermute | solution.py:314
  4.8 2.3 %shard_map.86 = f32[96,384]{1,0:T(8,128)} custom-call(s32[3]{0:T(128)} %pad_add_fusion.lat.where, f32[16,128,384]{2,1,0:T(8,128)} %bitcast.6, f32[128,384]{1,0:T(8,128)} %depth.5, f32[128,384]{1,0:T(8,128)} %rotation.5, f32[5,128,384]{2,1,0:T(8,128)} %diff.5, s32[128,384]{1,0:T(8,128)} %mask.9), custom_call_target="tpu_custom_call" | custom-call | flops 4194304 | bytes 8388608 | tf_op jit(solution)/shard_map/pallas_call | solution.py:120
  7.2 0.0 copy-start.4
  7.2 3.1 %collective-permute-start = (f32[96,384]{1,0:T(8,128)}, f32[96,384]{1,0:T(8,128)S(1)}, u32[]{:S(2)}, u32[]{:S(2)}) collective-permute-start(f32[96,384]{1,0:T(8,128)} %shard_map.86), channel_id=1, source_target_pairs={{0,1},{1,0},{2,3},{3,2},{4,5},{5,4},{6,7},{7,6},{8,9},{9,8},{10,11... | collective-permute-start | bytes 442376 | tf_op jit(solution)/shard_map/ppermute | solution.py:128
  10.3 3.5 %shard_map.87 = (f32[128,128]{1,0:T(8,128)}, f32[128,128]{1,0:T(8,128)}) custom-call(f32[16,128,384]{2,1,0:T(8,128)} %bitcast.7, f32[128,384]{1,0:T(8,128)} %depth.5, f32[128,384]{1,0:T(8,128)} %rotation.5, f32[5,128,384]{2,1,0:T(8,128)} %diff.5, s32[128,384]{1,0:T(8,128)} %mask.9), custom_call_target="tpu_custom_call" | custom-call | flops 4194304 | bytes 8388608 | tf_op jit(solution)/shard_map/pallas_call | solution.py:130
  13.8 0.3 collective-permute-done.rows
  14.2 0.9 copy-done.22
  15.0 0.8 copy-done.23
  15.9 0.7 shard_map.88
  16.5 1.6 %collective-permute-start.1 = (f32[136,128]{1,0:T(8,128)S(1)}, f32[136,128]{1,0:T(8,128)S(1)}, u32[]{:S(2)}, u32[]{:S(2)}) collective-permute-start(f32[136,128]{1,0:T(8,128)S(1)} %get-tuple-element.16), channel_id=1, source_target_pairs={{0,2},{2,4},{4,6},{6,8},{8,10},{10,12},{12,14},{14,16},{16,18},{18... | collective-permute-start | bytes 208904 | tf_op jit(solution)/shard_map/ppermute | solution.py:141
  18.1 5.4 %collective-permute-start.2 = (f32[136,128]{1,0:T(8,128)S(1)}, f32[136,128]{1,0:T(8,128)S(1)}, u32[]{:S(2)}, u32[]{:S(2)}) collective-permute-start(f32[136,128]{1,0:T(8,128)S(1)} %get-tuple-element.17), channel_id=1, source_target_pairs={{2,0},{4,2},{6,4},{8,6},{10,8},{12,10},{14,12},{16,14},{18,16},{20... | collective-permute-start | bytes 208904 | tf_op jit(solution)/shard_map/ppermute | solution.py:141
  23.5 2.2 %collective-permute-done.1.fw = f32[136,128]{1,0:T(8,128)S(1)} collective-permute-done((f32[136,128]{1,0:T(8,128)S(1)}, f32[136,128]{1,0:T(8,128)S(1)}, u32[]{:S(2)}, u32[]{:S(2)}) %collective-permute-start.1) | collective-permute-done | bytes 69664 | tf_op jit(solution)/shard_map/ppermute | solution.py:141
  25.7 0.0 collective-permute-done.2.fe
  25.7 0.8 shard_map.90
  26.5 1.3 %collective-permute-start.5 = (f32[16,8,384]{2,1,0:T(8,128)}, f32[16,8,384]{2,1,0:T(8,128)}, u32[]{:S(2)}, u32[]{:S(2)}) collective-permute-start(f32[16,8,384]{2,1,0:T(8,128)} %shard_map.90), channel_id=1, source_target_pairs={{0,64},{1,65},{2,66},{3,67},{4,68},{5,69},{6,70},{7,71},{8,72},{9,... | collective-permute-start | bytes 589832 | tf_op jit(solution)/shard_map/ppermute | solution.py:314
  27.8 1.4 %collective-permute-start.6 = (f32[16,8,384]{2,1,0:T(8,128)}, f32[16,8,384]{2,1,0:T(8,128)}, u32[]{:S(2)}, u32[]{:S(2)}) collective-permute-start(f32[16,8,384]{2,1,0:T(8,128)} %shard_map.90), channel_id=1, source_target_pairs={{0,224},{1,225},{2,226},{3,227},{4,228},{5,229},{6,230},{7,231},{8... | collective-permute-start | bytes 589832 | tf_op jit(solution)/shard_map/ppermute | solution.py:314
  29.2 0.0 collective-permute-done.6
  29.2 1.0 select_select_fusion.halo.refs_6_
  30.2 0.0 copy-start
  30.2 0.0 copy-start.3
  30.2 0.0 copy-start.10
  30.3 0.0 copy-start.11
  30.3 0.0 copy-start.12
  30.3 2.2 %copy-done.14 = f32[16,72,384]{2,1,0:T(8,128)S(1)} copy-done((f32[16,72,384]{2,1,0:T(8,128)S(1)}, f32[16,72,384]{2,1,0:T(8,128)}, u32[]{:S(2)}) %copy-start.14) | copy-done | bytes 1769496
  32.5 0.7 shard_map.91
  33.2 0.8 collective-permute-start.7
  34.0 0.8 collective-permute-start.8
  34.8 0.0 copy-start.5
  34.8 1.6 %collective-permute-start.9 = (f32[16,80,384]{2,1,0:T(8,128)S(1)}, f32[16,80,384]{2,1,0:T(8,128)S(1)}, u32[]{:S(2)}, u32[]{:S(2)}) collective-permute-start(f32[16,80,384]{2,1,0:T(8,128)S(1)} %get-tuple-element.22), channel_id=1, source_target_pairs={{0,192},{224,160},{1,193},{225,161},{2,194},{226,162},{3,195},{227... | collective-permute-start | bytes 5898248 | tf_op jit(solution)/shard_map/ppermute | solution.py:314
  36.5 13.6 %shard_map.92 = (f32[16,128,384]{2,1,0:T(8,128)S(1)}, f32[8,72,512]{2,1,0:T(8,128)S(1)}) custom-call(s32[3]{0:T(128)S(1)} %copy-done.24, f32[16,128,384]{2,1,0:T(8,128)S(1)} %bitcast.8, f32[128,384]{1,0:T(8,128)S(1)} %copy-done.11, f32[128,384]{1,0:T(8,128)S(1)} %copy-done.12, f32[5,128,384]{2,1,0:T(8,128)S(1)} %copy-done.3, s32[128,384]{1,0:T(8,128)S(1)} %copy-done.10, ...), custom_call_target="tpu_custom_call" | custom-call | flops 268435456 | bytes 8388608 | tf_op jit(solution)/shard_map/pallas_call | solution.py:284
  50.1 21.3 %collective-permute-done.9.refs_4_ = f32[16,80,384]{2,1,0:T(8,128)S(1)} collective-permute-done((f32[16,80,384]{2,1,0:T(8,128)S(1)}, f32[16,80,384]{2,1,0:T(8,128)S(1)}, u32[]{:S(2)}, u32[]{:S(2)}) %collective-permute-start.9) | collective-permute-done | bytes 1966112 | tf_op jit(solution)/shard_map/ppermute | solution.py:314
  71.4 6.9 %shard_map.93.control.mine = f32[16,64,384]{2,1,0:T(8,128)S(1)} custom-call(s32[3]{0:T(128)S(1)} %copy-done.24, f32[16,72,384]{2,1,0:T(8,128)S(1)} %copy-done.5, f32[16,80,384]{2,1,0:T(8,128)S(1)} %collective-permute-done.7.refs_1_, f32[16,72,384]{2,1,0:T(8,128)S(1)} %copy-done.7, f32[16,80,384]{2,1,0:T(8,128)S(1)} %collective-permute-done.8.refs_3_, ...), custom_call_target="tpu_custom_call" | custom-call | flops 134217728 | bytes 8388608 | tf_op jit(solution)/shard_map/pallas_call | solution.py:453
  78.3 0.0 copy-start.1
  78.3 0.1 collective-permute-start.10
  78.4 1.2 %shard_map.94.earlier = f32[8,128]{1,0:T(8,128)S(1)} custom-call(s32[3]{0:T(128)S(1)} %copy-done.24, f32[16,128,384]{2,1,0:T(8,128)S(1)} %get-tuple-element.21.own, f32[16,64,384]{2,1,0:T(8,128)S(1)} %shard_map.93.control.mine, s32[128,384]{1,0:T(8,128)S(1)} %copy-done.10, s32[128,384]{1,0:T(8,128)S(1)} %copy-done.13, f32[8,128]{1,0:T(8,128)S(1)} %broadcast_in_dim.9.earlier), custom_call_target="tpu_custom_call" | custom-call | flops 4194304 | bytes 8388608 | tf_op jit(solution)/shard_map/pallas_call | solution.py:510
  79.6 0.0 copy-start.25
  79.6 2.2 %collective-permute-done.10.control.theirs = f32[16,64,384]{2,1,0:T(8,128)S(1)} collective-permute-done((f32[16,64,384]{2,1,0:T(8,128)S(1)}, f32[16,64,384]{2,1,0:T(8,128)S(1)}, u32[]{:S(2)}, u32[]{:S(2)}) %collective-permute-start.10) | collective-permute-done | bytes 1572896 | tf_op jit(solution)/shard_map/ppermute | solution.py:314
  81.8 1.4 %shard_map.95 = f32[32,8,128]{2,1,0:T(8,128)S(1)} custom-call(s32[3]{0:T(128)S(1)} %copy-done.24, f32[16,128,384]{2,1,0:T(8,128)S(1)} %get-tuple-element.21.own, f32[16,64,384]{2,1,0:T(8,128)S(1)} %collective-permute-done.10.control.theirs, s32[128,384]{1,0:T(8,128)S(1)} %copy-done.10, s32[128,384]{1,0:T(8,128)S(1)} %copy-done.13, ...), custom_call_target="tpu_custom_call" | custom-call | flops 4194304 | bytes 8388608 | tf_op jit(solution)/shard_map/pallas_call | solution.py:510
  83.2 1.2 %copy-done.8 = f32[16,64,384]{2,1,0:T(8,128)} copy-done((f32[16,64,384]{2,1,0:T(8,128)}, f32[16,64,384]{2,1,0:T(8,128)S(1)}, u32[]{:S(2)}) %copy-start.8) | copy-done | bytes 1572888
  84.3 0.6 copy-done.17
  85.0 9.5 %all-to-all-start = ((f32[32,8,128]{2,1,0:T(8,128)}), f32[32,8,128]{2,1,0:T(8,128)S(1)}, u32[]{:S(2)}, u32[]{:S(2)}) async-start(f32[32,8,128]{2,1,0:T(8,128)} %copy-done.17), calls=%async_computation | async-start | bytes 262144 | tf_op jit(solution)/shard_map/all_to_all | solution.py:592
  94.5 10.8 %all-to-all-done.parts = f32[32,8,128]{2,1,0:T(8,128)S(1)} async-done(((f32[32,8,128]{2,1,0:T(8,128)}), f32[32,8,128]{2,1,0:T(8,128)S(1)}, u32[]{:S(2)}, u32[]{:S(2)}) %all-to-all-start) | async-done | bytes 131104 | tf_op jit(solution)/shard_map/all_to_all | solution.py:592
  105.2 1.4 %copy-done.2 = f32[16,64,384]{2,1,0:T(8,128)S(1)} copy-done((f32[16,64,384]{2,1,0:T(8,128)S(1)}, f32[16,64,384]{2,1,0:T(8,128)}, u32[]{:S(2)}) %copy-start.2) | copy-done | bytes 1572888
  106.7 1.4 %copy-done.9 = f32[16,64,384]{2,1,0:T(8,128)S(1)} copy-done((f32[16,64,384]{2,1,0:T(8,128)S(1)}, f32[16,64,384]{2,1,0:T(8,128)}, u32[]{:S(2)}) %copy-start.9) | copy-done | bytes 1572888
  108.1 4.4 %shard_map.96 = (f32[16,128,384]{2,1,0:T(8,128)}, f32[1,16]{1,0:T(1,128)}) custom-call(s32[3]{0:T(128)S(1)} %copy-done.24, f32[16,128,384]{2,1,0:T(8,128)S(1)} %get-tuple-element.21.own, f32[16,64,384]{2,1,0:T(8,128)S(1)} %copy-done.2, f32[16,64,384]{2,1,0:T(8,128)S(1)} %copy-done.9, s32[128,384]{1,0:T(8,128)S(1)} %copy-done.13, ...), custom_call_target="tpu_custom_call" | custom-call | flops 4194304 | bytes 10485760 | tf_op jit(solution)/shard_map/pallas_call | solution.py:566
  (44 shorter events, 0.1 us)
Async XLA Ops:
  2.1 28.1 %collective-permute-start.3 = (f32[16,72,384]{2,1,0:T(8,128)}, f32[16,72,384]{2,1,0:T(8,128)S(1)}, u32[]{:S(2)}, u32[]{:S(2)}) collective-permute-start(f32[16,72,384]{2,1,0:T(8,128)} %get-tuple-element.18.top.refs_0_), channel_id=1, source_target_pairs={{0,64},{1,65},{2,66},{3,67},{4,68},{5,69},{6,70},{7,71},{8,72},{9,... | collective-permute-start | bytes 5308424 | tf_op jit(solution)/shard_map/ppermute | solution.py:314
  2.9 27.4 %collective-permute-start.4 = (f32[16,72,384]{2,1,0:T(8,128)}, f32[16,72,384]{2,1,0:T(8,128)}, u32[]{:S(2)}, u32[]{:S(2)}) collective-permute-start(f32[16,72,384]{2,1,0:T(8,128)} %get-tuple-element.19.low), channel_id=1, source_target_pairs={{0,224},{1,225},{2,226},{3,227},{4,228},{5,229},{6,230},{7,231},{8... | collective-permute-start | bytes 5308424 | tf_op jit(solution)/shard_map/ppermute | solution.py:314
  7.2 7.0 %copy-start.24 = (s32[3]{0:T(128)S(1)}, s32[3]{0:T(128)}, u32[]{:S(2)}) copy-start(s32[3]{0:T(128)} %pad_add_fusion.lat.where) | copy-start | bytes 40
  7.2 23.1 %copy-start.4 = (f32[16,72,384]{2,1,0:T(8,128)S(1)}, f32[16,72,384]{2,1,0:T(8,128)}, u32[]{:S(2)}) copy-start(f32[16,72,384]{2,1,0:T(8,128)} %get-tuple-element.18.top.refs_0_) | copy-start | bytes 5308420
  7.2 6.9 %collective-permute-start = (f32[96,384]{1,0:T(8,128)}, f32[96,384]{1,0:T(8,128)S(1)}, u32[]{:S(2)}, u32[]{:S(2)}) collective-permute-start(f32[96,384]{1,0:T(8,128)} %shard_map.86), channel_id=1, source_target_pairs={{0,1},{1,0},{2,3},{3,2},{4,5},{5,4},{6,7},{7,6},{8,9},{9,8},{10,11... | collective-permute-start | bytes 442376 | tf_op jit(solution)/shard_map/ppermute | solution.py:128
  14.2 11.5 %copy-start.15 = (f32[96,384]{1,0:T(8,128)}, f32[96,384]{1,0:T(8,128)S(1)}, u32[]{:S(2)}) copy-start(f32[96,384]{1,0:T(8,128)S(1)} %collective-permute-done.rows) | copy-start | bytes 442372
  14.2 0.9 copy-start.22
  15.0 0.8 copy-start.23
  16.5 9.1 %collective-permute-start.1 = (f32[136,128]{1,0:T(8,128)S(1)}, f32[136,128]{1,0:T(8,128)S(1)}, u32[]{:S(2)}, u32[]{:S(2)}) collective-permute-start(f32[136,128]{1,0:T(8,128)S(1)} %get-tuple-element.16), channel_id=1, source_target_pairs={{0,2},{2,4},{4,6},{6,8},{8,10},{10,12},{12,14},{14,16},{16,18},{18... | collective-permute-start | bytes 208904 | tf_op jit(solution)/shard_map/ppermute | solution.py:141
  18.1 7.6 %collective-permute-start.2 = (f32[136,128]{1,0:T(8,128)S(1)}, f32[136,128]{1,0:T(8,128)S(1)}, u32[]{:S(2)}, u32[]{:S(2)}) collective-permute-start(f32[136,128]{1,0:T(8,128)S(1)} %get-tuple-element.17), channel_id=1, source_target_pairs={{2,0},{4,2},{6,4},{8,6},{10,8},{12,10},{14,12},{16,14},{18,16},{20... | collective-permute-start | bytes 208904 | tf_op jit(solution)/shard_map/ppermute | solution.py:141
  25.7 0.8 copy-start.18
  25.7 2.1 %copy-start.20 = (f32[136,128]{1,0:T(8,128)}, f32[136,128]{1,0:T(8,128)S(1)}, u32[]{:S(2)}) copy-start(f32[136,128]{1,0:T(8,128)S(1)} %collective-permute-done.2.fe) | copy-start | bytes 208900
  26.5 2.7 %collective-permute-start.5 = (f32[16,8,384]{2,1,0:T(8,128)}, f32[16,8,384]{2,1,0:T(8,128)}, u32[]{:S(2)}, u32[]{:S(2)}) collective-permute-start(f32[16,8,384]{2,1,0:T(8,128)} %shard_map.90), channel_id=1, source_target_pairs={{0,64},{1,65},{2,66},{3,67},{4,68},{5,69},{6,70},{7,71},{8,72},{9,... | collective-permute-start | bytes 589832 | tf_op jit(solution)/shard_map/ppermute | solution.py:314
  27.8 1.4 %collective-permute-start.6 = (f32[16,8,384]{2,1,0:T(8,128)}, f32[16,8,384]{2,1,0:T(8,128)}, u32[]{:S(2)}, u32[]{:S(2)}) collective-permute-start(f32[16,8,384]{2,1,0:T(8,128)} %shard_map.90), channel_id=1, source_target_pairs={{0,224},{1,225},{2,226},{3,227},{4,228},{5,229},{6,230},{7,231},{8... | collective-permute-start | bytes 589832 | tf_op jit(solution)/shard_map/ppermute | solution.py:314
  29.2 7.2 %copy-start.16 = (f32[96,384]{1,0:T(8,128)S(1)}, f32[96,384]{1,0:T(8,128)}, u32[]{:S(2)}) copy-start(f32[96,384]{1,0:T(8,128)} %copy-done.15) | copy-start | bytes 442372
  29.2 7.2 %copy-start.19 = (f32[136,128]{1,0:T(8,128)S(1)}, f32[136,128]{1,0:T(8,128)}, u32[]{:S(2)}) copy-start(f32[136,128]{1,0:T(8,128)} %copy-done.18) | copy-start | bytes 208900
  29.2 7.2 %copy-start.21 = (f32[136,128]{1,0:T(8,128)S(1)}, f32[136,128]{1,0:T(8,128)}, u32[]{:S(2)}) copy-start(f32[136,128]{1,0:T(8,128)} %copy-done.20) | copy-start | bytes 208900
  30.2 6.2 %copy-start = (f32[1,16,128,384]{3,2,1,0:T(8,128)S(1)}, f32[1,16,128,384]{3,2,1,0:T(8,128)}, u32[]{:S(2)}) copy-start(f32[1,16,128,384]{3,2,1,0:T(8,128)} %param.7) | copy-start | bytes 9437188
  30.2 6.2 %copy-start.3 = (f32[5,128,384]{2,1,0:T(8,128)S(1)}, f32[5,128,384]{2,1,0:T(8,128)}, u32[]{:S(2)}) copy-start(f32[5,128,384]{2,1,0:T(8,128)} %diff.5) | copy-start | bytes 2949124
  30.2 6.2 %copy-start.10 = (s32[128,384]{1,0:T(8,128)S(1)}, s32[128,384]{1,0:T(8,128)}, u32[]{:S(2)}) copy-start(s32[128,384]{1,0:T(8,128)} %mask.9) | copy-start | bytes 589828
  30.3 6.2 %copy-start.11 = (f32[128,384]{1,0:T(8,128)S(1)}, f32[128,384]{1,0:T(8,128)}, u32[]{:S(2)}) copy-start(f32[128,384]{1,0:T(8,128)} %depth.5) | copy-start | bytes 589828
  30.3 6.2 %copy-start.12 = (f32[128,384]{1,0:T(8,128)S(1)}, f32[128,384]{1,0:T(8,128)}, u32[]{:S(2)}) copy-start(f32[128,384]{1,0:T(8,128)} %rotation.5) | copy-start | bytes 589828
  30.3 2.9 %copy-start.6 = (f32[16,72,384]{2,1,0:T(8,128)}, f32[16,72,384]{2,1,0:T(8,128)S(1)}, u32[]{:S(2)}) copy-start(f32[16,72,384]{2,1,0:T(8,128)S(1)} %collective-permute-done.3.p1.refs_2_) | copy-start | bytes 5308420
  30.3 2.2 %copy-start.14 = (f32[16,72,384]{2,1,0:T(8,128)S(1)}, f32[16,72,384]{2,1,0:T(8,128)}, u32[]{:S(2)}) copy-start(f32[16,72,384]{2,1,0:T(8,128)} %get-tuple-element.19.low) | copy-start | bytes 5308420
  33.2 16.9 %collective-permute-start.7 = (f32[16,80,384]{2,1,0:T(8,128)S(1)}, f32[16,80,384]{2,1,0:T(8,128)S(1)}, u32[]{:S(2)}, u32[]{:S(2)}) collective-permute-start(f32[16,80,384]{2,1,0:T(8,128)S(1)} %get-tuple-element.20.gate), channel_id=1, source_target_pairs={{0,32},{1,33},{2,34},{3,35},{4,36},{5,37},{6,38},{7,39},{8,40},{9,... | collective-permute-start | bytes 5898248 | tf_op jit(solution)/shard_map/ppermute | solution.py:314
  34.0 16.1 %collective-permute-start.8 = (f32[16,80,384]{2,1,0:T(8,128)S(1)}, f32[16,80,384]{2,1,0:T(8,128)S(1)}, u32[]{:S(2)}, u32[]{:S(2)}) collective-permute-start(f32[16,80,384]{2,1,0:T(8,128)S(1)} %get-tuple-element.20.gate), channel_id=1, source_target_pairs={{0,96},{64,128},{1,97},{65,129},{2,98},{66,130},{3,99},{67,131},{4... | collective-permute-start | bytes 5898248 | tf_op jit(solution)/shard_map/ppermute | solution.py:314
  34.8 36.6 %copy-start.5 = (f32[16,72,384]{2,1,0:T(8,128)S(1)}, f32[16,72,384]{2,1,0:T(8,128)}, u32[]{:S(2)}) copy-start(f32[16,72,384]{2,1,0:T(8,128)} %get-tuple-element.18.top.refs_0_) | copy-start | bytes 5308420
  34.8 36.6 %copy-start.7 = (f32[16,72,384]{2,1,0:T(8,128)S(1)}, f32[16,72,384]{2,1,0:T(8,128)}, u32[]{:S(2)}) copy-start(f32[16,72,384]{2,1,0:T(8,128)} %copy-done.6) | copy-start | bytes 5308420
  34.8 36.6 %collective-permute-start.9 = (f32[16,80,384]{2,1,0:T(8,128)S(1)}, f32[16,80,384]{2,1,0:T(8,128)S(1)}, u32[]{:S(2)}, u32[]{:S(2)}) collective-permute-start(f32[16,80,384]{2,1,0:T(8,128)S(1)} %get-tuple-element.22), channel_id=1, source_target_pairs={{0,192},{224,160},{1,193},{225,161},{2,194},{226,162},{3,195},{227... | collective-permute-start | bytes 5898248 | tf_op jit(solution)/shard_map/ppermute | solution.py:314
  71.4 7.0 %copy-start.13 = (s32[128,384]{1,0:T(8,128)S(1)}, s32[128,384]{1,0:T(8,128)}, u32[]{:S(2)}) copy-start(s32[128,384]{1,0:T(8,128)} %region.5) | copy-start | bytes 589828
  78.3 1.3 %copy-start.1 = (f32[16,64,384]{2,1,0:T(8,128)}, f32[16,64,384]{2,1,0:T(8,128)S(1)}, u32[]{:S(2)}) copy-start(f32[16,64,384]{2,1,0:T(8,128)S(1)} %shard_map.93.control.mine) | copy-start | bytes 4718596
  78.3 3.5 %collective-permute-start.10 = (f32[16,64,384]{2,1,0:T(8,128)S(1)}, f32[16,64,384]{2,1,0:T(8,128)S(1)}, u32[]{:S(2)}, u32[]{:S(2)}) collective-permute-start(f32[16,64,384]{2,1,0:T(8,128)S(1)} %shard_map.93.control.mine), channel_id=1, source_target_pairs={{0,32},{32,0},{64,96},{96,64},{128,160},{160,128},{192,224},{224,1... | collective-permute-start | bytes 4718600 | tf_op jit(solution)/shard_map/ppermute | solution.py:314
  79.6 14.9 %copy-start.25 = (f32[16]{0:T(128)S(1)}, f32[16]{0:T(128)}, u32[]{:S(2)}) copy-start(f32[16]{0:T(128)} %param.13) | copy-start | bytes 196
  83.2 1.2 %copy-start.8 = (f32[16,64,384]{2,1,0:T(8,128)}, f32[16,64,384]{2,1,0:T(8,128)S(1)}, u32[]{:S(2)}) copy-start(f32[16,64,384]{2,1,0:T(8,128)S(1)} %collective-permute-done.10.control.theirs) | copy-start | bytes 4718596
  84.3 0.6 copy-start.17
  85.0 20.3 %all-to-all-start = ((f32[32,8,128]{2,1,0:T(8,128)}), f32[32,8,128]{2,1,0:T(8,128)S(1)}, u32[]{:S(2)}, u32[]{:S(2)}) async-start(f32[32,8,128]{2,1,0:T(8,128)} %copy-done.17), calls=%async_computation | async-start | bytes 262144 | tf_op jit(solution)/shard_map/all_to_all | solution.py:592
  105.2 1.4 %copy-start.2 = (f32[16,64,384]{2,1,0:T(8,128)S(1)}, f32[16,64,384]{2,1,0:T(8,128)}, u32[]{:S(2)}) copy-start(f32[16,64,384]{2,1,0:T(8,128)} %copy-done.1) | copy-start | bytes 4718596
  106.7 1.4 %copy-start.9 = (f32[16,64,384]{2,1,0:T(8,128)S(1)}, f32[16,64,384]{2,1,0:T(8,128)}, u32[]{:S(2)}) copy-start(f32[16,64,384]{2,1,0:T(8,128)} %copy-done.8) | copy-start | bytes 4718596

commit v6 on v5

--- a/solution.py
+++ b/solution.py
@@ -22,13 +22,14 @@
 F32 = jnp.float32
 
 
-def call(kernel, out, in_specs, out_specs, scratch=(), flops=1 << 22, nbytes=1 << 23, mib=12):
+def call(kernel, out, in_specs, out_specs, scratch=(), flops=1 << 22, nbytes=1 << 23, mib=12, aliases=None):
     return pl.pallas_call(
         kernel,
         out_shape=out,
         in_specs=in_specs,
         out_specs=out_specs,
         scratch_shapes=list(scratch),
+        input_output_aliases=aliases or {},
         compiler_params=pltpu.CompilerParams(vmem_limit_bytes=mib << 20),
         cost_estimate=pl.CostEstimate(flops=flops, bytes_accessed=nbytes, transcendentals=0),
     )
@@ -133,7 +134,7 @@
         [HBM] * 5,
         [VMEM] * 2,
         [strip, strip, pltpu.VMEM((ROWS, COLS), jnp.int32), pltpu.SemaphoreType.DMA((9,))],
-        mib=60,
+        mib=58,
     )(state, *statics)
     west, east = call(corners_kernel, [shape(ROWS_X, 128)] * 2, [SMEM] + [VMEM] * 3, [VMEM] * 2)(
         where, rows, west, east
@@ -336,7 +337,7 @@
 STAGE = [pltpu.VMEM((2, CH, HALF_X, COLS), F32), pltpu.SemaphoreType.DMA((4 * CHUNKS,))]
 
 
-def cut_kernel(where, state, top, low, buffer, sem):
+def cut_kernel(where, state, low, top, buffer, sem):
     @pl.when(where[2] == 0)
     def _():
         staged(
@@ -346,63 +347,43 @@
 
 def spread_first(where, state):
     shape = jax.ShapeDtypeStruct((CH, HALF_X, COLS), F32)
-    top, low = call(cut_kernel, [shape, shape], [SMEM, HBM], [HBM] * 2, STAGE, mib=62)(where, state)
-    return top, low, send(top, [(0, 2)]), send(low, [(0, 7)])
-
-
-def relay_kernel(where, top, low, p1, m1, halo, u, v, buffer, sem, ride, ride_sem):
+    low, top = call(cut_kernel, [shape, shape], [SMEM, HBM], [HBM] * 2, STAGE, mib=62)(where, state)
+    return low, top, send(top, [(0, 2)]), send(low, [(0, 7)])
+
+
+def relay_kernel(where, u, v, p1, m1, gate, u_out, v_out, buffer, sem):
+    @pl.when(where[2] == 2)
+    def _():
+        staged([(p1, u_out)], buffer, sem)
+
+    @pl.when(where[2] == 7)
+    def _():
+        staged([(m1, v_out)], buffer, sem)
+
+
+def spread_rest(where, u, v, p1, m1, halo):
     m = where[2]
-
-    def move(pairs):
-        one = pltpu.make_async_copy(halo, ride, ride_sem.at[0])
-        one.start()
-        one.wait()
-        more = [
-            pltpu.make_async_copy(ride, dst.at[:, HALF_X : HALF_X + 8, :], ride_sem.at[1 + i])
-            for i, (_, dst) in enumerate(pairs)
-        ]
-        for copy in more:
-            copy.start()
-        staged(pairs, buffer, sem)
-        for copy in more:
-            copy.wait()
-
-    @pl.when(m == 0)
-    def _():
-        move([(low, u), (top, v)])
-
-    @pl.when(m == 2)
-    def _():
-        move([(p1, u)])
-
-    @pl.when(m == 7)
-    def _():
-        move([(m1, v)])
-
-
-def spread_rest(where, top, low, p1, m1, halo):
-    m = where[2]
-    for_two, for_seven = send(halo, [(0, 2)]), send(halo, [(0, 7)])
-    halo = jnp.where(m == 2, for_two, jnp.where(m == 7, for_seven, halo))
-    shape = jax.ShapeDtypeStruct((CH, HALF_X + 8, COLS), F32)
+    known = jnp.where(m == 1, send(halo, [(0, 1)]), halo)
     u, v = call(
-        relay_kernel,
-        [shape, shape],
-        [SMEM] + [HBM] * 4 + [ANY],
-        [HBM] * 2,
-        STAGE + [pltpu.VMEM((CH, 8, COLS), F32), pltpu.SemaphoreType.DMA((3,))],
-    )(where, top, low, p1, m1, halo)
+        relay_kernel, [u, v], [SMEM] + [HBM] * 4 + [ANY], [HBM] * 2, STAGE, mib=58, aliases={1: 0, 2: 1}
+    )(where, u, v, p1, m1, halo)
     p2 = send(u, [(0, 3), (2, 4)])
     m2 = send(v, [(0, 6), (7, 5)])
     e0 = send(u, [(0, 1)])
-    return (top, e0, p1, p2, m2, m1), halo, u
-
-
-HOLDER = ((0,), (1,), (2,), (3, 4), (5, 6), (7,))
+    return (v, e0, u, p2, m2), (known, send(known, [(0, 3), (1, 6)])), u
+
+
+def spread_halo_rest(m, known, came):
+    known = jnp.where((m == 3) | (m == 6), came, known)
+    return known, send(known, [(0, 2), (1, 7), (3, 4), (6, 5)])
+
+
+HOLDER = ((0, 7), (1,), (2,), (3, 4), (5, 6))
+HALO_HOLDER = (0, 0, 1, 0, 1, 1, 0, 1)
 
 
 def control_kernel(where, *refs):
-    arrays, (early, static, out, x, y, ub, vb, h2, near, halo, strip, sem) = refs[:6], refs[6:]
+    arrays, halos, (static, out, x, y, ub, vb, h2, near, halo, strip, sem) = refs[:5], refs[5:7], refs[7:]
     first = where[1] == 0
     m = where[2]
     for array, members in zip(arrays, HOLDER):
@@ -410,11 +391,9 @@
             r0, r1 = (0, HALF) if member % 2 == 0 else (8, 0)
 
             @pl.when(m == member)
-            def _(array=array, r0=r0, r1=r1):
+            def _(array=array, r0=r0, r1=r1, source=halos[HALO_HOLDER[member]]):
                 one = pltpu.make_async_copy(array.at[:, r0 : r0 + HALF, :], x.at[:, 0:HALF, 0:COLS], sem.at[0])
                 two = pltpu.make_async_copy(array.at[:, r1 : r1 + 8, :], near, sem.at[1])
-                rides = array.shape[1] > HALF_X
-                source = array.at[:, HALF_X : HALF_X + 8, :] if rides else early
                 three = pltpu.make_async_copy(source, halo, sem.at[2])
                 one.start()
                 two.start()
@@ -449,11 +428,11 @@
     two_steps(x, static, y, ub, vb, h2, out)
 
 
-def control_steps(where, arrays, halo, static):
+def control_steps(where, arrays, halos, static):
     return call(
         control_kernel,
         jax.ShapeDtypeStruct((CH, HALF, COLS), F32),
-        [SMEM] + [HBM] * 6 + [ANY, VMEM],
+        [SMEM] + [HBM] * 5 + [ANY] * 2 + [VMEM],
         VMEM,
         [pltpu.VMEM((CH, HALF_X, COLS_X), F32)]
         + step_scratch(HALF_X)
@@ -461,7 +440,7 @@
         + [pltpu.VMEM((ROWS_X, 128), F32), pltpu.SemaphoreType.DMA((3,))],
         flops=1 << 27,
         mib=16,
-    )(where, *arrays, halo, static)
+    )(where, *arrays, *halos, static)
 
 
 def sums_kernel(other, where, own, control, mask, region, earlier, out, *copy):
@@ -583,9 +562,11 @@
     first = spread_first(where, state)
     halos = exchange(where, state, statics)
     halo = call(control_halo_kernel, jax.ShapeDtypeStruct((CH, 8, COLS), F32), [VMEM] * 3, VMEM)(*halos)
-    arrays, halo, gate = spread_rest(where, *first, halo)
+    arrays, control_halos, gate = spread_rest(where, *first, halo)
     own, static = own_steps(where, state, statics, halos, gate)
-    mine = control_steps(where, arrays, halo, static)
+    came, static = lax.optimization_barrier((control_halos[1], static))
+    control_halos = spread_halo_rest(m, control_halos[0], came)
+    mine = control_steps(where, arrays, control_halos, static)
     theirs = send(mine, [(i, i ^ 1) for i in range(8)])
     parts = half_sums(False, where, own, mine, mask, region, jnp.zeros((8, 128), F32))
     parts = half_sums(True, where, own, theirs, mask, region, parts)

time: 113 us -> 113 us (level)
  waiting for transfers between devices: 36.7 us -> 18.5 us
  starting transfers between devices: 28.1 us -> 39.9 us
  local copies, waits for them, and re-layouts: 8.61 us -> 11.8 us
  other arithmetic: 1.68 us -> 3.41 us
  Pallas kernels: 36.2 us -> 37.5 us
    ppermute x8 -> x9, waiting for transfers between devices: 23.4 us -> 5.03 us  [send(): return lax.ppermute(value, 'member', pairs)]
    ppermute x8 -> x9, starting transfers between devices: 8.6 us -> 20.3 us  [send(): return lax.ppermute(value, 'member', pairs)]
    unnamed x52 -> x46, local copies, waits for them, and re-layouts: 8.6 us -> 11.8 us
    select_n x1 -> x2, other arithmetic: 1.02 us -> 2.81 us  [the longest x1 1.62 us: spread_rest(): known = jnp.where(m == 1, send(halo, [(0, 1)]), halo)]
  transfers between devices with their start and end apart: 12 -> 13, of which waited for: 5 -> 5; matrix products, arithmetic and copies ran while one was open for 1% -> 3% of each run, Pallas kernels for 20% -> 20%
where the time goes in v6:
time: 113 us; the launch traced here: 112 us
  starting transfers between devices  39.9 us (35%)
  Pallas kernels  37.5 us (33%)
  waiting for transfers between devices  18.5 us (16%)
  local copies, waits for them, and re-layouts  11.8 us (10%)
  other arithmetic  3.41 us (3%)
    ppermute x9, starting transfers between devices, send(): return lax.ppermute(value, 'member', pairs)  20.3 us
    pallas_call x1, Pallas kernels, own_steps(): call(own_kernel, [jax.ShapeDtypeStruct((CH, ROWS, COLS), F32), jax.ShapeD...  13.6 us
    unnamed x46, local copies, waits for them, and re-layouts  11.8 us
    all_to_all x1, waiting for transfers between devices, per_device(): parts = lax.all_to_all(parts, ('lon', 'lat'), 0, 0)  10.9 us
    all_to_all x1, starting transfers between devices, per_device(): parts = lax.all_to_all(parts, ('lon', 'lat'), 0, 0)  9.59 us
    pallas_call x1, Pallas kernels, control_steps(): call(control_kernel, jax.ShapeDtypeStruct((CH, HALF, COLS), F32), [SMEM]...  7.94 us
    ppermute x1, starting transfers between devices, exchange(): lax.ppermute(west, 'lon', down)  5.38 us
    ppermute x9, waiting for transfers between devices, send(): return lax.ppermute(value, 'member', pairs)  5.03 us
  transfers between devices with their start and end apart: 13, of which 5 were waited for; matrix products, arithmetic and copies ran while one was open for 3% of the time, Pallas kernels for 20%

profile of v6, /device:TPU:24, one launch (start us, length us, event | category | flops | bytes accessed | tf_op | source)
XLA Modules:
  0.0 112.0 jit_solution(1748969220692672602)
XLA Ops:
  0.6 0.6 pad_add_fusion.lat.where
  1.2 0.8 shard_map.89
  2.1 0.8 collective-permute-start.3
  2.9 1.9 %collective-permute-start.4 = (f32[16,72,384]{2,1,0:T(8,128)}, f32[16,72,384]{2,1,0:T(8,128)}, u32[]{:S(2)}, u32[]{:S(2)}) collective-permute-start(f32[16,72,384]{2,1,0:T(8,128)} %get-tuple-element.20.u), channel_id=1, source_target_pairs={{0,224},{1,225},{2,226},{3,227},{4,228},{5,229},{6,230},{7,231},{8... | collective-permute-start | bytes 5308424 | tf_op jit(solution)/shard_map/ppermute | solution.py:315
  4.8 2.4 %shard_map.86 = f32[96,384]{1,0:T(8,128)} custom-call(s32[3]{0:T(128)} %pad_add_fusion.lat.where, f32[16,128,384]{2,1,0:T(8,128)} %bitcast.6, f32[128,384]{1,0:T(8,128)} %depth.5, f32[128,384]{1,0:T(8,128)} %rotation.5, f32[5,128,384]{2,1,0:T(8,128)} %diff.5, s32[128,384]{1,0:T(8,128)} %mask.9), custom_call_target="tpu_custom_call" | custom-call | flops 4194304 | bytes 8388608 | tf_op jit(solution)/shard_map/pallas_call | solution.py:121
  7.1 3.1 %collective-permute-start = (f32[96,384]{1,0:T(8,128)}, f32[96,384]{1,0:T(8,128)S(1)}, u32[]{:S(2)}, u32[]{:S(2)}) collective-permute-start(f32[96,384]{1,0:T(8,128)} %shard_map.86), channel_id=1, source_target_pairs={{0,1},{1,0},{2,3},{3,2},{4,5},{5,4},{6,7},{7,6},{8,9},{9,8},{10,11... | collective-permute-start | bytes 442376 | tf_op jit(solution)/shard_map/ppermute | solution.py:129
  10.2 3.5 %shard_map.87 = (f32[128,128]{1,0:T(8,128)}, f32[128,128]{1,0:T(8,128)}) custom-call(f32[16,128,384]{2,1,0:T(8,128)} %bitcast.7, f32[128,384]{1,0:T(8,128)} %depth.5, f32[128,384]{1,0:T(8,128)} %rotation.5, f32[5,128,384]{2,1,0:T(8,128)} %diff.5, s32[128,384]{1,0:T(8,128)} %mask.9), custom_call_target="tpu_custom_call" | custom-call | flops 4194304 | bytes 8388608 | tf_op jit(solution)/shard_map/pallas_call | solution.py:131
  13.8 0.3 collective-permute-done.rows
  14.1 0.9 copy-done.17
  15.0 0.8 copy-done.18
  15.8 0.7 shard_map.88
  16.5 1.6 %collective-permute-start.1 = (f32[136,128]{1,0:T(8,128)S(1)}, f32[136,128]{1,0:T(8,128)S(1)}, u32[]{:S(2)}, u32[]{:S(2)}) collective-permute-start(f32[136,128]{1,0:T(8,128)S(1)} %get-tuple-element.18), channel_id=1, source_target_pairs={{0,2},{2,4},{4,6},{6,8},{8,10},{10,12},{12,14},{14,16},{16,18},{18... | collective-permute-start | bytes 208904 | tf_op jit(solution)/shard_map/ppermute | solution.py:142
  18.0 5.4 %collective-permute-start.2 = (f32[136,128]{1,0:T(8,128)S(1)}, f32[136,128]{1,0:T(8,128)S(1)}, u32[]{:S(2)}, u32[]{:S(2)}) collective-permute-start(f32[136,128]{1,0:T(8,128)S(1)} %get-tuple-element.19), channel_id=1, source_target_pairs={{2,0},{4,2},{6,4},{8,6},{10,8},{12,10},{14,12},{16,14},{18,16},{20... | collective-permute-start | bytes 208904 | tf_op jit(solution)/shard_map/ppermute | solution.py:142
  23.4 2.2 %collective-permute-done.1.fw = f32[136,128]{1,0:T(8,128)S(1)} collective-permute-done((f32[136,128]{1,0:T(8,128)S(1)}, f32[136,128]{1,0:T(8,128)S(1)}, u32[]{:S(2)}, u32[]{:S(2)}) %collective-permute-start.1) | collective-permute-done | bytes 69664 | tf_op jit(solution)/shard_map/ppermute | solution.py:142
  25.6 0.0 collective-permute-done.2.fe
  25.6 0.8 shard_map.90.gate
  26.4 0.0 copy-start.21
  26.4 1.2 %copy-done.21 = f32[16,72,384]{2,1,0:T(8,128)} copy-done((f32[16,72,384]{2,1,0:T(8,128)}, f32[16,72,384]{2,1,0:T(8,128)S(1)}, u32[]{:S(2)}) %copy-start.21) | copy-done | bytes 1769496
  27.6 1.0 shard_map.91
  28.6 1.9 %collective-permute-start.5 = (f32[16,72,384]{2,1,0:T(8,128)}, f32[16,72,384]{2,1,0:T(8,128)}, u32[]{:S(2)}, u32[]{:S(2)}) collective-permute-start(f32[16,72,384]{2,1,0:T(8,128)} %get-tuple-element.22.gate.refs_2_), channel_id=1, source_target_pairs={{0,32},{1,33},{2,34},{3,35},{4,36},{5,37},{6,38},{7,39},{8,40},{9,... | collective-permute-start | bytes 5308424 | tf_op jit(solution)/shard_map/ppermute | solution.py:315
  30.5 1.9 %collective-permute-start.6 = (f32[16,72,384]{2,1,0:T(8,128)}, f32[16,72,384]{2,1,0:T(8,128)}, u32[]{:S(2)}, u32[]{:S(2)}) collective-permute-start(f32[16,72,384]{2,1,0:T(8,128)} %get-tuple-element.22.gate.refs_2_), channel_id=1, source_target_pairs={{0,96},{64,128},{1,97},{65,129},{2,98},{66,130},{3,99},{67,131},{4... | collective-permute-start | bytes 5308424 | tf_op jit(solution)/shard_map/ppermute | solution.py:315
  32.4 1.3 %collective-permute-start.7 = (f32[16,72,384]{2,1,0:T(8,128)}, f32[16,72,384]{2,1,0:T(8,128)}, u32[]{:S(2)}, u32[]{:S(2)}) collective-permute-start(f32[16,72,384]{2,1,0:T(8,128)} %get-tuple-element.24.refs_0_), channel_id=1, source_target_pairs={{0,192},{224,160},{1,193},{225,161},{2,194},{226,162},{3,195},{227... | collective-permute-start | bytes 5308424 | tf_op jit(solution)/shard_map/ppermute | solution.py:315
  33.7 1.4 %collective-permute-start.8 = (f32[16,8,384]{2,1,0:T(8,128)}, f32[16,8,384]{2,1,0:T(8,128)}, u32[]{:S(2)}, u32[]{:S(2)}) collective-permute-start(f32[16,8,384]{2,1,0:T(8,128)} %shard_map.90.gate), channel_id=1, source_target_pairs={{0,32},{1,33},{2,34},{3,35},{4,36},{5,37},{6,38},{7,39},{8,40},{9,... | collective-permute-start | bytes 589832 | tf_op jit(solution)/shard_map/ppermute | solution.py:315
  35.0 1.6 %broadcast_select_fusion = f32[16,8,384]{2,1,0:T(8,128)} fusion(f32[16,8,384]{2,1,0:T(8,128)} %collective-permute-done.8, f32[16,8,384]{2,1,0:T(8,128)} %shard_map.90.gate, pred[]{:T(512)S(6)} %eq.13), kind=kLoop, calls=%fused_computation | loop fusion | flops 49152 | bytes 589825 | tf_op jit(solution)/shard_map/jit(_where)/select_n | solution.py:366
  36.6 1.3 %collective-permute-start.9 = (f32[16,8,384]{2,1,0:T(8,128)}, f32[16,8,384]{2,1,0:T(8,128)}, u32[]{:S(2)}, u32[]{:S(2)}) collective-permute-start(f32[16,8,384]{2,1,0:T(8,128)} %broadcast_select_fusion), channel_id=1, source_target_pairs={{0,96},{32,192},{1,97},{33,193},{2,98},{34,194},{3,99},{35,195},{4... | collective-permute-start | bytes 589832 | tf_op jit(solution)/shard_map/ppermute | solution.py:315
  38.0 1.5 %copy-done.3 = f32[16,72,384]{2,1,0:T(8,128)S(1)} copy-done((f32[16,72,384]{2,1,0:T(8,128)S(1)}, f32[16,72,384]{2,1,0:T(8,128)}, u32[]{:S(2)}) %copy-start.3) | copy-done | bytes 1769496
  39.5 1.2 %copy-done.4 = f32[5,128,384]{2,1,0:T(8,128)S(1)} copy-done((f32[5,128,384]{2,1,0:T(8,128)S(1)}, f32[5,128,384]{2,1,0:T(8,128)}, u32[]{:S(2)}) %copy-start.4) | copy-done | bytes 983064
  40.7 0.9 copy-done.8
  41.6 0.9 copy-done.11
  42.5 0.9 copy-done.14
  43.4 0.9 copy-done.16
  44.3 13.6 %shard_map.92 = (f32[16,128,384]{2,1,0:T(8,128)S(1)}, f32[8,72,512]{2,1,0:T(8,128)S(1)}) custom-call(s32[3]{0:T(128)S(1)} %copy-done.20, f32[16,128,384]{2,1,0:T(8,128)S(1)} %bitcast.8, f32[128,384]{1,0:T(8,128)S(1)} %copy-done.7, f32[128,384]{1,0:T(8,128)S(1)} %copy-done.8, f32[5,128,384]{2,1,0:T(8,128)S(1)} %copy-done.4, s32[128,384]{1,0:T(8,128)S(1)} %copy-done.6, ...), custom_call_target="tpu_custom_call" | custom-call | flops 268435456 | bytes 8388608 | tf_op jit(solution)/shard_map/pallas_call | solution.py:285
  57.9 0.0 copy-start.1
  57.9 1.2 %broadcast_select_fusion.1.refs_5_ = f32[16,8,384]{2,1,0:T(8,128)S(1)} fusion(f32[16,8,384]{2,1,0:T(8,128)} %collective-permute-done.9, f32[16,8,384]{2,1,0:T(8,128)} %broadcast_select_fusion, pred[]{:T(512)S(6)} %or.3), kind=kLoop, calls=%fused_computation.1 | loop fusion | flops 49152 | bytes 589825 | tf_op jit(solution)/shard_map/jit(_where)/select_n | solution.py:377
  59.1 0.0 copy-start.9
  59.1 1.4 %collective-permute-start.10 = (f32[16,8,384]{2,1,0:T(8,128)S(1)}, f32[16,8,384]{2,1,0:T(8,128)S(1)}, u32[]{:S(2)}, u32[]{:S(2)}) collective-permute-start(f32[16,8,384]{2,1,0:T(8,128)S(1)} %broadcast_select_fusion.1.refs_5_), channel_id=1, source_target_pairs={{0,64},{32,224},{96,128},{192,160},{1,65},{33,225},{97,129},{193,1... | collective-permute-start | bytes 589832 | tf_op jit(solution)/shard_map/ppermute | solution.py:315
  60.6 3.2 %collective-permute-done.10.refs_6_ = f32[16,8,384]{2,1,0:T(8,128)S(1)} collective-permute-done((f32[16,8,384]{2,1,0:T(8,128)S(1)}, f32[16,8,384]{2,1,0:T(8,128)S(1)}, u32[]{:S(2)}, u32[]{:S(2)}) %collective-permute-start.10) | collective-permute-done | bytes 196640 | tf_op jit(solution)/shard_map/ppermute | solution.py:315
  63.7 7.9 %shard_map.93.control.mine = f32[16,64,384]{2,1,0:T(8,128)S(1)} custom-call(s32[3]{0:T(128)S(1)} %copy-done.20, f32[16,72,384]{2,1,0:T(8,128)S(1)} %copy-done.5, f32[16,72,384]{2,1,0:T(8,128)} %collective-permute-done.5.refs_1_, f32[16,72,384]{2,1,0:T(8,128)S(1)} %copy-done.3, f32[16,72,384]{2,1,0:T(8,128)} %collective-permute-done.6.refs_3_, ...), custom_call_target="tpu_custom_call" | custom-call | flops 134217728 | bytes 8388608 | tf_op jit(solution)/shard_map/pallas_call | solution.py:432
  71.7 8.5 %collective-permute-start.11 = (f32[16,64,384]{2,1,0:T(8,128)S(1)}, f32[16,64,384]{2,1,0:T(8,128)S(1)}, u32[]{:S(2)}, u32[]{:S(2)}) collective-permute-start(f32[16,64,384]{2,1,0:T(8,128)S(1)} %shard_map.93.control.mine), channel_id=1, source_target_pairs={{0,32},{32,0},{64,96},{96,64},{128,160},{160,128},{192,224},{224,1... | collective-permute-start | bytes 4718600 | tf_op jit(solution)/shard_map/ppermute | solution.py:315
  80.2 1.2 %shard_map.94.earlier = f32[8,128]{1,0:T(8,128)S(1)} custom-call(s32[3]{0:T(128)S(1)} %copy-done.20, f32[16,128,384]{2,1,0:T(8,128)S(1)} %get-tuple-element.23.own, f32[16,64,384]{2,1,0:T(8,128)S(1)} %shard_map.93.control.mine, s32[128,384]{1,0:T(8,128)S(1)} %copy-done.6, s32[128,384]{1,0:T(8,128)S(1)} %copy-done.9, f32[8,128]{1,0:T(8,128)S(1)} %broadcast_in_dim.9.earlier), custom_call_target="tpu_custom_call" | custom-call | flops 4194304 | bytes 8388608 | tf_op jit(solution)/shard_map/pallas_call | solution.py:489
  81.3 0.0 copy-start.22
  81.4 1.9 %collective-permute-done.11.control.theirs = f32[16,64,384]{2,1,0:T(8,128)S(1)} collective-permute-done((f32[16,64,384]{2,1,0:T(8,128)S(1)}, f32[16,64,384]{2,1,0:T(8,128)S(1)}, u32[]{:S(2)}, u32[]{:S(2)}) %collective-permute-start.11) | collective-permute-done | bytes 1572896 | tf_op jit(solution)/shard_map/ppermute | solution.py:315
  83.2 1.3 %shard_map.95 = f32[32,8,128]{2,1,0:T(8,128)S(1)} custom-call(s32[3]{0:T(128)S(1)} %copy-done.20, f32[16,128,384]{2,1,0:T(8,128)S(1)} %get-tuple-element.23.own, f32[16,64,384]{2,1,0:T(8,128)S(1)} %collective-permute-done.11.control.theirs, s32[128,384]{1,0:T(8,128)S(1)} %copy-done.6, s32[128,384]{1,0:T(8,128)S(1)} %copy-done.9, f32[8,128]{1,0:T(8,128)S(1)} %shard_map.94.earlier), custom_call_target="tpu_custom_call" | custom-call | flops 4194304 | bytes 8388608 | tf_op jit(solution)/shard_map/pallas_call | solution.py:489
  84.6 0.6 copy-done.12
  85.2 9.6 %all-to-all-start = ((f32[32,8,128]{2,1,0:T(8,128)}), f32[32,8,128]{2,1,0:T(8,128)S(1)}, u32[]{:S(2)}, u32[]{:S(2)}) async-start(f32[32,8,128]{2,1,0:T(8,128)} %copy-done.12), calls=%async_computation | async-start | bytes 262144 | tf_op jit(solution)/shard_map/all_to_all | solution.py:573
  94.8 10.9 %all-to-all-done.parts = f32[32,8,128]{2,1,0:T(8,128)S(1)} async-done(((f32[32,8,128]{2,1,0:T(8,128)}), f32[32,8,128]{2,1,0:T(8,128)S(1)}, u32[]{:S(2)}, u32[]{:S(2)}) %all-to-all-start) | async-done | bytes 131104 | tf_op jit(solution)/shard_map/all_to_all | solution.py:573
  105.8 1.9 %copy-done.2 = f32[16,128,384]{2,1,0:T(8,128)S(1)} copy-done((f32[16,128,384]{2,1,0:T(8,128)S(1)}, f32[16,128,384]{2,1,0:T(8,128)}, u32[]{:S(2)}) %copy-start.2) | copy-done | bytes 3145752
  107.7 4.4 %shard_map.96 = (f32[16,128,384]{2,1,0:T(8,128)}, f32[1,16]{1,0:T(1,128)}) custom-call(s32[3]{0:T(128)S(1)} %copy-done.20, f32[16,128,384]{2,1,0:T(8,128)S(1)} %copy-done.2, f32[16,64,384]{2,1,0:T(8,128)S(1)} %shard_map.93.control.mine, f32[16,64,384]{2,1,0:T(8,128)S(1)} %collective-permute-done.11.control.theirs, s32[128,384]{1,0:T(8,128)S(1)} %copy-done.9, ...), custom_call_target="tpu_custom_call" | custom-call | flops 4194304 | bytes 10485760 | tf_op jit(solution)/shard_map/pallas_call | solution.py:545
  (41 shorter events, 0.1 us)
Async XLA Ops:
  2.1 24.3 %collective-permute-start.3 = (f32[16,72,384]{2,1,0:T(8,128)}, f32[16,72,384]{2,1,0:T(8,128)S(1)}, u32[]{:S(2)}, u32[]{:S(2)}) collective-permute-start(f32[16,72,384]{2,1,0:T(8,128)} %get-tuple-element.21.v), channel_id=1, source_target_pairs={{0,64},{1,65},{2,66},{3,67},{4,68},{5,69},{6,70},{7,71},{8,72},{9,... | collective-permute-start | bytes 5308424 | tf_op jit(solution)/shard_map/ppermute | solution.py:315
  2.9 24.8 %collective-permute-start.4 = (f32[16,72,384]{2,1,0:T(8,128)}, f32[16,72,384]{2,1,0:T(8,128)}, u32[]{:S(2)}, u32[]{:S(2)}) collective-permute-start(f32[16,72,384]{2,1,0:T(8,128)} %get-tuple-element.20.u), channel_id=1, source_target_pairs={{0,224},{1,225},{2,226},{3,227},{4,228},{5,229},{6,230},{7,231},{8... | collective-permute-start | bytes 5308424 | tf_op jit(solution)/shard_map/ppermute | solution.py:315
  7.1 7.0 %copy-start.19 = (s32[3]{0:T(128)S(1)}, s32[3]{0:T(128)}, u32[]{:S(2)}) copy-start(s32[3]{0:T(128)} %pad_add_fusion.lat.where) | copy-start | bytes 40
  7.1 6.9 %collective-permute-start = (f32[96,384]{1,0:T(8,128)}, f32[96,384]{1,0:T(8,128)S(1)}, u32[]{:S(2)}, u32[]{:S(2)}) collective-permute-start(f32[96,384]{1,0:T(8,128)} %shard_map.86), channel_id=1, source_target_pairs={{0,1},{1,0},{2,3},{3,2},{4,5},{5,4},{6,7},{7,6},{8,9},{9,8},{10,11... | collective-permute-start | bytes 442376 | tf_op jit(solution)/shard_map/ppermute | solution.py:129
  14.1 14.5 %copy-start.10 = (f32[96,384]{1,0:T(8,128)}, f32[96,384]{1,0:T(8,128)S(1)}, u32[]{:S(2)}) copy-start(f32[96,384]{1,0:T(8,128)S(1)} %collective-permute-done.rows) | copy-start | bytes 442372
  14.1 0.9 copy-start.17
  15.0 0.8 copy-start.18
  16.5 9.1 %collective-permute-start.1 = (f32[136,128]{1,0:T(8,128)S(1)}, f32[136,128]{1,0:T(8,128)S(1)}, u32[]{:S(2)}, u32[]{:S(2)}) collective-permute-start(f32[136,128]{1,0:T(8,128)S(1)} %get-tuple-element.18), channel_id=1, source_target_pairs={{0,2},{2,4},{4,6},{6,8},{8,10},{10,12},{12,14},{14,16},{16,18},{18... | collective-permute-start | bytes 208904 | tf_op jit(solution)/shard_map/ppermute | solution.py:142
  18.0 7.6 %collective-permute-start.2 = (f32[136,128]{1,0:T(8,128)S(1)}, f32[136,128]{1,0:T(8,128)S(1)}, u32[]{:S(2)}, u32[]{:S(2)}) collective-permute-start(f32[136,128]{1,0:T(8,128)S(1)} %get-tuple-element.19), channel_id=1, source_target_pairs={{2,0},{4,2},{6,4},{8,6},{10,8},{12,10},{14,12},{16,14},{18,16},{20... | collective-permute-start | bytes 208904 | tf_op jit(solution)/shard_map/ppermute | solution.py:142
  25.6 0.8 copy-start.13
  25.6 0.8 copy-start.15
  26.4 11.6 %copy-start.6 = (s32[128,384]{1,0:T(8,128)S(1)}, s32[128,384]{1,0:T(8,128)}, u32[]{:S(2)}) copy-start(s32[128,384]{1,0:T(8,128)} %mask.9) | copy-start | bytes 589828
  26.4 11.6 %copy-start.7 = (f32[128,384]{1,0:T(8,128)S(1)}, f32[128,384]{1,0:T(8,128)}, u32[]{:S(2)}) copy-start(f32[128,384]{1,0:T(8,128)} %depth.5) | copy-start | bytes 589828
  26.4 11.6 %copy-start.20 = (s32[3]{0:T(128)S(1)}, s32[3]{0:T(128)}, u32[]{:S(2)}) copy-start(s32[3]{0:T(128)} %pad_add_fusion.lat.where) | copy-start | bytes 40
  26.4 1.2 %copy-start.21 = (f32[16,72,384]{2,1,0:T(8,128)}, f32[16,72,384]{2,1,0:T(8,128)S(1)}, u32[]{:S(2)}) copy-start(f32[16,72,384]{2,1,0:T(8,128)S(1)} %collective-permute-done.3.p1) | copy-start | bytes 5308420
  27.6 10.3 %copy-start = (f32[1,16,128,384]{3,2,1,0:T(8,128)S(1)}, f32[1,16,128,384]{3,2,1,0:T(8,128)}, u32[]{:S(2)}) copy-start(f32[1,16,128,384]{3,2,1,0:T(8,128)} %param.7) | copy-start | bytes 9437188
  28.6 35.1 %collective-permute-start.5 = (f32[16,72,384]{2,1,0:T(8,128)}, f32[16,72,384]{2,1,0:T(8,128)}, u32[]{:S(2)}, u32[]{:S(2)}) collective-permute-start(f32[16,72,384]{2,1,0:T(8,128)} %get-tuple-element.22.gate.refs_2_), channel_id=1, source_target_pairs={{0,32},{1,33},{2,34},{3,35},{4,36},{5,37},{6,38},{7,39},{8,40},{9,... | collective-permute-start | bytes 5308424 | tf_op jit(solution)/shard_map/ppermute | solution.py:315
  30.5 33.2 %collective-permute-start.6 = (f32[16,72,384]{2,1,0:T(8,128)}, f32[16,72,384]{2,1,0:T(8,128)}, u32[]{:S(2)}, u32[]{:S(2)}) collective-permute-start(f32[16,72,384]{2,1,0:T(8,128)} %get-tuple-element.22.gate.refs_2_), channel_id=1, source_target_pairs={{0,96},{64,128},{1,97},{65,129},{2,98},{66,130},{3,99},{67,131},{4... | collective-permute-start | bytes 5308424 | tf_op jit(solution)/shard_map/ppermute | solution.py:315
  32.4 31.4 %collective-permute-start.7 = (f32[16,72,384]{2,1,0:T(8,128)}, f32[16,72,384]{2,1,0:T(8,128)}, u32[]{:S(2)}, u32[]{:S(2)}) collective-permute-start(f32[16,72,384]{2,1,0:T(8,128)} %get-tuple-element.24.refs_0_), channel_id=1, source_target_pairs={{0,192},{224,160},{1,193},{225,161},{2,194},{226,162},{3,195},{227... | collective-permute-start | bytes 5308424 | tf_op jit(solution)/shard_map/ppermute | solution.py:315
  33.7 1.4 %collective-permute-start.8 = (f32[16,8,384]{2,1,0:T(8,128)}, f32[16,8,384]{2,1,0:T(8,128)}, u32[]{:S(2)}, u32[]{:S(2)}) collective-permute-start(f32[16,8,384]{2,1,0:T(8,128)} %shard_map.90.gate), channel_id=1, source_target_pairs={{0,32},{1,33},{2,34},{3,35},{4,36},{5,37},{6,38},{7,39},{8,40},{9,... | collective-permute-start | bytes 589832 | tf_op jit(solution)/shard_map/ppermute | solution.py:315
  36.6 21.3 %collective-permute-start.9 = (f32[16,8,384]{2,1,0:T(8,128)}, f32[16,8,384]{2,1,0:T(8,128)}, u32[]{:S(2)}, u32[]{:S(2)}) collective-permute-start(f32[16,8,384]{2,1,0:T(8,128)} %broadcast_select_fusion), channel_id=1, source_target_pairs={{0,96},{32,192},{1,97},{33,193},{2,98},{34,194},{3,99},{35,195},{4... | collective-permute-start | bytes 589832 | tf_op jit(solution)/shard_map/ppermute | solution.py:315
  38.0 1.5 %copy-start.3 = (f32[16,72,384]{2,1,0:T(8,128)S(1)}, f32[16,72,384]{2,1,0:T(8,128)}, u32[]{:S(2)}) copy-start(f32[16,72,384]{2,1,0:T(8,128)} %get-tuple-element.22.gate.refs_2_) | copy-start | bytes 5308420
  39.5 1.2 %copy-start.4 = (f32[5,128,384]{2,1,0:T(8,128)S(1)}, f32[5,128,384]{2,1,0:T(8,128)}, u32[]{:S(2)}) copy-start(f32[5,128,384]{2,1,0:T(8,128)} %diff.5) | copy-start | bytes 2949124
  40.7 0.9 copy-start.8
  41.6 0.9 copy-start.11
  42.5 0.9 copy-start.14
  43.4 0.9 copy-start.16
  44.3 19.5 %copy-start.5 = (f32[16,72,384]{2,1,0:T(8,128)S(1)}, f32[16,72,384]{2,1,0:T(8,128)}, u32[]{:S(2)}) copy-start(f32[16,72,384]{2,1,0:T(8,128)} %get-tuple-element.24.refs_0_) | copy-start | bytes 5308420
  57.9 25.3 %copy-start.1 = (f32[16,128,384]{2,1,0:T(8,128)}, f32[16,128,384]{2,1,0:T(8,128)S(1)}, u32[]{:S(2)}) copy-start(f32[16,128,384]{2,1,0:T(8,128)S(1)} %get-tuple-element.23.own) | copy-start | bytes 9437188
  59.1 21.1 %copy-start.9 = (s32[128,384]{1,0:T(8,128)S(1)}, s32[128,384]{1,0:T(8,128)}, u32[]{:S(2)}) copy-start(s32[128,384]{1,0:T(8,128)} %region.5) | copy-start | bytes 589828
  59.1 4.6 %collective-permute-start.10 = (f32[16,8,384]{2,1,0:T(8,128)S(1)}, f32[16,8,384]{2,1,0:T(8,128)S(1)}, u32[]{:S(2)}, u32[]{:S(2)}) collective-permute-start(f32[16,8,384]{2,1,0:T(8,128)S(1)} %broadcast_select_fusion.1.refs_5_), channel_id=1, source_target_pairs={{0,64},{32,224},{96,128},{192,160},{1,65},{33,225},{97,129},{193,1... | collective-permute-start | bytes 589832 | tf_op jit(solution)/shard_map/ppermute | solution.py:315
  71.7 11.5 %collective-permute-start.11 = (f32[16,64,384]{2,1,0:T(8,128)S(1)}, f32[16,64,384]{2,1,0:T(8,128)S(1)}, u32[]{:S(2)}, u32[]{:S(2)}) collective-permute-start(f32[16,64,384]{2,1,0:T(8,128)S(1)} %shard_map.93.control.mine), channel_id=1, source_target_pairs={{0,32},{32,0},{64,96},{96,64},{128,160},{160,128},{192,224},{224,1... | collective-permute-start | bytes 4718600 | tf_op jit(solution)/shard_map/ppermute | solution.py:315
  81.3 13.5 %copy-start.22 = (f32[16]{0:T(128)S(1)}, f32[16]{0:T(128)}, u32[]{:S(2)}) copy-start(f32[16]{0:T(128)} %param.13) | copy-start | bytes 196
  84.6 0.6 copy-start.12
  85.2 20.6 %all-to-all-start = ((f32[32,8,128]{2,1,0:T(8,128)}), f32[32,8,128]{2,1,0:T(8,128)S(1)}, u32[]{:S(2)}, u32[]{:S(2)}) async-start(f32[32,8,128]{2,1,0:T(8,128)} %copy-done.12), calls=%async_computation | async-start | bytes 262144 | tf_op jit(solution)/shard_map/all_to_all | solution.py:573
  105.8 1.9 %copy-start.2 = (f32[16,128,384]{2,1,0:T(8,128)S(1)}, f32[16,128,384]{2,1,0:T(8,128)}, u32[]{:S(2)}) copy-start(f32[16,128,384]{2,1,0:T(8,128)} %copy-done.1) | copy-start | bytes 9437188

commit v7 on v6

--- a/solution.py
+++ b/solution.py
@@ -160,7 +160,7 @@
     return pl.ds(pl.multiple_of(t * 8, 8), 8)
 
 
-def step(x, static, ub, vb, h2, store, count, tiles):
+def step(x, static, ub, vb, h2, store, count, tiles, ready):
     sub = iota((8, COLS_X), 0)
 
     def around(t):
@@ -189,6 +189,7 @@
         vb[c, :] = v
         return 0
 
+    ready(0)
     lax.fori_loop(0, count, sums, 0)
 
     def surface(t, _):
@@ -198,6 +199,7 @@
         h2[c, :] = static[7, c, :] * (x[0, c, :] - (0.25 / LEV) * static[0, c, :] * div)
         return 0
 
+    ready(1)
     lax.fori_loop(0, count, surface, 0)
 
     def rest(t, _):
@@ -230,10 +232,11 @@
             store(1 + 2 * LEV + l, c, oc * (c0 - 0.05 * (u2 * cx + v2 * cy)))
         return 0
 
+    ready(2)
     lax.fori_loop(0, tiles, rest, 0)
 
 
-def two_steps(x, static, y, ub, vb, h2, out):
+def two_steps(x, static, y, ub, vb, h2, out, ready=lambda stage: None):
     count = x.shape[1] // 8
 
     def keep(ch, c, value):
@@ -242,8 +245,8 @@
     def give(ch, c, value):
         out[ch, c, :] = value[:, :COLS]
 
-    step(x, static, ub, vb, h2, keep, count, count)
-    step(y, static, ub, vb, h2, give, count, count - 1)
+    step(x, static, ub, vb, h2, keep, count, count, ready)
+    step(y, static, ub, vb, h2, give, count, count - 1, lambda stage: None)
 
 
 def step_scratch(rows):
@@ -252,33 +255,46 @@
 
 def own_kernel(where, state, depth, rotation, diff, mask, fw, fe, rows, gate, out, part, x, land, y, ub, vb, h2, sem):
     main = (slice(0, ROWS), slice(0, COLS))
-    copies = [
-        pltpu.make_async_copy(state, x.at[(slice(0, CH),) + main], sem.at[0]),
-        pltpu.make_async_copy(depth, x.at[(CH,) + main], sem.at[1]),
-        pltpu.make_async_copy(rotation, x.at[(CH + 1,) + main], sem.at[2]),
-        pltpu.make_async_copy(diff, x.at[(slice(CH + 2, CH + 2 + LEV),) + main], sem.at[3]),
+
+    def fetch_into(i, src, at):
+        copy = pltpu.make_async_copy(src, x.at[(at,) + main], sem.at[i])
+        copy.start()
+        return copy
+
+    flow, heat = slice(1, 1 + 2 * LEV), slice(1 + 2 * LEV, CH)
+    now = [fetch_into(0, state.at[flow], flow)]
+    soon = [fetch_into(1, state.at[0], 0), fetch_into(2, depth, CH)]
+    soon.append(pltpu.make_async_copy(mask, land, sem.at[3]))
+    soon[-1].start()
+    late = [
+        fetch_into(4, state.at[heat], heat),
+        fetch_into(5, rotation, CH + 1),
+        fetch_into(6, diff, slice(CH + 2, CH + 2 + LEV)),
     ]
-    copies.append(pltpu.make_async_copy(mask, land, sem.at[4]))
-    for copy in copies:
-        copy.start()
     fill_halo(x, where, fw, fe, rows)
-    for copy in copies:
-        copy.wait()
-    x[(FIELDS - 1,) + main] = land[...].astype(F32)
+
+    def ready(stage):
+        for copy in (now, soon, late)[stage]:
+            copy.wait()
+        if stage == 1:
+            x[(FIELDS - 1,) + main] = land[...].astype(F32)
+
+    two_steps(x, x.at[CH:FIELDS], y, ub, vb, h2, out, ready)
     first = where[1] == 0
     tiles = HALF // 8
     sub = iota((8, COLS_X), 0)
+
+    def body(t, _):
+        c, g = tile_at(t), tile_at(t + jnp.where(first, 0, tiles))
+        for j in range(CH, FIELDS):
+            part[j - CH, c, :] = x[j, g, :]
+        return 0
+
+    lax.fori_loop(0, tiles, body, 0)
     for j in range(CH, FIELDS):
-
-        def body(t, _):
-            part[j - CH, tile_at(t), :] = x[j, tile_at(t + jnp.where(first, 0, tiles)), :]
-            return 0
-
-        lax.fori_loop(0, tiles, body, 0)
         n = x[j, tile_at(jnp.where(first, tiles, 2 * tiles)), :]
         p = x[j, tile_at(jnp.where(first, 2 * tiles, tiles - 1)), :]
         part[j - CH, HALF:HALF_X, :] = jnp.where(sub < 4, n, p)
-    two_steps(x, x.at[CH:FIELDS], y, ub, vb, h2, out)
 
 
 def own_steps(where, state, statics, halos, gate):
@@ -292,9 +308,9 @@
         [VMEM] * 2,
         [pltpu.VMEM((FIELDS, ROWS_X, COLS_X), F32), pltpu.VMEM((ROWS, COLS), jnp.int32)]
         + step_scratch(ROWS_X)
-        + [pltpu.SemaphoreType.DMA((5,))],
+        + [pltpu.SemaphoreType.DMA((7,))],
         flops=1 << 28,
-        mib=28,
+        mib=60,
     )(where, state, *statics, *halos, gate)
 
 
@@ -362,23 +378,37 @@
 
 
 def spread_rest(where, u, v, p1, m1, halo):
-    m = where[2]
-    known = jnp.where(m == 1, send(halo, [(0, 1)]), halo)
     u, v = call(
         relay_kernel, [u, v], [SMEM] + [HBM] * 4 + [ANY], [HBM] * 2, STAGE, mib=58, aliases={1: 0, 2: 1}
     )(where, u, v, p1, m1, halo)
     p2 = send(u, [(0, 3), (2, 4)])
     m2 = send(v, [(0, 6), (7, 5)])
-    e0 = send(u, [(0, 1)])
-    return (v, e0, u, p2, m2), (known, send(known, [(0, 3), (1, 6)])), u
-
-
-def spread_halo_rest(m, known, came):
-    known = jnp.where((m == 3) | (m == 6), came, known)
+    return (v, u, p2, m2), (halo, send(halo, [(0, 1)]), send(halo, [(0, 3)]), send(halo, [(0, 6)]))
+
+
+def known_kernel(where, own, one, three, six, gate, out, sem):
+    for member, ref in ((0, own), (1, one), (3, three), (6, six)):
+
+        @pl.when(where[2] == member)
+        def _(ref=ref):
+            copy = pltpu.make_async_copy(ref, out, sem.at[0])
+            copy.start()
+            copy.wait()
+
+
+def spread_halo_rest(where, halos, gate):
+    known = call(
+        known_kernel,
+        jax.ShapeDtypeStruct((CH, 8, COLS), F32),
+        [SMEM] + [ANY] * 5,
+        VMEM,
+        [pltpu.SemaphoreType.DMA((1,))],
+        mib=8,
+    )(where, *halos, gate)
     return known, send(known, [(0, 2), (1, 7), (3, 4), (6, 5)])
 
 
-HOLDER = ((0, 7), (1,), (2,), (3, 4), (5, 6))
+HOLDER = ((0, 7), (2,), (3, 4), (5, 6), (1,))
 HALO_HOLDER = (0, 0, 1, 0, 1, 1, 0, 1)
 
 
@@ -562,10 +592,11 @@
     first = spread_first(where, state)
     halos = exchange(where, state, statics)
     halo = call(control_halo_kernel, jax.ShapeDtypeStruct((CH, 8, COLS), F32), [VMEM] * 3, VMEM)(*halos)
-    arrays, control_halos, gate = spread_rest(where, *first, halo)
-    own, static = own_steps(where, state, statics, halos, gate)
-    came, static = lax.optimization_barrier((control_halos[1], static))
-    control_halos = spread_halo_rest(m, control_halos[0], came)
+    arrays, control_halos = spread_rest(where, *first, halo)
+    own, static = own_steps(where, state, statics, halos, arrays[1])
+    control_halos = spread_halo_rest(where, control_halos, static)
+    late, static = lax.optimization_barrier((arrays[1], static))
+    arrays += (send(late, [(0, 1)]),)
     mine = control_steps(where, arrays, control_halos, static)
     theirs = send(mine, [(i, i ^ 1) for i in range(8)])
     parts = half_sums(False, where, own, mine, mask, region, jnp.zeros((8, 128), F32))

time: 113 us -> 117 us (1.035)
  waiting for transfers between devices: 18.5 us -> 31 us
  starting transfers between devices: 39.9 us -> 30.5 us
  other arithmetic: 3.41 us -> 0.64 us
  Pallas kernels: 37.5 us -> 39.8 us
    ppermute x9 -> x10, waiting for transfers between devices: 5.03 us -> 17.7 us  [send(): return lax.ppermute(value, 'member', pairs)]
    ppermute x9 -> x10, starting transfers between devices: 20.3 us -> 10.9 us  [send(): return lax.ppermute(value, 'member', pairs)]
    select_n x2 -> x0, other arithmetic: 2.81 us -> none  [the longest x1 1.62 us: spread_rest(): known = jnp.where(m == 1, send(halo, [(0, 1)]), halo)]
    pallas_call x1, Pallas kernels: 13.6 us -> 15.6 us  [own_steps(): call(own_kernel, [jax.ShapeDtypeStruct((CH, ROWS, COLS), F32), jax.ShapeD...]
    unnamed x46 -> x48, local copies, waits for them, and re-layouts: 11.8 us -> 12.3 us
  transfers between devices with their start and end apart: 13 -> 14, of which waited for: 5 -> 6; matrix products, arithmetic and copies ran while one was open for 3% -> 0% of each run, Pallas kernels for 20% -> 21%
where the time goes in v7:
time: 117 us; the launch traced here: 115 us
  Pallas kernels  39.8 us (34%)
  waiting for transfers between devices  31 us (26%)
  starting transfers between devices  30.5 us (26%)
  local copies, waits for them, and re-layouts  12.3 us (11%)
    ppermute x10, waiting for transfers between devices, send(): return lax.ppermute(value, 'member', pairs)  17.7 us
    pallas_call x1, Pallas kernels, own_steps(): call(own_kernel, [jax.ShapeDtypeStruct((CH, ROWS, COLS), F32), jax.ShapeD...  15.6 us
    unnamed x48, local copies, waits for them, and re-layouts  12.3 us
    ppermute x10, starting transfers between devices, send(): return lax.ppermute(value, 'member', pairs)  10.9 us
    all_to_all x1, waiting for transfers between devices, per_device(): parts = lax.all_to_all(parts, ('lon', 'lat'), 0, 0)  10.8 us
    all_to_all x1, starting transfers between devices, per_device(): parts = lax.all_to_all(parts, ('lon', 'lat'), 0, 0)  9.49 us
    pallas_call x1, Pallas kernels, control_steps(): call(control_kernel, jax.ShapeDtypeStruct((CH, HALF, COLS), F32), [SMEM]...  8.22 us
    ppermute x1, starting transfers between devices, exchange(): lax.ppermute(west, 'lon', down)  5.38 us
  transfers between devices with their start and end apart: 14, of which 6 were waited for; matrix products, arithmetic and copies ran while one was open for 0% of the time, Pallas kernels for 21%

profile of v7, /device:TPU:24, one launch (start us, length us, event | category | flops | bytes accessed | tf_op | source)
XLA Modules:
  0.0 115.2 jit_solution(16325498309226487957)
XLA Ops:
  0.6 0.6 pad_add_fusion.lat.where
  1.3 0.8 shard_map.89
  2.1 0.8 collective-permute-start.3
  2.9 1.9 %collective-permute-start.4 = (f32[16,72,384]{2,1,0:T(8,128)}, f32[16,72,384]{2,1,0:T(8,128)}, u32[]{:S(2)}, u32[]{:S(2)}) collective-permute-start(f32[16,72,384]{2,1,0:T(8,128)} %get-tuple-element.20.u), channel_id=1, source_target_pairs={{0,224},{1,225},{2,226},{3,227},{4,228},{5,229},{6,230},{7,231},{8... | collective-permute-start | bytes 5308424 | tf_op jit(solution)/shard_map/ppermute | solution.py:331
  4.8 2.4 %shard_map.86 = f32[96,384]{1,0:T(8,128)} custom-call(s32[3]{0:T(128)} %pad_add_fusion.lat.where, f32[16,128,384]{2,1,0:T(8,128)} %bitcast.6, f32[128,384]{1,0:T(8,128)} %depth.5, f32[128,384]{1,0:T(8,128)} %rotation.5, f32[5,128,384]{2,1,0:T(8,128)} %diff.5, s32[128,384]{1,0:T(8,128)} %mask.9), custom_call_target="tpu_custom_call" | custom-call | flops 4194304 | bytes 8388608 | tf_op jit(solution)/shard_map/pallas_call | solution.py:121
  7.2 3.1 %collective-permute-start = (f32[96,384]{1,0:T(8,128)}, f32[96,384]{1,0:T(8,128)S(1)}, u32[]{:S(2)}, u32[]{:S(2)}) collective-permute-start(f32[96,384]{1,0:T(8,128)} %shard_map.86), channel_id=1, source_target_pairs={{0,1},{1,0},{2,3},{3,2},{4,5},{5,4},{6,7},{7,6},{8,9},{9,8},{10,11... | collective-permute-start | bytes 442376 | tf_op jit(solution)/shard_map/ppermute | solution.py:129
  10.3 3.5 %shard_map.87 = (f32[128,128]{1,0:T(8,128)}, f32[128,128]{1,0:T(8,128)}) custom-call(f32[16,128,384]{2,1,0:T(8,128)} %bitcast.7, f32[128,384]{1,0:T(8,128)} %depth.5, f32[128,384]{1,0:T(8,128)} %rotation.5, f32[5,128,384]{2,1,0:T(8,128)} %diff.5, s32[128,384]{1,0:T(8,128)} %mask.9), custom_call_target="tpu_custom_call" | custom-call | flops 4194304 | bytes 8388608 | tf_op jit(solution)/shard_map/pallas_call | solution.py:131
  13.8 0.3 collective-permute-done.rows
  14.2 0.9 copy-done.18
  15.0 0.8 copy-done.19
  15.9 0.7 shard_map.88
  16.5 1.6 %collective-permute-start.1 = (f32[136,128]{1,0:T(8,128)S(1)}, f32[136,128]{1,0:T(8,128)S(1)}, u32[]{:S(2)}, u32[]{:S(2)}) collective-permute-start(f32[136,128]{1,0:T(8,128)S(1)} %get-tuple-element.18), channel_id=1, source_target_pairs={{0,2},{2,4},{4,6},{6,8},{8,10},{10,12},{12,14},{14,16},{16,18},{18... | collective-permute-start | bytes 208904 | tf_op jit(solution)/shard_map/ppermute | solution.py:142
  18.1 5.4 %collective-permute-start.2 = (f32[136,128]{1,0:T(8,128)S(1)}, f32[136,128]{1,0:T(8,128)S(1)}, u32[]{:S(2)}, u32[]{:S(2)}) collective-permute-start(f32[136,128]{1,0:T(8,128)S(1)} %get-tuple-element.19), channel_id=1, source_target_pairs={{2,0},{4,2},{6,4},{8,6},{10,8},{12,10},{14,12},{16,14},{18,16},{20... | collective-permute-start | bytes 208904 | tf_op jit(solution)/shard_map/ppermute | solution.py:142
  23.5 2.2 %collective-permute-done.1.fw = f32[136,128]{1,0:T(8,128)S(1)} collective-permute-done((f32[136,128]{1,0:T(8,128)S(1)}, f32[136,128]{1,0:T(8,128)S(1)}, u32[]{:S(2)}, u32[]{:S(2)}) %collective-permute-start.1) | collective-permute-done | bytes 69664 | tf_op jit(solution)/shard_map/ppermute | solution.py:142
  25.7 0.1 shard_map.90.gate.own
  25.8 0.7 copy-done.12
  26.5 0.0 collective-permute-done.3.p1
  26.5 0.0 collective-permute-done.4.m1
  26.5 1.2 %copy-done.22 = f32[16,72,384]{2,1,0:T(8,128)} copy-done((f32[16,72,384]{2,1,0:T(8,128)}, f32[16,72,384]{2,1,0:T(8,128)S(1)}, u32[]{:S(2)}) %copy-start.22) | copy-done | bytes 1769496
  27.7 0.8 shard_map.91
  28.5 1.9 %collective-permute-start.5 = (f32[16,72,384]{2,1,0:T(8,128)}, f32[16,72,384]{2,1,0:T(8,128)}, u32[]{:S(2)}, u32[]{:S(2)}) collective-permute-start(f32[16,72,384]{2,1,0:T(8,128)} %get-tuple-element.26.gate.refs_1_), channel_id=1, source_target_pairs={{0,96},{64,128},{1,97},{65,129},{2,98},{66,130},{3,99},{67,131},{4... | collective-permute-start | bytes 5308424 | tf_op jit(solution)/shard_map/ppermute | solution.py:331
  30.5 1.4 %collective-permute-start.6 = (f32[16,72,384]{2,1,0:T(8,128)}, f32[16,72,384]{2,1,0:T(8,128)}, u32[]{:S(2)}, u32[]{:S(2)}) collective-permute-start(f32[16,72,384]{2,1,0:T(8,128)} %get-tuple-element.24.refs_0_), channel_id=1, source_target_pairs={{0,192},{224,160},{1,193},{225,161},{2,194},{226,162},{3,195},{227... | collective-permute-start | bytes 5308424 | tf_op jit(solution)/shard_map/ppermute | solution.py:331
  31.9 15.6 %shard_map.92 = (f32[16,128,384]{2,1,0:T(8,128)}, f32[8,72,512]{2,1,0:T(8,128)}) custom-call(s32[3]{0:T(128)} %pad_add_fusion.lat.where, f32[16,128,384]{2,1,0:T(8,128)} %bitcast.8, f32[128,384]{1,0:T(8,128)} %depth.5, f32[128,384]{1,0:T(8,128)} %rotation.5, f32[5,128,384]{2,1,0:T(8,128)} %diff.5, s32[128,384]{1,0:T(8,128)} %mask.9, f32[136,128]{1,0:T(8,128)} %copy-done.16, ...), custom_call_target="tpu_custom_call" | custom-call | flops 268435456 | bytes 8388608 | tf_op jit(solution)/shard_map/pallas_call | solution.py:301
  47.5 0.9 collective-permute-start.7
  48.4 0.7 collective-permute-start.8
  49.1 0.7 collective-permute-start.9
  49.8 1.3 %collective-permute-start.10 = (f32[16,8,384]{2,1,0:T(8,128)S(1)}, f32[16,8,384]{2,1,0:T(8,128)S(1)}, u32[]{:S(2)}, u32[]{:S(2)}) collective-permute-start(f32[16,8,384]{2,1,0:T(8,128)S(1)} %copy-done.13), channel_id=1, source_target_pairs={{0,192},{1,193},{2,194},{3,195},{4,196},{5,197},{6,198},{7,199},{8... | collective-permute-start | bytes 589832 | tf_op jit(solution)/shard_map/ppermute | solution.py:331
  51.1 12.4 %collective-permute-done.10.six = f32[16,8,384]{2,1,0:T(8,128)S(1)} collective-permute-done((f32[16,8,384]{2,1,0:T(8,128)S(1)}, f32[16,8,384]{2,1,0:T(8,128)S(1)}, u32[]{:S(2)}, u32[]{:S(2)}) %collective-permute-start.10) | collective-permute-done | bytes 196640 | tf_op jit(solution)/shard_map/ppermute | solution.py:331
  63.6 1.3 %copy-done.9 = f32[8,72,512]{2,1,0:T(8,128)S(1)} copy-done((f32[8,72,512]{2,1,0:T(8,128)S(1)}, f32[8,72,512]{2,1,0:T(8,128)}, u32[]{:S(2)}) %copy-start.9) | copy-done | bytes 1179672
  64.8 0.8 shard_map.93.refs_5_
  65.7 1.3 %collective-permute-start.11 = (f32[16,8,384]{2,1,0:T(8,128)S(1)}, f32[16,8,384]{2,1,0:T(8,128)S(1)}, u32[]{:S(2)}, u32[]{:S(2)}) collective-permute-start(f32[16,8,384]{2,1,0:T(8,128)S(1)} %shard_map.93.refs_5_), channel_id=1, source_target_pairs={{0,64},{32,224},{96,128},{192,160},{1,65},{33,225},{97,129},{193,1... | collective-permute-start | bytes 589832 | tf_op jit(solution)/shard_map/ppermute | solution.py:331
  67.0 3.2 %collective-permute-done.11.refs_6_ = f32[16,8,384]{2,1,0:T(8,128)S(1)} collective-permute-done((f32[16,8,384]{2,1,0:T(8,128)S(1)}, f32[16,8,384]{2,1,0:T(8,128)S(1)}, u32[]{:S(2)}, u32[]{:S(2)}) %collective-permute-start.11) | collective-permute-done | bytes 196640 | tf_op jit(solution)/shard_map/ppermute | solution.py:331
  70.2 1.5 %copy-done.5 = f32[16,72,384]{2,1,0:T(8,128)S(1)} copy-done((f32[16,72,384]{2,1,0:T(8,128)S(1)}, f32[16,72,384]{2,1,0:T(8,128)}, u32[]{:S(2)}) %copy-start.5) | copy-done | bytes 1769496
  71.6 1.3 %copy-done.10 = f32[8,72,512]{2,1,0:T(8,128)S(1)} copy-done((f32[8,72,512]{2,1,0:T(8,128)S(1)}, f32[8,72,512]{2,1,0:T(8,128)}, u32[]{:S(2)}) %copy-start.10) | copy-done | bytes 1179672
  72.9 8.2 %shard_map.94.control.mine = f32[16,64,384]{2,1,0:T(8,128)S(1)} custom-call(s32[3]{0:T(128)S(1)} %copy-done.21, f32[16,72,384]{2,1,0:T(8,128)S(1)} %copy-done.5, f32[16,72,384]{2,1,0:T(8,128)S(1)} %copy-done.2, f32[16,72,384]{2,1,0:T(8,128)} %collective-permute-done.5.refs_2_, f32[16,72,384]{2,1,0:T(8,128)} %collective-permute-done.6.refs_3_, ...), custom_call_target="tpu_custom_call" | custom-call | flops 134217728 | bytes 8388608 | tf_op jit(solution)/shard_map/pallas_call | solution.py:462
  81.1 0.1 collective-permute-start.12
  81.3 1.2 %shard_map.95.earlier = f32[8,128]{1,0:T(8,128)S(1)} custom-call(s32[3]{0:T(128)S(1)} %copy-done.21, f32[16,128,384]{2,1,0:T(8,128)S(1)} %copy-done, f32[16,64,384]{2,1,0:T(8,128)S(1)} %shard_map.94.control.mine, s32[128,384]{1,0:T(8,128)S(1)} %copy-done.8, s32[128,384]{1,0:T(8,128)S(1)} %copy-done.11, f32[8,128]{1,0:T(8,128)S(1)} %broadcast_in_dim.9.earlier), custom_call_target="tpu_custom_call" | custom-call | flops 4194304 | bytes 8388608 | tf_op jit(solution)/shard_map/pallas_call | solution.py:519
  82.5 0.0 copy-start.23
  82.5 2.2 %collective-permute-done.12.control.theirs = f32[16,64,384]{2,1,0:T(8,128)S(1)} collective-permute-done((f32[16,64,384]{2,1,0:T(8,128)S(1)}, f32[16,64,384]{2,1,0:T(8,128)S(1)}, u32[]{:S(2)}, u32[]{:S(2)}) %collective-permute-start.12) | collective-permute-done | bytes 1572896 | tf_op jit(solution)/shard_map/ppermute | solution.py:331
  84.6 1.3 %shard_map.96 = f32[32,8,128]{2,1,0:T(8,128)S(1)} custom-call(s32[3]{0:T(128)S(1)} %copy-done.21, f32[16,128,384]{2,1,0:T(8,128)S(1)} %copy-done, f32[16,64,384]{2,1,0:T(8,128)S(1)} %collective-permute-done.12.control.theirs, s32[128,384]{1,0:T(8,128)S(1)} %copy-done.8, s32[128,384]{1,0:T(8,128)S(1)} %copy-done.11, f32[8,128]{1,0:T(8,128)S(1)} %shard_map.95.earlier), custom_call_target="tpu_custom_call" | custom-call | flops 4194304 | bytes 8388608 | tf_op jit(solution)/shard_map/pallas_call | solution.py:519
  86.0 0.0 copy-start.6
  86.0 1.1 copy-done.6
  87.1 0.6 copy-done.15
  87.8 9.5 %all-to-all-start = ((f32[32,8,128]{2,1,0:T(8,128)}), f32[32,8,128]{2,1,0:T(8,128)S(1)}, u32[]{:S(2)}, u32[]{:S(2)}) async-start(f32[32,8,128]{2,1,0:T(8,128)} %copy-done.15), calls=%async_computation | async-start | bytes 262144 | tf_op jit(solution)/shard_map/all_to_all | solution.py:604
  97.3 10.8 %all-to-all-done.parts = f32[32,8,128]{2,1,0:T(8,128)S(1)} async-done(((f32[32,8,128]{2,1,0:T(8,128)}), f32[32,8,128]{2,1,0:T(8,128)S(1)}, u32[]{:S(2)}, u32[]{:S(2)}) %all-to-all-start) | async-done | bytes 131104 | tf_op jit(solution)/shard_map/all_to_all | solution.py:604
  108.1 1.4 %copy-done.4 = f32[16,64,384]{2,1,0:T(8,128)S(1)} copy-done((f32[16,64,384]{2,1,0:T(8,128)S(1)}, f32[16,64,384]{2,1,0:T(8,128)}, u32[]{:S(2)}) %copy-start.4) | copy-done | bytes 1572888
  109.5 1.4 %copy-done.7 = f32[16,64,384]{2,1,0:T(8,128)S(1)} copy-done((f32[16,64,384]{2,1,0:T(8,128)S(1)}, f32[16,64,384]{2,1,0:T(8,128)}, u32[]{:S(2)}) %copy-start.7) | copy-done | bytes 1572888
  110.9 4.4 %shard_map.97 = (f32[16,128,384]{2,1,0:T(8,128)}, f32[1,16]{1,0:T(1,128)}) custom-call(s32[3]{0:T(128)S(1)} %copy-done.21, f32[16,128,384]{2,1,0:T(8,128)S(1)} %copy-done, f32[16,64,384]{2,1,0:T(8,128)S(1)} %copy-done.4, f32[16,64,384]{2,1,0:T(8,128)S(1)} %copy-done.7, s32[128,384]{1,0:T(8,128)S(1)} %copy-done.11, f32[32,8,128]{2,1,0:T(8,128)S(1)} %all-to-all-done.parts, ...), custom_call_target="tpu_custom_call" | custom-call | flops 4194304 | bytes 10485760 | tf_op jit(solution)/shard_map/pallas_call | solution.py:575
  (44 shorter events, 0.1 us)
Async XLA Ops:
  2.1 24.3 %collective-permute-start.3 = (f32[16,72,384]{2,1,0:T(8,128)}, f32[16,72,384]{2,1,0:T(8,128)S(1)}, u32[]{:S(2)}, u32[]{:S(2)}) collective-permute-start(f32[16,72,384]{2,1,0:T(8,128)} %get-tuple-element.21.v), channel_id=1, source_target_pairs={{0,64},{1,65},{2,66},{3,67},{4,68},{5,69},{6,70},{7,71},{8,72},{9,... | collective-permute-start | bytes 5308424 | tf_op jit(solution)/shard_map/ppermute | solution.py:331
  2.9 23.6 %collective-permute-start.4 = (f32[16,72,384]{2,1,0:T(8,128)}, f32[16,72,384]{2,1,0:T(8,128)}, u32[]{:S(2)}, u32[]{:S(2)}) collective-permute-start(f32[16,72,384]{2,1,0:T(8,128)} %get-tuple-element.20.u), channel_id=1, source_target_pairs={{0,224},{1,225},{2,226},{3,227},{4,228},{5,229},{6,230},{7,231},{8... | collective-permute-start | bytes 5308424 | tf_op jit(solution)/shard_map/ppermute | solution.py:331
  7.2 7.0 %copy-start.20 = (s32[3]{0:T(128)S(1)}, s32[3]{0:T(128)}, u32[]{:S(2)}) copy-start(s32[3]{0:T(128)} %pad_add_fusion.lat.where) | copy-start | bytes 40
  7.2 6.9 %collective-permute-start = (f32[96,384]{1,0:T(8,128)}, f32[96,384]{1,0:T(8,128)S(1)}, u32[]{:S(2)}, u32[]{:S(2)}) collective-permute-start(f32[96,384]{1,0:T(8,128)} %shard_map.86), channel_id=1, source_target_pairs={{0,1},{1,0},{2,3},{3,2},{4,5},{5,4},{6,7},{7,6},{8,9},{9,8},{10,11... | collective-permute-start | bytes 442376 | tf_op jit(solution)/shard_map/ppermute | solution.py:129
  14.1 14.4 %copy-start.14 = (f32[96,384]{1,0:T(8,128)}, f32[96,384]{1,0:T(8,128)S(1)}, u32[]{:S(2)}) copy-start(f32[96,384]{1,0:T(8,128)S(1)} %collective-permute-done.rows) | copy-start | bytes 442372
  14.1 0.9 copy-start.18
  15.0 0.8 copy-start.19
  16.5 9.1 %collective-permute-start.1 = (f32[136,128]{1,0:T(8,128)S(1)}, f32[136,128]{1,0:T(8,128)S(1)}, u32[]{:S(2)}, u32[]{:S(2)}) collective-permute-start(f32[136,128]{1,0:T(8,128)S(1)} %get-tuple-element.18), channel_id=1, source_target_pairs={{0,2},{2,4},{4,6},{6,8},{8,10},{10,12},{12,14},{14,16},{16,18},{18... | collective-permute-start | bytes 208904 | tf_op jit(solution)/shard_map/ppermute | solution.py:142
  18.1 7.6 %collective-permute-start.2 = (f32[136,128]{1,0:T(8,128)S(1)}, f32[136,128]{1,0:T(8,128)S(1)}, u32[]{:S(2)}, u32[]{:S(2)}) collective-permute-start(f32[136,128]{1,0:T(8,128)S(1)} %get-tuple-element.19), channel_id=1, source_target_pairs={{2,0},{4,2},{6,4},{8,6},{10,8},{12,10},{14,12},{16,14},{18,16},{20... | collective-permute-start | bytes 208904 | tf_op jit(solution)/shard_map/ppermute | solution.py:142
  25.7 2.8 %copy-start.16 = (f32[136,128]{1,0:T(8,128)}, f32[136,128]{1,0:T(8,128)S(1)}, u32[]{:S(2)}) copy-start(f32[136,128]{1,0:T(8,128)S(1)} %collective-permute-done.1.fw) | copy-start | bytes 208900
  25.7 2.8 %copy-start.17 = (f32[136,128]{1,0:T(8,128)}, f32[136,128]{1,0:T(8,128)S(1)}, u32[]{:S(2)}) copy-start(f32[136,128]{1,0:T(8,128)S(1)} %collective-permute-done.2.fe) | copy-start | bytes 208900
  25.8 0.7 copy-start.12
  26.5 1.2 %copy-start.22 = (f32[16,72,384]{2,1,0:T(8,128)}, f32[16,72,384]{2,1,0:T(8,128)S(1)}, u32[]{:S(2)}) copy-start(f32[16,72,384]{2,1,0:T(8,128)S(1)} %collective-permute-done.3.p1) | copy-start | bytes 5308420
  28.5 41.6 %collective-permute-start.5 = (f32[16,72,384]{2,1,0:T(8,128)}, f32[16,72,384]{2,1,0:T(8,128)}, u32[]{:S(2)}, u32[]{:S(2)}) collective-permute-start(f32[16,72,384]{2,1,0:T(8,128)} %get-tuple-element.26.gate.refs_1_), channel_id=1, source_target_pairs={{0,96},{64,128},{1,97},{65,129},{2,98},{66,130},{3,99},{67,131},{4... | collective-permute-start | bytes 5308424 | tf_op jit(solution)/shard_map/ppermute | solution.py:331
  30.5 17.1 %copy-start.1 = (f32[16,72,384]{2,1,0:T(8,128)S(1)}, f32[16,72,384]{2,1,0:T(8,128)}, u32[]{:S(2)}) copy-start(f32[16,72,384]{2,1,0:T(8,128)} %get-tuple-element.26.gate.refs_1_) | copy-start | bytes 5308420
  30.5 18.0 %copy-start.13 = (f32[16,8,384]{2,1,0:T(8,128)S(1)}, f32[16,8,384]{2,1,0:T(8,128)}, u32[]{:S(2)}) copy-start(f32[16,8,384]{2,1,0:T(8,128)} %copy-done.12) | copy-start | bytes 589828
  30.5 33.1 %copy-start.21 = (s32[3]{0:T(128)S(1)}, s32[3]{0:T(128)}, u32[]{:S(2)}) copy-start(s32[3]{0:T(128)} %pad_add_fusion.lat.where) | copy-start | bytes 40
  30.5 39.7 %collective-permute-start.6 = (f32[16,72,384]{2,1,0:T(8,128)}, f32[16,72,384]{2,1,0:T(8,128)}, u32[]{:S(2)}, u32[]{:S(2)}) collective-permute-start(f32[16,72,384]{2,1,0:T(8,128)} %get-tuple-element.24.refs_0_), channel_id=1, source_target_pairs={{0,192},{224,160},{1,193},{225,161},{2,194},{226,162},{3,195},{227... | collective-permute-start | bytes 5308424 | tf_op jit(solution)/shard_map/ppermute | solution.py:331
  47.5 22.6 %copy-start.2 = (f32[16,72,384]{2,1,0:T(8,128)S(1)}, f32[16,72,384]{2,1,0:T(8,128)}, u32[]{:S(2)}) copy-start(f32[16,72,384]{2,1,0:T(8,128)} %get-tuple-element.26.gate.refs_1_) | copy-start | bytes 5308420
  47.5 22.6 %collective-permute-start.7 = (f32[16,72,384]{2,1,0:T(8,128)S(1)}, f32[16,72,384]{2,1,0:T(8,128)S(1)}, u32[]{:S(2)}, u32[]{:S(2)}) collective-permute-start(f32[16,72,384]{2,1,0:T(8,128)S(1)} %copy-done.1), channel_id=1, source_target_pairs={{0,32},{1,33},{2,34},{3,35},{4,36},{5,37},{6,38},{7,39},{8,40},{9,... | collective-permute-start | bytes 5308424 | tf_op jit(solution)/shard_map/ppermute | solution.py:331
  48.4 1.4 %collective-permute-start.8 = (f32[16,8,384]{2,1,0:T(8,128)S(1)}, f32[16,8,384]{2,1,0:T(8,128)S(1)}, u32[]{:S(2)}, u32[]{:S(2)}) collective-permute-start(f32[16,8,384]{2,1,0:T(8,128)S(1)} %copy-done.13), channel_id=1, source_target_pairs={{0,32},{1,33},{2,34},{3,35},{4,36},{5,37},{6,38},{7,39},{8,40},{9,... | collective-permute-start | bytes 589832 | tf_op jit(solution)/shard_map/ppermute | solution.py:331
  49.1 2.0 %collective-permute-start.9 = (f32[16,8,384]{2,1,0:T(8,128)S(1)}, f32[16,8,384]{2,1,0:T(8,128)S(1)}, u32[]{:S(2)}, u32[]{:S(2)}) collective-permute-start(f32[16,8,384]{2,1,0:T(8,128)S(1)} %copy-done.13), channel_id=1, source_target_pairs={{0,96},{1,97},{2,98},{3,99},{4,100},{5,101},{6,102},{7,103},{8,104... | collective-permute-start | bytes 589832 | tf_op jit(solution)/shard_map/ppermute | solution.py:331
  49.8 13.7 %collective-permute-start.10 = (f32[16,8,384]{2,1,0:T(8,128)S(1)}, f32[16,8,384]{2,1,0:T(8,128)S(1)}, u32[]{:S(2)}, u32[]{:S(2)}) collective-permute-start(f32[16,8,384]{2,1,0:T(8,128)S(1)} %copy-done.13), channel_id=1, source_target_pairs={{0,192},{1,193},{2,194},{3,195},{4,196},{5,197},{6,198},{7,199},{8... | collective-permute-start | bytes 589832 | tf_op jit(solution)/shard_map/ppermute | solution.py:331
  63.6 1.3 %copy-start.9 = (f32[8,72,512]{2,1,0:T(8,128)S(1)}, f32[8,72,512]{2,1,0:T(8,128)}, u32[]{:S(2)}) copy-start(f32[8,72,512]{2,1,0:T(8,128)} %get-tuple-element.27.gate.refs_7_) | copy-start | bytes 3538948
  64.8 16.4 %copy-start.8 = (s32[128,384]{1,0:T(8,128)S(1)}, s32[128,384]{1,0:T(8,128)}, u32[]{:S(2)}) copy-start(s32[128,384]{1,0:T(8,128)} %mask.9) | copy-start | bytes 589828
  64.8 16.4 %copy-start.11 = (s32[128,384]{1,0:T(8,128)S(1)}, s32[128,384]{1,0:T(8,128)}, u32[]{:S(2)}) copy-start(s32[128,384]{1,0:T(8,128)} %region.5) | copy-start | bytes 589828
  65.7 4.5 %collective-permute-start.11 = (f32[16,8,384]{2,1,0:T(8,128)S(1)}, f32[16,8,384]{2,1,0:T(8,128)S(1)}, u32[]{:S(2)}, u32[]{:S(2)}) collective-permute-start(f32[16,8,384]{2,1,0:T(8,128)S(1)} %shard_map.93.refs_5_), channel_id=1, source_target_pairs={{0,64},{32,224},{96,128},{192,160},{1,65},{33,225},{97,129},{193,1... | collective-permute-start | bytes 589832 | tf_op jit(solution)/shard_map/ppermute | solution.py:331
  70.2 1.5 %copy-start.5 = (f32[16,72,384]{2,1,0:T(8,128)S(1)}, f32[16,72,384]{2,1,0:T(8,128)}, u32[]{:S(2)}) copy-start(f32[16,72,384]{2,1,0:T(8,128)} %get-tuple-element.24.refs_0_) | copy-start | bytes 5308420
  71.6 1.3 %copy-start.10 = (f32[8,72,512]{2,1,0:T(8,128)S(1)}, f32[8,72,512]{2,1,0:T(8,128)}, u32[]{:S(2)}) copy-start(f32[8,72,512]{2,1,0:T(8,128)} %get-tuple-element.27.gate.refs_7_) | copy-start | bytes 3538948
  72.9 8.4 %copy-start = (f32[16,128,384]{2,1,0:T(8,128)S(1)}, f32[16,128,384]{2,1,0:T(8,128)}, u32[]{:S(2)}) copy-start(f32[16,128,384]{2,1,0:T(8,128)} %get-tuple-element.23.own) | copy-start | bytes 9437188
  81.1 1.3 %copy-start.3 = (f32[16,64,384]{2,1,0:T(8,128)}, f32[16,64,384]{2,1,0:T(8,128)S(1)}, u32[]{:S(2)}) copy-start(f32[16,64,384]{2,1,0:T(8,128)S(1)} %shard_map.94.control.mine) | copy-start | bytes 4718596
  81.1 3.5 %collective-permute-start.12 = (f32[16,64,384]{2,1,0:T(8,128)S(1)}, f32[16,64,384]{2,1,0:T(8,128)S(1)}, u32[]{:S(2)}, u32[]{:S(2)}) collective-permute-start(f32[16,64,384]{2,1,0:T(8,128)S(1)} %shard_map.94.control.mine), channel_id=1, source_target_pairs={{0,32},{32,0},{64,96},{96,64},{128,160},{160,128},{192,224},{224,1... | collective-permute-start | bytes 4718600 | tf_op jit(solution)/shard_map/ppermute | solution.py:331
  82.5 14.8 %copy-start.23 = (f32[16]{0:T(128)S(1)}, f32[16]{0:T(128)}, u32[]{:S(2)}) copy-start(f32[16]{0:T(128)} %param.13) | copy-start | bytes 196
  86.0 1.1 copy-start.6
  87.1 0.6 copy-start.15
  87.8 20.3 %all-to-all-start = ((f32[32,8,128]{2,1,0:T(8,128)}), f32[32,8,128]{2,1,0:T(8,128)S(1)}, u32[]{:S(2)}, u32[]{:S(2)}) async-start(f32[32,8,128]{2,1,0:T(8,128)} %copy-done.15), calls=%async_computation | async-start | bytes 262144 | tf_op jit(solution)/shard_map/all_to_all | solution.py:604
  108.1 1.4 %copy-start.4 = (f32[16,64,384]{2,1,0:T(8,128)S(1)}, f32[16,64,384]{2,1,0:T(8,128)}, u32[]{:S(2)}) copy-start(f32[16,64,384]{2,1,0:T(8,128)} %copy-done.3) | copy-start | bytes 4718596
  109.5 1.4 %copy-start.7 = (f32[16,64,384]{2,1,0:T(8,128)S(1)}, f32[16,64,384]{2,1,0:T(8,128)}, u32[]{:S(2)}) copy-start(f32[16,64,384]{2,1,0:T(8,128)} %copy-done.6) | copy-start | bytes 4718596

commit v8 on v7

--- a/solution.py
+++ b/solution.py
@@ -374,19 +374,10 @@
 
     @pl.when(where[2] == 7)
     def _():
-        staged([(m1, v_out)], buffer, sem)
-
-
-def spread_rest(where, u, v, p1, m1, halo):
-    u, v = call(
-        relay_kernel, [u, v], [SMEM] + [HBM] * 4 + [ANY], [HBM] * 2, STAGE, mib=58, aliases={1: 0, 2: 1}
-    )(where, u, v, p1, m1, halo)
-    p2 = send(u, [(0, 3), (2, 4)])
-    m2 = send(v, [(0, 6), (7, 5)])
-    return (v, u, p2, m2), (halo, send(halo, [(0, 1)]), send(halo, [(0, 3)]), send(halo, [(0, 6)]))
-
-
-def known_kernel(where, own, one, three, six, gate, out, sem):
+        staged([(m1, v_out), (m1, u_out)], buffer, sem)
+
+
+def known_kernel(where, own, one, three, six, out, sem):
     for member, ref in ((0, own), (1, one), (3, three), (6, six)):
 
         @pl.when(where[2] == member)
@@ -396,24 +387,30 @@
             copy.wait()
 
 
-def spread_halo_rest(where, halos, gate):
+def spread_rest(where, u, v, p1, m1, halo):
+    came = [send(halo, [(0, member)]) for member in (1, 3, 6)]
     known = call(
         known_kernel,
         jax.ShapeDtypeStruct((CH, 8, COLS), F32),
-        [SMEM] + [ANY] * 5,
+        [SMEM] + [ANY] * 4,
         VMEM,
         [pltpu.SemaphoreType.DMA((1,))],
         mib=8,
-    )(where, *halos, gate)
-    return known, send(known, [(0, 2), (1, 7), (3, 4), (6, 5)])
-
-
-HOLDER = ((0, 7), (2,), (3, 4), (5, 6), (1,))
+    )(where, halo, *came)
+    u, v = call(
+        relay_kernel, [u, v], [SMEM] + [HBM] * 4 + [ANY], [HBM] * 2, STAGE, mib=58, aliases={1: 0, 2: 1}
+    )(where, u, v, p1, m1, known)
+    p2 = send(u, [(0, 3), (2, 4), (7, 1)])
+    m2 = send(v, [(0, 6), (7, 5)])
+    return (v, u, p2, m2), (known, send(known, [(0, 2), (1, 7), (3, 4), (6, 5)]))
+
+
+HOLDER = ((0, 7), (2,), (1, 3, 4), (5, 6))
 HALO_HOLDER = (0, 0, 1, 0, 1, 1, 0, 1)
 
 
 def control_kernel(where, *refs):
-    arrays, halos, (static, out, x, y, ub, vb, h2, near, halo, strip, sem) = refs[:5], refs[5:7], refs[7:]
+    arrays, halos, (static, out, x, y, ub, vb, h2, near, halo, strip, sem) = refs[:4], refs[4:6], refs[6:]
     first = where[1] == 0
     m = where[2]
     for array, members in zip(arrays, HOLDER):
@@ -462,7 +459,7 @@
     return call(
         control_kernel,
         jax.ShapeDtypeStruct((CH, HALF, COLS), F32),
-        [SMEM] + [HBM] * 5 + [ANY] * 2 + [VMEM],
+        [SMEM] + [HBM] * 4 + [ANY] * 2 + [VMEM],
         VMEM,
         [pltpu.VMEM((CH, HALF_X, COLS_X), F32)]
         + step_scratch(HALF_X)
@@ -594,9 +591,6 @@
     halo = call(control_halo_kernel, jax.ShapeDtypeStruct((CH, 8, COLS), F32), [VMEM] * 3, VMEM)(*halos)
     arrays, control_halos = spread_rest(where, *first, halo)
     own, static = own_steps(where, state, statics, halos, arrays[1])
-    control_halos = spread_halo_rest(where, control_halos, static)
-    late, static = lax.optimization_barrier((arrays[1], static))
-    arrays += (send(late, [(0, 1)]),)
     mine = control_steps(where, arrays, control_halos, static)
     theirs = send(mine, [(i, i ^ 1) for i in range(8)])
     parts = half_sums(False, where, own, mine, mask, region, jnp.zeros((8, 128), F32))

time: 117 us -> 118 us (level); the launches traced: 115 us -> 117 us
  local copies, waits for them, and re-layouts: 12.3 us -> 16.8 us
    unnamed x48 -> x50, local copies, waits for them, and re-layouts: 12.3 us -> 16.7 us
    pallas_call x1, Pallas kernels: 8.22 us -> 7.01 us  [control_steps(): call(control_kernel, jax.ShapeDtypeStruct((CH, HALF, COLS), F32), [SMEM]...]
    ppermute x10 -> x9, starting transfers between devices: 10.9 us -> 9.91 us  [send(): return lax.ppermute(value, 'member', pairs)]
    ppermute x10 -> x9, waiting for transfers between devices: 17.7 us -> 17.7 us  [send(): return lax.ppermute(value, 'member', pairs)]
  transfers between devices with their start and end apart: 14 -> 13, of which waited for: 6 -> 6; matrix products, arithmetic and copies ran while one was open for 0% -> 0% of each run, Pallas kernels for 21% -> 21%
where the time goes in v8:
time: 118 us; the launch traced here: 117 us
  Pallas kernels  38.7 us (33%)
  waiting for transfers between devices  31 us (26%)
  starting transfers between devices  29.5 us (25%)
  local copies, waits for them, and re-layouts  16.8 us (14%)
    ppermute x9, waiting for transfers between devices, send(): return lax.ppermute(value, 'member', pairs)  17.7 us
    unnamed x50, local copies, waits for them, and re-layouts  16.7 us
    pallas_call x1, Pallas kernels, own_steps(): call(own_kernel, [jax.ShapeDtypeStruct((CH, ROWS, COLS), F32), jax.ShapeD...  15.5 us
    all_to_all x1, waiting for transfers between devices, per_device(): parts = lax.all_to_all(parts, ('lon', 'lat'), 0, 0)  10.8 us
    ppermute x9, starting transfers between devices, send(): return lax.ppermute(value, 'member', pairs)  9.91 us
    all_to_all x1, starting transfers between devices, per_device(): parts = lax.all_to_all(parts, ('lon', 'lat'), 0, 0)  9.48 us
    pallas_call x1, Pallas kernels, control_steps(): call(control_kernel, jax.ShapeDtypeStruct((CH, HALF, COLS), F32), [SMEM]...  7.01 us
    ppermute x1, starting transfers between devices, exchange(): lax.ppermute(west, 'lon', down)  5.38 us
  transfers between devices with their start and end apart: 13, of which 6 were waited for; matrix products, arithmetic and copies ran while one was open for 0% of the time, Pallas kernels for 21%

profile of v8, /device:TPU:24, one launch (start us, length us, event | category | flops | bytes accessed | tf_op | source)
XLA Modules:
  0.0 117.4 jit_solution(12666076967892390857)
XLA Ops:
  0.6 0.6 pad_add_fusion.lat.where
  1.2 0.8 shard_map.89
  2.1 1.9 %collective-permute-start.3 = (f32[16,72,384]{2,1,0:T(8,128)}, f32[16,72,384]{2,1,0:T(8,128)}, u32[]{:S(2)}, u32[]{:S(2)}) collective-permute-start(f32[16,72,384]{2,1,0:T(8,128)} %get-tuple-element.19.v), channel_id=1, source_target_pairs={{0,64},{1,65},{2,66},{3,67},{4,68},{5,69},{6,70},{7,71},{8,72},{9,... | collective-permute-start | bytes 5308424 | tf_op jit(solution)/shard_map/ppermute | solution.py:331
  4.0 1.9 %collective-permute-start.4 = (f32[16,72,384]{2,1,0:T(8,128)}, f32[16,72,384]{2,1,0:T(8,128)}, u32[]{:S(2)}, u32[]{:S(2)}) collective-permute-start(f32[16,72,384]{2,1,0:T(8,128)} %get-tuple-element.18.u), channel_id=1, source_target_pairs={{0,224},{1,225},{2,226},{3,227},{4,228},{5,229},{6,230},{7,231},{8... | collective-permute-start | bytes 5308424 | tf_op jit(solution)/shard_map/ppermute | solution.py:331
  5.9 2.4 %shard_map.86 = f32[96,384]{1,0:T(8,128)} custom-call(s32[3]{0:T(128)} %pad_add_fusion.lat.where, f32[16,128,384]{2,1,0:T(8,128)} %bitcast.6, f32[128,384]{1,0:T(8,128)} %depth.5, f32[128,384]{1,0:T(8,128)} %rotation.5, f32[5,128,384]{2,1,0:T(8,128)} %diff.5, s32[128,384]{1,0:T(8,128)} %mask.9), custom_call_target="tpu_custom_call" | custom-call | flops 4194304 | bytes 8388608 | tf_op jit(solution)/shard_map/pallas_call | solution.py:121
  8.3 3.1 %collective-permute-start = (f32[96,384]{1,0:T(8,128)}, f32[96,384]{1,0:T(8,128)S(1)}, u32[]{:S(2)}, u32[]{:S(2)}) collective-permute-start(f32[96,384]{1,0:T(8,128)} %shard_map.86), channel_id=1, source_target_pairs={{0,1},{1,0},{2,3},{3,2},{4,5},{5,4},{6,7},{7,6},{8,9},{9,8},{10,11... | collective-permute-start | bytes 442376 | tf_op jit(solution)/shard_map/ppermute | solution.py:129
  11.4 3.5 %shard_map.87 = (f32[128,128]{1,0:T(8,128)}, f32[128,128]{1,0:T(8,128)}) custom-call(f32[16,128,384]{2,1,0:T(8,128)} %bitcast.7, f32[128,384]{1,0:T(8,128)} %depth.5, f32[128,384]{1,0:T(8,128)} %rotation.5, f32[5,128,384]{2,1,0:T(8,128)} %diff.5, s32[128,384]{1,0:T(8,128)} %mask.9), custom_call_target="tpu_custom_call" | custom-call | flops 4194304 | bytes 8388608 | tf_op jit(solution)/shard_map/pallas_call | solution.py:131
  14.9 0.3 collective-permute-done.rows
  15.2 0.9 copy-done.20
  16.1 0.8 copy-done.21
  17.0 0.7 shard_map.88
  17.6 1.6 %collective-permute-start.1 = (f32[136,128]{1,0:T(8,128)S(1)}, f32[136,128]{1,0:T(8,128)S(1)}, u32[]{:S(2)}, u32[]{:S(2)}) collective-permute-start(f32[136,128]{1,0:T(8,128)S(1)} %get-tuple-element.16), channel_id=1, source_target_pairs={{0,2},{2,4},{4,6},{6,8},{8,10},{10,12},{12,14},{14,16},{16,18},{18... | collective-permute-start | bytes 208904 | tf_op jit(solution)/shard_map/ppermute | solution.py:142
  19.2 5.4 %collective-permute-start.2 = (f32[136,128]{1,0:T(8,128)S(1)}, f32[136,128]{1,0:T(8,128)S(1)}, u32[]{:S(2)}, u32[]{:S(2)}) collective-permute-start(f32[136,128]{1,0:T(8,128)S(1)} %get-tuple-element.17), channel_id=1, source_target_pairs={{2,0},{4,2},{6,4},{8,6},{10,8},{12,10},{14,12},{16,14},{18,16},{20... | collective-permute-start | bytes 208904 | tf_op jit(solution)/shard_map/ppermute | solution.py:142
  24.6 2.2 %collective-permute-done.1.fw = f32[136,128]{1,0:T(8,128)S(1)} collective-permute-done((f32[136,128]{1,0:T(8,128)S(1)}, f32[136,128]{1,0:T(8,128)S(1)}, u32[]{:S(2)}, u32[]{:S(2)}) %collective-permute-start.1) | collective-permute-done | bytes 69664 | tf_op jit(solution)/shard_map/ppermute | solution.py:142
  26.8 0.1 shard_map.90.own
  26.9 0.7 collective-permute-start.5
  27.5 0.7 collective-permute-start.6
  28.2 1.3 %collective-permute-start.7 = (f32[16,8,384]{2,1,0:T(8,128)S(1)}, f32[16,8,384]{2,1,0:T(8,128)S(1)}, u32[]{:S(2)}, u32[]{:S(2)}) collective-permute-start(f32[16,8,384]{2,1,0:T(8,128)S(1)} %shard_map.90.own), channel_id=1, source_target_pairs={{0,192},{1,193},{2,194},{3,195},{4,196},{5,197},{6,198},{7,199},{8... | collective-permute-start | bytes 589832 | tf_op jit(solution)/shard_map/ppermute | solution.py:331
  29.5 9.1 %collective-permute-done.7.six = f32[16,8,384]{2,1,0:T(8,128)S(1)} collective-permute-done((f32[16,8,384]{2,1,0:T(8,128)S(1)}, f32[16,8,384]{2,1,0:T(8,128)S(1)}, u32[]{:S(2)}, u32[]{:S(2)}) %collective-permute-start.7) | collective-permute-done | bytes 196640 | tf_op jit(solution)/shard_map/ppermute | solution.py:331
  38.6 0.8 shard_map.91.gate.refs_4_
  39.5 0.0 copy-start.13
  39.5 0.7 copy-done.13
  40.2 1.0 shard_map.92
  41.2 0.8 collective-permute-start.8
  42.0 1.3 %collective-permute-start.9 = (f32[16,72,384]{2,1,0:T(8,128)}, f32[16,72,384]{2,1,0:T(8,128)S(1)}, u32[]{:S(2)}, u32[]{:S(2)}) collective-permute-start(f32[16,72,384]{2,1,0:T(8,128)} %get-tuple-element.22.refs_0_), channel_id=1, source_target_pairs={{0,192},{224,160},{1,193},{225,161},{2,194},{226,162},{3,195},{227... | collective-permute-start | bytes 5308424 | tf_op jit(solution)/shard_map/ppermute | solution.py:331
  43.3 1.3 %collective-permute-start.10 = (f32[16,8,384]{2,1,0:T(8,128)S(1)}, f32[16,8,384]{2,1,0:T(8,128)S(1)}, u32[]{:S(2)}, u32[]{:S(2)}) collective-permute-start(f32[16,8,384]{2,1,0:T(8,128)S(1)} %copy-done.14), channel_id=1, source_target_pairs={{0,64},{32,224},{96,128},{192,160},{1,65},{33,225},{97,129},{193,1... | collective-permute-start | bytes 589832 | tf_op jit(solution)/shard_map/ppermute | solution.py:331
  44.6 15.5 %shard_map.93 = (f32[16,128,384]{2,1,0:T(8,128)}, f32[8,72,512]{2,1,0:T(8,128)}) custom-call(s32[3]{0:T(128)} %pad_add_fusion.lat.where, f32[16,128,384]{2,1,0:T(8,128)} %bitcast.8, f32[128,384]{1,0:T(8,128)} %depth.5, f32[128,384]{1,0:T(8,128)} %rotation.5, f32[5,128,384]{2,1,0:T(8,128)} %diff.5, s32[128,384]{1,0:T(8,128)} %mask.9, f32[136,128]{1,0:T(8,128)} %copy-done.18, ...), custom_call_target="tpu_custom_call" | custom-call | flops 268435456 | bytes 8388608 | tf_op jit(solution)/shard_map/pallas_call | solution.py:301
  60.1 1.2 %copy-done.9 = f32[16,72,384]{2,1,0:T(8,128)} copy-done((f32[16,72,384]{2,1,0:T(8,128)}, f32[16,72,384]{2,1,0:T(8,128)S(1)}, u32[]{:S(2)}) %copy-start.9) | copy-done | bytes 1769496
  61.4 6.4 %collective-permute-done.9.refs_3_ = f32[16,72,384]{2,1,0:T(8,128)S(1)} collective-permute-done((f32[16,72,384]{2,1,0:T(8,128)}, f32[16,72,384]{2,1,0:T(8,128)S(1)}, u32[]{:S(2)}, u32[]{:S(2)}) %collective-permute-start.9) | collective-permute-done | bytes 1769504 | tf_op jit(solution)/shard_map/ppermute | solution.py:331
  67.8 1.3 %copy-done.11 = f32[16,72,384]{2,1,0:T(8,128)} copy-done((f32[16,72,384]{2,1,0:T(8,128)}, f32[16,72,384]{2,1,0:T(8,128)S(1)}, u32[]{:S(2)}) %copy-start.11) | copy-done | bytes 1769496
  69.1 1.5 %copy-done.1 = f32[16,72,384]{2,1,0:T(8,128)S(1)} copy-done((f32[16,72,384]{2,1,0:T(8,128)S(1)}, f32[16,72,384]{2,1,0:T(8,128)}, u32[]{:S(2)}) %copy-start.1) | copy-done | bytes 1769496
  70.6 1.5 %copy-done.4 = f32[16,72,384]{2,1,0:T(8,128)S(1)} copy-done((f32[16,72,384]{2,1,0:T(8,128)S(1)}, f32[16,72,384]{2,1,0:T(8,128)}, u32[]{:S(2)}) %copy-start.4) | copy-done | bytes 1769496
  72.1 1.5 %copy-done.10 = f32[16,72,384]{2,1,0:T(8,128)S(1)} copy-done((f32[16,72,384]{2,1,0:T(8,128)S(1)}, f32[16,72,384]{2,1,0:T(8,128)}, u32[]{:S(2)}) %copy-start.10) | copy-done | bytes 1769496
  73.6 1.5 %copy-done.12 = f32[16,72,384]{2,1,0:T(8,128)S(1)} copy-done((f32[16,72,384]{2,1,0:T(8,128)S(1)}, f32[16,72,384]{2,1,0:T(8,128)}, u32[]{:S(2)}) %copy-start.12) | copy-done | bytes 1769496
  75.0 1.3 %copy-done.16 = f32[8,72,512]{2,1,0:T(8,128)S(1)} copy-done((f32[8,72,512]{2,1,0:T(8,128)S(1)}, f32[8,72,512]{2,1,0:T(8,128)}, u32[]{:S(2)}) %copy-start.16) | copy-done | bytes 1179672
  76.3 7.0 %shard_map.94.control.mine = f32[16,64,384]{2,1,0:T(8,128)S(1)} custom-call(s32[3]{0:T(128)S(1)} %copy-done.23, f32[16,72,384]{2,1,0:T(8,128)S(1)} %copy-done.4, f32[16,72,384]{2,1,0:T(8,128)S(1)} %copy-done.1, f32[16,72,384]{2,1,0:T(8,128)S(1)} %copy-done.10, f32[16,72,384]{2,1,0:T(8,128)S(1)} %copy-done.12, f32[16,8,384]{2,1,0:T(8,128)S(1)} %copy-done.14, ...), custom_call_target="tpu_custom_call" | custom-call | flops 134217728 | bytes 8388608 | tf_op jit(solution)/shard_map/pallas_call | solution.py:459
  83.3 0.1 collective-permute-start.11
  83.5 1.2 shard_map.95.earlier
  84.7 0.0 copy-start.24
  84.7 2.2 %collective-permute-done.11.control.theirs = f32[16,64,384]{2,1,0:T(8,128)S(1)} collective-permute-done((f32[16,64,384]{2,1,0:T(8,128)S(1)}, f32[16,64,384]{2,1,0:T(8,128)S(1)}, u32[]{:S(2)}, u32[]{:S(2)}) %collective-permute-start.11) | collective-permute-done | bytes 1572896 | tf_op jit(solution)/shard_map/ppermute | solution.py:331
  86.8 1.4 %shard_map.96 = f32[32,8,128]{2,1,0:T(8,128)S(1)} custom-call(s32[3]{0:T(128)S(1)} %copy-done.23, f32[16,128,384]{2,1,0:T(8,128)S(1)} %copy-done, f32[16,64,384]{2,1,0:T(8,128)S(1)} %collective-permute-done.11.control.theirs, s32[128,384]{1,0:T(8,128)S(1)} %copy-done.7, s32[128,384]{1,0:T(8,128)S(1)} %copy-done.8, f32[8,128]{1,0:T(8,128)S(1)} %shard_map.95.earlier), custom_call_target="tpu_custom_call" | custom-call | flops 4194304 | bytes 8388608 | tf_op jit(solution)/shard_map/pallas_call | solution.py:516
  88.2 1.1 copy-done.5
  89.3 0.6 copy-done.17
  90.0 9.5 %all-to-all-start = ((f32[32,8,128]{2,1,0:T(8,128)}), f32[32,8,128]{2,1,0:T(8,128)S(1)}, u32[]{:S(2)}, u32[]{:S(2)}) async-start(f32[32,8,128]{2,1,0:T(8,128)} %copy-done.17), calls=%async_computation | async-start | bytes 262144 | tf_op jit(solution)/shard_map/all_to_all | solution.py:598
  99.5 10.8 %all-to-all-done.parts = f32[32,8,128]{2,1,0:T(8,128)S(1)} async-done(((f32[32,8,128]{2,1,0:T(8,128)}), f32[32,8,128]{2,1,0:T(8,128)S(1)}, u32[]{:S(2)}, u32[]{:S(2)}) %all-to-all-start) | async-done | bytes 131104 | tf_op jit(solution)/shard_map/all_to_all | solution.py:598
  110.3 1.4 %copy-done.3 = f32[16,64,384]{2,1,0:T(8,128)S(1)} copy-done((f32[16,64,384]{2,1,0:T(8,128)S(1)}, f32[16,64,384]{2,1,0:T(8,128)}, u32[]{:S(2)}) %copy-start.3) | copy-done | bytes 1572888
  111.7 1.4 %copy-done.6 = f32[16,64,384]{2,1,0:T(8,128)S(1)} copy-done((f32[16,64,384]{2,1,0:T(8,128)S(1)}, f32[16,64,384]{2,1,0:T(8,128)}, u32[]{:S(2)}) %copy-start.6) | copy-done | bytes 1572888
  113.1 4.4 %shard_map.97 = (f32[16,128,384]{2,1,0:T(8,128)}, f32[1,16]{1,0:T(1,128)}) custom-call(s32[3]{0:T(128)S(1)} %copy-done.23, f32[16,128,384]{2,1,0:T(8,128)S(1)} %copy-done, f32[16,64,384]{2,1,0:T(8,128)S(1)} %copy-done.3, f32[16,64,384]{2,1,0:T(8,128)S(1)} %copy-done.6, s32[128,384]{1,0:T(8,128)S(1)} %copy-done.8, f32[32,8,128]{2,1,0:T(8,128)S(1)} %all-to-all-done.parts, ...), custom_call_target="tpu_custom_call" | custom-call | flops 4194304 | bytes 10485760 | tf_op jit(solution)/shard_map/pallas_call | solution.py:572
  (44 shorter events, 0.1 us)
Async XLA Ops:
  2.1 38.1 %collective-permute-start.3 = (f32[16,72,384]{2,1,0:T(8,128)}, f32[16,72,384]{2,1,0:T(8,128)}, u32[]{:S(2)}, u32[]{:S(2)}) collective-permute-start(f32[16,72,384]{2,1,0:T(8,128)} %get-tuple-element.19.v), channel_id=1, source_target_pairs={{0,64},{1,65},{2,66},{3,67},{4,68},{5,69},{6,70},{7,71},{8,72},{9,... | collective-permute-start | bytes 5308424 | tf_op jit(solution)/shard_map/ppermute | solution.py:331
  4.0 36.2 %collective-permute-start.4 = (f32[16,72,384]{2,1,0:T(8,128)}, f32[16,72,384]{2,1,0:T(8,128)}, u32[]{:S(2)}, u32[]{:S(2)}) collective-permute-start(f32[16,72,384]{2,1,0:T(8,128)} %get-tuple-element.18.u), channel_id=1, source_target_pairs={{0,224},{1,225},{2,226},{3,227},{4,228},{5,229},{6,230},{7,231},{8... | collective-permute-start | bytes 5308424 | tf_op jit(solution)/shard_map/ppermute | solution.py:331
  8.3 7.0 %copy-start.22 = (s32[3]{0:T(128)S(1)}, s32[3]{0:T(128)}, u32[]{:S(2)}) copy-start(s32[3]{0:T(128)} %pad_add_fusion.lat.where) | copy-start | bytes 40
  8.3 6.9 %collective-permute-start = (f32[96,384]{1,0:T(8,128)}, f32[96,384]{1,0:T(8,128)S(1)}, u32[]{:S(2)}, u32[]{:S(2)}) collective-permute-start(f32[96,384]{1,0:T(8,128)} %shard_map.86), channel_id=1, source_target_pairs={{0,1},{1,0},{2,3},{3,2},{4,5},{5,4},{6,7},{7,6},{8,9},{9,8},{10,11... | collective-permute-start | bytes 442376 | tf_op jit(solution)/shard_map/ppermute | solution.py:129
  15.2 25.9 %copy-start.15 = (f32[96,384]{1,0:T(8,128)}, f32[96,384]{1,0:T(8,128)S(1)}, u32[]{:S(2)}) copy-start(f32[96,384]{1,0:T(8,128)S(1)} %collective-permute-done.rows) | copy-start | bytes 442372
  15.2 0.9 copy-start.20
  16.1 0.8 copy-start.21
  17.6 9.1 %collective-permute-start.1 = (f32[136,128]{1,0:T(8,128)S(1)}, f32[136,128]{1,0:T(8,128)S(1)}, u32[]{:S(2)}, u32[]{:S(2)}) collective-permute-start(f32[136,128]{1,0:T(8,128)S(1)} %get-tuple-element.16), channel_id=1, source_target_pairs={{0,2},{2,4},{4,6},{6,8},{8,10},{10,12},{12,14},{14,16},{16,18},{18... | collective-permute-start | bytes 208904 | tf_op jit(solution)/shard_map/ppermute | solution.py:142
  19.2 7.6 %collective-permute-start.2 = (f32[136,128]{1,0:T(8,128)S(1)}, f32[136,128]{1,0:T(8,128)S(1)}, u32[]{:S(2)}, u32[]{:S(2)}) collective-permute-start(f32[136,128]{1,0:T(8,128)S(1)} %get-tuple-element.17), channel_id=1, source_target_pairs={{2,0},{4,2},{6,4},{8,6},{10,8},{12,10},{14,12},{16,14},{18,16},{20... | collective-permute-start | bytes 208904 | tf_op jit(solution)/shard_map/ppermute | solution.py:142
  26.8 14.4 %copy-start.18 = (f32[136,128]{1,0:T(8,128)}, f32[136,128]{1,0:T(8,128)S(1)}, u32[]{:S(2)}) copy-start(f32[136,128]{1,0:T(8,128)S(1)} %collective-permute-done.1.fw) | copy-start | bytes 208900
  26.8 14.4 %copy-start.19 = (f32[136,128]{1,0:T(8,128)}, f32[136,128]{1,0:T(8,128)S(1)}, u32[]{:S(2)}) copy-start(f32[136,128]{1,0:T(8,128)S(1)} %collective-permute-done.2.fe) | copy-start | bytes 208900
  26.9 2.7 %collective-permute-start.5 = (f32[16,8,384]{2,1,0:T(8,128)S(1)}, f32[16,8,384]{2,1,0:T(8,128)S(1)}, u32[]{:S(2)}, u32[]{:S(2)}) collective-permute-start(f32[16,8,384]{2,1,0:T(8,128)S(1)} %shard_map.90.own), channel_id=1, source_target_pairs={{0,32},{1,33},{2,34},{3,35},{4,36},{5,37},{6,38},{7,39},{8,40},{9,... | collective-permute-start | bytes 589832 | tf_op jit(solution)/shard_map/ppermute | solution.py:331
  27.5 2.0 %collective-permute-start.6 = (f32[16,8,384]{2,1,0:T(8,128)S(1)}, f32[16,8,384]{2,1,0:T(8,128)S(1)}, u32[]{:S(2)}, u32[]{:S(2)}) collective-permute-start(f32[16,8,384]{2,1,0:T(8,128)S(1)} %shard_map.90.own), channel_id=1, source_target_pairs={{0,96},{1,97},{2,98},{3,99},{4,100},{5,101},{6,102},{7,103},{8,104... | collective-permute-start | bytes 589832 | tf_op jit(solution)/shard_map/ppermute | solution.py:331
  28.2 10.4 %collective-permute-start.7 = (f32[16,8,384]{2,1,0:T(8,128)S(1)}, f32[16,8,384]{2,1,0:T(8,128)S(1)}, u32[]{:S(2)}, u32[]{:S(2)}) collective-permute-start(f32[16,8,384]{2,1,0:T(8,128)S(1)} %shard_map.90.own), channel_id=1, source_target_pairs={{0,192},{1,193},{2,194},{3,195},{4,196},{5,197},{6,198},{7,199},{8... | collective-permute-start | bytes 589832 | tf_op jit(solution)/shard_map/ppermute | solution.py:331
  39.5 0.7 copy-start.13
  40.2 3.1 %copy-start.14 = (f32[16,8,384]{2,1,0:T(8,128)S(1)}, f32[16,8,384]{2,1,0:T(8,128)}, u32[]{:S(2)}) copy-start(f32[16,8,384]{2,1,0:T(8,128)} %copy-done.13) | copy-start | bytes 589828
  41.2 18.9 %collective-permute-start.8 = (f32[16,72,384]{2,1,0:T(8,128)}, f32[16,72,384]{2,1,0:T(8,128)S(1)}, u32[]{:S(2)}, u32[]{:S(2)}) collective-permute-start(f32[16,72,384]{2,1,0:T(8,128)} %get-tuple-element.20.gate.refs_1_), channel_id=1, source_target_pairs={{0,96},{64,128},{224,32},{1,97},{65,129},{225,33},{2,98},{66,130},... | collective-permute-start | bytes 5308424 | tf_op jit(solution)/shard_map/ppermute | solution.py:331
  42.0 27.2 %copy-start.23 = (s32[3]{0:T(128)S(1)}, s32[3]{0:T(128)}, u32[]{:S(2)}) copy-start(s32[3]{0:T(128)} %pad_add_fusion.lat.where) | copy-start | bytes 40
  42.0 25.8 %collective-permute-start.9 = (f32[16,72,384]{2,1,0:T(8,128)}, f32[16,72,384]{2,1,0:T(8,128)S(1)}, u32[]{:S(2)}, u32[]{:S(2)}) collective-permute-start(f32[16,72,384]{2,1,0:T(8,128)} %get-tuple-element.22.refs_0_), channel_id=1, source_target_pairs={{0,192},{224,160},{1,193},{225,161},{2,194},{226,162},{3,195},{227... | collective-permute-start | bytes 5308424 | tf_op jit(solution)/shard_map/ppermute | solution.py:331
  43.3 16.8 %collective-permute-start.10 = (f32[16,8,384]{2,1,0:T(8,128)S(1)}, f32[16,8,384]{2,1,0:T(8,128)S(1)}, u32[]{:S(2)}, u32[]{:S(2)}) collective-permute-start(f32[16,8,384]{2,1,0:T(8,128)S(1)} %copy-done.14), channel_id=1, source_target_pairs={{0,64},{32,224},{96,128},{192,160},{1,65},{33,225},{97,129},{193,1... | collective-permute-start | bytes 589832 | tf_op jit(solution)/shard_map/ppermute | solution.py:331
  60.1 1.2 %copy-start.9 = (f32[16,72,384]{2,1,0:T(8,128)}, f32[16,72,384]{2,1,0:T(8,128)S(1)}, u32[]{:S(2)}) copy-start(f32[16,72,384]{2,1,0:T(8,128)S(1)} %collective-permute-done.8.refs_2_) | copy-start | bytes 5308420
  67.8 1.3 %copy-start.11 = (f32[16,72,384]{2,1,0:T(8,128)}, f32[16,72,384]{2,1,0:T(8,128)S(1)}, u32[]{:S(2)}) copy-start(f32[16,72,384]{2,1,0:T(8,128)S(1)} %collective-permute-done.9.refs_3_) | copy-start | bytes 5308420
  69.1 1.5 %copy-start.1 = (f32[16,72,384]{2,1,0:T(8,128)S(1)}, f32[16,72,384]{2,1,0:T(8,128)}, u32[]{:S(2)}) copy-start(f32[16,72,384]{2,1,0:T(8,128)} %get-tuple-element.20.gate.refs_1_) | copy-start | bytes 5308420
  70.6 1.5 %copy-start.4 = (f32[16,72,384]{2,1,0:T(8,128)S(1)}, f32[16,72,384]{2,1,0:T(8,128)}, u32[]{:S(2)}) copy-start(f32[16,72,384]{2,1,0:T(8,128)} %get-tuple-element.22.refs_0_) | copy-start | bytes 5308420
  72.1 1.5 %copy-start.10 = (f32[16,72,384]{2,1,0:T(8,128)S(1)}, f32[16,72,384]{2,1,0:T(8,128)}, u32[]{:S(2)}) copy-start(f32[16,72,384]{2,1,0:T(8,128)} %copy-done.9) | copy-start | bytes 5308420
  73.6 1.5 %copy-start.12 = (f32[16,72,384]{2,1,0:T(8,128)S(1)}, f32[16,72,384]{2,1,0:T(8,128)}, u32[]{:S(2)}) copy-start(f32[16,72,384]{2,1,0:T(8,128)} %copy-done.11) | copy-start | bytes 5308420
  75.0 1.3 %copy-start.16 = (f32[8,72,512]{2,1,0:T(8,128)S(1)}, f32[8,72,512]{2,1,0:T(8,128)}, u32[]{:S(2)}) copy-start(f32[8,72,512]{2,1,0:T(8,128)} %get-tuple-element.23.refs_6_) | copy-start | bytes 3538948
  76.3 7.1 %copy-start = (f32[16,128,384]{2,1,0:T(8,128)S(1)}, f32[16,128,384]{2,1,0:T(8,128)}, u32[]{:S(2)}) copy-start(f32[16,128,384]{2,1,0:T(8,128)} %get-tuple-element.21.own) | copy-start | bytes 9437188
  76.3 7.2 %copy-start.7 = (s32[128,384]{1,0:T(8,128)S(1)}, s32[128,384]{1,0:T(8,128)}, u32[]{:S(2)}) copy-start(s32[128,384]{1,0:T(8,128)} %mask.9) | copy-start | bytes 589828
  76.3 7.2 %copy-start.8 = (s32[128,384]{1,0:T(8,128)S(1)}, s32[128,384]{1,0:T(8,128)}, u32[]{:S(2)}) copy-start(s32[128,384]{1,0:T(8,128)} %region.5) | copy-start | bytes 589828
  83.3 1.3 %copy-start.2 = (f32[16,64,384]{2,1,0:T(8,128)}, f32[16,64,384]{2,1,0:T(8,128)S(1)}, u32[]{:S(2)}) copy-start(f32[16,64,384]{2,1,0:T(8,128)S(1)} %shard_map.94.control.mine) | copy-start | bytes 4718596
  83.3 3.5 %collective-permute-start.11 = (f32[16,64,384]{2,1,0:T(8,128)S(1)}, f32[16,64,384]{2,1,0:T(8,128)S(1)}, u32[]{:S(2)}, u32[]{:S(2)}) collective-permute-start(f32[16,64,384]{2,1,0:T(8,128)S(1)} %shard_map.94.control.mine), channel_id=1, source_target_pairs={{0,32},{32,0},{64,96},{96,64},{128,160},{160,128},{192,224},{224,1... | collective-permute-start | bytes 4718600 | tf_op jit(solution)/shard_map/ppermute | solution.py:331
  84.7 14.8 %copy-start.24 = (f32[16]{0:T(128)S(1)}, f32[16]{0:T(128)}, u32[]{:S(2)}) copy-start(f32[16]{0:T(128)} %param.13) | copy-start | bytes 196
  88.2 1.1 copy-start.5
  89.3 0.6 copy-start.17
  90.0 20.3 %all-to-all-start = ((f32[32,8,128]{2,1,0:T(8,128)}), f32[32,8,128]{2,1,0:T(8,128)S(1)}, u32[]{:S(2)}, u32[]{:S(2)}) async-start(f32[32,8,128]{2,1,0:T(8,128)} %copy-done.17), calls=%async_computation | async-start | bytes 262144 | tf_op jit(solution)/shard_map/all_to_all | solution.py:598
  110.3 1.4 %copy-start.3 = (f32[16,64,384]{2,1,0:T(8,128)S(1)}, f32[16,64,384]{2,1,0:T(8,128)}, u32[]{:S(2)}) copy-start(f32[16,64,384]{2,1,0:T(8,128)} %copy-done.2) | copy-start | bytes 4718596
  111.7 1.4 %copy-start.6 = (f32[16,64,384]{2,1,0:T(8,128)S(1)}, f32[16,64,384]{2,1,0:T(8,128)}, u32[]{:S(2)}) copy-start(f32[16,64,384]{2,1,0:T(8,128)} %copy-done.5) | copy-start | bytes 4718596

commit v9 on v8

--- a/solution.py
+++ b/solution.py
@@ -310,7 +310,7 @@
         + step_scratch(ROWS_X)
         + [pltpu.SemaphoreType.DMA((7,))],
         flops=1 << 28,
-        mib=60,
+        mib=28,
     )(where, state, *statics, *halos, gate)
 
 
@@ -398,7 +398,7 @@
         mib=8,
     )(where, halo, *came)
     u, v = call(
-        relay_kernel, [u, v], [SMEM] + [HBM] * 4 + [ANY], [HBM] * 2, STAGE, mib=58, aliases={1: 0, 2: 1}
+        relay_kernel, [u, v], [SMEM] + [HBM] * 4 + [ANY], [HBM] * 2, STAGE, mib=40, aliases={1: 0, 2: 1}
     )(where, u, v, p1, m1, known)
     p2 = send(u, [(0, 3), (2, 4), (7, 1)])
     m2 = send(v, [(0, 6), (7, 5)])

time: 118 us -> 108 us (0.915)
  local copies, waits for them, and re-layouts: 16.8 us -> 6.37 us
  waiting for transfers between devices: 31 us -> 34.4 us
  Pallas kernels: 38.7 us -> 36.2 us
    unnamed x50 -> x32, local copies, waits for them, and re-layouts: 16.7 us -> 6.36 us
    ppermute x9, waiting for transfers between devices: 17.7 us -> 21.2 us  [send(): return lax.ppermute(value, 'member', pairs)]
    pallas_call x1, Pallas kernels: 15.5 us -> 13.2 us  [own_steps(): call(own_kernel, [jax.ShapeDtypeStruct((CH, ROWS, COLS), F32), jax.ShapeD...]
where the time goes in v9:
time: 108 us; the launch traced here: 107 us
  Pallas kernels  36.2 us (34%)
  waiting for transfers between devices  34.4 us (32%)
  starting transfers between devices  28.5 us (26%)
  local copies, waits for them, and re-layouts  6.37 us (6%)
    ppermute x9, waiting for transfers between devices, send(): return lax.ppermute(value, 'member', pairs)  21.2 us
    pallas_call x1, Pallas kernels, own_steps(): call(own_kernel, [jax.ShapeDtypeStruct((CH, ROWS, COLS), F32), jax.ShapeD...  13.2 us
    all_to_all x1, waiting for transfers between devices, per_device(): parts = lax.all_to_all(parts, ('lon', 'lat'), 0, 0)  10.8 us
    all_to_all x1, starting transfers between devices, per_device(): parts = lax.all_to_all(parts, ('lon', 'lat'), 0, 0)  9.54 us
    ppermute x9, starting transfers between devices, send(): return lax.ppermute(value, 'member', pairs)  8.86 us
    pallas_call x1, Pallas kernels, control_steps(): call(control_kernel, jax.ShapeDtypeStruct((CH, HALF, COLS), F32), [SMEM]...  7.01 us
    unnamed x32, local copies, waits for them, and re-layouts  6.36 us
    ppermute x1, starting transfers between devices, exchange(): lax.ppermute(west, 'lon', down)  5.38 us
  transfers between devices with their start and end apart: 13, of which 6 were waited for; matrix products, arithmetic and copies ran while one was open for 0% of the time, Pallas kernels for 21%

profile of v9, /device:TPU:24, one launch (start us, length us, event | category | flops | bytes accessed | tf_op | source)
XLA Modules:
  0.0 107.1 jit_solution(14702047437851021132)
XLA Ops:
  0.6 0.7 pad_add_fusion.lat.where
  1.3 0.8 shard_map.89
  2.2 0.8 collective-permute-start.3
  2.9 1.9 %collective-permute-start.4 = (f32[16,72,384]{2,1,0:T(8,128)}, f32[16,72,384]{2,1,0:T(8,128)}, u32[]{:S(2)}, u32[]{:S(2)}) collective-permute-start(f32[16,72,384]{2,1,0:T(8,128)} %get-tuple-element.18.u), channel_id=1, source_target_pairs={{0,224},{1,225},{2,226},{3,227},{4,228},{5,229},{6,230},{7,231},{8... | collective-permute-start | bytes 5308424 | tf_op jit(solution)/shard_map/ppermute | solution.py:331
  4.8 2.4 %shard_map.86 = f32[96,384]{1,0:T(8,128)} custom-call(s32[3]{0:T(128)} %pad_add_fusion.lat.where, f32[16,128,384]{2,1,0:T(8,128)} %bitcast.6, f32[128,384]{1,0:T(8,128)} %depth.5, f32[128,384]{1,0:T(8,128)} %rotation.5, f32[5,128,384]{2,1,0:T(8,128)} %diff.5, s32[128,384]{1,0:T(8,128)} %mask.9), custom_call_target="tpu_custom_call" | custom-call | flops 4194304 | bytes 8388608 | tf_op jit(solution)/shard_map/pallas_call | solution.py:121
  7.2 3.1 %collective-permute-start = (f32[96,384]{1,0:T(8,128)}, f32[96,384]{1,0:T(8,128)S(1)}, u32[]{:S(2)}, u32[]{:S(2)}) collective-permute-start(f32[96,384]{1,0:T(8,128)} %shard_map.86), channel_id=1, source_target_pairs={{0,1},{1,0},{2,3},{3,2},{4,5},{5,4},{6,7},{7,6},{8,9},{9,8},{10,11... | collective-permute-start | bytes 442376 | tf_op jit(solution)/shard_map/ppermute | solution.py:129
  10.3 3.6 %shard_map.87 = (f32[128,128]{1,0:T(8,128)}, f32[128,128]{1,0:T(8,128)}) custom-call(f32[16,128,384]{2,1,0:T(8,128)} %bitcast.7, f32[128,384]{1,0:T(8,128)} %depth.5, f32[128,384]{1,0:T(8,128)} %rotation.5, f32[5,128,384]{2,1,0:T(8,128)} %diff.5, s32[128,384]{1,0:T(8,128)} %mask.9), custom_call_target="tpu_custom_call" | custom-call | flops 4194304 | bytes 8388608 | tf_op jit(solution)/shard_map/pallas_call | solution.py:131
  13.9 0.2 collective-permute-done.rows
  14.1 0.8 copy-done.12
  15.0 0.8 copy-done.13
  15.8 0.7 shard_map.88
  16.5 1.6 %collective-permute-start.1 = (f32[136,128]{1,0:T(8,128)S(1)}, f32[136,128]{1,0:T(8,128)S(1)}, u32[]{:S(2)}, u32[]{:S(2)}) collective-permute-start(f32[136,128]{1,0:T(8,128)S(1)} %get-tuple-element.16), channel_id=1, source_target_pairs={{0,2},{2,4},{4,6},{6,8},{8,10},{10,12},{12,14},{14,16},{16,18},{18... | collective-permute-start | bytes 208904 | tf_op jit(solution)/shard_map/ppermute | solution.py:142
  18.0 5.4 %collective-permute-start.2 = (f32[136,128]{1,0:T(8,128)S(1)}, f32[136,128]{1,0:T(8,128)S(1)}, u32[]{:S(2)}, u32[]{:S(2)}) collective-permute-start(f32[136,128]{1,0:T(8,128)S(1)} %get-tuple-element.17), channel_id=1, source_target_pairs={{2,0},{4,2},{6,4},{8,6},{10,8},{12,10},{14,12},{16,14},{18,16},{20... | collective-permute-start | bytes 208904 | tf_op jit(solution)/shard_map/ppermute | solution.py:142
  23.4 2.2 %collective-permute-done.1.fw = f32[136,128]{1,0:T(8,128)S(1)} collective-permute-done((f32[136,128]{1,0:T(8,128)S(1)}, f32[136,128]{1,0:T(8,128)S(1)}, u32[]{:S(2)}, u32[]{:S(2)}) %collective-permute-start.1) | collective-permute-done | bytes 69664 | tf_op jit(solution)/shard_map/ppermute | solution.py:142
  25.6 0.0 collective-permute-done.2.fe
  25.6 0.1 shard_map.90.own
  25.7 0.7 collective-permute-start.5
  26.4 0.7 collective-permute-start.6
  27.1 1.3 %collective-permute-start.7 = (f32[16,8,384]{2,1,0:T(8,128)S(1)}, f32[16,8,384]{2,1,0:T(8,128)S(1)}, u32[]{:S(2)}, u32[]{:S(2)}) collective-permute-start(f32[16,8,384]{2,1,0:T(8,128)S(1)} %shard_map.90.own), channel_id=1, source_target_pairs={{0,192},{1,193},{2,194},{3,195},{4,196},{5,197},{6,198},{7,199},{8... | collective-permute-start | bytes 589832 | tf_op jit(solution)/shard_map/ppermute | solution.py:331
  28.4 0.0 collective-permute-done.6.three
  28.4 9.1 %collective-permute-done.7.six = f32[16,8,384]{2,1,0:T(8,128)S(1)} collective-permute-done((f32[16,8,384]{2,1,0:T(8,128)S(1)}, f32[16,8,384]{2,1,0:T(8,128)S(1)}, u32[]{:S(2)}, u32[]{:S(2)}) %collective-permute-start.7) | collective-permute-done | bytes 196640 | tf_op jit(solution)/shard_map/ppermute | solution.py:331
  37.5 0.8 shard_map.91.gate.refs_4_
  38.3 0.0 copy-start.4
  38.3 0.0 copy-start.7
  38.3 0.0 copy-start.8
  38.4 0.0 copy-start.9
  38.4 0.0 collective-permute-done.3.p1
  38.4 0.0 copy-start
  38.4 0.7 shard_map.92
  39.1 0.9 collective-permute-start.8
  40.0 1.3 %collective-permute-start.9 = (f32[16,72,384]{2,1,0:T(8,128)}, f32[16,72,384]{2,1,0:T(8,128)S(1)}, u32[]{:S(2)}, u32[]{:S(2)}) collective-permute-start(f32[16,72,384]{2,1,0:T(8,128)} %get-tuple-element.22.refs_0_), channel_id=1, source_target_pairs={{0,192},{224,160},{1,193},{225,161},{2,194},{226,162},{3,195},{227... | collective-permute-start | bytes 5308424 | tf_op jit(solution)/shard_map/ppermute | solution.py:331
  41.3 1.3 %collective-permute-start.10 = (f32[16,8,384]{2,1,0:T(8,128)S(1)}, f32[16,8,384]{2,1,0:T(8,128)S(1)}, u32[]{:S(2)}, u32[]{:S(2)}) collective-permute-start(f32[16,8,384]{2,1,0:T(8,128)S(1)} %shard_map.91.gate.refs_4_), channel_id=1, source_target_pairs={{0,64},{32,224},{96,128},{192,160},{1,65},{33,225},{97,129},{193,1... | collective-permute-start | bytes 589832 | tf_op jit(solution)/shard_map/ppermute | solution.py:331
  42.7 13.2 %shard_map.93 = (f32[16,128,384]{2,1,0:T(8,128)S(1)}, f32[8,72,512]{2,1,0:T(8,128)S(1)}) custom-call(s32[3]{0:T(128)S(1)} %copy-done.14, f32[16,128,384]{2,1,0:T(8,128)S(1)} %bitcast.8, f32[128,384]{1,0:T(8,128)S(1)} %copy-done.8, f32[128,384]{1,0:T(8,128)S(1)} %copy-done.9, f32[5,128,384]{2,1,0:T(8,128)S(1)} %copy-done.4, s32[128,384]{1,0:T(8,128)S(1)} %copy-done.7, ...), custom_call_target="tpu_custom_call" | custom-call | flops 268435456 | bytes 8388608 | tf_op jit(solution)/shard_map/pallas_call | solution.py:301
  56.0 9.9 %collective-permute-done.9.refs_3_ = f32[16,72,384]{2,1,0:T(8,128)S(1)} collective-permute-done((f32[16,72,384]{2,1,0:T(8,128)}, f32[16,72,384]{2,1,0:T(8,128)S(1)}, u32[]{:S(2)}, u32[]{:S(2)}) %collective-permute-start.9) | collective-permute-done | bytes 1769504 | tf_op jit(solution)/shard_map/ppermute | solution.py:331
  65.9 7.0 %shard_map.94.control.mine = f32[16,64,384]{2,1,0:T(8,128)S(1)} custom-call(s32[3]{0:T(128)S(1)} %copy-done.14, f32[16,72,384]{2,1,0:T(8,128)} %get-tuple-element.22.refs_0_, f32[16,72,384]{2,1,0:T(8,128)S(1)} %get-tuple-element.20.gate.refs_1_, f32[16,72,384]{2,1,0:T(8,128)S(1)} %collective-permute-done.8.refs_2_, ...), custom_call_target="tpu_custom_call" | custom-call | flops 134217728 | bytes 8388608 | tf_op jit(solution)/shard_map/pallas_call | solution.py:459
  72.9 0.0 copy-start.2
  72.9 0.1 collective-permute-start.11
  73.0 1.2 %shard_map.95.earlier = f32[8,128]{1,0:T(8,128)S(1)} custom-call(s32[3]{0:T(128)S(1)} %copy-done.14, f32[16,128,384]{2,1,0:T(8,128)S(1)} %get-tuple-element.21.own, f32[16,64,384]{2,1,0:T(8,128)S(1)} %shard_map.94.control.mine, s32[128,384]{1,0:T(8,128)S(1)} %copy-done.7, s32[128,384]{1,0:T(8,128)S(1)} %copy-done.10, f32[8,128]{1,0:T(8,128)S(1)} %broadcast_in_dim.9.earlier), custom_call_target="tpu_custom_call" | custom-call | flops 4194304 | bytes 8388608 | tf_op jit(solution)/shard_map/pallas_call | solution.py:516
  74.2 0.0 copy-start.15
  74.2 2.2 %collective-permute-done.11.control.theirs = f32[16,64,384]{2,1,0:T(8,128)S(1)} collective-permute-done((f32[16,64,384]{2,1,0:T(8,128)S(1)}, f32[16,64,384]{2,1,0:T(8,128)S(1)}, u32[]{:S(2)}, u32[]{:S(2)}) %collective-permute-start.11) | collective-permute-done | bytes 1572896 | tf_op jit(solution)/shard_map/ppermute | solution.py:331
  76.4 1.3 %shard_map.96 = f32[32,8,128]{2,1,0:T(8,128)S(1)} custom-call(s32[3]{0:T(128)S(1)} %copy-done.14, f32[16,128,384]{2,1,0:T(8,128)S(1)} %get-tuple-element.21.own, f32[16,64,384]{2,1,0:T(8,128)S(1)} %collective-permute-done.11.control.theirs, s32[128,384]{1,0:T(8,128)S(1)} %copy-done.7, s32[128,384]{1,0:T(8,128)S(1)} %copy-done.10, f32[8,128]{1,0:T(8,128)S(1)} %shard_map.95.earlier), custom_call_target="tpu_custom_call" | custom-call | flops 4194304 | bytes 8388608 | tf_op jit(solution)/shard_map/pallas_call | solution.py:516
  77.8 1.2 %copy-done.5 = f32[16,64,384]{2,1,0:T(8,128)} copy-done((f32[16,64,384]{2,1,0:T(8,128)}, f32[16,64,384]{2,1,0:T(8,128)S(1)}, u32[]{:S(2)}) %copy-start.5) | copy-done | bytes 1572888
  78.9 0.6 copy-done.11
  79.6 9.5 %all-to-all-start = ((f32[32,8,128]{2,1,0:T(8,128)}), f32[32,8,128]{2,1,0:T(8,128)S(1)}, u32[]{:S(2)}, u32[]{:S(2)}) async-start(f32[32,8,128]{2,1,0:T(8,128)} %copy-done.11), calls=%async_computation | async-start | bytes 262144 | tf_op jit(solution)/shard_map/all_to_all | solution.py:598
  89.1 10.8 %all-to-all-done.parts = f32[32,8,128]{2,1,0:T(8,128)S(1)} async-done(((f32[32,8,128]{2,1,0:T(8,128)}), f32[32,8,128]{2,1,0:T(8,128)S(1)}, u32[]{:S(2)}, u32[]{:S(2)}) %all-to-all-start) | async-done | bytes 131104 | tf_op jit(solution)/shard_map/all_to_all | solution.py:598
  99.9 1.4 %copy-done.3 = f32[16,64,384]{2,1,0:T(8,128)S(1)} copy-done((f32[16,64,384]{2,1,0:T(8,128)S(1)}, f32[16,64,384]{2,1,0:T(8,128)}, u32[]{:S(2)}) %copy-start.3) | copy-done | bytes 1572888
  101.3 1.4 %copy-done.6 = f32[16,64,384]{2,1,0:T(8,128)S(1)} copy-done((f32[16,64,384]{2,1,0:T(8,128)S(1)}, f32[16,64,384]{2,1,0:T(8,128)}, u32[]{:S(2)}) %copy-start.6) | copy-done | bytes 1572888
  102.7 4.4 %shard_map.97 = (f32[16,128,384]{2,1,0:T(8,128)}, f32[1,16]{1,0:T(1,128)}) custom-call(s32[3]{0:T(128)S(1)} %copy-done.14, f32[16,128,384]{2,1,0:T(8,128)S(1)} %get-tuple-element.21.own, f32[16,64,384]{2,1,0:T(8,128)S(1)} %copy-done.3, f32[16,64,384]{2,1,0:T(8,128)S(1)} %copy-done.6, s32[128,384]{1,0:T(8,128)S(1)} %copy-done.10, ...), custom_call_target="tpu_custom_call" | custom-call | flops 4194304 | bytes 10485760 | tf_op jit(solution)/shard_map/pallas_call | solution.py:572
  (26 shorter events, 0.1 us)
Async XLA Ops:
  2.2 36.2 %collective-permute-start.3 = (f32[16,72,384]{2,1,0:T(8,128)}, f32[16,72,384]{2,1,0:T(8,128)S(1)}, u32[]{:S(2)}, u32[]{:S(2)}) collective-permute-start(f32[16,72,384]{2,1,0:T(8,128)} %get-tuple-element.19.v), channel_id=1, source_target_pairs={{0,64},{1,65},{2,66},{3,67},{4,68},{5,69},{6,70},{7,71},{8,72},{9,... | collective-permute-start | bytes 5308424 | tf_op jit(solution)/shard_map/ppermute | solution.py:331
  2.9 35.4 %collective-permute-start.4 = (f32[16,72,384]{2,1,0:T(8,128)}, f32[16,72,384]{2,1,0:T(8,128)}, u32[]{:S(2)}, u32[]{:S(2)}) collective-permute-start(f32[16,72,384]{2,1,0:T(8,128)} %get-tuple-element.18.u), channel_id=1, source_target_pairs={{0,224},{1,225},{2,226},{3,227},{4,228},{5,229},{6,230},{7,231},{8... | collective-permute-start | bytes 5308424 | tf_op jit(solution)/shard_map/ppermute | solution.py:331
  7.2 7.0 %copy-start.14 = (s32[3]{0:T(128)S(1)}, s32[3]{0:T(128)}, u32[]{:S(2)}) copy-start(s32[3]{0:T(128)} %pad_add_fusion.lat.where) | copy-start | bytes 40
  7.2 6.9 %collective-permute-start = (f32[96,384]{1,0:T(8,128)}, f32[96,384]{1,0:T(8,128)S(1)}, u32[]{:S(2)}, u32[]{:S(2)}) collective-permute-start(f32[96,384]{1,0:T(8,128)} %shard_map.86), channel_id=1, source_target_pairs={{0,1},{1,0},{2,3},{3,2},{4,5},{5,4},{6,7},{7,6},{8,9},{9,8},{10,11... | collective-permute-start | bytes 442376 | tf_op jit(solution)/shard_map/ppermute | solution.py:129
  10.3 28.1 %copy-start.1 = (f32[16,72,384]{2,1,0:T(8,128)S(1)}, f32[16,72,384]{2,1,0:T(8,128)}, u32[]{:S(2)}) copy-start(f32[16,72,384]{2,1,0:T(8,128)} %get-tuple-element.18.u) | copy-start | bytes 5308420
  14.1 0.8 copy-start.12
  15.0 0.8 copy-start.13
  16.5 9.1 %collective-permute-start.1 = (f32[136,128]{1,0:T(8,128)S(1)}, f32[136,128]{1,0:T(8,128)S(1)}, u32[]{:S(2)}, u32[]{:S(2)}) collective-permute-start(f32[136,128]{1,0:T(8,128)S(1)} %get-tuple-element.16), channel_id=1, source_target_pairs={{0,2},{2,4},{4,6},{6,8},{8,10},{10,12},{12,14},{14,16},{16,18},{18... | collective-permute-start | bytes 208904 | tf_op jit(solution)/shard_map/ppermute | solution.py:142
  18.0 7.6 %collective-permute-start.2 = (f32[136,128]{1,0:T(8,128)S(1)}, f32[136,128]{1,0:T(8,128)S(1)}, u32[]{:S(2)}, u32[]{:S(2)}) collective-permute-start(f32[136,128]{1,0:T(8,128)S(1)} %get-tuple-element.17), channel_id=1, source_target_pairs={{2,0},{4,2},{6,4},{8,6},{10,8},{12,10},{14,12},{16,14},{18,16},{20... | collective-permute-start | bytes 208904 | tf_op jit(solution)/shard_map/ppermute | solution.py:142
  25.7 2.7 %collective-permute-start.5 = (f32[16,8,384]{2,1,0:T(8,128)S(1)}, f32[16,8,384]{2,1,0:T(8,128)S(1)}, u32[]{:S(2)}, u32[]{:S(2)}) collective-permute-start(f32[16,8,384]{2,1,0:T(8,128)S(1)} %shard_map.90.own), channel_id=1, source_target_pairs={{0,32},{1,33},{2,34},{3,35},{4,36},{5,37},{6,38},{7,39},{8,40},{9,... | collective-permute-start | bytes 589832 | tf_op jit(solution)/shard_map/ppermute | solution.py:331
  26.4 2.0 %collective-permute-start.6 = (f32[16,8,384]{2,1,0:T(8,128)S(1)}, f32[16,8,384]{2,1,0:T(8,128)S(1)}, u32[]{:S(2)}, u32[]{:S(2)}) collective-permute-start(f32[16,8,384]{2,1,0:T(8,128)S(1)} %shard_map.90.own), channel_id=1, source_target_pairs={{0,96},{1,97},{2,98},{3,99},{4,100},{5,101},{6,102},{7,103},{8,104... | collective-permute-start | bytes 589832 | tf_op jit(solution)/shard_map/ppermute | solution.py:331
  27.1 10.4 %collective-permute-start.7 = (f32[16,8,384]{2,1,0:T(8,128)S(1)}, f32[16,8,384]{2,1,0:T(8,128)S(1)}, u32[]{:S(2)}, u32[]{:S(2)}) collective-permute-start(f32[16,8,384]{2,1,0:T(8,128)S(1)} %shard_map.90.own), channel_id=1, source_target_pairs={{0,192},{1,193},{2,194},{3,195},{4,196},{5,197},{6,198},{7,199},{8... | collective-permute-start | bytes 589832 | tf_op jit(solution)/shard_map/ppermute | solution.py:331
  38.3 4.3 %copy-start.4 = (f32[5,128,384]{2,1,0:T(8,128)S(1)}, f32[5,128,384]{2,1,0:T(8,128)}, u32[]{:S(2)}) copy-start(f32[5,128,384]{2,1,0:T(8,128)} %diff.5) | copy-start | bytes 2949124
  38.3 4.3 %copy-start.7 = (s32[128,384]{1,0:T(8,128)S(1)}, s32[128,384]{1,0:T(8,128)}, u32[]{:S(2)}) copy-start(s32[128,384]{1,0:T(8,128)} %mask.9) | copy-start | bytes 589828
  38.3 4.3 %copy-start.8 = (f32[128,384]{1,0:T(8,128)S(1)}, f32[128,384]{1,0:T(8,128)}, u32[]{:S(2)}) copy-start(f32[128,384]{1,0:T(8,128)} %depth.5) | copy-start | bytes 589828
  38.4 4.3 %copy-start.9 = (f32[128,384]{1,0:T(8,128)S(1)}, f32[128,384]{1,0:T(8,128)}, u32[]{:S(2)}) copy-start(f32[128,384]{1,0:T(8,128)} %rotation.5) | copy-start | bytes 589828
  38.4 4.3 %copy-start = (f32[1,16,128,384]{3,2,1,0:T(8,128)S(1)}, f32[1,16,128,384]{3,2,1,0:T(8,128)}, u32[]{:S(2)}) copy-start(f32[1,16,128,384]{3,2,1,0:T(8,128)} %param.7) | copy-start | bytes 9437188
  39.1 16.8 %collective-permute-start.8 = (f32[16,72,384]{2,1,0:T(8,128)S(1)}, f32[16,72,384]{2,1,0:T(8,128)S(1)}, u32[]{:S(2)}, u32[]{:S(2)}) collective-permute-start(f32[16,72,384]{2,1,0:T(8,128)S(1)} %get-tuple-element.20.gate.refs_1_), channel_id=1, source_target_pairs={{0,96},{64,128},{224,32},{1,97},{65,129},{225,33},{2,98},{66,130},... | collective-permute-start | bytes 5308424 | tf_op jit(solution)/shard_map/ppermute | solution.py:331
  40.0 25.8 %collective-permute-start.9 = (f32[16,72,384]{2,1,0:T(8,128)}, f32[16,72,384]{2,1,0:T(8,128)S(1)}, u32[]{:S(2)}, u32[]{:S(2)}) collective-permute-start(f32[16,72,384]{2,1,0:T(8,128)} %get-tuple-element.22.refs_0_), channel_id=1, source_target_pairs={{0,192},{224,160},{1,193},{225,161},{2,194},{226,162},{3,195},{227... | collective-permute-start | bytes 5308424 | tf_op jit(solution)/shard_map/ppermute | solution.py:331
  41.3 14.6 %collective-permute-start.10 = (f32[16,8,384]{2,1,0:T(8,128)S(1)}, f32[16,8,384]{2,1,0:T(8,128)S(1)}, u32[]{:S(2)}, u32[]{:S(2)}) collective-permute-start(f32[16,8,384]{2,1,0:T(8,128)S(1)} %shard_map.91.gate.refs_4_), channel_id=1, source_target_pairs={{0,64},{32,224},{96,128},{192,160},{1,65},{33,225},{97,129},{193,1... | collective-permute-start | bytes 589832 | tf_op jit(solution)/shard_map/ppermute | solution.py:331
  65.9 7.1 %copy-start.10 = (s32[128,384]{1,0:T(8,128)S(1)}, s32[128,384]{1,0:T(8,128)}, u32[]{:S(2)}) copy-start(s32[128,384]{1,0:T(8,128)} %region.5) | copy-start | bytes 589828
  72.9 1.3 %copy-start.2 = (f32[16,64,384]{2,1,0:T(8,128)}, f32[16,64,384]{2,1,0:T(8,128)S(1)}, u32[]{:S(2)}) copy-start(f32[16,64,384]{2,1,0:T(8,128)S(1)} %shard_map.94.control.mine) | copy-start | bytes 4718596
  72.9 3.5 %collective-permute-start.11 = (f32[16,64,384]{2,1,0:T(8,128)S(1)}, f32[16,64,384]{2,1,0:T(8,128)S(1)}, u32[]{:S(2)}, u32[]{:S(2)}) collective-permute-start(f32[16,64,384]{2,1,0:T(8,128)S(1)} %shard_map.94.control.mine), channel_id=1, source_target_pairs={{0,32},{32,0},{64,96},{96,64},{128,160},{160,128},{192,224},{224,1... | collective-permute-start | bytes 4718600 | tf_op jit(solution)/shard_map/ppermute | solution.py:331
  74.2 14.9 %copy-start.15 = (f32[16]{0:T(128)S(1)}, f32[16]{0:T(128)}, u32[]{:S(2)}) copy-start(f32[16]{0:T(128)} %param.13) | copy-start | bytes 196
  77.8 1.2 %copy-start.5 = (f32[16,64,384]{2,1,0:T(8,128)}, f32[16,64,384]{2,1,0:T(8,128)S(1)}, u32[]{:S(2)}) copy-start(f32[16,64,384]{2,1,0:T(8,128)S(1)} %collective-permute-done.11.control.theirs) | copy-start | bytes 4718596
  78.9 0.6 copy-start.11
  79.6 20.3 %all-to-all-start = ((f32[32,8,128]{2,1,0:T(8,128)}), f32[32,8,128]{2,1,0:T(8,128)S(1)}, u32[]{:S(2)}, u32[]{:S(2)}) async-start(f32[32,8,128]{2,1,0:T(8,128)} %copy-done.11), calls=%async_computation | async-start | bytes 262144 | tf_op jit(solution)/shard_map/all_to_all | solution.py:598
  99.9 1.4 %copy-start.3 = (f32[16,64,384]{2,1,0:T(8,128)S(1)}, f32[16,64,384]{2,1,0:T(8,128)}, u32[]{:S(2)}) copy-start(f32[16,64,384]{2,1,0:T(8,128)} %copy-done.2) | copy-start | bytes 4718596
  101.3 1.4 %copy-start.6 = (f32[16,64,384]{2,1,0:T(8,128)S(1)}, f32[16,64,384]{2,1,0:T(8,128)}, u32[]{:S(2)}) copy-start(f32[16,64,384]{2,1,0:T(8,128)} %copy-done.5) | copy-start | bytes 4718596

commit v10 on v9

--- a/solution.py
+++ b/solution.py
@@ -377,8 +377,8 @@
         staged([(m1, v_out), (m1, u_out)], buffer, sem)
 
 
-def known_kernel(where, own, one, three, six, out, sem):
-    for member, ref in ((0, own), (1, one), (3, three), (6, six)):
+def known_kernel(where, own, three, six, out, sem):
+    for member, ref in ((0, own), (3, three), (6, six)):
 
         @pl.when(where[2] == member)
         def _(ref=ref):
@@ -388,11 +388,11 @@
 
 
 def spread_rest(where, u, v, p1, m1, halo):
-    came = [send(halo, [(0, member)]) for member in (1, 3, 6)]
+    came = [send(halo, [(0, member)]) for member in (3, 6)]
     known = call(
         known_kernel,
         jax.ShapeDtypeStruct((CH, 8, COLS), F32),
-        [SMEM] + [ANY] * 4,
+        [SMEM] + [ANY] * 3,
         VMEM,
         [pltpu.SemaphoreType.DMA((1,))],
         mib=8,
@@ -402,15 +402,15 @@
     )(where, u, v, p1, m1, known)
     p2 = send(u, [(0, 3), (2, 4), (7, 1)])
     m2 = send(v, [(0, 6), (7, 5)])
-    return (v, u, p2, m2), (known, send(known, [(0, 2), (1, 7), (3, 4), (6, 5)]))
+    return (v, u, p2, m2), (known, send(known, [(0, 1), (3, 2), (6, 7)]), send(known, [(3, 4), (6, 5)]))
 
 
 HOLDER = ((0, 7), (2,), (1, 3, 4), (5, 6))
-HALO_HOLDER = (0, 0, 1, 0, 1, 1, 0, 1)
+HALO_HOLDER = (0, 1, 1, 0, 2, 2, 0, 1)
 
 
 def control_kernel(where, *refs):
-    arrays, halos, (static, out, x, y, ub, vb, h2, near, halo, strip, sem) = refs[:4], refs[4:6], refs[6:]
+    arrays, halos, (static, out, x, y, ub, vb, h2, near, halo, strip, sem) = refs[:4], refs[4:7], refs[7:]
     first = where[1] == 0
     m = where[2]
     for array, members in zip(arrays, HOLDER):
@@ -459,7 +459,7 @@
     return call(
         control_kernel,
         jax.ShapeDtypeStruct((CH, HALF, COLS), F32),
-        [SMEM] + [HBM] * 4 + [ANY] * 2 + [VMEM],
+        [SMEM] + [HBM] * 4 + [ANY] * 3 + [VMEM],
         VMEM,
         [pltpu.VMEM((CH, HALF_X, COLS_X), F32)]
         + step_scratch(HALF_X)

time: 108 us -> 106 us (0.981)
  waiting for transfers between devices: 34.4 us -> 32.4 us
    ppermute x9, waiting for transfers between devices: 21.2 us -> 19.3 us  [send(): return lax.ppermute(value, 'member', pairs)]
where the time goes in v10:
time: 106 us
  Pallas kernels  36.2 us (34%)
  waiting for transfers between devices  32.4 us (31%)
  starting transfers between devices  29.1 us (27%)
  local copies, waits for them, and re-layouts  6.37 us (6%)
    ppermute x9, waiting for transfers between devices, send(): return lax.ppermute(value, 'member', pairs)  19.3 us
    pallas_call x1, Pallas kernels, own_steps(): call(own_kernel, [jax.ShapeDtypeStruct((CH, ROWS, COLS), F32), jax.ShapeD...  13.2 us
    all_to_all x1, waiting for transfers between devices, per_device(): parts = lax.all_to_all(parts, ('lon', 'lat'), 0, 0)  10.8 us
    all_to_all x1, starting transfers between devices, per_device(): parts = lax.all_to_all(parts, ('lon', 'lat'), 0, 0)  9.54 us
    ppermute x9, starting transfers between devices, send(): return lax.ppermute(value, 'member', pairs)  9.49 us
    pallas_call x1, Pallas kernels, control_steps(): call(control_kernel, jax.ShapeDtypeStruct((CH, HALF, COLS), F32), [SMEM]...  7.01 us
    unnamed x32, local copies, waits for them, and re-layouts  6.36 us
    ppermute x1, starting transfers between devices, exchange(): lax.ppermute(west, 'lon', down)  5.38 us
  transfers between devices with their start and end apart: 13, of which 6 were waited for; matrix products, arithmetic and copies ran while one was open for 0% of the time, Pallas kernels for 21%

profile of v10, /device:TPU:24, one launch (start us, length us, event | category | flops | bytes accessed | tf_op | source)
XLA Modules:
  0.0 105.8 jit_solution(4098823076337012592)
XLA Ops:
  0.6 0.7 pad_add_fusion.lat.where
  1.3 0.8 shard_map.89
  2.2 0.8 collective-permute-start.3
  2.9 1.9 %collective-permute-start.4 = (f32[16,72,384]{2,1,0:T(8,128)}, f32[16,72,384]{2,1,0:T(8,128)}, u32[]{:S(2)}, u32[]{:S(2)}) collective-permute-start(f32[16,72,384]{2,1,0:T(8,128)} %get-tuple-element.18.u), channel_id=1, source_target_pairs={{0,224},{1,225},{2,226},{3,227},{4,228},{5,229},{6,230},{7,231},{8... | collective-permute-start | bytes 5308424 | tf_op jit(solution)/shard_map/ppermute | solution.py:331
  4.8 2.4 %shard_map.86 = f32[96,384]{1,0:T(8,128)} custom-call(s32[3]{0:T(128)} %pad_add_fusion.lat.where, f32[16,128,384]{2,1,0:T(8,128)} %bitcast.6, f32[128,384]{1,0:T(8,128)} %depth.5, f32[128,384]{1,0:T(8,128)} %rotation.5, f32[5,128,384]{2,1,0:T(8,128)} %diff.5, s32[128,384]{1,0:T(8,128)} %mask.9), custom_call_target="tpu_custom_call" | custom-call | flops 4194304 | bytes 8388608 | tf_op jit(solution)/shard_map/pallas_call | solution.py:121
  7.2 3.1 %collective-permute-start = (f32[96,384]{1,0:T(8,128)}, f32[96,384]{1,0:T(8,128)S(1)}, u32[]{:S(2)}, u32[]{:S(2)}) collective-permute-start(f32[96,384]{1,0:T(8,128)} %shard_map.86), channel_id=1, source_target_pairs={{0,1},{1,0},{2,3},{3,2},{4,5},{5,4},{6,7},{7,6},{8,9},{9,8},{10,11... | collective-permute-start | bytes 442376 | tf_op jit(solution)/shard_map/ppermute | solution.py:129
  10.3 3.6 %shard_map.87 = (f32[128,128]{1,0:T(8,128)}, f32[128,128]{1,0:T(8,128)}) custom-call(f32[16,128,384]{2,1,0:T(8,128)} %bitcast.7, f32[128,384]{1,0:T(8,128)} %depth.5, f32[128,384]{1,0:T(8,128)} %rotation.5, f32[5,128,384]{2,1,0:T(8,128)} %diff.5, s32[128,384]{1,0:T(8,128)} %mask.9), custom_call_target="tpu_custom_call" | custom-call | flops 4194304 | bytes 8388608 | tf_op jit(solution)/shard_map/pallas_call | solution.py:131
  13.9 0.2 collective-permute-done.rows
  14.1 0.8 copy-done.12
  15.0 0.8 copy-done.13
  15.8 0.7 shard_map.88
  16.5 1.6 %collective-permute-start.1 = (f32[136,128]{1,0:T(8,128)S(1)}, f32[136,128]{1,0:T(8,128)S(1)}, u32[]{:S(2)}, u32[]{:S(2)}) collective-permute-start(f32[136,128]{1,0:T(8,128)S(1)} %get-tuple-element.16), channel_id=1, source_target_pairs={{0,2},{2,4},{4,6},{6,8},{8,10},{10,12},{12,14},{14,16},{16,18},{18... | collective-permute-start | bytes 208904 | tf_op jit(solution)/shard_map/ppermute | solution.py:142
  18.0 5.4 %collective-permute-start.2 = (f32[136,128]{1,0:T(8,128)S(1)}, f32[136,128]{1,0:T(8,128)S(1)}, u32[]{:S(2)}, u32[]{:S(2)}) collective-permute-start(f32[136,128]{1,0:T(8,128)S(1)} %get-tuple-element.17), channel_id=1, source_target_pairs={{2,0},{4,2},{6,4},{8,6},{10,8},{12,10},{14,12},{16,14},{18,16},{20... | collective-permute-start | bytes 208904 | tf_op jit(solution)/shard_map/ppermute | solution.py:142
  23.4 2.2 %collective-permute-done.1.fw = f32[136,128]{1,0:T(8,128)S(1)} collective-permute-done((f32[136,128]{1,0:T(8,128)S(1)}, f32[136,128]{1,0:T(8,128)S(1)}, u32[]{:S(2)}, u32[]{:S(2)}) %collective-permute-start.1) | collective-permute-done | bytes 69664 | tf_op jit(solution)/shard_map/ppermute | solution.py:142
  25.6 0.0 collective-permute-done.2.fe
  25.6 0.1 shard_map.90.own
  25.7 0.7 collective-permute-start.5
  26.4 1.3 %collective-permute-start.6 = (f32[16,8,384]{2,1,0:T(8,128)S(1)}, f32[16,8,384]{2,1,0:T(8,128)S(1)}, u32[]{:S(2)}, u32[]{:S(2)}) collective-permute-start(f32[16,8,384]{2,1,0:T(8,128)S(1)} %shard_map.90.own), channel_id=1, source_target_pairs={{0,192},{1,193},{2,194},{3,195},{4,196},{5,197},{6,198},{7,199},{8... | collective-permute-start | bytes 589832 | tf_op jit(solution)/shard_map/ppermute | solution.py:331
  27.7 0.0 collective-permute-done.5.three
  27.7 8.5 %collective-permute-done.6.six = f32[16,8,384]{2,1,0:T(8,128)S(1)} collective-permute-done((f32[16,8,384]{2,1,0:T(8,128)S(1)}, f32[16,8,384]{2,1,0:T(8,128)S(1)}, u32[]{:S(2)}, u32[]{:S(2)}) %collective-permute-start.6) | collective-permute-done | bytes 196640 | tf_op jit(solution)/shard_map/ppermute | solution.py:331
  36.2 0.8 shard_map.91.gate.refs_4_
  37.0 0.0 copy-start.4
  37.0 0.0 copy-start.7
  37.0 0.0 copy-start.8
  37.0 0.0 copy-start.9
  37.0 0.0 collective-permute-done.3.p1
  37.1 0.0 copy-start
  37.1 0.7 shard_map.92
  37.8 0.9 collective-permute-start.7
  38.7 1.3 %collective-permute-start.8 = (f32[16,72,384]{2,1,0:T(8,128)}, f32[16,72,384]{2,1,0:T(8,128)S(1)}, u32[]{:S(2)}, u32[]{:S(2)}) collective-permute-start(f32[16,72,384]{2,1,0:T(8,128)} %get-tuple-element.22.refs_0_), channel_id=1, source_target_pairs={{0,192},{224,160},{1,193},{225,161},{2,194},{226,162},{3,195},{227... | collective-permute-start | bytes 5308424 | tf_op jit(solution)/shard_map/ppermute | solution.py:331
  40.0 1.3 %collective-permute-start.9 = (f32[16,8,384]{2,1,0:T(8,128)S(1)}, f32[16,8,384]{2,1,0:T(8,128)S(1)}, u32[]{:S(2)}, u32[]{:S(2)}) collective-permute-start(f32[16,8,384]{2,1,0:T(8,128)S(1)} %shard_map.91.gate.refs_4_), channel_id=1, source_target_pairs={{0,32},{96,64},{192,224},{1,33},{97,65},{193,225},{2,34},{98,66},{... | collective-permute-start | bytes 589832 | tf_op jit(solution)/shard_map/ppermute | solution.py:331
  41.3 1.3 %collective-permute-start.10 = (f32[16,8,384]{2,1,0:T(8,128)S(1)}, f32[16,8,384]{2,1,0:T(8,128)S(1)}, u32[]{:S(2)}, u32[]{:S(2)}) collective-permute-start(f32[16,8,384]{2,1,0:T(8,128)S(1)} %shard_map.91.gate.refs_4_), channel_id=1, source_target_pairs={{96,128},{192,160},{97,129},{193,161},{98,130},{194,162},{99,131},... | collective-permute-start | bytes 589832 | tf_op jit(solution)/shard_map/ppermute | solution.py:331
  42.7 13.2 %shard_map.93 = (f32[16,128,384]{2,1,0:T(8,128)S(1)}, f32[8,72,512]{2,1,0:T(8,128)S(1)}) custom-call(s32[3]{0:T(128)S(1)} %copy-done.14, f32[16,128,384]{2,1,0:T(8,128)S(1)} %bitcast.8, f32[128,384]{1,0:T(8,128)S(1)} %copy-done.8, f32[128,384]{1,0:T(8,128)S(1)} %copy-done.9, f32[5,128,384]{2,1,0:T(8,128)S(1)} %copy-done.4, s32[128,384]{1,0:T(8,128)S(1)} %copy-done.7, ...), custom_call_target="tpu_custom_call" | custom-call | flops 268435456 | bytes 8388608 | tf_op jit(solution)/shard_map/pallas_call | solution.py:301
  56.0 8.6 %collective-permute-done.8.refs_3_ = f32[16,72,384]{2,1,0:T(8,128)S(1)} collective-permute-done((f32[16,72,384]{2,1,0:T(8,128)}, f32[16,72,384]{2,1,0:T(8,128)S(1)}, u32[]{:S(2)}, u32[]{:S(2)}) %collective-permute-start.8) | collective-permute-done | bytes 1769504 | tf_op jit(solution)/shard_map/ppermute | solution.py:331
  64.6 7.0 %shard_map.94.control.mine = f32[16,64,384]{2,1,0:T(8,128)S(1)} custom-call(s32[3]{0:T(128)S(1)} %copy-done.14, f32[16,72,384]{2,1,0:T(8,128)} %get-tuple-element.22.refs_0_, f32[16,72,384]{2,1,0:T(8,128)S(1)} %get-tuple-element.20.gate.refs_1_, f32[16,72,384]{2,1,0:T(8,128)S(1)} %collective-permute-done.7.refs_2_, ...), custom_call_target="tpu_custom_call" | custom-call | flops 134217728 | bytes 8388608 | tf_op jit(solution)/shard_map/pallas_call | solution.py:459
  71.6 0.0 copy-start.2
  71.6 0.1 collective-permute-start.11
  71.7 1.2 %shard_map.95.earlier = f32[8,128]{1,0:T(8,128)S(1)} custom-call(s32[3]{0:T(128)S(1)} %copy-done.14, f32[16,128,384]{2,1,0:T(8,128)S(1)} %get-tuple-element.21.own, f32[16,64,384]{2,1,0:T(8,128)S(1)} %shard_map.94.control.mine, s32[128,384]{1,0:T(8,128)S(1)} %copy-done.7, s32[128,384]{1,0:T(8,128)S(1)} %copy-done.10, f32[8,128]{1,0:T(8,128)S(1)} %broadcast_in_dim.9.earlier), custom_call_target="tpu_custom_call" | custom-call | flops 4194304 | bytes 8388608 | tf_op jit(solution)/shard_map/pallas_call | solution.py:516
  72.9 0.0 copy-start.15
  72.9 2.2 %collective-permute-done.11.control.theirs = f32[16,64,384]{2,1,0:T(8,128)S(1)} collective-permute-done((f32[16,64,384]{2,1,0:T(8,128)S(1)}, f32[16,64,384]{2,1,0:T(8,128)S(1)}, u32[]{:S(2)}, u32[]{:S(2)}) %collective-permute-start.11) | collective-permute-done | bytes 1572896 | tf_op jit(solution)/shard_map/ppermute | solution.py:331
  75.1 1.3 %shard_map.96 = f32[32,8,128]{2,1,0:T(8,128)S(1)} custom-call(s32[3]{0:T(128)S(1)} %copy-done.14, f32[16,128,384]{2,1,0:T(8,128)S(1)} %get-tuple-element.21.own, f32[16,64,384]{2,1,0:T(8,128)S(1)} %collective-permute-done.11.control.theirs, s32[128,384]{1,0:T(8,128)S(1)} %copy-done.7, s32[128,384]{1,0:T(8,128)S(1)} %copy-done.10, f32[8,128]{1,0:T(8,128)S(1)} %shard_map.95.earlier), custom_call_target="tpu_custom_call" | custom-call | flops 4194304 | bytes 8388608 | tf_op jit(solution)/shard_map/pallas_call | solution.py:516
  76.4 1.2 %copy-done.5 = f32[16,64,384]{2,1,0:T(8,128)} copy-done((f32[16,64,384]{2,1,0:T(8,128)}, f32[16,64,384]{2,1,0:T(8,128)S(1)}, u32[]{:S(2)}) %copy-start.5) | copy-done | bytes 1572888
  77.6 0.6 copy-done.11
  78.3 9.5 %all-to-all-start = ((f32[32,8,128]{2,1,0:T(8,128)}), f32[32,8,128]{2,1,0:T(8,128)S(1)}, u32[]{:S(2)}, u32[]{:S(2)}) async-start(f32[32,8,128]{2,1,0:T(8,128)} %copy-done.11), calls=%async_computation | async-start | bytes 262144 | tf_op jit(solution)/shard_map/all_to_all | solution.py:598
  87.8 10.8 %all-to-all-done.parts = f32[32,8,128]{2,1,0:T(8,128)S(1)} async-done(((f32[32,8,128]{2,1,0:T(8,128)}), f32[32,8,128]{2,1,0:T(8,128)S(1)}, u32[]{:S(2)}, u32[]{:S(2)}) %all-to-all-start) | async-done | bytes 131104 | tf_op jit(solution)/shard_map/all_to_all | solution.py:598
  98.6 1.4 %copy-done.3 = f32[16,64,384]{2,1,0:T(8,128)S(1)} copy-done((f32[16,64,384]{2,1,0:T(8,128)S(1)}, f32[16,64,384]{2,1,0:T(8,128)}, u32[]{:S(2)}) %copy-start.3) | copy-done | bytes 1572888
  100.0 1.4 %copy-done.6 = f32[16,64,384]{2,1,0:T(8,128)S(1)} copy-done((f32[16,64,384]{2,1,0:T(8,128)S(1)}, f32[16,64,384]{2,1,0:T(8,128)}, u32[]{:S(2)}) %copy-start.6) | copy-done | bytes 1572888
  101.4 4.4 %shard_map.97 = (f32[16,128,384]{2,1,0:T(8,128)}, f32[1,16]{1,0:T(1,128)}) custom-call(s32[3]{0:T(128)S(1)} %copy-done.14, f32[16,128,384]{2,1,0:T(8,128)S(1)} %get-tuple-element.21.own, f32[16,64,384]{2,1,0:T(8,128)S(1)} %copy-done.3, f32[16,64,384]{2,1,0:T(8,128)S(1)} %copy-done.6, s32[128,384]{1,0:T(8,128)S(1)} %copy-done.10, ...), custom_call_target="tpu_custom_call" | custom-call | flops 4194304 | bytes 10485760 | tf_op jit(solution)/shard_map/pallas_call | solution.py:572
  (26 shorter events, 0.1 us)
Async XLA Ops:
  2.2 34.9 %collective-permute-start.3 = (f32[16,72,384]{2,1,0:T(8,128)}, f32[16,72,384]{2,1,0:T(8,128)S(1)}, u32[]{:S(2)}, u32[]{:S(2)}) collective-permute-start(f32[16,72,384]{2,1,0:T(8,128)} %get-tuple-element.19.v), channel_id=1, source_target_pairs={{0,64},{1,65},{2,66},{3,67},{4,68},{5,69},{6,70},{7,71},{8,72},{9,... | collective-permute-start | bytes 5308424 | tf_op jit(solution)/shard_map/ppermute | solution.py:331
  2.9 34.1 %collective-permute-start.4 = (f32[16,72,384]{2,1,0:T(8,128)}, f32[16,72,384]{2,1,0:T(8,128)}, u32[]{:S(2)}, u32[]{:S(2)}) collective-permute-start(f32[16,72,384]{2,1,0:T(8,128)} %get-tuple-element.18.u), channel_id=1, source_target_pairs={{0,224},{1,225},{2,226},{3,227},{4,228},{5,229},{6,230},{7,231},{8... | collective-permute-start | bytes 5308424 | tf_op jit(solution)/shard_map/ppermute | solution.py:331
  7.2 7.0 %copy-start.14 = (s32[3]{0:T(128)S(1)}, s32[3]{0:T(128)}, u32[]{:S(2)}) copy-start(s32[3]{0:T(128)} %pad_add_fusion.lat.where) | copy-start | bytes 40
  7.2 6.9 %collective-permute-start = (f32[96,384]{1,0:T(8,128)}, f32[96,384]{1,0:T(8,128)S(1)}, u32[]{:S(2)}, u32[]{:S(2)}) collective-permute-start(f32[96,384]{1,0:T(8,128)} %shard_map.86), channel_id=1, source_target_pairs={{0,1},{1,0},{2,3},{3,2},{4,5},{5,4},{6,7},{7,6},{8,9},{9,8},{10,11... | collective-permute-start | bytes 442376 | tf_op jit(solution)/shard_map/ppermute | solution.py:129
  10.3 26.8 %copy-start.1 = (f32[16,72,384]{2,1,0:T(8,128)S(1)}, f32[16,72,384]{2,1,0:T(8,128)}, u32[]{:S(2)}) copy-start(f32[16,72,384]{2,1,0:T(8,128)} %get-tuple-element.18.u) | copy-start | bytes 5308420
  14.1 0.8 copy-start.12
  15.0 0.8 copy-start.13
  16.5 9.1 %collective-permute-start.1 = (f32[136,128]{1,0:T(8,128)S(1)}, f32[136,128]{1,0:T(8,128)S(1)}, u32[]{:S(2)}, u32[]{:S(2)}) collective-permute-start(f32[136,128]{1,0:T(8,128)S(1)} %get-tuple-element.16), channel_id=1, source_target_pairs={{0,2},{2,4},{4,6},{6,8},{8,10},{10,12},{12,14},{14,16},{16,18},{18... | collective-permute-start | bytes 208904 | tf_op jit(solution)/shard_map/ppermute | solution.py:142
  18.0 7.6 %collective-permute-start.2 = (f32[136,128]{1,0:T(8,128)S(1)}, f32[136,128]{1,0:T(8,128)S(1)}, u32[]{:S(2)}, u32[]{:S(2)}) collective-permute-start(f32[136,128]{1,0:T(8,128)S(1)} %get-tuple-element.17), channel_id=1, source_target_pairs={{2,0},{4,2},{6,4},{8,6},{10,8},{12,10},{14,12},{16,14},{18,16},{20... | collective-permute-start | bytes 208904 | tf_op jit(solution)/shard_map/ppermute | solution.py:142
  25.7 2.0 %collective-permute-start.5 = (f32[16,8,384]{2,1,0:T(8,128)S(1)}, f32[16,8,384]{2,1,0:T(8,128)S(1)}, u32[]{:S(2)}, u32[]{:S(2)}) collective-permute-start(f32[16,8,384]{2,1,0:T(8,128)S(1)} %shard_map.90.own), channel_id=1, source_target_pairs={{0,96},{1,97},{2,98},{3,99},{4,100},{5,101},{6,102},{7,103},{8,104... | collective-permute-start | bytes 589832 | tf_op jit(solution)/shard_map/ppermute | solution.py:331
  26.4 9.8 %collective-permute-start.6 = (f32[16,8,384]{2,1,0:T(8,128)S(1)}, f32[16,8,384]{2,1,0:T(8,128)S(1)}, u32[]{:S(2)}, u32[]{:S(2)}) collective-permute-start(f32[16,8,384]{2,1,0:T(8,128)S(1)} %shard_map.90.own), channel_id=1, source_target_pairs={{0,192},{1,193},{2,194},{3,195},{4,196},{5,197},{6,198},{7,199},{8... | collective-permute-start | bytes 589832 | tf_op jit(solution)/shard_map/ppermute | solution.py:331
  37.0 5.6 %copy-start.4 = (f32[5,128,384]{2,1,0:T(8,128)S(1)}, f32[5,128,384]{2,1,0:T(8,128)}, u32[]{:S(2)}) copy-start(f32[5,128,384]{2,1,0:T(8,128)} %diff.5) | copy-start | bytes 2949124
  37.0 5.6 %copy-start.7 = (s32[128,384]{1,0:T(8,128)S(1)}, s32[128,384]{1,0:T(8,128)}, u32[]{:S(2)}) copy-start(s32[128,384]{1,0:T(8,128)} %mask.9) | copy-start | bytes 589828
  37.0 5.6 %copy-start.8 = (f32[128,384]{1,0:T(8,128)S(1)}, f32[128,384]{1,0:T(8,128)}, u32[]{:S(2)}) copy-start(f32[128,384]{1,0:T(8,128)} %depth.5) | copy-start | bytes 589828
  37.0 5.6 %copy-start.9 = (f32[128,384]{1,0:T(8,128)S(1)}, f32[128,384]{1,0:T(8,128)}, u32[]{:S(2)}) copy-start(f32[128,384]{1,0:T(8,128)} %rotation.5) | copy-start | bytes 589828
  37.1 5.6 %copy-start = (f32[1,16,128,384]{3,2,1,0:T(8,128)S(1)}, f32[1,16,128,384]{3,2,1,0:T(8,128)}, u32[]{:S(2)}) copy-start(f32[1,16,128,384]{3,2,1,0:T(8,128)} %param.7) | copy-start | bytes 9437188
  37.8 18.1 %collective-permute-start.7 = (f32[16,72,384]{2,1,0:T(8,128)S(1)}, f32[16,72,384]{2,1,0:T(8,128)S(1)}, u32[]{:S(2)}, u32[]{:S(2)}) collective-permute-start(f32[16,72,384]{2,1,0:T(8,128)S(1)} %get-tuple-element.20.gate.refs_1_), channel_id=1, source_target_pairs={{0,96},{64,128},{224,32},{1,97},{65,129},{225,33},{2,98},{66,130},... | collective-permute-start | bytes 5308424 | tf_op jit(solution)/shard_map/ppermute | solution.py:331
  38.7 25.8 %collective-permute-start.8 = (f32[16,72,384]{2,1,0:T(8,128)}, f32[16,72,384]{2,1,0:T(8,128)S(1)}, u32[]{:S(2)}, u32[]{:S(2)}) collective-permute-start(f32[16,72,384]{2,1,0:T(8,128)} %get-tuple-element.22.refs_0_), channel_id=1, source_target_pairs={{0,192},{224,160},{1,193},{225,161},{2,194},{226,162},{3,195},{227... | collective-permute-start | bytes 5308424 | tf_op jit(solution)/shard_map/ppermute | solution.py:331
  40.0 15.9 %collective-permute-start.9 = (f32[16,8,384]{2,1,0:T(8,128)S(1)}, f32[16,8,384]{2,1,0:T(8,128)S(1)}, u32[]{:S(2)}, u32[]{:S(2)}) collective-permute-start(f32[16,8,384]{2,1,0:T(8,128)S(1)} %shard_map.91.gate.refs_4_), channel_id=1, source_target_pairs={{0,32},{96,64},{192,224},{1,33},{97,65},{193,225},{2,34},{98,66},{... | collective-permute-start | bytes 589832 | tf_op jit(solution)/shard_map/ppermute | solution.py:331
  41.3 14.6 %collective-permute-start.10 = (f32[16,8,384]{2,1,0:T(8,128)S(1)}, f32[16,8,384]{2,1,0:T(8,128)S(1)}, u32[]{:S(2)}, u32[]{:S(2)}) collective-permute-start(f32[16,8,384]{2,1,0:T(8,128)S(1)} %shard_map.91.gate.refs_4_), channel_id=1, source_target_pairs={{96,128},{192,160},{97,129},{193,161},{98,130},{194,162},{99,131},... | collective-permute-start | bytes 589832 | tf_op jit(solution)/shard_map/ppermute | solution.py:331
  64.6 7.1 %copy-start.10 = (s32[128,384]{1,0:T(8,128)S(1)}, s32[128,384]{1,0:T(8,128)}, u32[]{:S(2)}) copy-start(s32[128,384]{1,0:T(8,128)} %region.5) | copy-start | bytes 589828
  71.6 1.3 %copy-start.2 = (f32[16,64,384]{2,1,0:T(8,128)}, f32[16,64,384]{2,1,0:T(8,128)S(1)}, u32[]{:S(2)}) copy-start(f32[16,64,384]{2,1,0:T(8,128)S(1)} %shard_map.94.control.mine) | copy-start | bytes 4718596
  71.6 3.5 %collective-permute-start.11 = (f32[16,64,384]{2,1,0:T(8,128)S(1)}, f32[16,64,384]{2,1,0:T(8,128)S(1)}, u32[]{:S(2)}, u32[]{:S(2)}) collective-permute-start(f32[16,64,384]{2,1,0:T(8,128)S(1)} %shard_map.94.control.mine), channel_id=1, source_target_pairs={{0,32},{32,0},{64,96},{96,64},{128,160},{160,128},{192,224},{224,1... | collective-permute-start | bytes 4718600 | tf_op jit(solution)/shard_map/ppermute | solution.py:331
  72.9 14.9 %copy-start.15 = (f32[16]{0:T(128)S(1)}, f32[16]{0:T(128)}, u32[]{:S(2)}) copy-start(f32[16]{0:T(128)} %param.13) | copy-start | bytes 196
  76.4 1.2 %copy-start.5 = (f32[16,64,384]{2,1,0:T(8,128)}, f32[16,64,384]{2,1,0:T(8,128)S(1)}, u32[]{:S(2)}) copy-start(f32[16,64,384]{2,1,0:T(8,128)S(1)} %collective-permute-done.11.control.theirs) | copy-start | bytes 4718596
  77.6 0.6 copy-start.11
  78.3 20.3 %all-to-all-start = ((f32[32,8,128]{2,1,0:T(8,128)}), f32[32,8,128]{2,1,0:T(8,128)S(1)}, u32[]{:S(2)}, u32[]{:S(2)}) async-start(f32[32,8,128]{2,1,0:T(8,128)} %copy-done.11), calls=%async_computation | async-start | bytes 262144 | tf_op jit(solution)/shard_map/all_to_all | solution.py:598
  98.6 1.4 %copy-start.3 = (f32[16,64,384]{2,1,0:T(8,128)S(1)}, f32[16,64,384]{2,1,0:T(8,128)}, u32[]{:S(2)}) copy-start(f32[16,64,384]{2,1,0:T(8,128)} %copy-done.2) | copy-start | bytes 4718596
  100.0 1.4 %copy-start.6 = (f32[16,64,384]{2,1,0:T(8,128)S(1)}, f32[16,64,384]{2,1,0:T(8,128)}, u32[]{:S(2)}) copy-start(f32[16,64,384]{2,1,0:T(8,128)} %copy-done.5) | copy-start | bytes 4718596

commit v11 on v10

--- a/solution.py
+++ b/solution.py
@@ -82,7 +82,7 @@
 LEFT, RIGHT = slice(0, 128), slice(COLS - 128, COLS)
 
 
-def strips_kernel(state, depth, rotation, diff, mask, west, east, lo, hi, land, sem):
+def strips_kernel(state, depth, rotation, diff, mask, both, lo, hi, land, sem):
     full = slice(None)
     cuts = [(lo, (full, LEFT)), (hi, (full, RIGHT))]
     fetch(sources(state, depth, rotation, diff, mask), mask, cuts, land, (full, full), sem)
@@ -91,11 +91,11 @@
     w = e = jnp.zeros((ROWS, 128), F32)
     for k in range(FIELDS):
         w, e = put(k, lo[k], hi[k], w, e)
-    west[...] = w
-    east[...] = e
-
-
-def corners_kernel(lat, rows, west, east, west_out, east_out):
+    both[0] = w
+    both[1] = e
+
+
+def corners_kernel(lat, rows, both, west_out, east_out):
     got = (iota((8, 128), 0) < 4) == (lat[0] == 0)
     w = e = jnp.zeros((8, 128), F32)
     for k in range(FIELDS):
@@ -104,8 +104,8 @@
         if flip:
             a, b = pltpu.roll(a, 4, 0), pltpu.roll(b, 4, 0)
         w, e = put(k, a, b, w, e)
-    west_out[0:ROWS, :] = west[...]
-    east_out[0:ROWS, :] = east[...]
+    west_out[0:ROWS, :] = both[0]
+    east_out[0:ROWS, :] = both[1]
     west_out[ROWS:ROWS_X, :] = jnp.where(got, w, 0.0)
     east_out[ROWS:ROWS_X, :] = jnp.where(got, e, 0.0)
 
@@ -128,16 +128,16 @@
     )(where, state, *statics)
     rows = lax.ppermute(rows, "lat", [(0, 1), (1, 0)])
     strip = pltpu.VMEM((FIELDS, ROWS, 128), F32)
-    west, east = call(
+    both = call(
         strips_kernel,
-        [shape(ROWS, 128)] * 2,
+        shape(2, ROWS, 128),
         [HBM] * 5,
-        [VMEM] * 2,
+        VMEM,
         [strip, strip, pltpu.VMEM((ROWS, COLS), jnp.int32), pltpu.SemaphoreType.DMA((9,))],
         mib=58,
     )(state, *statics)
-    west, east = call(corners_kernel, [shape(ROWS_X, 128)] * 2, [SMEM] + [VMEM] * 3, [VMEM] * 2)(
-        where, rows, west, east
+    west, east = call(corners_kernel, [shape(ROWS_X, 128)] * 2, [SMEM] + [VMEM] * 2, [VMEM] * 2)(
+        where, rows, both
     )
     return lax.ppermute(east, "lon", up), lax.ppermute(west, "lon", down), rows
 
@@ -523,7 +523,7 @@
     )(where, own, control, mask, region, earlier)
 
 
-BLOCK = 4
+BLOCK = 2
 
 
 def final_kernel(where, own, mine, theirs, region, parts, target, out, growth, cell):

time: 106 us -> 108 us (1.019)
  Pallas kernels: 36.2 us -> 38.1 us
    pallas_call x1, Pallas kernels: 4.36 us -> 5.84 us  [rescale(): pl.pallas_call(final_kernel, grid=(CH // BLOCK,), out_shape=[jax.ShapeDty...]
    unnamed x32 -> x30, local copies, waits for them, and re-layouts: 6.36 us -> 5.61 us
where the time goes in v11:
time: 108 us; the launch traced here: 107 us
  Pallas kernels  38.1 us (35%)
  waiting for transfers between devices  32.2 us (30%)
  starting transfers between devices  29.5 us (27%)
  local copies, waits for them, and re-layouts  5.62 us (5%)
    ppermute x9, waiting for transfers between devices, send(): return lax.ppermute(value, 'member', pairs)  19 us
    pallas_call x1, Pallas kernels, own_steps(): call(own_kernel, [jax.ShapeDtypeStruct((CH, ROWS, COLS), F32), jax.ShapeD...  13.5 us
    all_to_all x1, waiting for transfers between devices, per_device(): parts = lax.all_to_all(parts, ('lon', 'lat'), 0, 0)  10.8 us
    all_to_all x1, starting transfers between devices, per_device(): parts = lax.all_to_all(parts, ('lon', 'lat'), 0, 0)  9.97 us
    ppermute x9, starting transfers between devices, send(): return lax.ppermute(value, 'member', pairs)  9.5 us
    pallas_call x1, Pallas kernels, control_steps(): call(control_kernel, jax.ShapeDtypeStruct((CH, HALF, COLS), F32), [SMEM]...  7.18 us
    pallas_call x1, Pallas kernels, rescale(): pl.pallas_call(final_kernel, grid=(CH // BLOCK,), out_shape=[jax.ShapeDty...  5.84 us
    unnamed x30, local copies, waits for them, and re-layouts  5.61 us
  transfers between devices with their start and end apart: 13, of which 6 were waited for; matrix products, arithmetic and copies ran while one was open for 0% of the time, Pallas kernels for 21%

profile of v11, /device:TPU:24, one launch (start us, length us, event | category | flops | bytes accessed | tf_op | source)
XLA Modules:
  0.0 107.1 jit_solution(11201782731945087613)
XLA Ops:
  0.6 0.7 pad_add_fusion.lat.where
  1.3 0.8 shard_map.89
  2.1 0.8 collective-permute-start.3
  2.9 1.9 %collective-permute-start.4 = (f32[16,72,384]{2,1,0:T(8,128)}, f32[16,72,384]{2,1,0:T(8,128)}, u32[]{:S(2)}, u32[]{:S(2)}) collective-permute-start(f32[16,72,384]{2,1,0:T(8,128)} %get-tuple-element.14.u), channel_id=1, source_target_pairs={{0,224},{1,225},{2,226},{3,227},{4,228},{5,229},{6,230},{7,231},{8... | collective-permute-start | bytes 5308424 | tf_op jit(solution)/shard_map/ppermute | solution.py:331
  4.8 2.4 %shard_map.86 = f32[96,384]{1,0:T(8,128)} custom-call(s32[3]{0:T(128)} %pad_add_fusion.lat.where, f32[16,128,384]{2,1,0:T(8,128)} %bitcast.6, f32[128,384]{1,0:T(8,128)} %depth.5, f32[128,384]{1,0:T(8,128)} %rotation.5, f32[5,128,384]{2,1,0:T(8,128)} %diff.5, s32[128,384]{1,0:T(8,128)} %mask.9), custom_call_target="tpu_custom_call" | custom-call | flops 4194304 | bytes 8388608 | tf_op jit(solution)/shard_map/pallas_call | solution.py:121
  7.2 3.1 %collective-permute-start = (f32[96,384]{1,0:T(8,128)}, f32[96,384]{1,0:T(8,128)S(1)}, u32[]{:S(2)}, u32[]{:S(2)}) collective-permute-start(f32[96,384]{1,0:T(8,128)} %shard_map.86), channel_id=1, source_target_pairs={{0,1},{1,0},{2,3},{3,2},{4,5},{5,4},{6,7},{7,6},{8,9},{9,8},{10,11... | collective-permute-start | bytes 442376 | tf_op jit(solution)/shard_map/ppermute | solution.py:129
  10.3 3.7 %shard_map.87.both = f32[2,128,128]{2,1,0:T(8,128)} custom-call(f32[16,128,384]{2,1,0:T(8,128)} %bitcast.7, f32[128,384]{1,0:T(8,128)} %depth.5, f32[128,384]{1,0:T(8,128)} %rotation.5, f32[5,128,384]{2,1,0:T(8,128)} %diff.5, s32[128,384]{1,0:T(8,128)} %mask.9), custom_call_target="tpu_custom_call" | custom-call | flops 4194304 | bytes 8388608 | tf_op jit(solution)/shard_map/pallas_call | solution.py:131
  13.9 0.2 collective-permute-done.rows
  14.1 0.9 copy-done.12
  15.0 0.7 shard_map.88
  15.7 1.6 %collective-permute-start.1 = (f32[136,128]{1,0:T(8,128)S(1)}, f32[136,128]{1,0:T(8,128)S(1)}, u32[]{:S(2)}, u32[]{:S(2)}) collective-permute-start(f32[136,128]{1,0:T(8,128)S(1)} %get-tuple-element.12), channel_id=1, source_target_pairs={{0,2},{2,4},{4,6},{6,8},{8,10},{10,12},{12,14},{14,16},{16,18},{18... | collective-permute-start | bytes 208904 | tf_op jit(solution)/shard_map/ppermute | solution.py:142
  17.2 5.4 %collective-permute-start.2 = (f32[136,128]{1,0:T(8,128)S(1)}, f32[136,128]{1,0:T(8,128)S(1)}, u32[]{:S(2)}, u32[]{:S(2)}) collective-permute-start(f32[136,128]{1,0:T(8,128)S(1)} %get-tuple-element.13), channel_id=1, source_target_pairs={{2,0},{4,2},{6,4},{8,6},{10,8},{12,10},{14,12},{16,14},{18,16},{20... | collective-permute-start | bytes 208904 | tf_op jit(solution)/shard_map/ppermute | solution.py:142
  22.6 2.2 %collective-permute-done.1.fw = f32[136,128]{1,0:T(8,128)S(1)} collective-permute-done((f32[136,128]{1,0:T(8,128)S(1)}, f32[136,128]{1,0:T(8,128)S(1)}, u32[]{:S(2)}, u32[]{:S(2)}) %collective-permute-start.1) | collective-permute-done | bytes 69664 | tf_op jit(solution)/shard_map/ppermute | solution.py:142
  24.8 0.0 collective-permute-done.2.fe
  24.8 0.1 shard_map.90.own
  24.9 0.7 collective-permute-start.5
  25.6 1.3 %collective-permute-start.6 = (f32[16,8,384]{2,1,0:T(8,128)S(1)}, f32[16,8,384]{2,1,0:T(8,128)S(1)}, u32[]{:S(2)}, u32[]{:S(2)}) collective-permute-start(f32[16,8,384]{2,1,0:T(8,128)S(1)} %shard_map.90.own), channel_id=1, source_target_pairs={{0,192},{1,193},{2,194},{3,195},{4,196},{5,197},{6,198},{7,199},{8... | collective-permute-start | bytes 589832 | tf_op jit(solution)/shard_map/ppermute | solution.py:331
  26.9 8.5 %collective-permute-done.6.six = f32[16,8,384]{2,1,0:T(8,128)S(1)} collective-permute-done((f32[16,8,384]{2,1,0:T(8,128)S(1)}, f32[16,8,384]{2,1,0:T(8,128)S(1)}, u32[]{:S(2)}, u32[]{:S(2)}) %collective-permute-start.6) | collective-permute-done | bytes 196640 | tf_op jit(solution)/shard_map/ppermute | solution.py:331
  35.4 0.8 shard_map.91.gate.refs_4_
  36.2 0.0 copy-start.4
  36.2 0.0 copy-start.7
  36.3 0.0 copy-start.8
  36.3 0.0 copy-start.9
  36.3 0.0 collective-permute-done.3.p1
  36.3 0.0 collective-permute-done.4.m1
  36.3 0.0 copy-start
  36.3 0.7 shard_map.92
  37.0 0.9 collective-permute-start.7
  37.9 1.3 %collective-permute-start.8 = (f32[16,72,384]{2,1,0:T(8,128)}, f32[16,72,384]{2,1,0:T(8,128)S(1)}, u32[]{:S(2)}, u32[]{:S(2)}) collective-permute-start(f32[16,72,384]{2,1,0:T(8,128)} %get-tuple-element.18.refs_0_), channel_id=1, source_target_pairs={{0,192},{224,160},{1,193},{225,161},{2,194},{226,162},{3,195},{227... | collective-permute-start | bytes 5308424 | tf_op jit(solution)/shard_map/ppermute | solution.py:331
  39.2 1.3 %collective-permute-start.9 = (f32[16,8,384]{2,1,0:T(8,128)S(1)}, f32[16,8,384]{2,1,0:T(8,128)S(1)}, u32[]{:S(2)}, u32[]{:S(2)}) collective-permute-start(f32[16,8,384]{2,1,0:T(8,128)S(1)} %shard_map.91.gate.refs_4_), channel_id=1, source_target_pairs={{0,32},{96,64},{192,224},{1,33},{97,65},{193,225},{2,34},{98,66},{... | collective-permute-start | bytes 589832 | tf_op jit(solution)/shard_map/ppermute | solution.py:331
  40.6 1.3 %collective-permute-start.10 = (f32[16,8,384]{2,1,0:T(8,128)S(1)}, f32[16,8,384]{2,1,0:T(8,128)S(1)}, u32[]{:S(2)}, u32[]{:S(2)}) collective-permute-start(f32[16,8,384]{2,1,0:T(8,128)S(1)} %shard_map.91.gate.refs_4_), channel_id=1, source_target_pairs={{96,128},{192,160},{97,129},{193,161},{98,130},{194,162},{99,131},... | collective-permute-start | bytes 589832 | tf_op jit(solution)/shard_map/ppermute | solution.py:331
  41.9 13.5 %shard_map.93 = (f32[16,128,384]{2,1,0:T(8,128)S(1)}, f32[8,72,512]{2,1,0:T(8,128)S(1)}) custom-call(s32[3]{0:T(128)S(1)} %copy-done.13, f32[16,128,384]{2,1,0:T(8,128)S(1)} %bitcast.8, f32[128,384]{1,0:T(8,128)S(1)} %copy-done.8, f32[128,384]{1,0:T(8,128)S(1)} %copy-done.9, f32[5,128,384]{2,1,0:T(8,128)S(1)} %copy-done.4, s32[128,384]{1,0:T(8,128)S(1)} %copy-done.7, ...), custom_call_target="tpu_custom_call" | custom-call | flops 268435456 | bytes 8388608 | tf_op jit(solution)/shard_map/pallas_call | solution.py:301
  55.4 0.0 collective-permute-done.10.refs_6_
  55.4 8.4 %collective-permute-done.8.refs_3_ = f32[16,72,384]{2,1,0:T(8,128)S(1)} collective-permute-done((f32[16,72,384]{2,1,0:T(8,128)}, f32[16,72,384]{2,1,0:T(8,128)S(1)}, u32[]{:S(2)}, u32[]{:S(2)}) %collective-permute-start.8) | collective-permute-done | bytes 1769504 | tf_op jit(solution)/shard_map/ppermute | solution.py:331
  63.8 7.2 %shard_map.94.control.mine = f32[16,64,384]{2,1,0:T(8,128)S(1)} custom-call(s32[3]{0:T(128)S(1)} %copy-done.13, f32[16,72,384]{2,1,0:T(8,128)} %get-tuple-element.18.refs_0_, f32[16,72,384]{2,1,0:T(8,128)S(1)} %get-tuple-element.16.gate.refs_1_, f32[16,72,384]{2,1,0:T(8,128)S(1)} %collective-permute-done.7.refs_2_, ...), custom_call_target="tpu_custom_call" | custom-call | flops 134217728 | bytes 8388608 | tf_op jit(solution)/shard_map/pallas_call | solution.py:459
  71.0 0.0 copy-start.2
  71.0 0.1 collective-permute-start.11
  71.1 1.2 %shard_map.95.earlier = f32[8,128]{1,0:T(8,128)S(1)} custom-call(s32[3]{0:T(128)S(1)} %copy-done.13, f32[16,128,384]{2,1,0:T(8,128)S(1)} %get-tuple-element.17.own, f32[16,64,384]{2,1,0:T(8,128)S(1)} %shard_map.94.control.mine, s32[128,384]{1,0:T(8,128)S(1)} %copy-done.7, s32[128,384]{1,0:T(8,128)S(1)} %copy-done.10, f32[8,128]{1,0:T(8,128)S(1)} %broadcast_in_dim.9.earlier), custom_call_target="tpu_custom_call" | custom-call | flops 4194304 | bytes 8388608 | tf_op jit(solution)/shard_map/pallas_call | solution.py:516
  72.3 0.0 copy-start.14
  72.3 2.2 %collective-permute-done.11.control.theirs = f32[16,64,384]{2,1,0:T(8,128)S(1)} collective-permute-done((f32[16,64,384]{2,1,0:T(8,128)S(1)}, f32[16,64,384]{2,1,0:T(8,128)S(1)}, u32[]{:S(2)}, u32[]{:S(2)}) %collective-permute-start.11) | collective-permute-done | bytes 1572896 | tf_op jit(solution)/shard_map/ppermute | solution.py:331
  74.5 1.4 %shard_map.96 = f32[32,8,128]{2,1,0:T(8,128)S(1)} custom-call(s32[3]{0:T(128)S(1)} %copy-done.13, f32[16,128,384]{2,1,0:T(8,128)S(1)} %get-tuple-element.17.own, f32[16,64,384]{2,1,0:T(8,128)S(1)} %collective-permute-done.11.control.theirs, s32[128,384]{1,0:T(8,128)S(1)} %copy-done.7, s32[128,384]{1,0:T(8,128)S(1)} %copy-done.10, f32[8,128]{1,0:T(8,128)S(1)} %shard_map.95.earlier), custom_call_target="tpu_custom_call" | custom-call | flops 4194304 | bytes 8388608 | tf_op jit(solution)/shard_map/pallas_call | solution.py:516
  75.9 1.2 %copy-done.5 = f32[16,64,384]{2,1,0:T(8,128)} copy-done((f32[16,64,384]{2,1,0:T(8,128)}, f32[16,64,384]{2,1,0:T(8,128)S(1)}, u32[]{:S(2)}) %copy-start.5) | copy-done | bytes 1572888
  77.0 0.7 copy-done.11
  77.7 10.0 %all-to-all-start = ((f32[32,8,128]{2,1,0:T(8,128)}), f32[32,8,128]{2,1,0:T(8,128)S(1)}, u32[]{:S(2)}, u32[]{:S(2)}) async-start(f32[32,8,128]{2,1,0:T(8,128)} %copy-done.11), calls=%async_computation | async-start | bytes 262144 | tf_op jit(solution)/shard_map/all_to_all | solution.py:598
  87.7 10.8 %all-to-all-done.parts = f32[32,8,128]{2,1,0:T(8,128)S(1)} async-done(((f32[32,8,128]{2,1,0:T(8,128)}), f32[32,8,128]{2,1,0:T(8,128)S(1)}, u32[]{:S(2)}, u32[]{:S(2)}) %all-to-all-start) | async-done | bytes 131104 | tf_op jit(solution)/shard_map/all_to_all | solution.py:598
  98.5 1.4 %copy-done.3 = f32[16,64,384]{2,1,0:T(8,128)S(1)} copy-done((f32[16,64,384]{2,1,0:T(8,128)S(1)}, f32[16,64,384]{2,1,0:T(8,128)}, u32[]{:S(2)}) %copy-start.3) | copy-done | bytes 1572888
  99.9 1.4 %copy-done.6 = f32[16,64,384]{2,1,0:T(8,128)S(1)} copy-done((f32[16,64,384]{2,1,0:T(8,128)S(1)}, f32[16,64,384]{2,1,0:T(8,128)}, u32[]{:S(2)}) %copy-start.6) | copy-done | bytes 1572888
  101.3 5.8 %shard_map.97 = (f32[16,128,384]{2,1,0:T(8,128)}, f32[1,16]{1,0:T(1,128)}) custom-call(s32[3]{0:T(128)S(1)} %copy-done.13, f32[16,128,384]{2,1,0:T(8,128)S(1)} %get-tuple-element.17.own, f32[16,64,384]{2,1,0:T(8,128)S(1)} %copy-done.3, f32[16,64,384]{2,1,0:T(8,128)S(1)} %copy-done.6, s32[128,384]{1,0:T(8,128)S(1)} %copy-done.10, ...), custom_call_target="tpu_custom_call" | custom-call | flops 4194304 | bytes 10485760 | tf_op jit(solution)/shard_map/pallas_call | solution.py:572
  (24 shorter events, 0.1 us)
Async XLA Ops:
  2.1 34.1 %collective-permute-start.3 = (f32[16,72,384]{2,1,0:T(8,128)}, f32[16,72,384]{2,1,0:T(8,128)S(1)}, u32[]{:S(2)}, u32[]{:S(2)}) collective-permute-start(f32[16,72,384]{2,1,0:T(8,128)} %get-tuple-element.15.v), channel_id=1, source_target_pairs={{0,64},{1,65},{2,66},{3,67},{4,68},{5,69},{6,70},{7,71},{8,72},{9,... | collective-permute-start | bytes 5308424 | tf_op jit(solution)/shard_map/ppermute | solution.py:331
  2.9 33.4 %collective-permute-start.4 = (f32[16,72,384]{2,1,0:T(8,128)}, f32[16,72,384]{2,1,0:T(8,128)}, u32[]{:S(2)}, u32[]{:S(2)}) collective-permute-start(f32[16,72,384]{2,1,0:T(8,128)} %get-tuple-element.14.u), channel_id=1, source_target_pairs={{0,224},{1,225},{2,226},{3,227},{4,228},{5,229},{6,230},{7,231},{8... | collective-permute-start | bytes 5308424 | tf_op jit(solution)/shard_map/ppermute | solution.py:331
  7.2 7.0 %copy-start.13 = (s32[3]{0:T(128)S(1)}, s32[3]{0:T(128)}, u32[]{:S(2)}) copy-start(s32[3]{0:T(128)} %pad_add_fusion.lat.where) | copy-start | bytes 40
  7.2 6.9 %collective-permute-start = (f32[96,384]{1,0:T(8,128)}, f32[96,384]{1,0:T(8,128)S(1)}, u32[]{:S(2)}, u32[]{:S(2)}) collective-permute-start(f32[96,384]{1,0:T(8,128)} %shard_map.86), channel_id=1, source_target_pairs={{0,1},{1,0},{2,3},{3,2},{4,5},{5,4},{6,7},{7,6},{8,9},{9,8},{10,11... | collective-permute-start | bytes 442376 | tf_op jit(solution)/shard_map/ppermute | solution.py:129
  10.3 26.0 %copy-start.1 = (f32[16,72,384]{2,1,0:T(8,128)S(1)}, f32[16,72,384]{2,1,0:T(8,128)}, u32[]{:S(2)}) copy-start(f32[16,72,384]{2,1,0:T(8,128)} %get-tuple-element.14.u) | copy-start | bytes 5308420
  14.1 0.9 copy-start.12
  15.7 9.1 %collective-permute-start.1 = (f32[136,128]{1,0:T(8,128)S(1)}, f32[136,128]{1,0:T(8,128)S(1)}, u32[]{:S(2)}, u32[]{:S(2)}) collective-permute-start(f32[136,128]{1,0:T(8,128)S(1)} %get-tuple-element.12), channel_id=1, source_target_pairs={{0,2},{2,4},{4,6},{6,8},{8,10},{10,12},{12,14},{14,16},{16,18},{18... | collective-permute-start | bytes 208904 | tf_op jit(solution)/shard_map/ppermute | solution.py:142
  17.2 7.6 %collective-permute-start.2 = (f32[136,128]{1,0:T(8,128)S(1)}, f32[136,128]{1,0:T(8,128)S(1)}, u32[]{:S(2)}, u32[]{:S(2)}) collective-permute-start(f32[136,128]{1,0:T(8,128)S(1)} %get-tuple-element.13), channel_id=1, source_target_pairs={{2,0},{4,2},{6,4},{8,6},{10,8},{12,10},{14,12},{16,14},{18,16},{20... | collective-permute-start | bytes 208904 | tf_op jit(solution)/shard_map/ppermute | solution.py:142
  24.9 2.0 %collective-permute-start.5 = (f32[16,8,384]{2,1,0:T(8,128)S(1)}, f32[16,8,384]{2,1,0:T(8,128)S(1)}, u32[]{:S(2)}, u32[]{:S(2)}) collective-permute-start(f32[16,8,384]{2,1,0:T(8,128)S(1)} %shard_map.90.own), channel_id=1, source_target_pairs={{0,96},{1,97},{2,98},{3,99},{4,100},{5,101},{6,102},{7,103},{8,104... | collective-permute-start | bytes 589832 | tf_op jit(solution)/shard_map/ppermute | solution.py:331
  25.6 9.8 %collective-permute-start.6 = (f32[16,8,384]{2,1,0:T(8,128)S(1)}, f32[16,8,384]{2,1,0:T(8,128)S(1)}, u32[]{:S(2)}, u32[]{:S(2)}) collective-permute-start(f32[16,8,384]{2,1,0:T(8,128)S(1)} %shard_map.90.own), channel_id=1, source_target_pairs={{0,192},{1,193},{2,194},{3,195},{4,196},{5,197},{6,198},{7,199},{8... | collective-permute-start | bytes 589832 | tf_op jit(solution)/shard_map/ppermute | solution.py:331
  36.2 5.6 %copy-start.4 = (f32[5,128,384]{2,1,0:T(8,128)S(1)}, f32[5,128,384]{2,1,0:T(8,128)}, u32[]{:S(2)}) copy-start(f32[5,128,384]{2,1,0:T(8,128)} %diff.5) | copy-start | bytes 2949124
  36.2 5.6 %copy-start.7 = (s32[128,384]{1,0:T(8,128)S(1)}, s32[128,384]{1,0:T(8,128)}, u32[]{:S(2)}) copy-start(s32[128,384]{1,0:T(8,128)} %mask.9) | copy-start | bytes 589828
  36.3 5.6 %copy-start.8 = (f32[128,384]{1,0:T(8,128)S(1)}, f32[128,384]{1,0:T(8,128)}, u32[]{:S(2)}) copy-start(f32[128,384]{1,0:T(8,128)} %depth.5) | copy-start | bytes 589828
  36.3 5.6 %copy-start.9 = (f32[128,384]{1,0:T(8,128)S(1)}, f32[128,384]{1,0:T(8,128)}, u32[]{:S(2)}) copy-start(f32[128,384]{1,0:T(8,128)} %rotation.5) | copy-start | bytes 589828
  36.3 5.6 %copy-start = (f32[1,16,128,384]{3,2,1,0:T(8,128)S(1)}, f32[1,16,128,384]{3,2,1,0:T(8,128)}, u32[]{:S(2)}) copy-start(f32[1,16,128,384]{3,2,1,0:T(8,128)} %param.7) | copy-start | bytes 9437188
  37.0 18.4 %collective-permute-start.7 = (f32[16,72,384]{2,1,0:T(8,128)S(1)}, f32[16,72,384]{2,1,0:T(8,128)S(1)}, u32[]{:S(2)}, u32[]{:S(2)}) collective-permute-start(f32[16,72,384]{2,1,0:T(8,128)S(1)} %get-tuple-element.16.gate.refs_1_), channel_id=1, source_target_pairs={{0,96},{64,128},{224,32},{1,97},{65,129},{225,33},{2,98},{66,130},... | collective-permute-start | bytes 5308424 | tf_op jit(solution)/shard_map/ppermute | solution.py:331
  37.9 25.8 %collective-permute-start.8 = (f32[16,72,384]{2,1,0:T(8,128)}, f32[16,72,384]{2,1,0:T(8,128)S(1)}, u32[]{:S(2)}, u32[]{:S(2)}) collective-permute-start(f32[16,72,384]{2,1,0:T(8,128)} %get-tuple-element.18.refs_0_), channel_id=1, source_target_pairs={{0,192},{224,160},{1,193},{225,161},{2,194},{226,162},{3,195},{227... | collective-permute-start | bytes 5308424 | tf_op jit(solution)/shard_map/ppermute | solution.py:331
  39.2 16.2 %collective-permute-start.9 = (f32[16,8,384]{2,1,0:T(8,128)S(1)}, f32[16,8,384]{2,1,0:T(8,128)S(1)}, u32[]{:S(2)}, u32[]{:S(2)}) collective-permute-start(f32[16,8,384]{2,1,0:T(8,128)S(1)} %shard_map.91.gate.refs_4_), channel_id=1, source_target_pairs={{0,32},{96,64},{192,224},{1,33},{97,65},{193,225},{2,34},{98,66},{... | collective-permute-start | bytes 589832 | tf_op jit(solution)/shard_map/ppermute | solution.py:331
  40.6 14.9 %collective-permute-start.10 = (f32[16,8,384]{2,1,0:T(8,128)S(1)}, f32[16,8,384]{2,1,0:T(8,128)S(1)}, u32[]{:S(2)}, u32[]{:S(2)}) collective-permute-start(f32[16,8,384]{2,1,0:T(8,128)S(1)} %shard_map.91.gate.refs_4_), channel_id=1, source_target_pairs={{96,128},{192,160},{97,129},{193,161},{98,130},{194,162},{99,131},... | collective-permute-start | bytes 589832 | tf_op jit(solution)/shard_map/ppermute | solution.py:331
  63.8 7.3 %copy-start.10 = (s32[128,384]{1,0:T(8,128)S(1)}, s32[128,384]{1,0:T(8,128)}, u32[]{:S(2)}) copy-start(s32[128,384]{1,0:T(8,128)} %region.5) | copy-start | bytes 589828
  71.0 1.3 %copy-start.2 = (f32[16,64,384]{2,1,0:T(8,128)}, f32[16,64,384]{2,1,0:T(8,128)S(1)}, u32[]{:S(2)}) copy-start(f32[16,64,384]{2,1,0:T(8,128)S(1)} %shard_map.94.control.mine) | copy-start | bytes 4718596
  71.0 3.5 %collective-permute-start.11 = (f32[16,64,384]{2,1,0:T(8,128)S(1)}, f32[16,64,384]{2,1,0:T(8,128)S(1)}, u32[]{:S(2)}, u32[]{:S(2)}) collective-permute-start(f32[16,64,384]{2,1,0:T(8,128)S(1)} %shard_map.94.control.mine), channel_id=1, source_target_pairs={{0,32},{32,0},{64,96},{96,64},{128,160},{160,128},{192,224},{224,1... | collective-permute-start | bytes 4718600 | tf_op jit(solution)/shard_map/ppermute | solution.py:331
  72.3 15.4 %copy-start.14 = (f32[16]{0:T(128)S(1)}, f32[16]{0:T(128)}, u32[]{:S(2)}) copy-start(f32[16]{0:T(128)} %param.13) | copy-start | bytes 196
  75.8 1.2 %copy-start.5 = (f32[16,64,384]{2,1,0:T(8,128)}, f32[16,64,384]{2,1,0:T(8,128)S(1)}, u32[]{:S(2)}) copy-start(f32[16,64,384]{2,1,0:T(8,128)S(1)} %collective-permute-done.11.control.theirs) | copy-start | bytes 4718596
  77.0 0.7 copy-start.11
  77.7 20.8 %all-to-all-start = ((f32[32,8,128]{2,1,0:T(8,128)}), f32[32,8,128]{2,1,0:T(8,128)S(1)}, u32[]{:S(2)}, u32[]{:S(2)}) async-start(f32[32,8,128]{2,1,0:T(8,128)} %copy-done.11), calls=%async_computation | async-start | bytes 262144 | tf_op jit(solution)/shard_map/all_to_all | solution.py:598
  98.5 1.4 %copy-start.3 = (f32[16,64,384]{2,1,0:T(8,128)S(1)}, f32[16,64,384]{2,1,0:T(8,128)}, u32[]{:S(2)}) copy-start(f32[16,64,384]{2,1,0:T(8,128)} %copy-done.2) | copy-start | bytes 4718596
  99.9 1.4 %copy-start.6 = (f32[16,64,384]{2,1,0:T(8,128)S(1)}, f32[16,64,384]{2,1,0:T(8,128)}, u32[]{:S(2)}) copy-start(f32[16,64,384]{2,1,0:T(8,128)} %copy-done.5) | copy-start | bytes 4718596
